TPU v7x, 32 devices: a whole 2x2x4 slice. The times are simulated.
32 devices in a mesh: face: 8 (over z, y), elem: 4 (over x, core).
Axes of the slice: x: 2, y: 2, z: 4, core: 2. Of those that a mesh axis runs over, the one named last changes fastest.
Arguments:
- trace_old: bfloat16 [2048, 128], P(('face', 'elem')), may hold values from -1.5 to 1.5
- new_owner: int32 [2048, 1], P(('face', 'elem')), may hold values from 0 to 7; in each aligned block of 64 rows (0 to 63, 64 to 127, ...) at most 16 rows name the same one
- mortar_tiles: bfloat16 [3072, 6144], P(('face', 'elem')), may hold values from -0.625 to 0.625
- mortar_owner: int32 [3072, 1], P(('face', 'elem')), may hold values from 0 to 7; in each aligned block of 96 rows (0 to 95, 96 to 191, ...) at most 24 rows name the same one
- mortar_coarse: int32 [3072], P(('face', 'elem')), may hold values from 0 to 15
- interior_rhs: bfloat16 [288, 512], P(('face', 'elem')), may hold values from -1.5 to 1.5
- local_inverse: bfloat16 [288, 512, 512], P(('face', 'elem')), may hold values from -0.25 to 0.25
- coupling: bfloat16 [288, 512, 384], P(('face', 'elem')), may hold values from -1.1953125 to 1.1953125
- connectivity: int32 [288, 3], P(('face', 'elem')), may hold values from 0 to 511
Outputs:
- schur_blocks: bfloat16 [288, 384, 384], P(('face', 'elem'))
- slot_residual: float32 [4096, 128], P(('face', 'elem'))
- coarse_blocks: float32 [512, 4096], P(('face', 'elem'))
Inputs may be any that keep to these rules, and one draw needn't show every extreme that they name: `new_owner`: in each aligned block of 64 rows no owner is named by more than 16 rows, a bound that some block reaches. `mortar_owner`: in each aligned block of 96 rows no owner is named by more than 24 rows, a bound that some block reaches.
All inputs are finite; a program needn't handle non-finite values.
Results may differ from a plain program's by a relative error of at most 0.0075.
Values may be sent and summed in bfloat16 or wider, within the bound.
No kernel may reach another device: no remote copies, remote signals or barrier semaphores. Data moves between devices by JAX's collectives and lax.ppermute only.
A program may use at most 64 MiB of HBM per device.

v0:
```python
import jax
import jax.numpy as jnp
from jax import lax
from jax.sharding import PartitionSpec as P

FACE_COEFFS = 128
FACES_PER_ELEM = 3
MROW = 64
MCOL = 96
NC = 16


def place_matrix(owners, owner_count, capacity):
    slots_all = jnp.arange(owner_count, dtype=jnp.int32)
    onehot = (owners[:, None] == slots_all[None, :]).astype(jnp.int32)
    ranks = jnp.cumsum(onehot, axis=0) - onehot
    my_rank = jnp.sum(ranks * onehot, axis=1)
    target = owners * capacity + my_rank
    buffer_slots = jnp.arange(owner_count * capacity, dtype=jnp.int32)
    return buffer_slots[:, None] == target[None, :]


def shards(
    trace_old,
    new_owner,
    mortar_tiles,
    mortar_owner,
    mortar_coarse,
    interior_rhs,
    local_inverse,
    coupling,
    connectivity,
):
    face_count = lax.axis_size("face")
    row_count = trace_old.shape[0]
    tile_count = mortar_tiles.shape[0]
    elements = interior_rhs.shape[0]
    capacity = max(2, 2 * row_count // face_count)
    tile_capacity = max(2, 2 * tile_count // face_count)
    trace_place = place_matrix(new_owner[:, 0], face_count, capacity)
    trace_buffer = jnp.dot(
        trace_place.astype(jnp.bfloat16), trace_old, preferred_element_type=jnp.float32
    )
    trace_buffer = trace_buffer.astype(jnp.bfloat16).reshape(face_count, capacity, FACE_COEFFS)
    tile_place = place_matrix(mortar_owner[:, 0], face_count, tile_capacity)
    coarse_buffer = jnp.sum(tile_place.astype(jnp.int32) * mortar_coarse[None, :], axis=1).reshape(
        face_count, tile_capacity
    )
    received = lax.all_to_all(trace_buffer, "face", split_axis=0, concat_axis=0, tiled=True)
    tile_buffer = jnp.dot(
        tile_place.astype(jnp.bfloat16), mortar_tiles, preferred_element_type=jnp.float32
    )
    tile_buffer = tile_buffer.astype(jnp.bfloat16).reshape(face_count, tile_capacity, MROW * MCOL)
    tiles_in, coarse_in = (
        lax.all_to_all(tile_buffer, "face", split_axis=0, concat_axis=0, tiled=True),
        lax.all_to_all(coarse_buffer, "face", split_axis=0, concat_axis=0, tiled=True),
    )
    tile_mats = tiles_in.reshape(face_count * tile_capacity, MROW, MCOL)
    gram_blocks = jnp.einsum(
        "tmn,tkn->tmk", tile_mats, tile_mats, preferred_element_type=jnp.float32
    )
    gram_blocks = gram_blocks.reshape(face_count * tile_capacity, MROW * MROW)
    weights = jnp.einsum(
        "eik,ekt->eit", local_inverse, coupling, preferred_element_type=jnp.float32
    ).astype(jnp.bfloat16)
    schur_blocks = (
        -jnp.einsum("eit,eiu->etu", coupling, weights, preferred_element_type=jnp.float32)
    ).astype(jnp.bfloat16)
    solved_rhs = jnp.einsum(
        "eik,ek->ei", local_inverse, interior_rhs, preferred_element_type=jnp.float32
    )
    coarse_ids = jnp.arange(NC, dtype=jnp.int32)
    coarse_hot = (coarse_ids[:, None] == coarse_in.reshape(-1)[None, :]).astype(jnp.float32)
    coarse_blocks = jnp.dot(coarse_hot, gram_blocks, precision=lax.Precision.HIGHEST)
    own_rows = received.reshape(face_count * capacity, FACE_COEFFS)
    trace_table = lax.all_gather(own_rows, "elem", axis=0, tiled=True)
    lam_rows = jnp.take(trace_table, connectivity.reshape(-1), axis=0).reshape(
        elements, FACES_PER_ELEM * FACE_COEFFS
    )
    interior = solved_rhs - jnp.einsum(
        "eit,et->ei", weights, lam_rows, preferred_element_type=jnp.float32
    )
    interior = interior.astype(jnp.bfloat16)
    element_share = jnp.einsum("eit,ei->et", coupling, interior, preferred_element_type=jnp.float32)
    element_share = element_share.reshape(elements * FACES_PER_ELEM, FACE_COEFFS)
    slot_ids = jnp.arange(trace_table.shape[0], dtype=jnp.int32)
    slot_hot = (slot_ids[:, None] == connectivity.reshape(-1)[None, :]).astype(jnp.float32)
    partial_sums = jnp.dot(slot_hot, element_share, precision=lax.Precision.HIGHEST)
    assembled_matrix = lax.psum_scatter(
        partial_sums.astype(jnp.bfloat16), "elem", scatter_dimension=0, tiled=True
    ).astype(jnp.float32)
    slot_residual = own_rows.astype(jnp.float32) - assembled_matrix
    return (schur_blocks, slot_residual, coarse_blocks)


def solution(mesh):
    return jax.shard_map(
        shards,
        mesh=mesh,
        in_specs=(
            P(("face", "elem"), None),
            P(("face", "elem"), None),
            P(("face", "elem"), None),
            P(("face", "elem"), None),
            P(("face", "elem")),
            P(("face", "elem"), None),
            P(("face", "elem"), None, None),
            P(("face", "elem"), None, None),
            P(("face", "elem"), None),
        ),
        out_specs=(
            P(("face", "elem"), None, None),
            P(("face", "elem"), None),
            P(("face", "elem"), None),
        ),
        check_vma=False,
    )
```

profile of v0, /device:TPU:0, one launch (start us, length us, event | category | flops | bytes accessed | tf_op | source)
XLA Modules:
  0.0 127.8 jit_solution(16499144941029283139)
XLA Ops:
  7.2 1.5 %fusion.3 = s32[96,8]{1,0:T(8,128)} fusion(s32[96]{0:T(128)} %bitcast.54), kind=kLoop, calls=%fused_computation.16 | loop fusion | flops 1536 | bytes 3456 | tf_op jit(solution)/shard_map/convert_element_type | solution.py:15
  8.7 1.5 %reduce_window_sum.23 = s32[96,8]{1,0:T(8,128)} reduce-window(s32[96,8]{1,0:T(8,128)} %fusion.3, s32[]{:T(128)} %constant.25.clone.1), window={size=96x1 pad=95_0x0_0}, to_apply=%region_3.4 | reduce-window | flops 72960 | bytes 6148 | tf_op jit(solution)/shard_map/jit(cumsum)/reduce_window_sum | solution.py:16
  13.3 7.3 %all-to-all-start.1 = ((s32[8,1,24]{2,1,0:T(1,128)}), s32[8,1,24]{2,1,0:T(1,128)S(1)}, u32[]{:S(2)}, u32[]{:S(2)}) async-start(s32[8,1,24]{2,1,0:T(1,128)} %all_to_all.13), calls=%async_computation.2 | async-start | bytes 8192 | tf_op jit(solution)/shard_map/all_to_all | solution.py:56
  20.6 1.3 %fusion.6 = s32[64,8]{1,0:T(8,128)} fusion(s32[64]{0:T(128)} %bitcast.56), kind=kLoop, calls=%fused_computation.22 | loop fusion | flops 1024 | bytes 2304 | tf_op jit(solution)/shard_map/convert_element_type | solution.py:15
  22.0 1.4 %reduce_window_sum.22 = s32[64,8]{1,0:T(8,128)} reduce-window(s32[64,8]{1,0:T(8,128)} %fusion.6, s32[]{:T(128)} %constant.25.clone.1), window={size=64x1 pad=63_0x0_0}, to_apply=%region_0.0 | reduce-window | flops 32256 | bytes 4100 | tf_op jit(solution)/shard_map/jit(cumsum)/reduce_window_sum | solution.py:16
  25.0 1.5 %convolution_convert_fusion.3 = bf16[128,128]{1,0:T(8,128)(2,1)} fusion(bf16[64,128]{1,0:T(8,128)(2,1)} %param.9, s32[64]{0:T(128)S(1)} %multiply_add_fusion.1), kind=kOutput, calls=%fused_computation.6 | convolution fusion | flops 2121728 | bytes 49408 | tf_op jit(solution)/shard_map/dot_general | solution.py:41
  27.0 5.5 %all-to-all-start = ((bf16[8,16,128]{2,1,0:T(8,128)(2,1)}), bf16[8,16,128]{2,1,0:T(8,128)(2,1)}, u32[]{:S(2)}, u32[]{:S(2)}) async-start(bf16[8,16,128]{2,1,0:T(8,128)(2,1)} %bitcast.49), calls=%async_computation | async-start | bytes 65536 | tf_op jit(solution)/shard_map/all_to_all | solution.py:49
  32.5 3.4 %convolution_convert_fusion = bf16[192,6144]{1,0:T(8,128)(2,1)} fusion(bf16[96,6144]{1,0:T(8,128)(2,1)} %param.11, s32[96]{0:T(128)S(1)} %multiply_add_fusion), kind=kOutput, calls=%fused_computation.1 | convolution fusion | flops 227690496 | bytes 3539328 | tf_op jit(solution)/shard_map/dot_general | solution.py:50
  35.9 3.4 %all-to-all-done = bf16[8,16,128]{2,1,0:T(8,128)(2,1)} async-done(((bf16[8,16,128]{2,1,0:T(8,128)(2,1)}), bf16[8,16,128]{2,1,0:T(8,128)(2,1)}, u32[]{:S(2)}, u32[]{:S(2)}) %all-to-all-start) | async-done | bytes 32800 | tf_op jit(solution)/shard_map/all_to_all | solution.py:49
  39.3 4.4 %all-to-all-start.2 = ((bf16[8,24,6144]{2,1,0:T(8,128)(2,1)}), bf16[8,24,6144]{2,1,0:T(8,128)(2,1)}, u32[]{:S(2)}, u32[]{:S(2)}) async-start(bf16[8,24,6144]{2,1,0:T(8,128)(2,1)} %bitcast.48), calls=%async_computation.3 | async-start | bytes 4718592 | tf_op jit(solution)/shard_map/all_to_all | solution.py:55
  45.3 4.3 %fusion.9 = f32[9,1,512]{2,1,0:T(1,128)} fusion(bf16[9,512,512]{2,1,0:T(8,128)(2,1)} %param.15, bf16[9,512,1]{1,0,2:T(8,128)(2,1)} %bitcast.53), kind=kOutput, calls=%fused_computation.26 | convolution fusion | flops 4718592 | bytes 4746240 | tf_op jit(solution)/shard_map/eik,ek->ei/dot_general | solution.py:69
  49.6 6.7 %convolution_convert_fusion.1 = bf16[9,512,384]{2,1,0:T(8,128)(2,1)} fusion(bf16[9,512,512]{2,1,0:T(8,128)(2,1)} %param.15, bf16[9,512,384]{2,1,0:T(8,128)(2,1)S(1)} %copy-done), kind=kOutput, calls=%fused_computation.4 | convolution fusion | flops 1813708800 | bytes 11796480 | tf_op jit(solution)/shard_map/eik,ekt->eit/dot_general | solution.py:63
  56.3 7.1 %all_gather.3 = bf16[512,128]{1,0:T(8,128)(2,1)} all-gather(bf16[128,128]{1,0:T(8,128)(2,1)} %bitcast.3), channel_id=1, replica_groups=mesh['face'=8,'elem'=4] {'elem'}, dimensions={0}, use_global_device_ids=true | all-gather | bytes 163840 | tf_op jit(solution)/shard_map/all_gather | solution.py:76
  63.4 2.1 %gather_fusion = bf16[27,128]{1,0:T(8,128)(2,1)} fusion(bf16[512,128]{1,0:T(8,128)(2,1)} %all_gather.3, s32[1024]{0:T(1024)S(1)} %pad_clamp_fusion), kind=kCustom, calls=%fused_computation | custom fusion | bytes 13932 | tf_op jit(solution)/shard_map/jit(_take)/gather | solution.py:77
  66.9 3.0 %fusion.13 = f32[9,1,512]{2,1,0:T(1,128)S(1)} fusion(bf16[9,512,384]{2,1,0:T(8,128)(2,1)} %convolution_convert_fusion.1, bf16[9,384,1]{1,0,2:T(8,128)(2,1)S(1)} %select_bitcast_fusion), kind=kOutput, calls=%fused_computation.31 | convolution fusion | flops 3538944 | bytes 3564288 | tf_op jit(solution)/shard_map/eit,et->ei/dot_general | solution.py:80
  71.9 1.5 %convolution_convert_fusion.2 = bf16[512,128]{1,0:T(8,128)(2,1)} fusion(f32[27,128]{1,0:T(8,128)S(1)} %reshape.92, s32[27]{0:T(128)} %eq.89), kind=kOutput, calls=%fused_computation.5 | convolution fusion | flops 21313024 | bytes 145004 | tf_op jit(solution)/shard_map/dot_general | solution.py:88
  73.4 5.6 %fusion = bf16[9,384,384]{1,2,0:T(8,128)(2,1)} fusion(bf16[9,512,384]{2,1,0:T(8,128)(2,1)} %convolution_convert_fusion.1, bf16[9,512,384]{2,1,0:T(8,128)(2,1)S(1)} %copy-done), kind=kOutput, calls=%fused_computation.3 | convolution fusion | flops 1361608704 | bytes 9732096 | tf_op jit(solution)/shard_map/eit,eiu->etu/dot_general | solution.py:67
  79.1 5.2 %copy.28 = bf16[9,384,384]{2,1,0:T(8,128)(2,1)} copy(bf16[9,384,384]{1,2,0:T(8,128)(2,1)} %fusion) | data formatting | bytes 5308416
  85.6 8.1 %reduce-scatter.2.cloned.1.call-done = bf16[128,128]{1,0:T(8,128)(2,1)} async-done(((bf16[512,128]{1,0:T(8,128)(2,1)}), bf16[128,128]{1,0:T(8,128)(2,1)}) %reduce-scatter.2.cloned.1.call-update) | async-done | bytes 32784 | tf_op jit(solution)/shard_map/reduce_scatter | solution.py:89
  93.6 1.4 %convert_subtract_fusion = f32[128,128]{1,0:T(8,128)} fusion(bf16[128,128]{1,0:T(8,128)(2,1)} %reduce-scatter.2.cloned.1.call-done, bf16[8,16,128]{2,1,0:T(8,128)(2,1)} %all-to-all-done), kind=kLoop, calls=%fused_computation.11 | loop fusion | flops 49152 | bytes 131072 | tf_op jit(solution)/shard_map/sub | solution.py:92
  95.8 6.3 %reshape.94 = bf16[192,64,96]{2,1,0:T(8,128)(2,1)} reshape(bf16[8,24,6144]{2,1,0:T(8,128)(2,1)} %all-to-all-done.2) | data formatting | bytes 4718592 | tf_op jit(solution)/shard_map/reshape | solution.py:58
  102.1 7.3 %fusion.17 = f32[192,64,64]{2,1,0:T(8,128)} fusion(bf16[192,64,96]{2,1,0:T(8,128)(2,1)} %reshape.94), kind=kOutput, calls=%fused_computation.42 | convolution fusion | flops 150994944 | bytes 5505024 | tf_op jit(solution)/shard_map/tmn,tkn->tmk/dot_general | solution.py:59
  109.3 6.7 %copy.27 = f32[192,64,64]{0,2,1:T(8,128)} copy(f32[192,64,64]{2,1,0:T(8,128)} %fusion.17) | data formatting | bytes 6291456 | tf_op jit(solution)/shard_map/tmn,tkn->tmk/dot_general | solution.py:59
  116.0 4.9 %fusion.12 = f32[16,4096]{1,0:T(8,128)} fusion(f32[192,4096]{0,1:T(8,128)} %bitcast.47, s32[192]{0:T(256)S(1)} %eq.99), kind=kOutput, calls=%fused_computation.30 | convolution fusion | flops 150998016 | bytes 3408640 | tf_op jit(solution)/shard_map/dot_general | solution.py:74
  (39 shorter events, 12.3 us)
Async XLA Ops:
  7.2 42.4 %copy-start = (bf16[9,512,384]{2,1,0:T(8,128)(2,1)S(1)}, bf16[9,512,384]{2,1,0:T(8,128)(2,1)}, u32[]{:S(2)}) copy-start(bf16[9,512,384]{2,1,0:T(8,128)(2,1)} %param.16) | copy-start | bytes 10616836
  13.3 13.7 %all-to-all-start.1 = ((s32[8,1,24]{2,1,0:T(1,128)}), s32[8,1,24]{2,1,0:T(1,128)S(1)}, u32[]{:S(2)}, u32[]{:S(2)}) async-start(s32[8,1,24]{2,1,0:T(1,128)} %all_to_all.13), calls=%async_computation.2 | async-start | bytes 8192 | tf_op jit(solution)/shard_map/all_to_all | solution.py:56
  27.0 12.3 %copy-start.2 = (s32[8,1,24]{2,1,0:T(1,128)}, s32[8,1,24]{2,1,0:T(1,128)S(1)}, u32[]{:S(2)}) copy-start(s32[8,1,24]{2,1,0:T(1,128)S(1)} %all-to-all-done.1) | copy-start | bytes 2308
  27.0 12.3 %all-to-all-start = ((bf16[8,16,128]{2,1,0:T(8,128)(2,1)}), bf16[8,16,128]{2,1,0:T(8,128)(2,1)}, u32[]{:S(2)}, u32[]{:S(2)}) async-start(bf16[8,16,128]{2,1,0:T(8,128)(2,1)} %bitcast.49), calls=%async_computation | async-start | bytes 65536 | tf_op jit(solution)/shard_map/all_to_all | solution.py:49
  32.5 11.2 %copy-start.4 = (s32[9,3]{0,1:T(4,128)S(1)}, s32[9,3]{0,1:T(4,128)}, u32[]{:S(2)}) copy-start(s32[9,3]{0,1:T(4,128)} %param.17) | copy-start | bytes 328
  39.3 56.5 %all-to-all-start.2 = ((bf16[8,24,6144]{2,1,0:T(8,128)(2,1)}), bf16[8,24,6144]{2,1,0:T(8,128)(2,1)}, u32[]{:S(2)}, u32[]{:S(2)}) async-start(bf16[8,24,6144]{2,1,0:T(8,128)(2,1)} %bitcast.48), calls=%async_computation.3 | async-start | bytes 4718592 | tf_op jit(solution)/shard_map/all_to_all | solution.py:55
  43.6 50.0 %reduce-scatter.2.cloned.1.call-start = ((), (), s32[]{:S(2)}) async-start(), calls=%async_computation.4 | async-start | bytes 163840 | tf_op jit(solution)/shard_map/reduce_scatter | solution.py:89
  66.2 3.7 %copy-start.1 = (f32[9,1,512]{2,1,0:T(1,128)S(1)}, f32[9,1,512]{2,1,0:T(1,128)}, u32[]{:S(2)}) copy-start(f32[9,1,512]{2,1,0:T(1,128)} %fusion.9) | copy-start | bytes 55300
  79.1 5.7 %copy-start.3 = (s32[8,1,24]{2,1,0:T(1,128)S(1)}, s32[8,1,24]{2,1,0:T(1,128)}, u32[]{:S(2)}) copy-start(s32[8,1,24]{2,1,0:T(1,128)} %copy-done.2) | copy-start | bytes 2308
Sparse Core Ops, SparseCore 0:
  73.5 20.0 reduce-scatter.1
where the time goes:
time: 129 us; the launch traced here: 128 us
  matrix products  38.8 us (30%)
  local copies, waits for them, and re-layouts  25.3 us (20%)
  starting transfers between devices  17.2 us (13%)
  between operations  14.1 us (11%)
  other arithmetic  12.7 us (10%)
  waiting for transfers between devices  12.7 us (10%)
  blocking collectives  7.06 us (5%)
    reduce_scatter x1, waiting for transfers between devices, shards(): lax.psum_scatter(partial_sums.astype(jnp.bfloat16), 'elem', scatter_dimen...  8.08 us
    all_to_all x1, starting transfers between devices, shards(): lax.all_to_all(coarse_buffer, 'face', split_axis=0, concat_axis=0, tiled=...  7.28 us
    dot_general x1, matrix products, shards(): jnp.einsum('tmn,tkn->tmk', tile_mats, tile_mats, preferred_element_type=j...  7.26 us
    all_gather x1, blocking collectives, shards(): trace_table = lax.all_gather(own_rows, 'elem', axis=0, tiled=True)  7.06 us
    dot_general x1, matrix products, shards(): jnp.einsum('eik,ekt->eit', local_inverse, coupling, preferred_element_typ...  6.72 us
    dot_general x1, local copies, waits for them, and re-layouts, shards(): jnp.einsum('tmn,tkn->tmk', tile_mats, tile_mats, preferred_element_type=j...  6.7 us
    reshape x1, local copies, waits for them, and re-layouts, shards(): tile_mats = tiles_in.reshape(face_count * tile_capacity, MROW, MCOL)  6.3 us
    unnamed x14, local copies, waits for them, and re-layouts  5.96 us
  transfers between devices with their start and end apart: 4, of which 4 were waited for; matrix products, arithmetic and copies ran while one was open for 36% of the time, Pallas kernels for 0%

commit v1 on v0

v1 whole, which is shorter than its diff:
```python
import functools

import jax
import jax.numpy as jnp
from jax import lax
from jax.experimental import pallas as pl
from jax.experimental.pallas import tpu as pltpu
from jax.sharding import PartitionSpec as P

FACE_COEFFS = 128
FACES_PER_ELEM = 3
MROW = 64
MCOL = 96
NC = 16
HALF = MROW // 2
LANES = 128
DENSE = HALF * MROW // LANES
OWNER_ROWS = NC * (DENSE + 1)
SHARE_ROWS = 32
SLOT_BASE = 16

BF16 = jnp.bfloat16
F32 = jnp.float32
I32 = jnp.int32

NT = (((1,), (1,)), ((), ()))
TN = (((0,), (0,)), ((), ()))


def iota(shape, dim):
    return lax.broadcasted_iota(I32, shape, dim)


def dot(left, right, dims=(((1,), (0,)), ((), ()))):
    return lax.dot_general(left, right, dims, preferred_element_type=F32)


def place_kernel(elem_count, face_count, capacity, owner_ref, trace_ref, out_ref):
    owners = owner_ref[...]
    rows = owners.shape[1]
    hot = (iota((face_count, rows), 0) == owners).astype(F32)
    earlier = (iota((rows, rows), 0) < iota((rows, rows), 1)).astype(BF16)
    rank = jnp.sum(hot * dot(hot.astype(BF16), earlier), axis=0, keepdims=True).astype(I32)
    target = owners * capacity + rank
    slots = out_ref.shape[0]
    block = iota((slots, rows), 0)
    owner_of = block // (elem_count * capacity)
    wanted = owner_of * capacity + lax.rem(block, capacity)
    place = (wanted == target).astype(BF16)
    out_ref[...] = dot(place, trace_ref[...]).astype(BF16)


def gram_kernel(pairs_at_once, owner_ref, coarse_ref, tiles_ref, out_ref, rows_ref, acc_ref):
    tiles = tiles_ref.shape[0]
    acc_ref[...] = jnp.zeros_like(acc_ref)
    lane = iota((tiles, LANES), 1)
    inside = lane < MCOL
    for group in range(MROW // 4):
        base = group * 3 * LANES
        one, two, three = (
            tiles_ref[:, base + k * LANES : base + (k + 1) * LANES].astype(F32) for k in range(3)
        )
        rolled = (
            one,
            pltpu.roll(jnp.where(lane < 64, two, one), 32, 1),
            pltpu.roll(jnp.where(lane < 32, three, two), 64, 1),
            pltpu.roll(three, 96, 1),
        )
        for k in range(4):
            rows_ref[pl.ds(4 * group + k, tiles, stride=MROW), :] = jnp.where(
                inside, rolled[k], 0.0
            )

    row = iota((HALF, LANES), 0)
    column = lax.rem(iota((HALF, LANES), 1), MROW)
    swapped = (column > row) & (column < HALF)
    diagonal = column == row
    low = iota((DENSE, LANES), 1) < MROW
    low_wide = iota((MROW, LANES), 1) < MROW
    low_row = iota((1, LANES), 1) < MROW

    def step(index, carry):
        for k in range(pairs_at_once):
            pair = index * pairs_at_once + k
            start = pl.multiple_of(pair * LANES, LANES)
            both = rows_ref[pl.ds(start, LANES), :].astype(BF16)
            gram = dot(both, both, NT)
            side = jnp.where(low_wide, gram[:MROW], gram[MROW:])
            lower = pltpu.roll(side[HALF:], LANES - HALF, 1)
            packed = jnp.where(swapped, lower, side[:HALF])
            diag = jnp.sum(jnp.where(diagonal, lower, 0.0), axis=0, keepdims=True)
            turned = pltpu.roll(packed, MROW, 1)
            first = jnp.where(low, packed[:DENSE], turned[DENSE:])
            second = jnp.where(low, turned[:DENSE], packed[DENSE:])
            for tile, dense, own in ((0, first, low_row), (1, second, ~low_row)):
                owner = owner_ref[2 * pair + tile]
                coarse = coarse_ref[2 * pair + tile]
                here = pl.multiple_of(owner * OWNER_ROWS + coarse * DENSE, DENSE)
                acc_ref[pl.ds(here, DENSE), :] += dense
                there = owner * OWNER_ROWS + NC * DENSE + coarse
                acc_ref[pl.ds(there, 1), :] += jnp.where(own, diag, 0.0)
        return carry

    lax.fori_loop(0, tiles // 2 // pairs_at_once, step, 0)
    out_ref[...] = acc_ref[...].astype(BF16)


def table_position(slot, elem_count, face_count, capacity):
    part = face_count * capacity
    inner = lax.rem(slot, part)
    block = lax.div(inner, capacity) * elem_count + lax.div(slot, part)
    return block * capacity + lax.rem(inner, capacity)


def main_kernel(
    position_of,
    conn_ref,
    table_ref,
    rhs_ref,
    inverse_ref,
    coupling_ref,
    schur_ref,
    share_ref,
    rhs_wide_ref,
    rhs_turned_ref,
    lam_ref,
    columns_ref,
):
    element = pl.program_id(0)
    elements = rhs_ref.shape[0]
    faces = elements * FACES_PER_ELEM
    trace = FACES_PER_ELEM * FACE_COEFFS

    @pl.when(element == 0)
    def _():
        rhs_wide_ref[...] = jnp.zeros_like(rhs_wide_ref)
        rhs_wide_ref[0:elements, :] = rhs_ref[...].astype(F32)
        rhs_turned_ref[...] = rhs_wide_ref[...].T.astype(BF16)
        row = iota((SHARE_ROWS, LANES), 0)
        positions = jnp.full((SHARE_ROWS, LANES), -1, I32)
        for k in range(faces):
            positions = jnp.where(row == k, position_of(conn_ref[k]), positions)
        slots = table_ref.shape[0]
        lane = iota((SHARE_ROWS, LANES), 1)
        hot = jnp.concatenate(
            [positions == lane + base for base in range(0, slots, LANES)], axis=1
        )
        lam_ref[...] = dot(hot.astype(BF16), table_ref[...])
        columns_ref[...] = jnp.zeros_like(columns_ref)

    coupling = coupling_ref[0]
    wide = jnp.concatenate([coupling, rhs_turned_ref[...]], axis=1)
    weights = dot(inverse_ref[0], wide).astype(BF16)
    condensed = dot(coupling, weights, TN)
    schur_ref[0] = (-condensed[:, :trace]).astype(BF16)

    total = jnp.where(iota((trace, LANES), 1) == element, condensed[:, trace:], 0.0)
    for face in range(FACES_PER_ELEM):
        lam = lam_ref[pl.ds(element * FACES_PER_ELEM + face, 1), :]
        total = total - condensed[:, face * LANES : (face + 1) * LANES] * lam
    sums = jnp.sum(total, axis=1, keepdims=True)
    lane = iota((LANES, LANES), 1)
    columns = columns_ref[...]
    for face in range(FACES_PER_ELEM):
        columns = jnp.where(
            lane == element * FACES_PER_ELEM + face,
            sums[face * FACE_COEFFS : (face + 1) * FACE_COEFFS],
            columns,
        )
    columns_ref[...] = columns

    @pl.when(element == elements - 1)
    def _():
        shares = columns_ref[...].T[:SHARE_ROWS]
        row = iota((SHARE_ROWS, LANES), 0)
        lane = iota((1, LANES), 1)
        high = jnp.full((1, LANES), -1, I32)
        rest = jnp.zeros((1, LANES), I32)
        for k in range(faces):
            high = jnp.where(lane == k, lax.div(conn_ref[k], SLOT_BASE), high)
            rest = jnp.where(lane == k, lax.rem(conn_ref[k], SLOT_BASE), rest)
        shares = jnp.where(row == faces, high.astype(F32), shares)
        shares = jnp.where(row == faces + 1, rest.astype(F32), shares)
        share_ref[...] = shares.astype(BF16)


def residual_kernel(elem_count, capacity, faces, table_ref, *refs):
    share_refs, out_ref = refs[:-1], refs[-1]
    mine = lax.axis_index("elem")
    own = out_ref.shape[0]
    slots = table_ref.shape[0]
    place = iota((own, slots), 0)
    position = (lax.div(place, capacity) * elem_count + mine) * capacity + lax.rem(place, capacity)
    pick = (iota((own, slots), 1) == position).astype(BF16)
    total = dot(pick, table_ref[...])
    slot = (iota((own, SHARE_ROWS), 0) + mine * own).astype(F32)
    for share_ref in share_refs:
        shares = share_ref[...]
        names = shares.astype(F32)
        named = names[faces : faces + 1, :SHARE_ROWS] * SLOT_BASE
        named = named + names[faces + 1 : faces + 2, :SHARE_ROWS]
        total = total - dot((slot == named).astype(BF16), shares)
    out_ref[...] = total


def coarse_kernel(got_ref, out_ref, sum_ref, full_ref):
    total = got_ref[0].astype(F32)
    for k in range(1, got_ref.shape[0]):
        total = total + got_ref[k].astype(F32)
    sum_ref[...] = total

    lane = iota((HALF, LANES), 1)
    row = iota((HALF, LANES), 0)
    wide_row = iota((MROW, LANES), 0)
    wide_lane = iota((MROW, LANES), 1)
    top = wide_row < HALF
    held = (top & ((wide_lane <= wide_row) | (wide_lane >= HALF))) | (
        (~top) & (wide_lane >= wide_row)
    )
    for block in range(NC):
        dense = sum_ref[block * DENSE : (block + 1) * DENSE, :]
        upper = jnp.concatenate([dense, pltpu.roll(dense, MROW, 1)], axis=0)
        diag = sum_ref[NC * DENSE + block : NC * DENSE + block + 1, :]
        diag = pltpu.roll(diag + pltpu.roll(diag, MROW, 1), HALF, 1)
        lower = jnp.where(lane == row + HALF, diag, pltpu.roll(upper, HALF, 1))
        given = jnp.concatenate([upper, lower], axis=0)
        turned = jnp.concatenate([given, given], axis=0).T[:MROW]
        full_ref[block * MROW : (block + 1) * MROW, :] = jnp.where(held, given, turned)
    low = iota((NC, LANES), 1) < MROW
    for chunk in range(HALF):
        left = full_ref[pl.ds(2 * chunk, NC, stride=MROW), :]
        right = full_ref[pl.ds(2 * chunk + 1, NC, stride=MROW), :]
        out_ref[:, chunk * LANES : (chunk + 1) * LANES] = jnp.where(
            low, left, pltpu.roll(right, MROW, 1)
        )


def vmem(count):
    return [pl.BlockSpec(memory_space=pltpu.VMEM)] * count


def params(mib):
    return pltpu.CompilerParams(vmem_limit_bytes=mib << 20)


def shards(
    trace_old,
    new_owner,
    mortar_tiles,
    mortar_owner,
    mortar_coarse,
    interior_rhs,
    local_inverse,
    coupling,
    connectivity,
):
    face_count = lax.axis_size("face")
    elem_count = lax.axis_size("elem")
    row_count = trace_old.shape[0]
    tile_count = mortar_tiles.shape[0]
    elements, modes = interior_rhs.shape
    faces = elements * FACES_PER_ELEM
    trace = FACES_PER_ELEM * FACE_COEFFS
    capacity = max(2, 2 * row_count // face_count)
    devices = face_count * elem_count
    slots = devices * capacity
    own = slots // elem_count

    placed = pl.pallas_call(
        functools.partial(place_kernel, elem_count, face_count, capacity),
        out_shape=jax.ShapeDtypeStruct((slots, FACE_COEFFS), BF16),
        in_specs=vmem(2),
        out_specs=pl.BlockSpec(memory_space=pltpu.VMEM),
        name="place",
    )(new_owner.reshape(1, row_count), trace_old)
    table = lax.all_to_all(
        placed.reshape(devices, capacity, FACE_COEFFS), ("face", "elem"), 0, 0, tiled=True
    ).reshape(slots, FACE_COEFFS)

    half_grams = pl.pallas_call(
        functools.partial(gram_kernel, 6),
        out_shape=jax.ShapeDtypeStruct((face_count * OWNER_ROWS, LANES), BF16),
        in_specs=[pl.BlockSpec(memory_space=pltpu.SMEM)] * 2 + vmem(1),
        out_specs=pl.BlockSpec(memory_space=pltpu.VMEM),
        scratch_shapes=[
            pltpu.VMEM((tile_count * MROW, LANES), F32),
            pltpu.VMEM((face_count * OWNER_ROWS, LANES), F32),
        ],
        compiler_params=params(40),
        name="gram",
    )(mortar_owner.reshape(tile_count), mortar_coarse, mortar_tiles)
    got = lax.all_to_all(
        half_grams.reshape(face_count, OWNER_ROWS, LANES), "face", 0, 0, tiled=True
    )

    slots_named, _ = lax.optimization_barrier((connectivity.reshape(faces), half_grams))
    position_of = functools.partial(
        table_position, elem_count=elem_count, face_count=face_count, capacity=capacity
    )
    schur_blocks, shares = pl.pallas_call(
        functools.partial(main_kernel, position_of),
        out_shape=(
            jax.ShapeDtypeStruct((elements, trace, trace), BF16),
            jax.ShapeDtypeStruct((SHARE_ROWS, LANES), BF16),
        ),
        grid=(elements,),
        in_specs=[
            pl.BlockSpec(memory_space=pltpu.SMEM),
            pl.BlockSpec((slots, FACE_COEFFS), lambda e: (0, 0)),
            pl.BlockSpec((elements, modes), lambda e: (0, 0)),
            pl.BlockSpec((1, modes, modes), lambda e: (e, 0, 0)),
            pl.BlockSpec((1, modes, trace), lambda e: (e, 0, 0)),
        ],
        out_specs=(
            pl.BlockSpec((1, trace, trace), lambda e: (e, 0, 0)),
            pl.BlockSpec((SHARE_ROWS, LANES), lambda e: (0, 0)),
        ),
        scratch_shapes=[
            pltpu.VMEM((LANES, modes), F32),
            pltpu.VMEM((modes, LANES), BF16),
            pltpu.VMEM((SHARE_ROWS, LANES), F32),
            pltpu.VMEM((LANES, LANES), F32),
        ],
        compiler_params=params(32),
        cost_estimate=pl.CostEstimate(
            flops=2 * elements * modes * trace * (modes + trace),
            bytes_accessed=2 * elements * (modes * (modes + trace) + trace * trace),
            transcendentals=0,
        ),
        name="condense",
    )(slots_named, table, interior_rhs, local_inverse, coupling)

    all_shares = [shares]
    for shift in range(1, elem_count):
        pairs = [(k, (k + shift) % elem_count) for k in range(elem_count)]
        all_shares.append(lax.ppermute(shares, "elem", pairs))

    coarse_blocks = pl.pallas_call(
        coarse_kernel,
        out_shape=jax.ShapeDtypeStruct((NC, MROW * MROW), F32),
        in_specs=vmem(1),
        out_specs=pl.BlockSpec(memory_space=pltpu.VMEM),
        scratch_shapes=[
            pltpu.VMEM((OWNER_ROWS, LANES), F32),
            pltpu.VMEM((NC * MROW, LANES), F32),
        ],
        compiler_params=params(32),
        name="coarse",
    )(got)

    slot_residual = pl.pallas_call(
        functools.partial(residual_kernel, elem_count, capacity, faces),
        out_shape=jax.ShapeDtypeStruct((own, FACE_COEFFS), F32),
        in_specs=vmem(1 + elem_count),
        out_specs=pl.BlockSpec(memory_space=pltpu.VMEM),
        name="residual",
    )(table, *all_shares)
    return schur_blocks, slot_residual, coarse_blocks


def solution(mesh):
    return jax.shard_map(
        shards,
        mesh=mesh,
        in_specs=(
            P(("face", "elem"), None),
            P(("face", "elem"), None),
            P(("face", "elem"), None),
            P(("face", "elem"), None),
            P(("face", "elem")),
            P(("face", "elem"), None),
            P(("face", "elem"), None, None),
            P(("face", "elem"), None, None),
            P(("face", "elem"), None),
        ),
        out_specs=(
            P(("face", "elem"), None, None),
            P(("face", "elem"), None),
            P(("face", "elem"), None),
        ),
        check_vma=False,
    )
```

time: 129 us -> 51.5 us (0.40)
  matrix products: 38.8 us -> 0 us
  Pallas kernels: 0 us -> 22.8 us
  local copies, waits for them, and re-layouts: 25.3 us -> 9.65 us
  between operations: 14.1 us -> 0.66 us
  other arithmetic: 12.7 us -> 0 us
  waiting for transfers between devices: 12.7 us -> 2.98 us
  blocking collectives: 7.06 us -> 0 us
  starting transfers between devices: 17.2 us -> 14.8 us
    dot_general x10 -> x0, matrix products: 38.8 us -> none  [the longest x1 7.26 us: shards(): jnp.einsum('tmn,tkn->tmk', tile_mats, tile_mats, preferred_element_type=j...]
    pallas_call x0 -> x5, Pallas kernels: none -> 22.8 us  [the longest x1 9.13 us: shards(): pl.pallas_call(functools.partial(main_kernel, position_of), out_shape=(ja...]
    reduce_scatter x1 -> x0, waiting for transfers between devices: 8.08 us -> none  [shards(): lax.psum_scatter(partial_sums.astype(jnp.bfloat16), 'elem', scatter_dimen...]
    dot_general x2 -> x0, local copies, waits for them, and re-layouts: 7.33 us -> none  [the longest x1 6.7 us: shards(): jnp.einsum('tmn,tkn->tmk', tile_mats, tile_mats, preferred_element_type=j...]
    all_gather x1 -> x0, blocking collectives: 7.06 us -> none  [shards(): trace_table = lax.all_gather(own_rows, 'elem', axis=0, tiled=True)]
    reshape x3 -> x1, local copies, waits for them, and re-layouts: 7.12 us -> 0.08 us  [shards(): connectivity.reshape(faces)]
    all_to_all x3 -> x2, waiting for transfers between devices: 4.62 us -> 0.01 us  [the longest x1 0.01 us: shards(): lax.all_to_all(half_grams.reshape(face_count, OWNER_ROWS, LANES), 'face',...]
    all_to_all x3 -> x2, starting transfers between devices: 17.1 us -> 13.1 us  [the longest x1 7.3 us: shards(): lax.all_to_all(placed.reshape(devices, capacity, FACE_COEFFS), ('face', '...]
  transfers between devices with their start and end apart: 4 -> 5, of which waited for: 4 -> 2; matrix products, arithmetic and copies ran while one was open for 36% -> 2% of each run, Pallas kernels for 0% -> 38%
where the time goes in v1:
time: 51.5 us; the launch traced here: 51 us
  Pallas kernels  22.8 us (44%)
  starting transfers between devices  14.8 us (29%)
  local copies, waits for them, and re-layouts  9.65 us (19%)
  waiting for transfers between devices  2.98 us (6%)
  between operations  0.66 us (1%)
    unnamed x23, local copies, waits for them, and re-layouts  9.57 us
    pallas_call x1, Pallas kernels, shards(): pl.pallas_call(functools.partial(main_kernel, position_of), out_shape=(ja...  9.13 us
    pallas_call x1, Pallas kernels, shards(): pl.pallas_call(functools.partial(gram_kernel, 6), out_shape=jax.ShapeDtyp...  8.37 us
    all_to_all x1, starting transfers between devices, shards(): lax.all_to_all(placed.reshape(devices, capacity, FACE_COEFFS), ('face', '...  7.3 us
    all_to_all x1, starting transfers between devices, shards(): lax.all_to_all(half_grams.reshape(face_count, OWNER_ROWS, LANES), 'face',...  5.83 us
    ppermute x3, waiting for transfers between devices, shards(): all_shares.append(lax.ppermute(shares, 'elem', pairs))  2.98 us
    pallas_call x1, Pallas kernels, shards(): pl.pallas_call(coarse_kernel, out_shape=jax.ShapeDtypeStruct((NC, MROW *...  1.85 us
    pallas_call x1, Pallas kernels, shards(): pl.pallas_call(functools.partial(residual_kernel, elem_count, capacity, f...  1.79 us
  transfers between devices with their start and end apart: 5, of which 2 were waited for; matrix products, arithmetic and copies ran while one was open for 2% of the time, Pallas kernels for 38%

profile of v1, /device:TPU:0, one launch (start us, length us, event | category | flops | bytes accessed | tf_op | source)
XLA Modules:
  0.0 51.0 jit_solution(13122728305254982628)
XLA Ops:
  0.6 1.7 %place.1 = bf16[512,128]{1,0:T(8,128)(2,1)} custom-call(s32[1,64]{1,0:T(1,128)} %bitcast.9, bf16[64,128]{1,0:T(8,128)(2,1)} %trace_ref.1), custom_call_target="tpu_custom_call" | custom-call | tf_op jit(solution)/shard_map/place/pallas_call | solution.py:269
  2.3 7.3 %all-to-all-start = ((bf16[32,16,128]{2,1,0:T(8,128)(2,1)}), bf16[32,16,128]{2,1,0:T(8,128)(2,1)S(1)}, u32[]{:S(2)}, u32[]{:S(2)}) async-start(bf16[32,16,128]{2,1,0:T(8,128)(2,1)} %bitcast.8), calls=%async_computation | async-start | bytes 262144 | tf_op jit(solution)/shard_map/all_to_all | solution.py:276
  9.6 0.0 copy-start
  9.6 1.3 %copy-done = bf16[96,6144]{1,0:T(8,128)(2,1)S(1)} copy-done((bf16[96,6144]{1,0:T(8,128)(2,1)S(1)}, bf16[96,6144]{1,0:T(8,128)(2,1)}, u32[]{:S(2)}) %copy-start) | copy-done | bytes 1179672
  10.9 0.7 %copy-done.3 = s32[96,1]{0,1:T(1,128)S(1)} copy-done((s32[96,1]{0,1:T(1,128)S(1)}, s32[96,1]{0,1:T(1,128)}, u32[]{:S(2)}) %copy-start.3) | copy-done | bytes 408
  11.6 0.7 %copy-done.4 = s32[96]{0:T(128)S(1)} copy-done((s32[96]{0:T(128)S(1)}, s32[96]{0:T(128)}, u32[]{:S(2)}) %copy-start.4) | copy-done | bytes 408
  12.2 8.4 %gram.1 = bf16[2176,128]{1,0:T(8,128)(2,1)} custom-call(s32[96]{0:T(128)S(1)} %bitcast.7, s32[96]{0:T(128)S(1)} %copy-done.4, bf16[96,6144]{1,0:T(8,128)(2,1)S(1)} %copy-done), custom_call_target="tpu_custom_call" | custom-call | tf_op jit(solution)/shard_map/gram/pallas_call | solution.py:280
  20.6 5.8 %all-to-all-start.1 = ((bf16[8,272,128]{2,1,0:T(8,128)(2,1)}), bf16[8,272,128]{2,1,0:T(8,128)(2,1)S(1)}, u32[]{:S(2)}, u32[]{:S(2)}) async-start(bf16[8,272,128]{2,1,0:T(8,128)(2,1)} %bitcast.4), calls=%async_computation.1 | async-start | bytes 1114112 | tf_op jit(solution)/shard_map/all_to_all | solution.py:292
  26.4 0.8 %copy.13 = s32[9,3]{1,0:T(8,128)S(1)} copy(s32[9,3]{0,1:T(4,128)} %param.17) | data formatting | bytes 216 | tf_op args[8]
  27.2 0.1 reshape.24.conn_ref
  27.3 2.3 %copy-done.5 = bf16[9,512,512]{2,1,0:T(8,128)(2,1)S(1)} copy-done((bf16[9,512,512]{2,1,0:T(8,128)(2,1)S(1)}, bf16[9,512,512]{2,1,0:T(8,128)(2,1)}, u32[]{:S(2)}) %copy-start.5) | copy-done | bytes 4718616
  29.6 2.0 %copy-done.6 = bf16[9,512,384]{2,1,0:T(8,128)(2,1)S(1)} copy-done((bf16[9,512,384]{2,1,0:T(8,128)(2,1)S(1)}, bf16[9,512,384]{2,1,0:T(8,128)(2,1)}, u32[]{:S(2)}) %copy-start.6) | copy-done | bytes 3538968
  31.6 0.7 %copy-done.7 = bf16[9,512]{1,0:T(8,128)(2,1)S(1)} copy-done((bf16[9,512]{1,0:T(8,128)(2,1)S(1)}, bf16[9,512]{1,0:T(8,128)(2,1)}, u32[]{:S(2)}) %copy-start.7) | copy-done | bytes 9240
  32.3 9.1 %condense.1 = (bf16[9,384,384]{2,1,0:T(8,128)(2,1)}, bf16[32,128]{1,0:T(8,128)(2,1)S(1)}) custom-call(s32[27]{0:T(128)S(1)} %reshape.24.conn_ref, bf16[512,128]{1,0:T(8,128)(2,1)S(1)} %bitcast.5, bf16[9,512]{1,0:T(8,128)(2,1)S(1)} %copy-done.7, bf16[9,512,512]{2,1,0:T(8,128)(2,1)S(1)} %copy-done.5, bf16[9,512,384]{2,1,0:T(8,128)(2,1)S(1)} %copy-done.6), custom_call_target="tpu_custom_call" | custom-call | flops 3170893824 | bytes 10911744 | tf_op jit(solution)/shard_map/condense/pallas_call | solution.py:300
  41.5 1.0 %collective-permute-start.2 = (bf16[32,128]{1,0:T(8,128)(2,1)S(1)}, bf16[32,128]{1,0:T(8,128)(2,1)S(1)}, u32[]{:S(2)}, u32[]{:S(2)}) collective-permute-start(bf16[32,128]{1,0:T(8,128)(2,1)S(1)} %get-tuple-element.8.refs_0_), channel_id=1, source_target_pairs={{0,3},{1,0},{2,1},{3,2},{4,7},{5,4},{6,5},{7,6},{8,11},{9,8},{10,9... | collective-permute-start | bytes 24584 | tf_op jit(solution)/shard_map/ppermute | solution.py:336
  42.4 0.6 %collective-permute-start.1 = (bf16[32,128]{1,0:T(8,128)(2,1)S(1)}, bf16[32,128]{1,0:T(8,128)(2,1)S(1)}, u32[]{:S(2)}, u32[]{:S(2)}) collective-permute-start(bf16[32,128]{1,0:T(8,128)(2,1)S(1)} %get-tuple-element.8.refs_0_), channel_id=1, source_target_pairs={{0,2},{1,3},{2,0},{3,1},{4,6},{5,7},{6,4},{7,5},{8,10},{9,11},{10,... | collective-permute-start | bytes 24584 | tf_op jit(solution)/shard_map/ppermute | solution.py:336
  43.0 0.2 collective-permute-start
  43.2 0.6 %collective-permute-done.2.refs_3_ = bf16[32,128]{1,0:T(8,128)(2,1)S(1)} collective-permute-done((bf16[32,128]{1,0:T(8,128)(2,1)S(1)}, bf16[32,128]{1,0:T(8,128)(2,1)S(1)}, u32[]{:S(2)}, u32[]{:S(2)}) %collective-permute-start.2) | collective-permute-done | bytes 8224 | tf_op jit(solution)/shard_map/ppermute | solution.py:336
  43.8 2.3 %collective-permute-done.1.refs_2_ = bf16[32,128]{1,0:T(8,128)(2,1)S(1)} collective-permute-done((bf16[32,128]{1,0:T(8,128)(2,1)S(1)}, bf16[32,128]{1,0:T(8,128)(2,1)S(1)}, u32[]{:S(2)}, u32[]{:S(2)}) %collective-permute-start.1) | collective-permute-done | bytes 8224 | tf_op jit(solution)/shard_map/ppermute | solution.py:336
  46.1 0.0 collective-permute-done.refs_1_
  46.2 0.6 %copy-done.9 = bf16[32,128]{1,0:T(8,128)(2,1)} copy-done((bf16[32,128]{1,0:T(8,128)(2,1)}, bf16[32,128]{1,0:T(8,128)(2,1)S(1)}, u32[]{:S(2)}) %copy-start.9) | copy-done | bytes 8216
  46.7 0.6 %copy-done.10 = bf16[32,128]{1,0:T(8,128)(2,1)} copy-done((bf16[32,128]{1,0:T(8,128)(2,1)}, bf16[32,128]{1,0:T(8,128)(2,1)S(1)}, u32[]{:S(2)}) %copy-start.10) | copy-done | bytes 8216
  47.3 1.8 %residual.1 = f32[128,128]{1,0:T(8,128)} custom-call(bf16[512,128]{1,0:T(8,128)(2,1)} %bitcast.6, bf16[32,128]{1,0:T(8,128)(2,1)} %copy-done.2, bf16[32,128]{1,0:T(8,128)(2,1)} %copy-done.10, bf16[32,128]{1,0:T(8,128)(2,1)} %copy-done.9, bf16[32,128]{1,0:T(8,128)(2,1)} %copy-done.8), custom_call_target="tpu_custom_call" | custom-call | tf_op jit(solution)/shard_map/residual/pallas_call | solution.py:351
  49.1 1.9 %coarse.1 = f32[16,4096]{1,0:T(8,128)} custom-call(bf16[8,272,128]{2,1,0:T(8,128)(2,1)S(1)} %all-to-all-done.1.got_ref), custom_call_target="tpu_custom_call" | custom-call | tf_op jit(solution)/shard_map/coarse/pallas_call | solution.py:338
  (15 shorter events, 0.0 us)
Async XLA Ops:
  2.3 18.3 %all-to-all-start = ((bf16[32,16,128]{2,1,0:T(8,128)(2,1)}), bf16[32,16,128]{2,1,0:T(8,128)(2,1)S(1)}, u32[]{:S(2)}, u32[]{:S(2)}) async-start(bf16[32,16,128]{2,1,0:T(8,128)(2,1)} %bitcast.8), calls=%async_computation | async-start | bytes 262144 | tf_op jit(solution)/shard_map/all_to_all | solution.py:276
  9.6 1.3 %copy-start = (bf16[96,6144]{1,0:T(8,128)(2,1)S(1)}, bf16[96,6144]{1,0:T(8,128)(2,1)}, u32[]{:S(2)}) copy-start(bf16[96,6144]{1,0:T(8,128)(2,1)} %tiles_ref.1) | copy-start | bytes 3538948
  10.9 0.7 %copy-start.3 = (s32[96,1]{0,1:T(1,128)S(1)}, s32[96,1]{0,1:T(1,128)}, u32[]{:S(2)}) copy-start(s32[96,1]{0,1:T(1,128)} %param.12) | copy-start | bytes 1156
  11.6 0.7 %copy-start.4 = (s32[96]{0:T(128)S(1)}, s32[96]{0:T(128)}, u32[]{:S(2)}) copy-start(s32[96]{0:T(128)} %coarse_ref.1) | copy-start | bytes 1156
  20.6 20.9 %copy-start.1 = (bf16[32,16,128]{2,1,0:T(8,128)(2,1)}, bf16[32,16,128]{2,1,0:T(8,128)(2,1)S(1)}, u32[]{:S(2)}) copy-start(bf16[32,16,128]{2,1,0:T(8,128)(2,1)S(1)} %all-to-all-done) | copy-start | bytes 393220
  20.6 28.5 %all-to-all-start.1 = ((bf16[8,272,128]{2,1,0:T(8,128)(2,1)}), bf16[8,272,128]{2,1,0:T(8,128)(2,1)S(1)}, u32[]{:S(2)}, u32[]{:S(2)}) async-start(bf16[8,272,128]{2,1,0:T(8,128)(2,1)} %bitcast.4), calls=%async_computation.1 | async-start | bytes 1114112 | tf_op jit(solution)/shard_map/all_to_all | solution.py:292
  27.3 2.3 %copy-start.5 = (bf16[9,512,512]{2,1,0:T(8,128)(2,1)S(1)}, bf16[9,512,512]{2,1,0:T(8,128)(2,1)}, u32[]{:S(2)}) copy-start(bf16[9,512,512]{2,1,0:T(8,128)(2,1)} %inverse_ref.1) | copy-start | bytes 14155780
  29.6 2.0 %copy-start.6 = (bf16[9,512,384]{2,1,0:T(8,128)(2,1)S(1)}, bf16[9,512,384]{2,1,0:T(8,128)(2,1)}, u32[]{:S(2)}) copy-start(bf16[9,512,384]{2,1,0:T(8,128)(2,1)} %coupling_ref.1) | copy-start | bytes 10616836
  31.6 0.7 %copy-start.7 = (bf16[9,512]{1,0:T(8,128)(2,1)S(1)}, bf16[9,512]{1,0:T(8,128)(2,1)}, u32[]{:S(2)}) copy-start(bf16[9,512]{1,0:T(8,128)(2,1)} %rhs_ref.1) | copy-start | bytes 27652
  41.5 4.7 %copy-start.2 = (bf16[32,128]{1,0:T(8,128)(2,1)}, bf16[32,128]{1,0:T(8,128)(2,1)S(1)}, u32[]{:S(2)}) copy-start(bf16[32,128]{1,0:T(8,128)(2,1)S(1)} %get-tuple-element.8.refs_0_) | copy-start | bytes 24580
  41.5 2.3 %collective-permute-start.2 = (bf16[32,128]{1,0:T(8,128)(2,1)S(1)}, bf16[32,128]{1,0:T(8,128)(2,1)S(1)}, u32[]{:S(2)}, u32[]{:S(2)}) collective-permute-start(bf16[32,128]{1,0:T(8,128)(2,1)S(1)} %get-tuple-element.8.refs_0_), channel_id=1, source_target_pairs={{0,3},{1,0},{2,1},{3,2},{4,7},{5,4},{6,5},{7,6},{8,11},{9,8},{10,9... | collective-permute-start | bytes 24584 | tf_op jit(solution)/shard_map/ppermute | solution.py:336
  42.4 3.7 %collective-permute-start.1 = (bf16[32,128]{1,0:T(8,128)(2,1)S(1)}, bf16[32,128]{1,0:T(8,128)(2,1)S(1)}, u32[]{:S(2)}, u32[]{:S(2)}) collective-permute-start(bf16[32,128]{1,0:T(8,128)(2,1)S(1)} %get-tuple-element.8.refs_0_), channel_id=1, source_target_pairs={{0,2},{1,3},{2,0},{3,1},{4,6},{5,7},{6,4},{7,5},{8,10},{9,11},{10,... | collective-permute-start | bytes 24584 | tf_op jit(solution)/shard_map/ppermute | solution.py:336
  43.0 3.1 %collective-permute-start = (bf16[32,128]{1,0:T(8,128)(2,1)S(1)}, bf16[32,128]{1,0:T(8,128)(2,1)S(1)}, u32[]{:S(2)}, u32[]{:S(2)}) collective-permute-start(bf16[32,128]{1,0:T(8,128)(2,1)S(1)} %get-tuple-element.8.refs_0_), channel_id=1, source_target_pairs={{0,1},{1,2},{2,3},{3,0},{4,5},{5,6},{6,7},{7,4},{8,9},{9,10},{10,1... | collective-permute-start | bytes 24584 | tf_op jit(solution)/shard_map/ppermute | solution.py:336
  43.8 2.4 %copy-start.8 = (bf16[32,128]{1,0:T(8,128)(2,1)}, bf16[32,128]{1,0:T(8,128)(2,1)S(1)}, u32[]{:S(2)}) copy-start(bf16[32,128]{1,0:T(8,128)(2,1)S(1)} %collective-permute-done.2.refs_3_) | copy-start | bytes 24580
  46.1 0.6 %copy-start.9 = (bf16[32,128]{1,0:T(8,128)(2,1)}, bf16[32,128]{1,0:T(8,128)(2,1)S(1)}, u32[]{:S(2)}) copy-start(bf16[32,128]{1,0:T(8,128)(2,1)S(1)} %collective-permute-done.1.refs_2_) | copy-start | bytes 24580
  46.7 0.6 %copy-start.10 = (bf16[32,128]{1,0:T(8,128)(2,1)}, bf16[32,128]{1,0:T(8,128)(2,1)S(1)}, u32[]{:S(2)}) copy-start(bf16[32,128]{1,0:T(8,128)(2,1)S(1)} %collective-permute-done.refs_1_) | copy-start | bytes 24580

commit v2 on v1

v2 whole, which is shorter than its diff:
```python
import functools

import jax
import jax.numpy as jnp
from jax import lax
from jax.experimental import pallas as pl
from jax.experimental.pallas import tpu as pltpu
from jax.sharding import PartitionSpec as P

FACE_COEFFS = 128
FACES_PER_ELEM = 3
MROW = 64
MCOL = 96
NC = 16
HALF = MROW // 2
LANES = 128
DENSE = HALF * MROW // LANES
OWNER_ROWS = NC * (DENSE + 1)
SHARE_ROWS = 32
SLOT_BASE = 16
CHUNK = 16
PITCH = MROW + 8
BIG = 63
SMALL = 16

BF16 = jnp.bfloat16
F32 = jnp.float32
I32 = jnp.int32

NT = (((1,), (1,)), ((), ()))
TN = (((0,), (0,)), ((), ()))


def iota(shape, dim):
    return lax.broadcasted_iota(I32, shape, dim)


def dot(left, right, dims=(((1,), (0,)), ((), ()))):
    return lax.dot_general(left, right, dims, preferred_element_type=F32)


def place_rows(elem_count, face_count, capacity, owners, rows_in, slots):
    rows = owners.shape[1]
    hot = (iota((face_count, rows), 0) == owners).astype(F32)
    earlier = (iota((rows, rows), 0) < iota((rows, rows), 1)).astype(BF16)
    rank = jnp.sum(hot * dot(hot.astype(BF16), earlier), axis=0, keepdims=True).astype(I32)
    target = owners * capacity + rank
    block = iota((slots, rows), 0)
    wanted = lax.div(block, elem_count * capacity) * capacity + lax.rem(block, capacity)
    return dot((wanted == target).astype(BF16), rows_in).astype(BF16)


def send_kernel(
    elem_count,
    face_count,
    capacity,
    new_owner_ref,
    trace_ref,
    owner_hbm,
    coarse_hbm,
    tiles_hbm,
    placed_ref,
    out_ref,
    owner_ref,
    coarse_ref,
    tiles_ref,
    rows_ref,
    *more,
):
    accs, diags, sems = more[:2], more[2:4], more[4]
    tiles = tiles_ref.shape[0]
    copies = [
        pltpu.make_async_copy(owner_hbm, owner_ref, sems.at[0]),
        pltpu.make_async_copy(coarse_hbm, coarse_ref, sems.at[1]),
        pltpu.make_async_copy(tiles_hbm, tiles_ref, sems.at[2]),
    ]
    for copy in copies:
        copy.start()
    for ref in (*accs, *diags):
        ref[...] = jnp.zeros_like(ref)
    placed_ref[...] = place_rows(
        elem_count,
        face_count,
        capacity,
        new_owner_ref[...],
        trace_ref[...],
        placed_ref.shape[0],
    )
    for copy in copies:
        copy.wait()

    lane = iota((CHUNK, LANES), 1)
    inside = lane < MCOL
    row = iota((HALF, LANES), 0)
    column = lax.rem(iota((HALF, LANES), 1), MROW)
    swapped = (column > row) & (column < HALF)
    diagonal = column == row
    low = iota((DENSE, LANES), 1) < MROW
    low_wide = iota((MROW, LANES), 1) < MROW
    low_row = iota((1, LANES), 1) < MROW

    for chunk in range(tiles // CHUNK):
        first_tile = chunk * CHUNK
        for group in range(MROW // 4):
            base = group * 3 * LANES
            one, two, three = (
                tiles_ref[
                    first_tile : first_tile + CHUNK, base + k * LANES : base + (k + 1) * LANES
                ].astype(F32)
                for k in range(3)
            )
            rolled = (
                one,
                pltpu.roll(jnp.where(lane < 64, two, one), 32, 1),
                pltpu.roll(jnp.where(lane < 32, three, two), 64, 1),
                pltpu.roll(three, 96, 1),
            )
            for k in range(4):
                rows_ref[pl.ds(first_tile * PITCH + 4 * group + k, CHUNK, stride=PITCH), :] = (
                    jnp.where(inside, rolled[k], 0.0)
                )
        for tile in range(first_tile, first_tile + CHUNK, 2):
            both = jnp.concatenate(
                [
                    rows_ref[t * PITCH : t * PITCH + MROW, :].astype(BF16)
                    for t in (tile, tile + 1)
                ],
                axis=0,
            )
            gram = dot(both, both, NT)
            side = jnp.where(low_wide, gram[:MROW], gram[MROW:])
            lower = pltpu.roll(side[HALF:], LANES - HALF, 1)
            packed = jnp.where(swapped, lower, side[:HALF])
            diag = jnp.sum(jnp.where(diagonal, lower, 0.0), axis=0, keepdims=True)
            turned = pltpu.roll(packed, MROW, 1)
            dense = (
                jnp.where(low, packed[:DENSE], turned[DENSE:]),
                jnp.where(low, turned[:DENSE], packed[DENSE:]),
            )
            own = (jnp.where(low_row, diag, 0.0), jnp.where(low_row, 0.0, diag))
            for k in range(2):
                block = owner_ref[tile + k] * NC + coarse_ref[tile + k]
                here = pl.ds(pl.multiple_of(block * DENSE, DENSE), DENSE)
                accs[k][here, :] += dense[k]
                diags[k][pl.ds(block, 1), :] += own[k]
    for owner in range(face_count):
        start, size = owner * OWNER_ROWS, NC * DENSE
        here = slice(owner * size, (owner + 1) * size)
        out_ref[start : start + size, :] = (accs[0][here, :] + accs[1][here, :]).astype(BF16)
        here = slice(owner * NC, (owner + 1) * NC)
        out_ref[start + size : start + size + NC, :] = (
            diags[0][here, :] + diags[1][here, :]
        ).astype(BF16)


def table_position(slot, elem_count, face_count, capacity):
    part = face_count * capacity
    inner = lax.rem(slot, part)
    block = lax.div(inner, capacity) * elem_count + lax.div(slot, part)
    return block * capacity + lax.rem(inner, capacity)


def main_kernel(
    position_of,
    table_ref,
    conn_hbm,
    rhs_hbm,
    inverse_hbm,
    coupling_hbm,
    schur_hbm,
    share_ref,
    conn_ref,
    rhs_ref,
    inverse_ref,
    coupling_ref,
    schur_ref,
    rhs_wide_ref,
    rhs_turned_ref,
    lam_ref,
    sum_ref,
    weight_a_ref,
    weight_b_ref,
    turned_a_ref,
    turned_b_ref,
    small_sems,
    inverse_sems,
    coupling_sems,
    schur_sems,
):
    elements = rhs_ref.shape[0]
    faces = elements * FACES_PER_ELEM
    trace = FACES_PER_ELEM * FACE_COEFFS
    small = [
        pltpu.make_async_copy(conn_hbm, conn_ref, small_sems.at[0]),
        pltpu.make_async_copy(rhs_hbm, rhs_ref, small_sems.at[1]),
    ]
    for copy in small:
        copy.start()

    def bring(e):
        return (
            pltpu.make_async_copy(inverse_hbm.at[e], inverse_ref.at[e], inverse_sems.at[e]),
            pltpu.make_async_copy(coupling_hbm.at[e], coupling_ref.at[e], coupling_sems.at[e]),
        )

    def leave(e):
        return pltpu.make_async_copy(schur_ref.at[e], schur_hbm.at[e], schur_sems.at[e])

    for e in range(elements):
        for copy in bring(e):
            copy.start()
    for copy in small:
        copy.wait()

    rhs_wide_ref[...] = jnp.zeros_like(rhs_wide_ref)
    rhs_wide_ref[0:elements, :] = rhs_ref[...].astype(F32)
    rhs_turned_ref[...] = rhs_wide_ref[...].T.astype(BF16)
    row = iota((SHARE_ROWS, LANES), 0)
    lane = iota((SHARE_ROWS, LANES), 1)
    positions = jnp.full((SHARE_ROWS, LANES), -1, I32)
    for k in range(faces):
        slot = conn_ref[k % FACES_PER_ELEM, k // FACES_PER_ELEM]
        positions = jnp.where(row == k, position_of(slot), positions)
    slots = table_ref.shape[0]
    hot = jnp.concatenate([positions == lane + base for base in range(0, slots, LANES)], axis=1)
    lam_ref[...] = dot(hot.astype(BF16), table_ref[...])

    def solve(e, weight_ref, turned_ref):
        coupling = coupling_ref[e]
        wide = jnp.concatenate([coupling, rhs_turned_ref[...]], axis=1)
        weight_ref[...] = dot(inverse_ref[e], wide).astype(BF16)
        turned_ref[...] = coupling.T

    def condense(e, weight_ref, turned_ref):
        condensed = dot(turned_ref[...], weight_ref[...])
        schur = (-condensed[:, :trace]).astype(BF16)
        schur_ref[e] = schur
        lam = [lam_ref[pl.ds(e * FACES_PER_ELEM + a, 1), :] for a in range(FACES_PER_ELEM)]
        own = (iota((1, LANES), 1) == e).astype(F32)
        vector = jnp.broadcast_to(jnp.concatenate([*lam, own], axis=1), (16, trace + LANES))
        matrix = jnp.concatenate([schur, condensed[:, trace:].astype(BF16)], axis=1)
        share = dot(vector.astype(BF16), matrix, NT)
        for a in range(FACES_PER_ELEM):
            sum_ref[pl.ds(e * FACES_PER_ELEM + a, 1), :] = share[
                0:1, a * FACE_COEFFS : (a + 1) * FACE_COEFFS
            ]

    even = (weight_a_ref, turned_a_ref)
    odd = (weight_b_ref, turned_b_ref)

    def advance(e, there, here):
        for copy in bring(e):
            copy.wait()
        solve(e, *there)
        condense(e - 1, *here)
        leave(e - 1).start()

    for copy in bring(0):
        copy.wait()
    solve(0, *even)

    def two(index, carry):
        advance(2 * index + 1, odd, even)
        advance(2 * index + 2, even, odd)
        return carry

    lax.fori_loop(0, (elements - 1) // 2, two, 0)
    if elements % 2 == 0:
        advance(elements - 1, odd, even)
    condense(elements - 1, *(odd if elements % 2 == 0 else even))
    leave(elements - 1).start()

    lane = iota((1, LANES), 1)
    high = jnp.full((1, LANES), -1, I32)
    rest = jnp.zeros((1, LANES), I32)
    for k in range(faces):
        slot = conn_ref[k % FACES_PER_ELEM, k // FACES_PER_ELEM]
        high = jnp.where(lane == k, lax.div(slot, SLOT_BASE), high)
        rest = jnp.where(lane == k, lax.rem(slot, SLOT_BASE), rest)
    shares = jnp.where(row < faces, sum_ref[...], 0.0)
    shares = jnp.where(row == faces, high.astype(F32), shares)
    shares = jnp.where(row == faces + 1, rest.astype(F32), shares)
    share_ref[...] = shares.astype(BF16)
    for e in range(elements):
        leave(e).wait()


def residual(elem_count, capacity, faces, own, table_ref, share_refs):
    mine = lax.axis_index("elem")
    slots = table_ref.shape[0]
    place = iota((own, slots), 0)
    position = (lax.div(place, capacity) * elem_count + mine) * capacity + lax.rem(place, capacity)
    pick = (iota((own, slots), 1) == position).astype(BF16)
    total = dot(pick, table_ref[...])
    slot = (iota((own, SHARE_ROWS), 0) + mine * own).astype(F32)
    for share_ref in share_refs:
        shares = share_ref[...]
        names = shares.astype(F32)
        named = names[faces : faces + 1, :SHARE_ROWS] * SLOT_BASE
        named = named + names[faces + 1 : faces + 2, :SHARE_ROWS]
        total = total - dot((slot == named).astype(BF16), shares)
    return total


def finish_kernel(elem_count, capacity, faces, got_ref, table_ref, *refs):
    share_refs = refs[:elem_count]
    residual_ref, out_ref, sum_ref, full_ref = refs[elem_count:]
    residual_ref[...] = residual(
        elem_count, capacity, faces, residual_ref.shape[0], table_ref, share_refs
    )
    total = got_ref[0].astype(F32)
    for k in range(1, got_ref.shape[0]):
        total = total + got_ref[k].astype(F32)
    sum_ref[...] = total

    lane = iota((HALF, LANES), 1)
    row = iota((HALF, LANES), 0)
    wide_row = iota((MROW, LANES), 0)
    wide_lane = iota((MROW, LANES), 1)
    top = wide_row < HALF
    held = (top & ((wide_lane <= wide_row) | (wide_lane >= HALF))) | (
        (~top) & (wide_lane >= wide_row)
    )
    for block in range(NC):
        dense = sum_ref[block * DENSE : (block + 1) * DENSE, :]
        upper = jnp.concatenate([dense, pltpu.roll(dense, MROW, 1)], axis=0)
        diag = sum_ref[NC * DENSE + block : NC * DENSE + block + 1, :]
        diag = pltpu.roll(diag + pltpu.roll(diag, MROW, 1), HALF, 1)
        lower = jnp.where(lane == row + HALF, diag, pltpu.roll(upper, HALF, 1))
        given = jnp.concatenate([upper, lower], axis=0)
        turned = jnp.concatenate([given, given], axis=0).T[:MROW]
        full_ref[block * MROW : (block + 1) * MROW, :] = jnp.where(held, given, turned)
    low = iota((NC, LANES), 1) < MROW
    for chunk in range(HALF):
        left = full_ref[pl.ds(2 * chunk, NC, stride=MROW), :]
        right = full_ref[pl.ds(2 * chunk + 1, NC, stride=MROW), :]
        out_ref[:, chunk * LANES : (chunk + 1) * LANES] = jnp.where(
            low, left, pltpu.roll(right, MROW, 1)
        )


ANY = pl.BlockSpec(memory_space=pl.ANY)
VMEM = pl.BlockSpec(memory_space=pltpu.VMEM)


def params(mib):
    return pltpu.CompilerParams(vmem_limit_bytes=mib << 20)


def shards(
    trace_old,
    new_owner,
    mortar_tiles,
    mortar_owner,
    mortar_coarse,
    interior_rhs,
    local_inverse,
    coupling,
    connectivity,
):
    face_count = lax.axis_size("face")
    elem_count = lax.axis_size("elem")
    row_count = trace_old.shape[0]
    tile_count = mortar_tiles.shape[0]
    elements, modes = interior_rhs.shape
    faces = elements * FACES_PER_ELEM
    trace = FACES_PER_ELEM * FACE_COEFFS
    capacity = max(2, 2 * row_count // face_count)
    devices = face_count * elem_count
    slots = devices * capacity
    own = slots // elem_count

    placed, half_grams = pl.pallas_call(
        functools.partial(send_kernel, elem_count, face_count, capacity),
        out_shape=(
            jax.ShapeDtypeStruct((slots, FACE_COEFFS), BF16),
            jax.ShapeDtypeStruct((face_count * OWNER_ROWS, LANES), BF16),
        ),
        in_specs=[VMEM, VMEM, ANY, ANY, ANY],
        out_specs=(VMEM, VMEM),
        scratch_shapes=[
            pltpu.SMEM((tile_count,), I32),
            pltpu.SMEM((tile_count,), I32),
            pltpu.VMEM(mortar_tiles.shape, BF16),
            pltpu.VMEM((tile_count * PITCH, LANES), F32),
            pltpu.VMEM((face_count * NC * DENSE, LANES), F32),
            pltpu.VMEM((face_count * NC * DENSE, LANES), F32),
            pltpu.VMEM((face_count * NC, LANES), F32),
            pltpu.VMEM((face_count * NC, LANES), F32),
            pltpu.SemaphoreType.DMA((3,)),
        ],
        compiler_params=params(BIG),
        name="send",
    )(
        new_owner.reshape(1, row_count),
        trace_old,
        mortar_owner.reshape(tile_count),
        mortar_coarse,
        mortar_tiles,
    )
    table = lax.all_to_all(
        placed.reshape(devices, capacity, FACE_COEFFS), ("face", "elem"), 0, 0, tiled=True
    ).reshape(slots, FACE_COEFFS)
    got = lax.all_to_all(
        half_grams.reshape(face_count, OWNER_ROWS, LANES), "face", 0, 0, tiled=True
    )

    position_of = functools.partial(
        table_position, elem_count=elem_count, face_count=face_count, capacity=capacity
    )
    schur_blocks, shares = pl.pallas_call(
        functools.partial(main_kernel, position_of),
        out_shape=(
            jax.ShapeDtypeStruct((elements, trace, trace), BF16),
            jax.ShapeDtypeStruct((SHARE_ROWS, LANES), BF16),
        ),
        in_specs=[VMEM, ANY, ANY, ANY, ANY],
        out_specs=(ANY, VMEM),
        scratch_shapes=[
            pltpu.SMEM((FACES_PER_ELEM, elements), I32),
            pltpu.VMEM((elements, modes), BF16),
            pltpu.VMEM((elements, modes, modes), BF16),
            pltpu.VMEM((elements, modes, trace), BF16),
            pltpu.VMEM((elements, trace, trace), BF16),
            pltpu.VMEM((LANES, modes), F32),
            pltpu.VMEM((modes, LANES), BF16),
            pltpu.VMEM((SHARE_ROWS, LANES), F32),
            pltpu.VMEM((SHARE_ROWS, LANES), F32),
            pltpu.VMEM((modes, trace + LANES), BF16),
            pltpu.VMEM((modes, trace + LANES), BF16),
            pltpu.VMEM((trace, modes), BF16),
            pltpu.VMEM((trace, modes), BF16),
            pltpu.SemaphoreType.DMA((2,)),
            pltpu.SemaphoreType.DMA((elements,)),
            pltpu.SemaphoreType.DMA((elements,)),
            pltpu.SemaphoreType.DMA((elements,)),
        ],
        compiler_params=params(BIG),
        cost_estimate=pl.CostEstimate(
            flops=2 * elements * modes * trace * (modes + trace),
            bytes_accessed=2 * elements * (modes * (modes + trace) + trace * trace),
            transcendentals=0,
        ),
        name="condense",
    )(table, connectivity.T, interior_rhs, local_inverse, coupling)

    all_shares = [shares]
    for shift in range(1, elem_count):
        pairs = [(k, (k + shift) % elem_count) for k in range(elem_count)]
        all_shares.append(lax.ppermute(shares, "elem", pairs))

    slot_residual, coarse_blocks = pl.pallas_call(
        functools.partial(finish_kernel, elem_count, capacity, faces),
        out_shape=(
            jax.ShapeDtypeStruct((own, FACE_COEFFS), F32),
            jax.ShapeDtypeStruct((NC, MROW * MROW), F32),
        ),
        in_specs=[VMEM] * (2 + elem_count),
        out_specs=(VMEM, VMEM),
        scratch_shapes=[
            pltpu.VMEM((OWNER_ROWS, LANES), F32),
            pltpu.VMEM((NC * MROW, LANES), F32),
        ],
        compiler_params=params(SMALL),
        name="finish",
    )(got, table, *all_shares)
    return schur_blocks, slot_residual, coarse_blocks


def solution(mesh):
    return jax.shard_map(
        shards,
        mesh=mesh,
        in_specs=(
            P(("face", "elem"), None),
            P(("face", "elem"), None),
            P(("face", "elem"), None),
            P(("face", "elem"), None),
            P(("face", "elem")),
            P(("face", "elem"), None),
            P(("face", "elem"), None, None),
            P(("face", "elem"), None, None),
            P(("face", "elem"), None),
        ),
        out_specs=(
            P(("face", "elem"), None, None),
            P(("face", "elem"), None),
            P(("face", "elem"), None),
        ),
        check_vma=False,
    )
```

time: 51.5 us -> 45.6 us (0.89)
  blocking collectives: 0 us -> 15.6 us
  starting transfers between devices: 14.8 us -> 5.42 us
  local copies, waits for them, and re-layouts: 9.65 us -> 0.7 us
  Pallas kernels: 22.8 us -> 19.4 us
    all_to_all x0 -> x1, blocking collectives: none -> 15.6 us  [shards(): lax.all_to_all(placed.reshape(devices, capacity, FACE_COEFFS), ('face', '...]
    unnamed x23 -> x4, local copies, waits for them, and re-layouts: 9.57 us -> 0.7 us
    all_to_all x1 -> x0, starting transfers between devices: 7.3 us -> none  [shards(): lax.all_to_all(placed.reshape(devices, capacity, FACE_COEFFS), ('face', '...]
    pallas_call x4 -> x2, Pallas kernels: 13.7 us -> 6.48 us  [the longest x1 4.6 us: shards(): pl.pallas_call(functools.partial(send_kernel, elem_count, face_count, cap...]
    pallas_call x1, Pallas kernels: 9.13 us -> 12.9 us  [shards(): pl.pallas_call(functools.partial(main_kernel, position_of), out_shape=(ja...]
    all_to_all x1, starting transfers between devices: 5.83 us -> 3.54 us  [shards(): lax.all_to_all(half_grams.reshape(face_count, OWNER_ROWS, LANES), 'face',...]
  transfers between devices with their start and end apart: 5 -> 4, of which waited for: 2 -> 2; matrix products, arithmetic and copies ran while one was open for 2% -> 0% of each run, Pallas kernels for 38% -> 29%
where the time goes in v2:
time: 45.6 us; the launch traced here: 45.1 us
  Pallas kernels  19.4 us (43%)
  blocking collectives  15.6 us (34%)
  starting transfers between devices  5.42 us (12%)
  waiting for transfers between devices  3.29 us (7%)
  local copies, waits for them, and re-layouts  0.7 us (2%)
  between operations  0.67 us (1%)
    all_to_all x1, blocking collectives, shards(): lax.all_to_all(placed.reshape(devices, capacity, FACE_COEFFS), ('face', '...  15.6 us
    pallas_call x1, Pallas kernels, shards(): pl.pallas_call(functools.partial(main_kernel, position_of), out_shape=(ja...  12.9 us
    pallas_call x1, Pallas kernels, shards(): pl.pallas_call(functools.partial(send_kernel, elem_count, face_count, cap...  4.6 us
    all_to_all x1, starting transfers between devices, shards(): lax.all_to_all(half_grams.reshape(face_count, OWNER_ROWS, LANES), 'face',...  3.54 us
    ppermute x3, waiting for transfers between devices, shards(): all_shares.append(lax.ppermute(shares, 'elem', pairs))  3.28 us
    ppermute x3, starting transfers between devices, shards(): all_shares.append(lax.ppermute(shares, 'elem', pairs))  1.89 us
    pallas_call x1, Pallas kernels, shards(): pl.pallas_call(functools.partial(finish_kernel, elem_count, capacity, fac...  1.88 us
  transfers between devices with their start and end apart: 4, of which 2 were waited for; matrix products, arithmetic and copies ran while one was open for 0% of the time, Pallas kernels for 29%

profile of v2, /device:TPU:0, one launch (start us, length us, event | category | flops | bytes accessed | tf_op | source)
XLA Modules:
  0.0 45.1 jit_solution(7141063980839711957)
XLA Ops:
  0.6 4.6 %send.1 = (bf16[512,128]{1,0:T(8,128)(2,1)}, bf16[2176,128]{1,0:T(8,128)(2,1)}) custom-call(s32[1,64]{1,0:T(1,128)} %bitcast.10, bf16[64,128]{1,0:T(8,128)(2,1)} %trace_ref.1, s32[96]{0:T(128)} %bitcast.11, s32[96]{0:T(128)} %coarse_hbm.1, bf16[96,6144]{1,0:T(8,128)(2,1)} %tiles_hbm.1), custom_call_target="tpu_custom_call" | custom-call | tf_op jit(solution)/shard_map/send/pallas_call | solution.py:373
  5.2 15.6 %all_to_all.10 = bf16[32,16,128]{2,1,0:T(8,128)(2,1)} all-to-all(bf16[32,16,128]{2,1,0:T(8,128)(2,1)} %bitcast.9), channel_id=1, replica_groups=mesh['face'=8,'elem'=4] {'face','elem'}, dimensions={0} | all-to-all | bytes 262144 | tf_op jit(solution)/shard_map/all_to_all | solution.py:401
  20.9 3.5 %all-to-all-start.1 = ((bf16[8,272,128]{2,1,0:T(8,128)(2,1)}), bf16[8,272,128]{2,1,0:T(8,128)(2,1)S(1)}, u32[]{:S(2)}, u32[]{:S(2)}) async-start(bf16[8,272,128]{2,1,0:T(8,128)(2,1)} %bitcast.8), calls=%async_computation.1 | async-start | bytes 1114112 | tf_op jit(solution)/shard_map/all_to_all | solution.py:404
  24.4 0.0 copy-start
  24.4 12.9 %condense.1 = (bf16[9,384,384]{2,1,0:T(8,128)(2,1)}, bf16[32,128]{1,0:T(8,128)(2,1)}) custom-call(bf16[512,128]{1,0:T(8,128)(2,1)} %bitcast.6, s32[3,9]{1,0:T(4,128)} %bitcast.12, bf16[9,512]{1,0:T(8,128)(2,1)} %rhs_hbm.1, bf16[9,512,512]{2,1,0:T(8,128)(2,1)} %inverse_hbm.1, bf16[9,512,384]{2,1,0:T(8,128)(2,1)} %coupling_hbm.1), custom_call_target="tpu_custom_call" | custom-call | flops 3170893824 | bytes 10911744 | tf_op jit(solution)/shard_map/condense/pallas_call | solution.py:411
  37.4 0.2 collective-permute-start.2
  37.6 1.7 %collective-permute-start.1 = (bf16[32,128]{1,0:T(8,128)(2,1)}, bf16[32,128]{1,0:T(8,128)(2,1)S(1)}, u32[]{:S(2)}, u32[]{:S(2)}) collective-permute-start(bf16[32,128]{1,0:T(8,128)(2,1)} %get-tuple-element.12.refs_0_), channel_id=1, source_target_pairs={{0,2},{1,3},{2,0},{3,1},{4,6},{5,7},{6,4},{7,5},{8,10},{9,11},{10,... | collective-permute-start | bytes 24584 | tf_op jit(solution)/shard_map/ppermute | solution.py:450
  39.3 0.0 collective-permute-start
  39.3 0.0 collective-permute-done.2.refs_3_
  39.3 2.2 %collective-permute-done.1.refs_2_ = bf16[32,128]{1,0:T(8,128)(2,1)S(1)} collective-permute-done((bf16[32,128]{1,0:T(8,128)(2,1)}, bf16[32,128]{1,0:T(8,128)(2,1)S(1)}, u32[]{:S(2)}, u32[]{:S(2)}) %collective-permute-start.1) | collective-permute-done | bytes 8224 | tf_op jit(solution)/shard_map/ppermute | solution.py:450
  41.4 1.1 %collective-permute-done.refs_1_ = bf16[32,128]{1,0:T(8,128)(2,1)S(1)} collective-permute-done((bf16[32,128]{1,0:T(8,128)(2,1)}, bf16[32,128]{1,0:T(8,128)(2,1)S(1)}, u32[]{:S(2)}, u32[]{:S(2)}) %collective-permute-start) | collective-permute-done | bytes 8224 | tf_op jit(solution)/shard_map/ppermute | solution.py:450
  42.5 0.0 all-to-all-done.1.got_ref
  42.5 0.0 copy-done
  42.5 0.0 copy-start.1
  42.5 0.7 %copy-done.1 = bf16[32,128]{1,0:T(8,128)(2,1)S(1)} copy-done((bf16[32,128]{1,0:T(8,128)(2,1)S(1)}, bf16[32,128]{1,0:T(8,128)(2,1)}, u32[]{:S(2)}) %copy-start.1) | copy-done | bytes 8216
  43.2 1.9 %finish.1 = (f32[128,128]{1,0:T(8,128)}, f32[16,4096]{1,0:T(8,128)}) custom-call(bf16[8,272,128]{2,1,0:T(8,128)(2,1)S(1)} %all-to-all-done.1.got_ref, bf16[512,128]{1,0:T(8,128)(2,1)S(1)} %bitcast.7, bf16[32,128]{1,0:T(8,128)(2,1)S(1)} %copy-done.1, bf16[32,128]{1,0:T(8,128)(2,1)S(1)} %collective-permute-done.refs_1_, ...), custom_call_target="tpu_custom_call" | custom-call | tf_op jit(solution)/shard_map/finish/pallas_call | solution.py:452
Async XLA Ops:
  20.9 21.7 %all-to-all-start.1 = ((bf16[8,272,128]{2,1,0:T(8,128)(2,1)}), bf16[8,272,128]{2,1,0:T(8,128)(2,1)S(1)}, u32[]{:S(2)}, u32[]{:S(2)}) async-start(bf16[8,272,128]{2,1,0:T(8,128)(2,1)} %bitcast.8), calls=%async_computation.1 | async-start | bytes 1114112 | tf_op jit(solution)/shard_map/all_to_all | solution.py:404
  24.4 18.1 %copy-start = (bf16[32,16,128]{2,1,0:T(8,128)(2,1)S(1)}, bf16[32,16,128]{2,1,0:T(8,128)(2,1)}, u32[]{:S(2)}) copy-start(bf16[32,16,128]{2,1,0:T(8,128)(2,1)} %all_to_all.10) | copy-start | bytes 393220
  37.4 1.9 %collective-permute-start.2 = (bf16[32,128]{1,0:T(8,128)(2,1)}, bf16[32,128]{1,0:T(8,128)(2,1)S(1)}, u32[]{:S(2)}, u32[]{:S(2)}) collective-permute-start(bf16[32,128]{1,0:T(8,128)(2,1)} %get-tuple-element.12.refs_0_), channel_id=1, source_target_pairs={{0,3},{1,0},{2,1},{3,2},{4,7},{5,4},{6,5},{7,6},{8,11},{9,8},{10,9... | collective-permute-start | bytes 24584 | tf_op jit(solution)/shard_map/ppermute | solution.py:450
  37.6 3.9 %collective-permute-start.1 = (bf16[32,128]{1,0:T(8,128)(2,1)}, bf16[32,128]{1,0:T(8,128)(2,1)S(1)}, u32[]{:S(2)}, u32[]{:S(2)}) collective-permute-start(bf16[32,128]{1,0:T(8,128)(2,1)} %get-tuple-element.12.refs_0_), channel_id=1, source_target_pairs={{0,2},{1,3},{2,0},{3,1},{4,6},{5,7},{6,4},{7,5},{8,10},{9,11},{10,... | collective-permute-start | bytes 24584 | tf_op jit(solution)/shard_map/ppermute | solution.py:450
  39.3 3.3 %collective-permute-start = (bf16[32,128]{1,0:T(8,128)(2,1)}, bf16[32,128]{1,0:T(8,128)(2,1)S(1)}, u32[]{:S(2)}, u32[]{:S(2)}) collective-permute-start(bf16[32,128]{1,0:T(8,128)(2,1)} %get-tuple-element.12.refs_0_), channel_id=1, source_target_pairs={{0,1},{1,2},{2,3},{3,0},{4,5},{5,6},{6,7},{7,4},{8,9},{9,10},{10,1... | collective-permute-start | bytes 24584 | tf_op jit(solution)/shard_map/ppermute | solution.py:450
  42.5 0.7 %copy-start.1 = (bf16[32,128]{1,0:T(8,128)(2,1)S(1)}, bf16[32,128]{1,0:T(8,128)(2,1)}, u32[]{:S(2)}) copy-start(bf16[32,128]{1,0:T(8,128)(2,1)} %get-tuple-element.12.refs_0_) | copy-start | bytes 24580

commit v3 on v2

--- a/solution.py
+++ b/solution.py
@@ -19,9 +19,9 @@
 SHARE_ROWS = 32
 SLOT_BASE = 16
 CHUNK = 16
+AHEAD = 3
+BIG = 62 << 20
 PITCH = MROW + 8
-BIG = 63
-SMALL = 16
 
 BF16 = jnp.bfloat16
 F32 = jnp.float32
@@ -50,16 +50,22 @@
     return dot((wanted == target).astype(BF16), rows_in).astype(BF16)
 
 
-def send_kernel(
-    elem_count,
+def place_kernel(elem_count, face_count, capacity, new_owner_ref, trace_ref, placed_ref):
+    placed_ref[...] = place_rows(
+        elem_count,
+        face_count,
+        capacity,
+        new_owner_ref[...],
+        trace_ref[...],
+        placed_ref.shape[0],
+    )
+
+
+def gram_kernel(
     face_count,
-    capacity,
-    new_owner_ref,
-    trace_ref,
     owner_hbm,
     coarse_hbm,
     tiles_hbm,
-    placed_ref,
     out_ref,
     owner_ref,
     coarse_ref,
@@ -78,14 +84,6 @@
         copy.start()
     for ref in (*accs, *diags):
         ref[...] = jnp.zeros_like(ref)
-    placed_ref[...] = place_rows(
-        elem_count,
-        face_count,
-        capacity,
-        new_owner_ref[...],
-        trace_ref[...],
-        placed_ref.shape[0],
-    )
     for copy in copies:
         copy.wait()
 
@@ -191,28 +189,27 @@
     faces = elements * FACES_PER_ELEM
     trace = FACES_PER_ELEM * FACE_COEFFS
     small = [
-        pltpu.make_async_copy(conn_hbm, conn_ref, small_sems.at[0]),
-        pltpu.make_async_copy(rhs_hbm, rhs_ref, small_sems.at[1]),
+        pltpu.make_async_copy(rhs_hbm, rhs_ref, small_sems.at[0]),
+        pltpu.make_async_copy(conn_hbm, conn_ref, small_sems.at[1]),
     ]
     for copy in small:
         copy.start()
 
     def bring(e):
         return (
+            pltpu.make_async_copy(coupling_hbm.at[e], coupling_ref.at[e], coupling_sems.at[e]),
             pltpu.make_async_copy(inverse_hbm.at[e], inverse_ref.at[e], inverse_sems.at[e]),
-            pltpu.make_async_copy(coupling_hbm.at[e], coupling_ref.at[e], coupling_sems.at[e]),
         )
 
     def leave(e):
         return pltpu.make_async_copy(schur_ref.at[e], schur_hbm.at[e], schur_sems.at[e])
 
-    for e in range(elements):
+    for e in range(min(AHEAD, elements)):
         for copy in bring(e):
             copy.start()
+    rhs_wide_ref[...] = jnp.zeros_like(rhs_wide_ref)
     for copy in small:
         copy.wait()
-
-    rhs_wide_ref[...] = jnp.zeros_like(rhs_wide_ref)
     rhs_wide_ref[0:elements, :] = rhs_ref[...].astype(F32)
     rhs_turned_ref[...] = rhs_wide_ref[...].T.astype(BF16)
     row = iota((SHARE_ROWS, LANES), 0)
@@ -249,6 +246,11 @@
     odd = (weight_b_ref, turned_b_ref)
 
     def advance(e, there, here):
+        @pl.when(e + AHEAD - 1 < elements)
+        def _():
+            for copy in bring(e + AHEAD - 1):
+                copy.start()
+
         for copy in bring(e):
             copy.wait()
         solve(e, *there)
@@ -302,12 +304,11 @@
     return total
 
 
-def finish_kernel(elem_count, capacity, faces, got_ref, table_ref, *refs):
-    share_refs = refs[:elem_count]
-    residual_ref, out_ref, sum_ref, full_ref = refs[elem_count:]
-    residual_ref[...] = residual(
-        elem_count, capacity, faces, residual_ref.shape[0], table_ref, share_refs
-    )
+def finish_kernel(elem_count, capacity, faces, got_ref, table_ref, share_hbm, *refs):
+    others = refs[: elem_count - 1]
+    residual_ref, out_ref, sum_ref, full_ref, share_ref, sem = refs[elem_count - 1 :]
+    copy = pltpu.make_async_copy(share_hbm, share_ref, sem)
+    copy.start()
     total = got_ref[0].astype(F32)
     for k in range(1, got_ref.shape[0]):
         total = total + got_ref[k].astype(F32)
@@ -337,14 +338,18 @@
         out_ref[:, chunk * LANES : (chunk + 1) * LANES] = jnp.where(
             low, left, pltpu.roll(right, MROW, 1)
         )
+    copy.wait()
+    residual_ref[...] = residual(
+        elem_count, capacity, faces, residual_ref.shape[0], table_ref, (share_ref, *others)
+    )
 
 
 ANY = pl.BlockSpec(memory_space=pl.ANY)
 VMEM = pl.BlockSpec(memory_space=pltpu.VMEM)
 
 
-def params(mib):
-    return pltpu.CompilerParams(vmem_limit_bytes=mib << 20)
+def params(limit):
+    return pltpu.CompilerParams(vmem_limit_bytes=limit)
 
 
 def shards(
@@ -370,41 +375,47 @@
     slots = devices * capacity
     own = slots // elem_count
 
-    placed, half_grams = pl.pallas_call(
-        functools.partial(send_kernel, elem_count, face_count, capacity),
-        out_shape=(
-            jax.ShapeDtypeStruct((slots, FACE_COEFFS), BF16),
-            jax.ShapeDtypeStruct((face_count * OWNER_ROWS, LANES), BF16),
-        ),
-        in_specs=[VMEM, VMEM, ANY, ANY, ANY],
-        out_specs=(VMEM, VMEM),
+    placed = pl.pallas_call(
+        functools.partial(place_kernel, elem_count, face_count, capacity),
+        out_shape=jax.ShapeDtypeStruct((slots, FACE_COEFFS), BF16),
+        in_specs=[VMEM, VMEM],
+        out_specs=VMEM,
+        compiler_params=params(BIG),
+        name="place",
+    )(new_owner.reshape(1, row_count), trace_old)
+    table = lax.all_to_all(
+        placed.reshape(devices, capacity, FACE_COEFFS), ("face", "elem"), 0, 0, tiled=True
+    ).reshape(slots, FACE_COEFFS)
+
+    blocks = face_count * NC
+    sums_shape = (blocks * DENSE, LANES)
+    half_grams = pl.pallas_call(
+        functools.partial(gram_kernel, face_count),
+        out_shape=jax.ShapeDtypeStruct((face_count * OWNER_ROWS, LANES), BF16),
+        in_specs=[ANY, ANY, ANY],
+        out_specs=VMEM,
         scratch_shapes=[
             pltpu.SMEM((tile_count,), I32),
             pltpu.SMEM((tile_count,), I32),
             pltpu.VMEM(mortar_tiles.shape, BF16),
             pltpu.VMEM((tile_count * PITCH, LANES), F32),
-            pltpu.VMEM((face_count * NC * DENSE, LANES), F32),
-            pltpu.VMEM((face_count * NC * DENSE, LANES), F32),
-            pltpu.VMEM((face_count * NC, LANES), F32),
-            pltpu.VMEM((face_count * NC, LANES), F32),
+            pltpu.VMEM(sums_shape, F32),
+            pltpu.VMEM(sums_shape, F32),
+            pltpu.VMEM((blocks, LANES), F32),
+            pltpu.VMEM((blocks, LANES), F32),
             pltpu.SemaphoreType.DMA((3,)),
         ],
         compiler_params=params(BIG),
-        name="send",
-    )(
-        new_owner.reshape(1, row_count),
-        trace_old,
-        mortar_owner.reshape(tile_count),
-        mortar_coarse,
-        mortar_tiles,
-    )
-    table = lax.all_to_all(
-        placed.reshape(devices, capacity, FACE_COEFFS), ("face", "elem"), 0, 0, tiled=True
-    ).reshape(slots, FACE_COEFFS)
+        cost_estimate=pl.CostEstimate(
+            flops=4 * tile_count * MROW * MROW * LANES, bytes_accessed=16 << 20, transcendentals=0
+        ),
+        name="gram",
+    )(mortar_owner.reshape(tile_count), mortar_coarse, mortar_tiles)
     got = lax.all_to_all(
         half_grams.reshape(face_count, OWNER_ROWS, LANES), "face", 0, 0, tiled=True
     )
 
+    slots_named, _ = lax.optimization_barrier((connectivity.T, half_grams))
     position_of = functools.partial(
         table_position, elem_count=elem_count, face_count=face_count, capacity=capacity
     )
@@ -442,7 +453,7 @@
             transcendentals=0,
         ),
         name="condense",
-    )(table, connectivity.T, interior_rhs, local_inverse, coupling)
+    )(table, slots_named, interior_rhs, local_inverse, coupling)
 
     all_shares = [shares]
     for shift in range(1, elem_count):
@@ -455,13 +466,15 @@
             jax.ShapeDtypeStruct((own, FACE_COEFFS), F32),
             jax.ShapeDtypeStruct((NC, MROW * MROW), F32),
         ),
-        in_specs=[VMEM] * (2 + elem_count),
+        in_specs=[VMEM, VMEM, ANY] + [VMEM] * (elem_count - 1),
         out_specs=(VMEM, VMEM),
         scratch_shapes=[
             pltpu.VMEM((OWNER_ROWS, LANES), F32),
             pltpu.VMEM((NC * MROW, LANES), F32),
+            pltpu.VMEM((SHARE_ROWS, LANES), BF16),
+            pltpu.SemaphoreType.DMA,
         ],
-        compiler_params=params(SMALL),
+        compiler_params=params(6 << 20),
         name="finish",
     )(got, table, *all_shares)
     return schur_blocks, slot_residual, coarse_blocks

time: 45.6 us -> 41.7 us (0.914)
  blocking collectives: 15.6 us -> 0 us
  starting transfers between devices: 5.42 us -> 12.7 us
  waiting for transfers between devices: 3.29 us -> 7.67 us
  local copies, waits for them, and re-layouts: 0.7 us -> 1.61 us
  Pallas kernels: 19.4 us -> 18.6 us
    all_to_all x1 -> x0, blocking collectives: 15.6 us -> none  [shards(): lax.all_to_all(placed.reshape(devices, capacity, FACE_COEFFS), ('face', '...]
    all_to_all x0 -> x1, starting transfers between devices: none -> 7.3 us  [shards(): lax.all_to_all(placed.reshape(devices, capacity, FACE_COEFFS), ('face', '...]
    all_to_all x0 -> x1, waiting for transfers between devices: none -> 4.38 us  [shards(): lax.all_to_all(placed.reshape(devices, capacity, FACE_COEFFS), ('face', '...]
    pallas_call x1, Pallas kernels: 12.9 us -> 11 us  [shards(): pl.pallas_call(functools.partial(main_kernel, position_of), out_shape=(ja...]
    pallas_call x1 -> x2, Pallas kernels: 4.6 us -> 5.53 us  [the longest x1 3.84 us: shards(): pl.pallas_call(functools.partial(gram_kernel, face_count), out_shape=jax....]
    unnamed x4 -> x6, local copies, waits for them, and re-layouts: 0.7 us -> 1.61 us
  transfers between devices with their start and end apart: 4 -> 5, of which waited for: 2 -> 3; matrix products, arithmetic and copies ran while one was open for 0% -> 0% of each run, Pallas kernels for 29% -> 36%
where the time goes in v3:
time: 41.7 us; the launch traced here: 41.2 us
  Pallas kernels  18.6 us (45%)
  starting transfers between devices  12.7 us (30%)
  waiting for transfers between devices  7.67 us (18%)
  local copies, waits for them, and re-layouts  1.61 us (4%)
  between operations  0.68 us (2%)
    pallas_call x1, Pallas kernels, shards(): pl.pallas_call(functools.partial(main_kernel, position_of), out_shape=(ja...  11 us
    all_to_all x1, starting transfers between devices, shards(): lax.all_to_all(placed.reshape(devices, capacity, FACE_COEFFS), ('face', '...  7.3 us
    all_to_all x1, waiting for transfers between devices, shards(): lax.all_to_all(placed.reshape(devices, capacity, FACE_COEFFS), ('face', '...  4.38 us
    pallas_call x1, Pallas kernels, shards(): pl.pallas_call(functools.partial(gram_kernel, face_count), out_shape=jax....  3.84 us
    all_to_all x1, starting transfers between devices, shards(): lax.all_to_all(half_grams.reshape(face_count, OWNER_ROWS, LANES), 'face',...  3.54 us
    ppermute x3, waiting for transfers between devices, shards(): all_shares.append(lax.ppermute(shares, 'elem', pairs))  3.28 us
    pallas_call x1, Pallas kernels, shards(): pl.pallas_call(functools.partial(finish_kernel, elem_count, capacity, fac...  2.02 us
    ppermute x3, starting transfers between devices, shards(): all_shares.append(lax.ppermute(shares, 'elem', pairs))  1.9 us
  transfers between devices with their start and end apart: 5, of which 3 were waited for; matrix products, arithmetic and copies ran while one was open for 0% of the time, Pallas kernels for 36%

profile of v3, /device:TPU:0, one launch (start us, length us, event | category | flops | bytes accessed | tf_op | source)
XLA Modules:
  0.0 41.2 jit_solution(15328511124426601733)
XLA Ops:
  0.6 1.7 %place.1 = bf16[512,128]{1,0:T(8,128)(2,1)} custom-call(s32[1,64]{1,0:T(1,128)} %bitcast.10, bf16[64,128]{1,0:T(8,128)(2,1)} %trace_ref.1), custom_call_target="tpu_custom_call" | custom-call | tf_op jit(solution)/shard_map/place/pallas_call | solution.py:378
  2.3 7.3 %all-to-all-start = ((bf16[32,16,128]{2,1,0:T(8,128)(2,1)}), bf16[32,16,128]{2,1,0:T(8,128)(2,1)S(1)}, u32[]{:S(2)}, u32[]{:S(2)}) async-start(bf16[32,16,128]{2,1,0:T(8,128)(2,1)} %bitcast.9), calls=%async_computation | async-start | bytes 262144 | tf_op jit(solution)/shard_map/all_to_all | solution.py:386
  9.6 3.8 %gram.1 = bf16[2176,128]{1,0:T(8,128)(2,1)} custom-call(s32[96]{0:T(128)} %bitcast.11, s32[96]{0:T(128)} %coarse_hbm.1, bf16[96,6144]{1,0:T(8,128)(2,1)} %tiles_hbm.1), custom_call_target="tpu_custom_call" | custom-call | flops 201326592 | bytes 16777216 | tf_op jit(solution)/shard_map/gram/pallas_call | solution.py:392
  13.5 4.4 %all-to-all-done = bf16[32,16,128]{2,1,0:T(8,128)(2,1)S(1)} async-done(((bf16[32,16,128]{2,1,0:T(8,128)(2,1)}), bf16[32,16,128]{2,1,0:T(8,128)(2,1)S(1)}, u32[]{:S(2)}, u32[]{:S(2)}) %all-to-all-start) | async-done | bytes 131104 | tf_op jit(solution)/shard_map/all_to_all | solution.py:386
  17.9 0.0 copy-start
  17.9 3.5 %all-to-all-start.1 = ((bf16[8,272,128]{2,1,0:T(8,128)(2,1)}), bf16[8,272,128]{2,1,0:T(8,128)(2,1)S(1)}, u32[]{:S(2)}, u32[]{:S(2)}) async-start(bf16[8,272,128]{2,1,0:T(8,128)(2,1)} %bitcast.8), calls=%async_computation.1 | async-start | bytes 1114112 | tf_op jit(solution)/shard_map/all_to_all | solution.py:414
  21.4 0.0 copy-done
  21.4 11.0 %condense.1 = (bf16[9,384,384]{2,1,0:T(8,128)(2,1)}, bf16[32,128]{1,0:T(8,128)(2,1)}) custom-call(bf16[512,128]{1,0:T(8,128)(2,1)} %bitcast.6, s32[3,9]{1,0:T(4,128)} %bitcast.12, bf16[9,512]{1,0:T(8,128)(2,1)} %rhs_hbm.1, bf16[9,512,512]{2,1,0:T(8,128)(2,1)} %inverse_hbm.1, bf16[9,512,384]{2,1,0:T(8,128)(2,1)} %coupling_hbm.1), custom_call_target="tpu_custom_call" | custom-call | flops 3170893824 | bytes 10911744 | tf_op jit(solution)/shard_map/condense/pallas_call | solution.py:422
  32.4 0.2 collective-permute-start.2
  32.6 1.7 %collective-permute-start.1 = (bf16[32,128]{1,0:T(8,128)(2,1)}, bf16[32,128]{1,0:T(8,128)(2,1)S(1)}, u32[]{:S(2)}, u32[]{:S(2)}) collective-permute-start(bf16[32,128]{1,0:T(8,128)(2,1)} %get-tuple-element.10.share_hbm), channel_id=1, source_target_pairs={{0,2},{1,3},{2,0},{3,1},{4,6},{5,7},{6,4},{7,5},{8,10},{9,11},{10,... | collective-permute-start | bytes 24584 | tf_op jit(solution)/shard_map/ppermute | solution.py:461
  34.3 0.0 collective-permute-start
  34.3 0.0 collective-permute-done.2.refs_2_
  34.3 2.2 %collective-permute-done.1.refs_1_ = bf16[32,128]{1,0:T(8,128)(2,1)S(1)} collective-permute-done((bf16[32,128]{1,0:T(8,128)(2,1)}, bf16[32,128]{1,0:T(8,128)(2,1)S(1)}, u32[]{:S(2)}, u32[]{:S(2)}) %collective-permute-start.1) | collective-permute-done | bytes 8224 | tf_op jit(solution)/shard_map/ppermute | solution.py:461
  36.5 1.1 %collective-permute-done.refs_0_ = bf16[32,128]{1,0:T(8,128)(2,1)S(1)} collective-permute-done((bf16[32,128]{1,0:T(8,128)(2,1)}, bf16[32,128]{1,0:T(8,128)(2,1)S(1)}, u32[]{:S(2)}, u32[]{:S(2)}) %collective-permute-start) | collective-permute-done | bytes 8224 | tf_op jit(solution)/shard_map/ppermute | solution.py:461
  37.6 0.0 all-to-all-done.1.got_ref
  37.6 0.0 copy-start.1
  37.6 0.9 %copy-done.1 = bf16[32,16,128]{2,1,0:T(8,128)(2,1)S(1)} copy-done((bf16[32,16,128]{2,1,0:T(8,128)(2,1)S(1)}, bf16[32,16,128]{2,1,0:T(8,128)(2,1)}, u32[]{:S(2)}) %copy-start.1) | copy-done | bytes 131096
  38.5 0.0 copy-start.2
  38.5 0.7 %copy-done.2 = bf16[32,128]{1,0:T(8,128)(2,1)S(1)} copy-done((bf16[32,128]{1,0:T(8,128)(2,1)S(1)}, bf16[32,128]{1,0:T(8,128)(2,1)}, u32[]{:S(2)}) %copy-start.2) | copy-done | bytes 8216
  39.2 2.0 %finish.1 = (f32[128,128]{1,0:T(8,128)}, f32[16,4096]{1,0:T(8,128)}) custom-call(bf16[8,272,128]{2,1,0:T(8,128)(2,1)S(1)} %all-to-all-done.1.got_ref, bf16[512,128]{1,0:T(8,128)(2,1)S(1)} %bitcast.7, bf16[32,128]{1,0:T(8,128)(2,1)S(1)} %copy-done.2, bf16[32,128]{1,0:T(8,128)(2,1)S(1)} %collective-permute-done.refs_0_, ...), custom_call_target="tpu_custom_call" | custom-call | tf_op jit(solution)/shard_map/finish/pallas_call | solution.py:463
Async XLA Ops:
  2.3 15.5 %all-to-all-start = ((bf16[32,16,128]{2,1,0:T(8,128)(2,1)}), bf16[32,16,128]{2,1,0:T(8,128)(2,1)S(1)}, u32[]{:S(2)}, u32[]{:S(2)}) async-start(bf16[32,16,128]{2,1,0:T(8,128)(2,1)} %bitcast.9), calls=%async_computation | async-start | bytes 262144 | tf_op jit(solution)/shard_map/all_to_all | solution.py:386
  17.9 3.5 %copy-start = (bf16[32,16,128]{2,1,0:T(8,128)(2,1)}, bf16[32,16,128]{2,1,0:T(8,128)(2,1)S(1)}, u32[]{:S(2)}) copy-start(bf16[32,16,128]{2,1,0:T(8,128)(2,1)S(1)} %all-to-all-done) | copy-start | bytes 393220
  17.9 19.8 %all-to-all-start.1 = ((bf16[8,272,128]{2,1,0:T(8,128)(2,1)}), bf16[8,272,128]{2,1,0:T(8,128)(2,1)S(1)}, u32[]{:S(2)}, u32[]{:S(2)}) async-start(bf16[8,272,128]{2,1,0:T(8,128)(2,1)} %bitcast.8), calls=%async_computation.1 | async-start | bytes 1114112 | tf_op jit(solution)/shard_map/all_to_all | solution.py:414
  32.4 1.9 %collective-permute-start.2 = (bf16[32,128]{1,0:T(8,128)(2,1)}, bf16[32,128]{1,0:T(8,128)(2,1)S(1)}, u32[]{:S(2)}, u32[]{:S(2)}) collective-permute-start(bf16[32,128]{1,0:T(8,128)(2,1)} %get-tuple-element.10.share_hbm), channel_id=1, source_target_pairs={{0,3},{1,0},{2,1},{3,2},{4,7},{5,4},{6,5},{7,6},{8,11},{9,8},{10,9... | collective-permute-start | bytes 24584 | tf_op jit(solution)/shard_map/ppermute | solution.py:461
  32.6 3.9 %collective-permute-start.1 = (bf16[32,128]{1,0:T(8,128)(2,1)}, bf16[32,128]{1,0:T(8,128)(2,1)S(1)}, u32[]{:S(2)}, u32[]{:S(2)}) collective-permute-start(bf16[32,128]{1,0:T(8,128)(2,1)} %get-tuple-element.10.share_hbm), channel_id=1, source_target_pairs={{0,2},{1,3},{2,0},{3,1},{4,6},{5,7},{6,4},{7,5},{8,10},{9,11},{10,... | collective-permute-start | bytes 24584 | tf_op jit(solution)/shard_map/ppermute | solution.py:461
  34.3 3.3 %collective-permute-start = (bf16[32,128]{1,0:T(8,128)(2,1)}, bf16[32,128]{1,0:T(8,128)(2,1)S(1)}, u32[]{:S(2)}, u32[]{:S(2)}) collective-permute-start(bf16[32,128]{1,0:T(8,128)(2,1)} %get-tuple-element.10.share_hbm), channel_id=1, source_target_pairs={{0,1},{1,2},{2,3},{3,0},{4,5},{5,6},{6,7},{7,4},{8,9},{9,10},{10,1... | collective-permute-start | bytes 24584 | tf_op jit(solution)/shard_map/ppermute | solution.py:461
  37.6 0.9 %copy-start.1 = (bf16[32,16,128]{2,1,0:T(8,128)(2,1)S(1)}, bf16[32,16,128]{2,1,0:T(8,128)(2,1)}, u32[]{:S(2)}) copy-start(bf16[32,16,128]{2,1,0:T(8,128)(2,1)} %copy-done) | copy-start | bytes 393220
  38.5 0.7 %copy-start.2 = (bf16[32,128]{1,0:T(8,128)(2,1)S(1)}, bf16[32,128]{1,0:T(8,128)(2,1)}, u32[]{:S(2)}) copy-start(bf16[32,128]{1,0:T(8,128)(2,1)} %get-tuple-element.10.share_hbm) | copy-start | bytes 24580

commit v4 on v3

--- a/solution.py
+++ b/solution.py
@@ -16,7 +16,9 @@
 LANES = 128
 DENSE = HALF * MROW // LANES
 OWNER_ROWS = NC * (DENSE + 1)
-SHARE_ROWS = 32
+PER_FACE = 16
+NAMED = FACES_PER_ELEM * PER_FACE
+SHARE_ROWS = NAMED + 16
 SLOT_BASE = 16
 CHUNK = 16
 AHEAD = 3
@@ -39,26 +41,22 @@
     return lax.dot_general(left, right, dims, preferred_element_type=F32)
 
 
-def place_rows(elem_count, face_count, capacity, owners, rows_in, slots):
-    rows = owners.shape[1]
+def place_kernel(face_count, capacity, owner_hbm, trace_hbm, placed_ref, owner_ref, trace_ref, sems):
+    copies = [
+        pltpu.make_async_copy(owner_hbm, owner_ref, sems.at[0]),
+        pltpu.make_async_copy(trace_hbm, trace_ref, sems.at[1]),
+    ]
+    for copy in copies:
+        copy.start()
+    slots, rows = placed_ref.shape[0], trace_ref.shape[0]
+    earlier = (iota((rows, rows), 0) < iota((rows, rows), 1)).astype(BF16)
+    for copy in copies:
+        copy.wait()
+    owners = owner_ref[...]
     hot = (iota((face_count, rows), 0) == owners).astype(F32)
-    earlier = (iota((rows, rows), 0) < iota((rows, rows), 1)).astype(BF16)
     rank = jnp.sum(hot * dot(hot.astype(BF16), earlier), axis=0, keepdims=True).astype(I32)
-    target = owners * capacity + rank
-    block = iota((slots, rows), 0)
-    wanted = lax.div(block, elem_count * capacity) * capacity + lax.rem(block, capacity)
-    return dot((wanted == target).astype(BF16), rows_in).astype(BF16)
-
-
-def place_kernel(elem_count, face_count, capacity, new_owner_ref, trace_ref, placed_ref):
-    placed_ref[...] = place_rows(
-        elem_count,
-        face_count,
-        capacity,
-        new_owner_ref[...],
-        trace_ref[...],
-        placed_ref.shape[0],
-    )
+    place = (iota((slots, rows), 0) == owners * capacity + rank).astype(BF16)
+    placed_ref[...] = dot(place, trace_ref[...]).astype(BF16)
 
 
 def gram_kernel(
@@ -151,49 +149,49 @@
         ).astype(BF16)
 
 
-def table_position(slot, elem_count, face_count, capacity):
-    part = face_count * capacity
-    inner = lax.rem(slot, part)
-    block = lax.div(inner, capacity) * elem_count + lax.div(slot, part)
-    return block * capacity + lax.rem(inner, capacity)
-
-
 def main_kernel(
-    position_of,
-    table_ref,
+    elem_count,
     conn_hbm,
     rhs_hbm,
     inverse_hbm,
     coupling_hbm,
-    schur_hbm,
-    share_ref,
-    conn_ref,
-    rhs_ref,
-    inverse_ref,
-    coupling_ref,
-    schur_ref,
-    rhs_wide_ref,
-    rhs_turned_ref,
-    lam_ref,
-    sum_ref,
-    weight_a_ref,
-    weight_b_ref,
-    turned_a_ref,
-    turned_b_ref,
-    small_sems,
-    inverse_sems,
-    coupling_sems,
-    schur_sems,
+    *refs,
 ):
+    tables_hbm = refs[:elem_count]
+    (
+        schur_hbm,
+        share_ref,
+        conn_ref,
+        rhs_ref,
+        table_ref,
+        inverse_ref,
+        coupling_ref,
+        schur_ref,
+        wide_ref,
+        rhs_turned_ref,
+        lam_turned_ref,
+        sum_ref,
+        weight_a_ref,
+        weight_b_ref,
+        turned_a_ref,
+        turned_b_ref,
+        small_sems,
+        table_sems,
+        inverse_sems,
+        coupling_sems,
+        schur_sems,
+    ) = refs[elem_count:]
     elements = rhs_ref.shape[0]
-    faces = elements * FACES_PER_ELEM
     trace = FACES_PER_ELEM * FACE_COEFFS
+    own = tables_hbm[0].shape[0]
+    mine = lax.axis_index("elem")
     small = [
         pltpu.make_async_copy(rhs_hbm, rhs_ref, small_sems.at[0]),
         pltpu.make_async_copy(conn_hbm, conn_ref, small_sems.at[1]),
     ]
-    for copy in small:
-        copy.start()
+    for k in range(elem_count):
+        there = table_ref.at[pl.ds(k * own, own)]
+        small.append(pltpu.make_async_copy(tables_hbm[k], there, table_sems.at[k]))
 
     def bring(e):
         return (
@@ -204,23 +202,30 @@
     def leave(e):
         return pltpu.make_async_copy(schur_ref.at[e], schur_hbm.at[e], schur_sems.at[e])
 
+    for copy in small:
+        copy.start()
     for e in range(min(AHEAD, elements)):
         for copy in bring(e):
             copy.start()
-    rhs_wide_ref[...] = jnp.zeros_like(rhs_wide_ref)
+    wide_ref[...] = jnp.zeros_like(wide_ref)
+    sum_ref[...] = jnp.zeros_like(sum_ref)
     for copy in small:
         copy.wait()
-    rhs_wide_ref[0:elements, :] = rhs_ref[...].astype(F32)
-    rhs_turned_ref[...] = rhs_wide_ref[...].T.astype(BF16)
-    row = iota((SHARE_ROWS, LANES), 0)
-    lane = iota((SHARE_ROWS, LANES), 1)
-    positions = jnp.full((SHARE_ROWS, LANES), -1, I32)
-    for k in range(faces):
-        slot = conn_ref[k % FACES_PER_ELEM, k // FACES_PER_ELEM]
-        positions = jnp.where(row == k, position_of(slot), positions)
+    wide_ref[0:elements, :] = rhs_ref[...].astype(F32)
+    rhs_turned_ref[...] = wide_ref[...].T.astype(BF16)
+    row = iota((PER_FACE, LANES), 0)
+    lane = iota((PER_FACE, LANES), 1)
     slots = table_ref.shape[0]
-    hot = jnp.concatenate([positions == lane + base for base in range(0, slots, LANES)], axis=1)
-    lam_ref[...] = dot(hot.astype(BF16), table_ref[...])
+    for a in range(FACES_PER_ELEM):
+        positions = jnp.full((PER_FACE, LANES), -1, I32)
+        for e in range(elements):
+            slot = conn_ref[a, e]
+            turn = lax.rem(mine + elem_count - lax.div(slot, own), elem_count)
+            positions = jnp.where(row == e, turn * own + lax.rem(slot, own), positions)
+        hot = jnp.concatenate([positions == lane + k for k in range(0, slots, LANES)], axis=1)
+        wide_ref[0:PER_FACE, a * LANES : (a + 1) * LANES] = dot(hot.astype(BF16), table_ref[...])
+    wide_ref[0:PER_FACE, trace:] = ((row == lane) & (row < elements)).astype(F32)
+    lam_turned_ref[...] = wide_ref[...].T.astype(BF16)
 
     def solve(e, weight_ref, turned_ref):
         coupling = coupling_ref[e]
@@ -232,15 +237,9 @@
         condensed = dot(turned_ref[...], weight_ref[...])
         schur = (-condensed[:, :trace]).astype(BF16)
         schur_ref[e] = schur
-        lam = [lam_ref[pl.ds(e * FACES_PER_ELEM + a, 1), :] for a in range(FACES_PER_ELEM)]
-        own = (iota((1, LANES), 1) == e).astype(F32)
-        vector = jnp.broadcast_to(jnp.concatenate([*lam, own], axis=1), (16, trace + LANES))
         matrix = jnp.concatenate([schur, condensed[:, trace:].astype(BF16)], axis=1)
-        share = dot(vector.astype(BF16), matrix, NT)
-        for a in range(FACES_PER_ELEM):
-            sum_ref[pl.ds(e * FACES_PER_ELEM + a, 1), :] = share[
-                0:1, a * FACE_COEFFS : (a + 1) * FACE_COEFFS
-            ]
+        share = dot(matrix, lam_turned_ref[...])
+        sum_ref[...] = jnp.where(iota((trace, LANES), 1) == e, share, sum_ref[...])
 
     even = (weight_a_ref, turned_a_ref)
     odd = (weight_b_ref, turned_b_ref)
@@ -275,40 +274,30 @@
     lane = iota((1, LANES), 1)
     high = jnp.full((1, LANES), -1, I32)
     rest = jnp.zeros((1, LANES), I32)
-    for k in range(faces):
-        slot = conn_ref[k % FACES_PER_ELEM, k // FACES_PER_ELEM]
-        high = jnp.where(lane == k, lax.div(slot, SLOT_BASE), high)
-        rest = jnp.where(lane == k, lax.rem(slot, SLOT_BASE), rest)
-    shares = jnp.where(row < faces, sum_ref[...], 0.0)
-    shares = jnp.where(row == faces, high.astype(F32), shares)
-    shares = jnp.where(row == faces + 1, rest.astype(F32), shares)
-    share_ref[...] = shares.astype(BF16)
+    for a in range(FACES_PER_ELEM):
+        here = slice(a * PER_FACE, (a + 1) * PER_FACE)
+        shares = sum_ref[a * LANES : (a + 1) * LANES, :].T
+        share_ref[here, :] = shares[:PER_FACE].astype(BF16)
+        for e in range(elements):
+            high = jnp.where(lane == a * PER_FACE + e, lax.div(conn_ref[a, e], SLOT_BASE), high)
+            rest = jnp.where(lane == a * PER_FACE + e, lax.rem(conn_ref[a, e], SLOT_BASE), rest)
+    names = jnp.where(row == 0, high, jnp.where(row == 1, rest, 0))
+    share_ref[NAMED:, :] = names.astype(F32).astype(BF16)
     for e in range(elements):
         leave(e).wait()
 
 
-def residual(elem_count, capacity, faces, own, table_ref, share_refs):
-    mine = lax.axis_index("elem")
-    slots = table_ref.shape[0]
-    place = iota((own, slots), 0)
-    position = (lax.div(place, capacity) * elem_count + mine) * capacity + lax.rem(place, capacity)
-    pick = (iota((own, slots), 1) == position).astype(BF16)
-    total = dot(pick, table_ref[...])
-    slot = (iota((own, SHARE_ROWS), 0) + mine * own).astype(F32)
-    for share_ref in share_refs:
-        shares = share_ref[...]
-        names = shares.astype(F32)
-        named = names[faces : faces + 1, :SHARE_ROWS] * SLOT_BASE
-        named = named + names[faces + 1 : faces + 2, :SHARE_ROWS]
-        total = total - dot((slot == named).astype(BF16), shares)
-    return total
-
-
-def finish_kernel(elem_count, capacity, faces, got_ref, table_ref, share_hbm, *refs):
-    others = refs[: elem_count - 1]
-    residual_ref, out_ref, sum_ref, full_ref, share_ref, sem = refs[elem_count - 1 :]
-    copy = pltpu.make_async_copy(share_hbm, share_ref, sem)
-    copy.start()
+def finish_kernel(elem_count, *refs):
+    ins = refs[: 2 + elem_count]
+    residual_ref, out_ref = refs[2 + elem_count : 4 + elem_count]
+    got_ref, table_ref, shares_ref, sum_ref, full_ref, sems = refs[4 + elem_count :]
+    places = [got_ref, table_ref] + [shares_ref.at[k] for k in range(elem_count)]
+    copies = [
+        pltpu.make_async_copy(ins[k], places[k], sems.at[k]) for k in range(2 + elem_count)
+    ]
+    for copy in copies:
+        copy.start()
+    copies[0].wait()
     total = got_ref[0].astype(F32)
     for k in range(1, got_ref.shape[0]):
         total = total + got_ref[k].astype(F32)
@@ -338,10 +327,17 @@
         out_ref[:, chunk * LANES : (chunk + 1) * LANES] = jnp.where(
             low, left, pltpu.roll(right, MROW, 1)
         )
-    copy.wait()
-    residual_ref[...] = residual(
-        elem_count, capacity, faces, residual_ref.shape[0], table_ref, (share_ref, *others)
-    )
+    for copy in copies[1:]:
+        copy.wait()
+    own = residual_ref.shape[0]
+    mine = lax.axis_index("elem")
+    slot = (iota((own, SHARE_ROWS), 0) + mine * own).astype(F32)
+    left = table_ref[...].astype(F32)
+    for k in range(elem_count):
+        names = shares_ref[k, NAMED:, :].astype(F32)
+        named = (names[0:1] * SLOT_BASE + names[1:2])[:, :SHARE_ROWS]
+        left = left - dot((slot == named).astype(BF16), shares_ref[k])
+    residual_ref[...] = left
 
 
 ANY = pl.BlockSpec(memory_space=pl.ANY)
@@ -350,6 +346,14 @@
 
 def params(limit):
     return pltpu.CompilerParams(vmem_limit_bytes=limit)
+
+
+def around(block, elem_count):
+    blocks = [block]
+    for shift in range(1, elem_count):
+        pairs = [(k, (k + shift) % elem_count) for k in range(elem_count)]
+        blocks.append(lax.ppermute(block, "elem", pairs))
+    return blocks
 
 
 def shards(
@@ -368,24 +372,27 @@
     row_count = trace_old.shape[0]
     tile_count = mortar_tiles.shape[0]
     elements, modes = interior_rhs.shape
-    faces = elements * FACES_PER_ELEM
     trace = FACES_PER_ELEM * FACE_COEFFS
     capacity = max(2, 2 * row_count // face_count)
-    devices = face_count * elem_count
-    slots = devices * capacity
-    own = slots // elem_count
+    own = face_count * capacity
 
     placed = pl.pallas_call(
-        functools.partial(place_kernel, elem_count, face_count, capacity),
-        out_shape=jax.ShapeDtypeStruct((slots, FACE_COEFFS), BF16),
-        in_specs=[VMEM, VMEM],
+        functools.partial(place_kernel, face_count, capacity),
+        out_shape=jax.ShapeDtypeStruct((own, FACE_COEFFS), BF16),
+        in_specs=[ANY, ANY],
         out_specs=VMEM,
+        scratch_shapes=[
+            pltpu.VMEM((1, row_count), I32),
+            pltpu.VMEM(trace_old.shape, BF16),
+            pltpu.SemaphoreType.DMA((2,)),
+        ],
         compiler_params=params(BIG),
         name="place",
     )(new_owner.reshape(1, row_count), trace_old)
-    table = lax.all_to_all(
-        placed.reshape(devices, capacity, FACE_COEFFS), ("face", "elem"), 0, 0, tiled=True
-    ).reshape(slots, FACE_COEFFS)
+    rows = lax.all_to_all(
+        placed.reshape(face_count, capacity, FACE_COEFFS), "face", 0, 0, tiled=True
+    ).reshape(own, FACE_COEFFS)
+    tables = around(rows, elem_count)
 
     blocks = face_count * NC
     sums_shape = (blocks * DENSE, LANES)
@@ -416,32 +423,31 @@
     )
 
     slots_named, _ = lax.optimization_barrier((connectivity.T, half_grams))
-    position_of = functools.partial(
-        table_position, elem_count=elem_count, face_count=face_count, capacity=capacity
-    )
     schur_blocks, shares = pl.pallas_call(
-        functools.partial(main_kernel, position_of),
+        functools.partial(main_kernel, elem_count),
         out_shape=(
             jax.ShapeDtypeStruct((elements, trace, trace), BF16),
             jax.ShapeDtypeStruct((SHARE_ROWS, LANES), BF16),
         ),
-        in_specs=[VMEM, ANY, ANY, ANY, ANY],
+        in_specs=[ANY] * (4 + elem_count),
         out_specs=(ANY, VMEM),
         scratch_shapes=[
             pltpu.SMEM((FACES_PER_ELEM, elements), I32),
             pltpu.VMEM((elements, modes), BF16),
+            pltpu.VMEM((elem_count * own, FACE_COEFFS), BF16),
             pltpu.VMEM((elements, modes, modes), BF16),
             pltpu.VMEM((elements, modes, trace), BF16),
             pltpu.VMEM((elements, trace, trace), BF16),
             pltpu.VMEM((LANES, modes), F32),
             pltpu.VMEM((modes, LANES), BF16),
-            pltpu.VMEM((SHARE_ROWS, LANES), F32),
-            pltpu.VMEM((SHARE_ROWS, LANES), F32),
+            pltpu.VMEM((trace + LANES, LANES), BF16),
+            pltpu.VMEM((trace, LANES), F32),
             pltpu.VMEM((modes, trace + LANES), BF16),
             pltpu.VMEM((modes, trace + LANES), BF16),
             pltpu.VMEM((trace, modes), BF16),
             pltpu.VMEM((trace, modes), BF16),
             pltpu.SemaphoreType.DMA((2,)),
+            pltpu.SemaphoreType.DMA((elem_count,)),
             pltpu.SemaphoreType.DMA((elements,)),
             pltpu.SemaphoreType.DMA((elements,)),
             pltpu.SemaphoreType.DMA((elements,)),
@@ -453,30 +459,27 @@
             transcendentals=0,
         ),
         name="condense",
-    )(table, slots_named, interior_rhs, local_inverse, coupling)
-
-    all_shares = [shares]
-    for shift in range(1, elem_count):
-        pairs = [(k, (k + shift) % elem_count) for k in range(elem_count)]
-        all_shares.append(lax.ppermute(shares, "elem", pairs))
+    )(slots_named, interior_rhs, local_inverse, coupling, *tables)
 
     slot_residual, coarse_blocks = pl.pallas_call(
-        functools.partial(finish_kernel, elem_count, capacity, faces),
+        functools.partial(finish_kernel, elem_count),
         out_shape=(
             jax.ShapeDtypeStruct((own, FACE_COEFFS), F32),
             jax.ShapeDtypeStruct((NC, MROW * MROW), F32),
         ),
-        in_specs=[VMEM, VMEM, ANY] + [VMEM] * (elem_count - 1),
+        in_specs=[ANY] * (2 + elem_count),
         out_specs=(VMEM, VMEM),
         scratch_shapes=[
+            pltpu.VMEM(got.shape, BF16),
+            pltpu.VMEM((own, FACE_COEFFS), BF16),
+            pltpu.VMEM((elem_count, SHARE_ROWS, LANES), BF16),
             pltpu.VMEM((OWNER_ROWS, LANES), F32),
             pltpu.VMEM((NC * MROW, LANES), F32),
-            pltpu.VMEM((SHARE_ROWS, LANES), BF16),
-            pltpu.SemaphoreType.DMA,
+            pltpu.SemaphoreType.DMA((2 + elem_count,)),
         ],
-        compiler_params=params(6 << 20),
+        compiler_params=params(BIG),
         name="finish",
-    )(got, table, *all_shares)
+    )(got, rows, *around(shares, elem_count))
     return schur_blocks, slot_residual, coarse_blocks
 
 

time: 41.7 us -> 46.5 us (1.12)
  starting transfers between devices: 12.7 us -> 14.4 us
  waiting for transfers between devices: 7.67 us -> 9.2 us
  Pallas kernels: 18.6 us -> 19.7 us
    ppermute x3 -> x6, waiting for transfers between devices: 3.28 us -> 6.37 us  [around(): blocks.append(lax.ppermute(block, 'elem', pairs))]
    ppermute x3 -> x6, starting transfers between devices: 1.9 us -> 3.56 us  [around(): blocks.append(lax.ppermute(block, 'elem', pairs))]
    all_to_all x1, waiting for transfers between devices: 4.38 us -> 2.83 us  [shards(): lax.all_to_all(placed.reshape(face_count, capacity, FACE_COEFFS), 'face',...]
    pallas_call x3, Pallas kernels: 14.7 us -> 15.9 us  [the longest x1 11.2 us: shards(): pl.pallas_call(functools.partial(main_kernel, elem_count), out_shape=(jax...]
    unnamed x6 -> x16, local copies, waits for them, and re-layouts: 1.61 us -> 2.02 us
  transfers between devices with their start and end apart: 5 -> 8, of which waited for: 3 -> 5; matrix products, arithmetic and copies ran while one was open for 0% -> 0% of each run, Pallas kernels for 36% -> 33%
where the time goes in v4:
time: 46.5 us; the launch traced here: 46.1 us
  Pallas kernels  19.7 us (42%)
  starting transfers between devices  14.4 us (31%)
  waiting for transfers between devices  9.2 us (20%)
  local copies, waits for them, and re-layouts  2.02 us (4%)
  between operations  0.71 us (2%)
    pallas_call x1, Pallas kernels, shards(): pl.pallas_call(functools.partial(main_kernel, elem_count), out_shape=(jax...  11.2 us
    all_to_all x1, starting transfers between devices, shards(): lax.all_to_all(placed.reshape(face_count, capacity, FACE_COEFFS), 'face',...  7.29 us
    ppermute x6, waiting for transfers between devices, around(): blocks.append(lax.ppermute(block, 'elem', pairs))  6.37 us
    pallas_call x1, Pallas kernels, shards(): pl.pallas_call(functools.partial(gram_kernel, face_count), out_shape=jax....  3.85 us
    ppermute x6, starting transfers between devices, around(): blocks.append(lax.ppermute(block, 'elem', pairs))  3.56 us
    all_to_all x1, starting transfers between devices, shards(): lax.all_to_all(half_grams.reshape(face_count, OWNER_ROWS, LANES), 'face',...  3.54 us
    pallas_call x1, Pallas kernels, shards(): pl.pallas_call(functools.partial(finish_kernel, elem_count), out_shape=(j...  3.07 us
    all_to_all x1, waiting for transfers between devices, shards(): lax.all_to_all(placed.reshape(face_count, capacity, FACE_COEFFS), 'face',...  2.83 us
  transfers between devices with their start and end apart: 8, of which 5 were waited for; matrix products, arithmetic and copies ran while one was open for 0% of the time, Pallas kernels for 33%

profile of v4, /device:TPU:0, one launch (start us, length us, event | category | flops | bytes accessed | tf_op | source)
XLA Modules:
  0.0 46.1 jit_solution(6676925870911584314)
XLA Ops:
  0.6 1.6 %place.1 = bf16[128,128]{1,0:T(8,128)(2,1)} custom-call(s32[1,64]{1,0:T(1,128)} %bitcast.13, bf16[64,128]{1,0:T(8,128)(2,1)} %trace_hbm.1), custom_call_target="tpu_custom_call" | custom-call | tf_op jit(solution)/shard_map/place/pallas_call | solution.py:379
  2.3 7.3 %all-to-all-start = ((bf16[8,16,128]{2,1,0:T(8,128)(2,1)}), bf16[8,16,128]{2,1,0:T(8,128)(2,1)S(1)}, u32[]{:S(2)}, u32[]{:S(2)}) async-start(bf16[8,16,128]{2,1,0:T(8,128)(2,1)} %bitcast.12), calls=%async_computation | async-start | bytes 65536 | tf_op jit(solution)/shard_map/all_to_all | solution.py:392
  9.6 3.8 %gram.1 = bf16[2176,128]{1,0:T(8,128)(2,1)} custom-call(s32[96]{0:T(128)} %bitcast.14, s32[96]{0:T(128)} %coarse_hbm.1, bf16[96,6144]{1,0:T(8,128)(2,1)} %tiles_hbm.1), custom_call_target="tpu_custom_call" | custom-call | flops 201326592 | bytes 16777216 | tf_op jit(solution)/shard_map/gram/pallas_call | solution.py:399
  13.4 2.8 %all-to-all-done = bf16[8,16,128]{2,1,0:T(8,128)(2,1)S(1)} async-done(((bf16[8,16,128]{2,1,0:T(8,128)(2,1)}), bf16[8,16,128]{2,1,0:T(8,128)(2,1)S(1)}, u32[]{:S(2)}, u32[]{:S(2)}) %all-to-all-start) | async-done | bytes 32800 | tf_op jit(solution)/shard_map/all_to_all | solution.py:392
  16.2 3.5 %all-to-all-start.1 = ((bf16[8,272,128]{2,1,0:T(8,128)(2,1)}), bf16[8,272,128]{2,1,0:T(8,128)(2,1)S(1)}, u32[]{:S(2)}, u32[]{:S(2)}) async-start(bf16[8,272,128]{2,1,0:T(8,128)(2,1)} %bitcast.6), calls=%async_computation.1 | async-start | bytes 1114112 | tf_op jit(solution)/shard_map/all_to_all | solution.py:421
  19.8 0.1 collective-permute-start.2
  19.9 1.6 %collective-permute-start.1 = (bf16[128,128]{1,0:T(8,128)(2,1)S(1)}, bf16[128,128]{1,0:T(8,128)(2,1)S(1)}, u32[]{:S(2)}, u32[]{:S(2)}) collective-permute-start(bf16[128,128]{1,0:T(8,128)(2,1)S(1)} %bitcast.8), channel_id=1, source_target_pairs={{0,2},{1,3},{2,0},{3,1},{4,6},{5,7},{6,4},{7,5},{8,10},{9,11},{10,... | collective-permute-start | bytes 98312 | tf_op jit(solution)/shard_map/ppermute | solution.py:355
  21.4 0.2 collective-permute-start
  21.6 0.0 collective-permute-done.2.refs_3_
  21.6 2.3 %collective-permute-done.1.refs_2_ = bf16[128,128]{1,0:T(8,128)(2,1)S(1)} collective-permute-done((bf16[128,128]{1,0:T(8,128)(2,1)S(1)}, bf16[128,128]{1,0:T(8,128)(2,1)S(1)}, u32[]{:S(2)}, u32[]{:S(2)}) %collective-permute-start.1) | collective-permute-done | bytes 32800 | tf_op jit(solution)/shard_map/ppermute | solution.py:355
  23.9 0.8 %collective-permute-done.refs_1_ = bf16[128,128]{1,0:T(8,128)(2,1)S(1)} collective-permute-done((bf16[128,128]{1,0:T(8,128)(2,1)S(1)}, bf16[128,128]{1,0:T(8,128)(2,1)S(1)}, u32[]{:S(2)}, u32[]{:S(2)}) %collective-permute-start) | collective-permute-done | bytes 32800 | tf_op jit(solution)/shard_map/ppermute | solution.py:355
  24.8 0.0 copy-start.7
  24.8 0.6 %copy-done.7 = bf16[128,128]{1,0:T(8,128)(2,1)} copy-done((bf16[128,128]{1,0:T(8,128)(2,1)}, bf16[128,128]{1,0:T(8,128)(2,1)S(1)}, u32[]{:S(2)}) %copy-start.7) | copy-done | bytes 32792
  25.4 11.2 %condense.1 = (bf16[9,384,384]{2,1,0:T(8,128)(2,1)}, bf16[64,128]{1,0:T(8,128)(2,1)}) custom-call(s32[3,9]{1,0:T(4,128)} %bitcast.15, bf16[9,512]{1,0:T(8,128)(2,1)} %rhs_hbm.1, bf16[9,512,512]{2,1,0:T(8,128)(2,1)} %inverse_hbm.1, bf16[9,512,384]{2,1,0:T(8,128)(2,1)} %coupling_hbm.1, bf16[128,128]{1,0:T(8,128)(2,1)} %bitcast.10, bf16[128,128]{1,0:T(8,128)(2,1)} %copy-done.7, ...), custom_call_target="tpu_custom_call" | custom-call | flops 3170893824 | bytes 10911744 | tf_op jit(solution)/shard_map/condense/pallas_call | solution.py:426
  36.6 0.1 collective-permute-start.5
  36.7 1.5 %collective-permute-start.4 = (bf16[64,128]{1,0:T(8,128)(2,1)}, bf16[64,128]{1,0:T(8,128)(2,1)S(1)}, u32[]{:S(2)}, u32[]{:S(2)}) collective-permute-start(bf16[64,128]{1,0:T(8,128)(2,1)} %get-tuple-element.10.refs_2_), channel_id=1, source_target_pairs={{0,2},{1,3},{2,0},{3,1},{4,6},{5,7},{6,4},{7,5},{8,10},{9,11},{10,... | collective-permute-start | bytes 49160 | tf_op jit(solution)/shard_map/ppermute | solution.py:355
  38.2 0.2 collective-permute-start.3
  38.4 0.0 collective-permute-done.5.refs_5_
  38.4 2.3 %collective-permute-done.4.refs_4_ = bf16[64,128]{1,0:T(8,128)(2,1)S(1)} collective-permute-done((bf16[64,128]{1,0:T(8,128)(2,1)}, bf16[64,128]{1,0:T(8,128)(2,1)S(1)}, u32[]{:S(2)}, u32[]{:S(2)}) %collective-permute-start.4) | collective-permute-done | bytes 16416 | tf_op jit(solution)/shard_map/ppermute | solution.py:355
  40.7 0.9 %collective-permute-done.3.refs_3_ = bf16[64,128]{1,0:T(8,128)(2,1)S(1)} collective-permute-done((bf16[64,128]{1,0:T(8,128)(2,1)}, bf16[64,128]{1,0:T(8,128)(2,1)S(1)}, u32[]{:S(2)}, u32[]{:S(2)}) %collective-permute-start.3) | collective-permute-done | bytes 16416 | tf_op jit(solution)/shard_map/ppermute | solution.py:355
  41.6 0.0 all-to-all-done.1.refs_0_
  41.6 0.6 %copy-done.4 = bf16[64,128]{1,0:T(8,128)(2,1)} copy-done((bf16[64,128]{1,0:T(8,128)(2,1)}, bf16[64,128]{1,0:T(8,128)(2,1)S(1)}, u32[]{:S(2)}) %copy-start.4) | copy-done | bytes 16408
  42.2 0.8 %copy-done = bf16[8,272,128]{2,1,0:T(8,128)(2,1)} copy-done((bf16[8,272,128]{2,1,0:T(8,128)(2,1)}, bf16[8,272,128]{2,1,0:T(8,128)(2,1)S(1)}, u32[]{:S(2)}) %copy-start) | copy-done | bytes 557080
  43.0 3.1 %finish.1 = (f32[128,128]{1,0:T(8,128)}, f32[16,4096]{1,0:T(8,128)}) custom-call(bf16[8,272,128]{2,1,0:T(8,128)(2,1)} %copy-done, bf16[128,128]{1,0:T(8,128)(2,1)} %bitcast.11, bf16[64,128]{1,0:T(8,128)(2,1)} %get-tuple-element.10.refs_2_, bf16[64,128]{1,0:T(8,128)(2,1)} %copy-done.4, bf16[64,128]{1,0:T(8,128)(2,1)} %copy-done.3, bf16[64,128]{1,0:T(8,128)(2,1)} %copy-done.2), custom_call_target="tpu_custom_call" | custom-call | tf_op jit(solution)/shard_map/finish/pallas_call | solution.py:464
  (12 shorter events, 0.0 us)
Async XLA Ops:
  2.3 14.0 %all-to-all-start = ((bf16[8,16,128]{2,1,0:T(8,128)(2,1)}), bf16[8,16,128]{2,1,0:T(8,128)(2,1)S(1)}, u32[]{:S(2)}, u32[]{:S(2)}) async-start(bf16[8,16,128]{2,1,0:T(8,128)(2,1)} %bitcast.12), calls=%async_computation | async-start | bytes 65536 | tf_op jit(solution)/shard_map/all_to_all | solution.py:392
  16.2 8.5 %copy-start.1 = (bf16[8,16,128]{2,1,0:T(8,128)(2,1)}, bf16[8,16,128]{2,1,0:T(8,128)(2,1)S(1)}, u32[]{:S(2)}) copy-start(bf16[8,16,128]{2,1,0:T(8,128)(2,1)S(1)} %all-to-all-done) | copy-start | bytes 98308
  16.2 25.3 %all-to-all-start.1 = ((bf16[8,272,128]{2,1,0:T(8,128)(2,1)}), bf16[8,272,128]{2,1,0:T(8,128)(2,1)S(1)}, u32[]{:S(2)}, u32[]{:S(2)}) async-start(bf16[8,272,128]{2,1,0:T(8,128)(2,1)} %bitcast.6), calls=%async_computation.1 | async-start | bytes 1114112 | tf_op jit(solution)/shard_map/all_to_all | solution.py:421
  19.8 1.8 %collective-permute-start.2 = (bf16[128,128]{1,0:T(8,128)(2,1)S(1)}, bf16[128,128]{1,0:T(8,128)(2,1)S(1)}, u32[]{:S(2)}, u32[]{:S(2)}) collective-permute-start(bf16[128,128]{1,0:T(8,128)(2,1)S(1)} %bitcast.7), channel_id=1, source_target_pairs={{0,3},{1,0},{2,1},{3,2},{4,7},{5,4},{6,5},{7,6},{8,11},{9,8},{10,9... | collective-permute-start | bytes 98312 | tf_op jit(solution)/shard_map/ppermute | solution.py:355
  19.9 4.1 %collective-permute-start.1 = (bf16[128,128]{1,0:T(8,128)(2,1)S(1)}, bf16[128,128]{1,0:T(8,128)(2,1)S(1)}, u32[]{:S(2)}, u32[]{:S(2)}) collective-permute-start(bf16[128,128]{1,0:T(8,128)(2,1)S(1)} %bitcast.8), channel_id=1, source_target_pairs={{0,2},{1,3},{2,0},{3,1},{4,6},{5,7},{6,4},{7,5},{8,10},{9,11},{10,... | collective-permute-start | bytes 98312 | tf_op jit(solution)/shard_map/ppermute | solution.py:355
  21.4 3.3 %collective-permute-start = (bf16[128,128]{1,0:T(8,128)(2,1)S(1)}, bf16[128,128]{1,0:T(8,128)(2,1)S(1)}, u32[]{:S(2)}, u32[]{:S(2)}) collective-permute-start(bf16[128,128]{1,0:T(8,128)(2,1)S(1)} %bitcast.9), channel_id=1, source_target_pairs={{0,1},{1,2},{2,3},{3,0},{4,5},{5,6},{6,7},{7,4},{8,9},{9,10},{10,1... | collective-permute-start | bytes 98312 | tf_op jit(solution)/shard_map/ppermute | solution.py:355
  21.6 3.2 %copy-start.5 = (bf16[128,128]{1,0:T(8,128)(2,1)}, bf16[128,128]{1,0:T(8,128)(2,1)S(1)}, u32[]{:S(2)}) copy-start(bf16[128,128]{1,0:T(8,128)(2,1)S(1)} %collective-permute-done.2.refs_3_) | copy-start | bytes 98308
  23.9 0.8 %copy-start.6 = (bf16[128,128]{1,0:T(8,128)(2,1)}, bf16[128,128]{1,0:T(8,128)(2,1)S(1)}, u32[]{:S(2)}) copy-start(bf16[128,128]{1,0:T(8,128)(2,1)S(1)} %collective-permute-done.1.refs_2_) | copy-start | bytes 98308
  24.8 0.6 %copy-start.7 = (bf16[128,128]{1,0:T(8,128)(2,1)}, bf16[128,128]{1,0:T(8,128)(2,1)S(1)}, u32[]{:S(2)}) copy-start(bf16[128,128]{1,0:T(8,128)(2,1)S(1)} %collective-permute-done.refs_1_) | copy-start | bytes 98308
  36.6 1.8 %collective-permute-start.5 = (bf16[64,128]{1,0:T(8,128)(2,1)}, bf16[64,128]{1,0:T(8,128)(2,1)S(1)}, u32[]{:S(2)}, u32[]{:S(2)}) collective-permute-start(bf16[64,128]{1,0:T(8,128)(2,1)} %get-tuple-element.10.refs_2_), channel_id=1, source_target_pairs={{0,3},{1,0},{2,1},{3,2},{4,7},{5,4},{6,5},{7,6},{8,11},{9,8},{10,9... | collective-permute-start | bytes 49160 | tf_op jit(solution)/shard_map/ppermute | solution.py:355
  36.7 4.0 %collective-permute-start.4 = (bf16[64,128]{1,0:T(8,128)(2,1)}, bf16[64,128]{1,0:T(8,128)(2,1)S(1)}, u32[]{:S(2)}, u32[]{:S(2)}) collective-permute-start(bf16[64,128]{1,0:T(8,128)(2,1)} %get-tuple-element.10.refs_2_), channel_id=1, source_target_pairs={{0,2},{1,3},{2,0},{3,1},{4,6},{5,7},{6,4},{7,5},{8,10},{9,11},{10,... | collective-permute-start | bytes 49160 | tf_op jit(solution)/shard_map/ppermute | solution.py:355
  38.2 3.4 %collective-permute-start.3 = (bf16[64,128]{1,0:T(8,128)(2,1)}, bf16[64,128]{1,0:T(8,128)(2,1)S(1)}, u32[]{:S(2)}, u32[]{:S(2)}) collective-permute-start(bf16[64,128]{1,0:T(8,128)(2,1)} %get-tuple-element.10.refs_2_), channel_id=1, source_target_pairs={{0,1},{1,2},{2,3},{3,0},{4,5},{5,6},{6,7},{7,4},{8,9},{9,10},{10,1... | collective-permute-start | bytes 49160 | tf_op jit(solution)/shard_map/ppermute | solution.py:355
  38.4 3.2 %copy-start.2 = (bf16[64,128]{1,0:T(8,128)(2,1)}, bf16[64,128]{1,0:T(8,128)(2,1)S(1)}, u32[]{:S(2)}) copy-start(bf16[64,128]{1,0:T(8,128)(2,1)S(1)} %collective-permute-done.5.refs_5_) | copy-start | bytes 49156
  40.7 0.9 %copy-start.3 = (bf16[64,128]{1,0:T(8,128)(2,1)}, bf16[64,128]{1,0:T(8,128)(2,1)S(1)}, u32[]{:S(2)}) copy-start(bf16[64,128]{1,0:T(8,128)(2,1)S(1)} %collective-permute-done.4.refs_4_) | copy-start | bytes 49156
  41.6 0.6 %copy-start.4 = (bf16[64,128]{1,0:T(8,128)(2,1)}, bf16[64,128]{1,0:T(8,128)(2,1)S(1)}, u32[]{:S(2)}) copy-start(bf16[64,128]{1,0:T(8,128)(2,1)S(1)} %collective-permute-done.3.refs_3_) | copy-start | bytes 49156
  42.2 0.8 %copy-start = (bf16[8,272,128]{2,1,0:T(8,128)(2,1)}, bf16[8,272,128]{2,1,0:T(8,128)(2,1)S(1)}, u32[]{:S(2)}) copy-start(bf16[8,272,128]{2,1,0:T(8,128)(2,1)S(1)} %all-to-all-done.1.refs_0_) | copy-start | bytes 1671172

commit v5 on v4

v5 whole, which is shorter than its diff:
```python
import functools

import jax
import jax.numpy as jnp
from jax import lax
from jax.experimental import pallas as pl
from jax.experimental.pallas import tpu as pltpu
from jax.sharding import PartitionSpec as P

FACE_COEFFS = 128
FACES_PER_ELEM = 3
MROW = 64
MCOL = 96
NC = 16
HALF = MROW // 2
LANES = 128
DENSE = HALF * MROW // LANES
OWNER_ROWS = NC * (DENSE + 1)
PER_FACE = 16
NAMED = FACES_PER_ELEM * PER_FACE
SHARE_ROWS = NAMED + 16
SLOT_BASE = 16
CHUNK = 16
MOST_PAIRED = 8
BIG = 62 << 20
PITCH = MROW + 8

BF16 = jnp.bfloat16
F32 = jnp.float32
I32 = jnp.int32

NT = (((1,), (1,)), ((), ()))
TN = (((0,), (0,)), ((), ()))


def iota(shape, dim):
    return lax.broadcasted_iota(I32, shape, dim)


def dot(left, right, dims=(((1,), (0,)), ((), ()))):
    return lax.dot_general(left, right, dims, preferred_element_type=F32)


def place_kernel(elem_count, face_count, capacity, paired, *refs):
    owners_hbm, traces_hbm = refs[:elem_count], refs[elem_count : 2 * elem_count]
    out_refs = refs[2 * elem_count : -3]
    owner_ref, trace_ref, sems = refs[-3:]
    copies = []
    for k in range(elem_count):
        copies.append(
            pltpu.make_async_copy(owners_hbm[k], owner_ref.at[k], sems.at[k])
        )
        copies.append(
            pltpu.make_async_copy(traces_hbm[k], trace_ref.at[k], sems.at[elem_count + k])
        )
    for copy in copies:
        copy.start()
    mine = lax.axis_index("face") if paired else 0
    rows = trace_ref.shape[1]
    block = elem_count * capacity
    slots = face_count * block
    earlier = (iota((rows, rows), 0) < iota((rows, rows), 1)).astype(BF16)
    slot = iota((slots, rows), 0)
    for copy in copies:
        copy.wait()
    placed = jnp.zeros((slots, FACE_COEFFS), F32)
    for k in range(elem_count):
        owners = owner_ref[k]
        hot = (iota((face_count, rows), 0) == owners).astype(F32)
        rank = jnp.sum(hot * dot(hot.astype(BF16), earlier), axis=0, keepdims=True).astype(I32)
        target = ((owners ^ mine) * elem_count + k) * capacity + rank
        placed = placed + dot((slot == target).astype(BF16), trace_ref[k])
    each = slots // len(out_refs)
    for k, out_ref in enumerate(out_refs):
        out_ref[...] = placed[k * each : (k + 1) * each].astype(BF16)


def gram_kernel(face_count, paired, owner_hbm, coarse_hbm, tiles_hbm, *refs):
    out_refs, refs = refs[:-9], refs[-9:]
    owner_ref, coarse_ref, tiles_ref, rows_ref = refs[:4]
    accs, diags, sems = refs[4:6], refs[6:8], refs[8]
    mine = lax.axis_index("face") if paired else 0
    tiles = tiles_ref.shape[0]
    copies = [
        pltpu.make_async_copy(owner_hbm, owner_ref, sems.at[0]),
        pltpu.make_async_copy(coarse_hbm, coarse_ref, sems.at[1]),
        pltpu.make_async_copy(tiles_hbm, tiles_ref, sems.at[2]),
    ]
    for copy in copies:
        copy.start()
    for ref in (*accs, *diags):
        ref[...] = jnp.zeros_like(ref)
    for copy in copies:
        copy.wait()

    lane = iota((CHUNK, LANES), 1)
    inside = lane < MCOL
    row = iota((HALF, LANES), 0)
    column = lax.rem(iota((HALF, LANES), 1), MROW)
    swapped = (column > row) & (column < HALF)
    diagonal = column == row
    low = iota((DENSE, LANES), 1) < MROW
    low_wide = iota((MROW, LANES), 1) < MROW
    low_row = iota((1, LANES), 1) < MROW

    for chunk in range(tiles // CHUNK):
        first_tile = chunk * CHUNK
        for group in range(MROW // 4):
            base = group * 3 * LANES
            one, two, three = (
                tiles_ref[
                    first_tile : first_tile + CHUNK, base + k * LANES : base + (k + 1) * LANES
                ].astype(F32)
                for k in range(3)
            )
            rolled = (
                one,
                pltpu.roll(jnp.where(lane < 64, two, one), 32, 1),
                pltpu.roll(jnp.where(lane < 32, three, two), 64, 1),
                pltpu.roll(three, 96, 1),
            )
            for k in range(4):
                rows_ref[pl.ds(first_tile * PITCH + 4 * group + k, CHUNK, stride=PITCH), :] = (
                    jnp.where(inside, rolled[k], 0.0)
                )
        for tile in range(first_tile, first_tile + CHUNK, 2):
            both = jnp.concatenate(
                [
                    rows_ref[t * PITCH : t * PITCH + MROW, :].astype(BF16)
                    for t in (tile, tile + 1)
                ],
                axis=0,
            )
            gram = dot(both, both, NT)
            side = jnp.where(low_wide, gram[:MROW], gram[MROW:])
            lower = pltpu.roll(side[HALF:], LANES - HALF, 1)
            packed = jnp.where(swapped, lower, side[:HALF])
            diag = jnp.sum(jnp.where(diagonal, lower, 0.0), axis=0, keepdims=True)
            turned = pltpu.roll(packed, MROW, 1)
            dense = (
                jnp.where(low, packed[:DENSE], turned[DENSE:]),
                jnp.where(low, turned[:DENSE], packed[DENSE:]),
            )
            own = (jnp.where(low_row, diag, 0.0), jnp.where(low_row, 0.0, diag))
            for k in range(2):
                block = (owner_ref[tile + k] ^ mine) * NC + coarse_ref[tile + k]
                here = pl.ds(pl.multiple_of(block * DENSE, DENSE), DENSE)
                accs[k][here, :] += dense[k]
                diags[k][pl.ds(block, 1), :] += own[k]
    size = NC * DENSE
    for owner in range(face_count):
        out_ref, start = (out_refs[owner], 0) if paired else (out_refs[0], owner * OWNER_ROWS)
        here = slice(owner * size, (owner + 1) * size)
        out_ref[start : start + size, :] = (accs[0][here, :] + accs[1][here, :]).astype(BF16)
        here = slice(owner * NC, (owner + 1) * NC)
        out_ref[start + size : start + size + NC, :] = (
            diags[0][here, :] + diags[1][here, :]
        ).astype(BF16)


def main_kernel(
    elem_count,
    face_count,
    paired,
    conn_hbm,
    rhs_hbm,
    inverse_hbm,
    coupling_hbm,
    *refs,
):
    refs, tables_hbm = refs[-20:], refs[:-20]
    (
        schur_hbm,
        share_ref,
        own_ref,
        conn_ref,
        rhs_ref,
        table_ref,
        inverse_ref,
        coupling_ref,
        schur_ref,
        wide_ref,
        rhs_turned_ref,
        vector_ref,
        sum_ref,
        turned_a_ref,
        turned_b_ref,
        product_a_ref,
        product_b_ref,
        small_sems,
        block_sems,
        schur_sems,
    ) = refs
    elements = rhs_ref.shape[0]
    trace = FACES_PER_ELEM * FACE_COEFFS
    slots = table_ref.shape[0]
    own = own_ref.shape[0]
    capacity = own // face_count
    my_elem = lax.axis_index("elem")
    my_face = lax.axis_index("face") if paired else 0
    small = [
        pltpu.make_async_copy(rhs_hbm, rhs_ref, small_sems.at[0]),
        pltpu.make_async_copy(conn_hbm, conn_ref, small_sems.at[1]),
    ]
    each = slots // len(tables_hbm)
    for k, table_hbm in enumerate(tables_hbm):
        there = table_ref.at[pl.ds(k * each, each)]
        small.append(pltpu.make_async_copy(table_hbm, there, small_sems.at[2 + k]))

    def coupling_copy(e):
        return pltpu.make_async_copy(coupling_hbm.at[e], coupling_ref.at[e], block_sems.at[0, e])

    def inverse_copy(e):
        return pltpu.make_async_copy(inverse_hbm.at[e], inverse_ref.at[e], block_sems.at[1, e])

    def leave(e):
        return pltpu.make_async_copy(schur_ref.at[e], schur_hbm.at[e], schur_sems.at[e])

    coupling_copy(0).start()
    for copy in small:
        copy.start()
    inverse_copy(0).start()
    coupling_copy(1).start()
    inverse_copy(1).start()
    coupling_copy(2).start()

    def turn(e, turned_ref):
        turned_ref[...] = coupling_ref[e].T

    def first(e, turned_ref, product_ref):
        product_ref[...] = dot(turned_ref[...], inverse_ref[e]).astype(BF16)

    def second(e, product_ref):
        wide = jnp.concatenate([coupling_ref[e], rhs_turned_ref[...]], axis=1)
        condensed = dot(product_ref[...], wide)
        schur_ref[e] = (-condensed[:, :trace]).astype(BF16)
        total = condensed * vector_ref[pl.ds(e, 1), :]
        total = sum(total[:, k * LANES : (k + 1) * LANES] for k in range(FACES_PER_ELEM + 1))
        sums = jnp.sum(total, axis=1, keepdims=True)
        sum_ref[...] = jnp.where(iota((trace, LANES), 1) == e, sums, sum_ref[...])

    turned = (turned_a_ref, turned_b_ref)
    product = (product_a_ref, product_b_ref)

    def advance(e, parity, turning=True, finishing=True):
        if turning:
            @pl.when(e + 2 < elements)
            def _():
                inverse_copy(e + 2).start()

            @pl.when(e + 3 < elements)
            def _():
                coupling_copy(e + 3).start()

            coupling_copy(e + 1).wait()
        inverse_copy(e).wait()
        if turning:
            turn(e + 1, turned[1 - parity])
        first(e, turned[parity], product[parity])
        if finishing:
            second(e - 1, product[1 - parity])
            leave(e - 1).start()

    coupling_copy(0).wait()
    turn(0, turned[0])
    for copy in small:
        copy.wait()
    wide_ref[...] = jnp.zeros_like(wide_ref)
    sum_ref[...] = jnp.zeros_like(sum_ref)
    wide_ref[0:elements, :] = rhs_ref[...].astype(F32)
    rhs_turned_ref[...] = wide_ref[...].T.astype(BF16)
    row = iota((PER_FACE, LANES), 0)
    lane = iota((PER_FACE, LANES), 1)

    def position(elem, inner):
        face = lax.div(inner, capacity) ^ my_face
        return (face * elem_count + (elem ^ my_elem)) * capacity + lax.rem(inner, capacity)

    for a in range(FACES_PER_ELEM):
        positions = jnp.full((PER_FACE, LANES), -1, I32)
        for e in range(elements):
            slot = conn_ref[a, e]
            positions = jnp.where(
                row == e, position(lax.div(slot, own), lax.rem(slot, own)), positions
            )
        hot = jnp.concatenate([positions == lane + k for k in range(0, slots, LANES)], axis=1)
        lam = dot(hot.astype(BF16), table_ref[...])
        vector_ref[:, a * LANES : (a + 1) * LANES] = -lam
    vector_ref[:, trace:] = (row == lane).astype(F32)
    place = position(my_elem, iota((own, slots), 0))
    pick = (iota((own, slots), 1) == place).astype(BF16)
    own_ref[...] = dot(pick, table_ref[...]).astype(BF16)

    advance(0, 0, finishing=False)

    def two(index, carry):
        advance(2 * index + 1, 1)
        advance(2 * index + 2, 0)
        return carry

    pairs = (elements - 2) // 2
    lax.fori_loop(0, pairs, two, 0)
    for e in range(2 * pairs + 1, elements):
        advance(e, e % 2, turning=e + 1 < elements)
    second(elements - 1, product[(elements - 1) % 2])
    leave(elements - 1).start()

    lane = iota((1, LANES), 1)
    high = jnp.full((1, LANES), -1, I32)
    rest = jnp.zeros((1, LANES), I32)
    for a in range(FACES_PER_ELEM):
        here = slice(a * PER_FACE, (a + 1) * PER_FACE)
        shares = sum_ref[a * LANES : (a + 1) * LANES, :].T
        share_ref[here, :] = shares[:PER_FACE].astype(BF16)
        for e in range(elements):
            high = jnp.where(lane == a * PER_FACE + e, lax.div(conn_ref[a, e], SLOT_BASE), high)
            rest = jnp.where(lane == a * PER_FACE + e, lax.rem(conn_ref[a, e], SLOT_BASE), rest)
    names = jnp.where(row == 0, high, jnp.where(row == 1, rest, 0))
    share_ref[NAMED:, :] = names.astype(F32).astype(BF16)
    for e in range(elements):
        leave(e).wait()


def finish_kernel(elem_count, face_count, *refs):
    ins, refs = refs[:-8], refs[-8:]
    residual_ref, out_ref, got_ref, own_ref, shares_ref, sum_ref, full_ref, sems = refs
    places = [own_ref] + [shares_ref.at[k] for k in range(elem_count)]
    parts = len(ins) - len(places)
    each = face_count // parts
    places += [got_ref.at[pl.ds(k * each, each)] for k in range(parts)]
    copies = [pltpu.make_async_copy(ins[k], places[k], sems.at[k]) for k in range(len(ins))]
    for copy in copies[1 + elem_count :] + copies[: 1 + elem_count]:
        copy.start()
    for copy in copies[1 + elem_count :]:
        copy.wait()
    total = got_ref[0].astype(F32)
    for k in range(1, got_ref.shape[0]):
        total = total + got_ref[k].astype(F32)
    sum_ref[...] = total

    lane = iota((HALF, LANES), 1)
    row = iota((HALF, LANES), 0)
    wide_row = iota((MROW, LANES), 0)
    wide_lane = iota((MROW, LANES), 1)
    top = wide_row < HALF
    held = (top & ((wide_lane <= wide_row) | (wide_lane >= HALF))) | (
        (~top) & (wide_lane >= wide_row)
    )
    for block in range(NC):
        dense = sum_ref[block * DENSE : (block + 1) * DENSE, :]
        upper = jnp.concatenate([dense, pltpu.roll(dense, MROW, 1)], axis=0)
        diag = sum_ref[NC * DENSE + block : NC * DENSE + block + 1, :]
        diag = pltpu.roll(diag + pltpu.roll(diag, MROW, 1), HALF, 1)
        lower = jnp.where(lane == row + HALF, diag, pltpu.roll(upper, HALF, 1))
        given = jnp.concatenate([upper, lower], axis=0)
        turned = jnp.concatenate([given, given], axis=0).T[:MROW]
        full_ref[block * MROW : (block + 1) * MROW, :] = jnp.where(held, given, turned)
    low = iota((NC, LANES), 1) < MROW
    for chunk in range(HALF):
        left = full_ref[pl.ds(2 * chunk, NC, stride=MROW), :]
        right = full_ref[pl.ds(2 * chunk + 1, NC, stride=MROW), :]
        out_ref[:, chunk * LANES : (chunk + 1) * LANES] = jnp.where(
            low, left, pltpu.roll(right, MROW, 1)
        )
    for copy in copies[: 1 + elem_count]:
        copy.wait()
    own = residual_ref.shape[0]
    mine = lax.axis_index("elem")
    slot = (iota((own, SHARE_ROWS), 0) + mine * own).astype(F32)
    left = own_ref[...].astype(F32)
    for k in range(elem_count):
        names = shares_ref[k, NAMED:, :].astype(F32)
        named = (names[0:1] * SLOT_BASE + names[1:2])[:, :SHARE_ROWS]
        left = left - dot((slot == named).astype(BF16), shares_ref[k])
    residual_ref[...] = left


ANY = pl.BlockSpec(memory_space=pl.ANY)
VMEM = pl.BlockSpec(memory_space=pltpu.VMEM)


def params(limit):
    return pltpu.CompilerParams(vmem_limit_bytes=limit)


def around(block, axis):
    count = lax.axis_size(axis)
    return [block] + [
        lax.ppermute(block, axis, [(i, i ^ k) for i in range(count)]) for k in range(1, count)
    ]


def exchange(blocks, face_count):
    if len(blocks) == 1:
        block = blocks[0]
        shaped = block.reshape(face_count, -1, LANES)
        return [lax.all_to_all(shaped, "face", 0, 0, tiled=True)]
    return [blocks[0]] + [
        lax.ppermute(blocks[k], "face", [(i, i ^ k) for i in range(face_count)])
        for k in range(1, face_count)
    ]


def shards(
    trace_old,
    new_owner,
    mortar_tiles,
    mortar_owner,
    mortar_coarse,
    interior_rhs,
    local_inverse,
    coupling,
    connectivity,
):
    face_count = lax.axis_size("face")
    elem_count = lax.axis_size("elem")
    row_count = trace_old.shape[0]
    tile_count = mortar_tiles.shape[0]
    elements, modes = interior_rhs.shape
    trace = FACES_PER_ELEM * FACE_COEFFS
    capacity = max(2, 2 * row_count // face_count)
    own = face_count * capacity

    slots = own * elem_count
    paired = face_count <= MOST_PAIRED
    parts = face_count if paired else 1

    owners = around(new_owner.reshape(1, row_count), "elem")
    traces = around(trace_old, "elem")
    blocks = face_count * NC
    sums_shape = (blocks * DENSE, LANES)
    half_grams = pl.pallas_call(
        functools.partial(gram_kernel, face_count, paired),
        out_shape=[jax.ShapeDtypeStruct((blocks * (DENSE + 1) // parts, LANES), BF16)] * parts,
        in_specs=[ANY, ANY, ANY],
        out_specs=[VMEM] * parts,
        scratch_shapes=[
            pltpu.SMEM((tile_count,), I32),
            pltpu.SMEM((tile_count,), I32),
            pltpu.VMEM(mortar_tiles.shape, BF16),
            pltpu.VMEM((tile_count * PITCH, LANES), F32),
            pltpu.VMEM(sums_shape, F32),
            pltpu.VMEM(sums_shape, F32),
            pltpu.VMEM((blocks, LANES), F32),
            pltpu.VMEM((blocks, LANES), F32),
            pltpu.SemaphoreType.DMA((3,)),
        ],
        compiler_params=params(BIG),
        cost_estimate=pl.CostEstimate(
            flops=4 * tile_count * MROW * MROW * LANES, bytes_accessed=12 << 20, transcendentals=0
        ),
        name="gram",
    )(mortar_owner.reshape(tile_count), mortar_coarse, mortar_tiles)

    placed = pl.pallas_call(
        functools.partial(place_kernel, elem_count, face_count, capacity, paired),
        out_shape=[jax.ShapeDtypeStruct((slots // parts, FACE_COEFFS), BF16)] * parts,
        in_specs=[ANY] * (2 * elem_count),
        out_specs=[VMEM] * parts,
        scratch_shapes=[
            pltpu.VMEM((elem_count, 1, row_count), I32),
            pltpu.VMEM((elem_count, *trace_old.shape), BF16),
            pltpu.SemaphoreType.DMA((2 * elem_count,)),
        ],
        compiler_params=params(BIG),
        name="place",
    )(*owners, *traces)
    tables = exchange(placed, face_count)
    half_grams, _ = lax.optimization_barrier((half_grams, placed))
    got = exchange(half_grams, face_count)

    schur_blocks, shares, own_rows = pl.pallas_call(
        functools.partial(main_kernel, elem_count, face_count, paired),
        out_shape=(
            jax.ShapeDtypeStruct((elements, trace, trace), BF16),
            jax.ShapeDtypeStruct((SHARE_ROWS, LANES), BF16),
            jax.ShapeDtypeStruct((own, FACE_COEFFS), BF16),
        ),
        in_specs=[ANY] * (4 + parts),
        out_specs=(ANY, VMEM, VMEM),
        scratch_shapes=[
            pltpu.SMEM((FACES_PER_ELEM, elements), I32),
            pltpu.VMEM((elements, modes), BF16),
            pltpu.VMEM((slots, FACE_COEFFS), BF16),
            pltpu.VMEM((elements, modes, modes), BF16),
            pltpu.VMEM((elements, modes, trace), BF16),
            pltpu.VMEM((elements, trace, trace), BF16),
            pltpu.VMEM((LANES, modes), F32),
            pltpu.VMEM((modes, LANES), BF16),
            pltpu.VMEM((PER_FACE, trace + LANES), F32),
            pltpu.VMEM((trace, LANES), F32),
            pltpu.VMEM((trace, modes), BF16),
            pltpu.VMEM((trace, modes), BF16),
            pltpu.VMEM((trace, modes), BF16),
            pltpu.VMEM((trace, modes), BF16),
            pltpu.SemaphoreType.DMA((2 + parts,)),
            pltpu.SemaphoreType.DMA((2, elements)),
            pltpu.SemaphoreType.DMA((elements,)),
        ],
        compiler_params=params(BIG),
        cost_estimate=pl.CostEstimate(
            flops=2 * elements * modes * trace * (modes + trace),
            bytes_accessed=2 * elements * (modes * (modes + trace) + trace * trace),
            transcendentals=0,
        ),
        name="condense",
    )(
        connectivity.T,
        interior_rhs,
        local_inverse,
        coupling,
        *(table.reshape(slots // parts, FACE_COEFFS) for table in tables),
    )

    got_each = (face_count // parts, OWNER_ROWS, LANES)
    slot_residual, coarse_blocks = pl.pallas_call(
        functools.partial(finish_kernel, elem_count, face_count),
        out_shape=(
            jax.ShapeDtypeStruct((own, FACE_COEFFS), F32),
            jax.ShapeDtypeStruct((NC, MROW * MROW), F32),
        ),
        in_specs=[ANY] * (1 + elem_count + parts),
        out_specs=(VMEM, VMEM),
        scratch_shapes=[
            pltpu.VMEM((face_count, OWNER_ROWS, LANES), BF16),
            pltpu.VMEM((own, FACE_COEFFS), BF16),
            pltpu.VMEM((elem_count, SHARE_ROWS, LANES), BF16),
            pltpu.VMEM((OWNER_ROWS, LANES), F32),
            pltpu.VMEM((NC * MROW, LANES), F32),
            pltpu.SemaphoreType.DMA((1 + elem_count + parts,)),
        ],
        compiler_params=params(BIG),
        name="finish",
    )(own_rows, *around(shares, "elem"), *(part.reshape(got_each) for part in got))
    return schur_blocks, slot_residual, coarse_blocks


def solution(mesh):
    return jax.shard_map(
        shards,
        mesh=mesh,
        in_specs=(
            P(("face", "elem"), None),
            P(("face", "elem"), None),
            P(("face", "elem"), None),
            P(("face", "elem"), None),
            P(("face", "elem")),
            P(("face", "elem"), None),
            P(("face", "elem"), None, None),
            P(("face", "elem"), None, None),
            P(("face", "elem"), None),
        ),
        out_specs=(
            P(("face", "elem"), None, None),
            P(("face", "elem"), None),
            P(("face", "elem"), None),
        ),
        check_vma=False,
    )
```

time: 46.5 us -> 63.3 us (1.36)
  starting transfers between devices: 14.4 us -> 29.1 us
  waiting for transfers between devices: 9.2 us -> 12.4 us
  Pallas kernels: 19.7 us -> 18.2 us
    ppermute x6 -> x23, starting transfers between devices: 3.56 us -> 29.1 us  [the longest x14 21.5 us: exchange(): lax.ppermute(blocks[k], 'face', [(i, i ^ k) for i in range(face_count)])]
    all_to_all x2 -> x0, starting transfers between devices: 10.8 us -> none  [the longest x1 7.29 us: shards(): lax.all_to_all(placed.reshape(face_count, capacity, FACE_COEFFS), 'face',...]
    ppermute x6 -> x23, waiting for transfers between devices: 6.37 us -> 12.4 us  [the longest x14 8.13 us: exchange(): lax.ppermute(blocks[k], 'face', [(i, i ^ k) for i in range(face_count)])]
    all_to_all x2 -> x0, waiting for transfers between devices: 2.83 us -> none  [the longest x1 2.83 us: shards(): lax.all_to_all(placed.reshape(face_count, capacity, FACE_COEFFS), 'face',...]
    pallas_call x4, Pallas kernels: 19.7 us -> 18.2 us  [the longest x1 9.17 us: shards(): pl.pallas_call(functools.partial(main_kernel, elem_count, face_count, pai...]
    unnamed x16 -> x56, local copies, waits for them, and re-layouts: 2.02 us -> 2.38 us
  transfers between devices with their start and end apart: 8 -> 23, of which waited for: 5 -> 6; matrix products, arithmetic and copies ran while one was open for 0% -> 0% of each run, Pallas kernels for 33% -> 20%
where the time goes in v5:
time: 63.3 us; the launch traced here: 63 us
  starting transfers between devices  29.1 us (46%)
  Pallas kernels  18.2 us (29%)
  waiting for transfers between devices  12.4 us (20%)
  local copies, waits for them, and re-layouts  2.38 us (4%)
  between operations  0.89 us (1%)
    ppermute x14, starting transfers between devices, exchange(): lax.ppermute(blocks[k], 'face', [(i, i ^ k) for i in range(face_count)])  21.5 us
    pallas_call x1, Pallas kernels, shards(): pl.pallas_call(functools.partial(main_kernel, elem_count, face_count, pai...  9.17 us
    ppermute x14, waiting for transfers between devices, exchange(): lax.ppermute(blocks[k], 'face', [(i, i ^ k) for i in range(face_count)])  8.13 us
    ppermute x9, starting transfers between devices, around(): lax.ppermute(block, axis, [(i, i ^ k) for i in range(count)])  7.62 us
    ppermute x9, waiting for transfers between devices, around(): lax.ppermute(block, axis, [(i, i ^ k) for i in range(count)])  4.25 us
    pallas_call x1, Pallas kernels, shards(): pl.pallas_call(functools.partial(gram_kernel, face_count, paired), out_sh...  3.74 us
    pallas_call x1, Pallas kernels, shards(): pl.pallas_call(functools.partial(finish_kernel, elem_count, face_count),...  3.19 us
    unnamed x56, local copies, waits for them, and re-layouts  2.38 us
  transfers between devices with their start and end apart: 23, of which 6 were waited for; matrix products, arithmetic and copies ran while one was open for 0% of the time, Pallas kernels for 20%

profile of v5, /device:TPU:0, one launch (start us, length us, event | category | flops | bytes accessed | tf_op | source)
XLA Modules:
  0.0 63.0 jit_solution(1448368828742131809)
XLA Ops:
  0.6 3.0 %collective-permute-start.4 = (bf16[64,128]{1,0:T(8,128)(2,1)}, bf16[64,128]{1,0:T(8,128)(2,1)S(1)}, u32[]{:S(2)}, u32[]{:S(2)}) collective-permute-start(bf16[64,128]{1,0:T(8,128)(2,1)} %refs_4_.1), channel_id=1, source_target_pairs={{0,2},{1,3},{2,0},{3,1},{4,6},{5,7},{6,4},{7,5},{8,10},{9,11},{10,... | collective-permute-start | bytes 49160 | tf_op jit(solution)/shard_map/ppermute | solution.py:389
  3.8 1.5 %collective-permute-start.2 = (s32[1,64]{1,0:T(1,128)}, s32[1,64]{1,0:T(1,128)S(1)}, u32[]{:S(2)}, u32[]{:S(2)}) collective-permute-start(s32[1,64]{1,0:T(1,128)} %bitcast.19), channel_id=1, source_target_pairs={{0,3},{1,2},{2,1},{3,0},{4,7},{5,6},{6,5},{7,4},{8,11},{9,10},{10,... | collective-permute-start | bytes 776 | tf_op jit(solution)/shard_map/ppermute | solution.py:389
  5.8 1.2 %collective-permute-done.2.refs_3_ = s32[1,64]{1,0:T(1,128)S(1)} collective-permute-done((s32[1,64]{1,0:T(1,128)}, s32[1,64]{1,0:T(1,128)S(1)}, u32[]{:S(2)}, u32[]{:S(2)}) %collective-permute-start.2) | collective-permute-done | bytes 288 | tf_op jit(solution)/shard_map/ppermute | solution.py:389
  7.6 1.5 %collective-permute-done.1.refs_2_ = s32[1,64]{1,0:T(1,128)S(1)} collective-permute-done((s32[1,64]{1,0:T(1,128)}, s32[1,64]{1,0:T(1,128)S(1)}, u32[]{:S(2)}, u32[]{:S(2)}) %collective-permute-start.1) | collective-permute-done | bytes 288 | tf_op jit(solution)/shard_map/ppermute | solution.py:389
  10.3 2.1 %place.1 = (bf16[64,128]{1,0:T(8,128)(2,1)}, bf16[64,128]{1,0:T(8,128)(2,1)}, bf16[64,128]{1,0:T(8,128)(2,1)}, bf16[64,128]{1,0:T(8,128)(2,1)}, bf16[64,128]{1,0...) custom-call(s32[1,64]{1,0:T(1,128)} %bitcast.22, s32[1,64]{1,0:T(1,128)} %copy-done.15, ...), custom_call_target="tpu_custom_call" | custom-call | tf_op jit(solution)/shard_map/place/pallas_call | solution.py:455
  12.4 1.6 %collective-permute-start.6 = (bf16[64,128]{1,0:T(8,128)(2,1)}, bf16[64,128]{1,0:T(8,128)(2,1)S(1)}, u32[]{:S(2)}, u32[]{:S(2)}) collective-permute-start(bf16[64,128]{1,0:T(8,128)(2,1)} %get-tuple-element.33), channel_id=1, source_target_pairs={{0,4},{4,0},{8,12},{12,8},{16,20},{20,16},{24,28},{28,24},{1,5},{5... | collective-permute-start | bytes 49160 | tf_op jit(solution)/shard_map/ppermute | solution.py:399
  14.0 1.6 %collective-permute-start.7 = (bf16[64,128]{1,0:T(8,128)(2,1)}, bf16[64,128]{1,0:T(8,128)(2,1)S(1)}, u32[]{:S(2)}, u32[]{:S(2)}) collective-permute-start(bf16[64,128]{1,0:T(8,128)(2,1)} %get-tuple-element.34), channel_id=1, source_target_pairs={{0,8},{4,12},{8,0},{12,4},{16,24},{20,28},{24,16},{28,20},{1,9},{5... | collective-permute-start | bytes 49160 | tf_op jit(solution)/shard_map/ppermute | solution.py:399
  16.0 2.6 %collective-permute-start.9 = (bf16[64,128]{1,0:T(8,128)(2,1)}, bf16[64,128]{1,0:T(8,128)(2,1)S(1)}, u32[]{:S(2)}, u32[]{:S(2)}) collective-permute-start(bf16[64,128]{1,0:T(8,128)(2,1)} %get-tuple-element.36), channel_id=1, source_target_pairs={{0,16},{4,20},{8,24},{12,28},{16,0},{20,4},{24,8},{28,12},{1,17},{... | collective-permute-start | bytes 49160 | tf_op jit(solution)/shard_map/ppermute | solution.py:399
  18.6 1.3 %collective-permute-start.10 = (bf16[64,128]{1,0:T(8,128)(2,1)}, bf16[64,128]{1,0:T(8,128)(2,1)S(1)}, u32[]{:S(2)}, u32[]{:S(2)}) collective-permute-start(bf16[64,128]{1,0:T(8,128)(2,1)} %get-tuple-element.37), channel_id=1, source_target_pairs={{0,20},{4,16},{8,28},{12,24},{16,4},{20,0},{24,12},{28,8},{1,21},{... | collective-permute-start | bytes 49160 | tf_op jit(solution)/shard_map/ppermute | solution.py:399
  19.9 3.6 %collective-permute-start.11 = (bf16[64,128]{1,0:T(8,128)(2,1)}, bf16[64,128]{1,0:T(8,128)(2,1)S(1)}, u32[]{:S(2)}, u32[]{:S(2)}) collective-permute-start(bf16[64,128]{1,0:T(8,128)(2,1)} %get-tuple-element.38), channel_id=1, source_target_pairs={{0,24},{4,28},{8,16},{12,20},{16,8},{20,12},{24,0},{28,4},{1,25},{... | collective-permute-start | bytes 49160 | tf_op jit(solution)/shard_map/ppermute | solution.py:399
  23.7 3.7 %gram.1 = (bf16[272,128]{1,0:T(8,128)(2,1)}, bf16[272,128]{1,0:T(8,128)(2,1)}, bf16[272,128]{1,0:T(8,128)(2,1)}, bf16[272,128]{1,0:T(8,128)(2,1)}, bf16[272,128]...) custom-call(s32[96]{0:T(128)} %bitcast.23, s32[96]{0:T(128)} %coarse_hbm.1, ...), custom_call_target="tpu_custom_call" | custom-call | flops 201326592 | bytes 12582912 | tf_op jit(solution)/shard_map/gram/pallas_call | solution.py:432
  27.4 1.6 %collective-permute-start.16 = (bf16[272,128]{1,0:T(8,128)(2,1)}, bf16[272,128]{1,0:T(8,128)(2,1)S(1)}, u32[]{:S(2)}, u32[]{:S(2)}) collective-permute-start(bf16[272,128]{1,0:T(8,128)(2,1)} %get-tuple-element.52), channel_id=1, source_target_pairs={{0,4},{4,0},{8,12},{12,8},{16,20},{20,16},{24,28},{28,24},{1,5},{5... | collective-permute-start | bytes 208904 | tf_op jit(solution)/shard_map/ppermute | solution.py:399
  29.1 1.2 %collective-permute-done.12.refs_7_ = bf16[64,128]{1,0:T(8,128)(2,1)S(1)} collective-permute-done((bf16[64,128]{1,0:T(8,128)(2,1)}, bf16[64,128]{1,0:T(8,128)(2,1)S(1)}, u32[]{:S(2)}, u32[]{:S(2)}) %collective-permute-start.12) | collective-permute-done | bytes 16416 | tf_op jit(solution)/shard_map/ppermute | solution.py:399
  30.9 9.2 %condense.1 = (bf16[9,384,384]{2,1,0:T(8,128)(2,1)}, bf16[64,128]{1,0:T(8,128)(2,1)}, bf16[128,128]{1,0:T(8,128)(2,1)}) custom-call(s32[3,9]{1,0:T(4,128)} %bitcast.24, bf16[9,512]{1,0:T(8,128)(2,1)} %rhs_hbm.1, bf16[9,512,512]{2,1,0:T(8,128)(2,1)} %inverse_hbm.1, bf16[9,512,384]{2,1,0:T(8,128)(2,1)} %coupling_hbm.1, ...), custom_call_target="tpu_custom_call" | custom-call | flops 3170893824 | bytes 10911744 | tf_op jit(solution)/shard_map/condense/pallas_call | solution.py:472
  40.1 1.1 %collective-permute-start.14 = (bf16[64,128]{1,0:T(8,128)(2,1)}, bf16[64,128]{1,0:T(8,128)(2,1)S(1)}, u32[]{:S(2)}, u32[]{:S(2)}) collective-permute-start(bf16[64,128]{1,0:T(8,128)(2,1)} %get-tuple-element.42.refs_1_), channel_id=1, source_target_pairs={{0,2},{1,3},{2,0},{3,1},{4,6},{5,7},{6,4},{7,5},{8,10},{9,11},{10,... | collective-permute-start | bytes 49160 | tf_op jit(solution)/shard_map/ppermute | solution.py:389
  41.3 0.7 %collective-permute-start.13 = (bf16[64,128]{1,0:T(8,128)(2,1)}, bf16[64,128]{1,0:T(8,128)(2,1)S(1)}, u32[]{:S(2)}, u32[]{:S(2)}) collective-permute-start(bf16[64,128]{1,0:T(8,128)(2,1)} %get-tuple-element.42.refs_1_), channel_id=1, source_target_pairs={{0,1},{1,0},{2,3},{3,2},{4,5},{5,4},{6,7},{7,6},{8,9},{9,8},{10,11... | collective-permute-start | bytes 49160 | tf_op jit(solution)/shard_map/ppermute | solution.py:389
  42.0 1.5 %collective-permute-done.15.refs_4_ = bf16[64,128]{1,0:T(8,128)(2,1)S(1)} collective-permute-done((bf16[64,128]{1,0:T(8,128)(2,1)}, bf16[64,128]{1,0:T(8,128)(2,1)S(1)}, u32[]{:S(2)}, u32[]{:S(2)}) %collective-permute-start.15) | collective-permute-done | bytes 16416 | tf_op jit(solution)/shard_map/ppermute | solution.py:389
  43.5 0.8 %collective-permute-start.18 = (bf16[272,128]{1,0:T(8,128)(2,1)S(1)}, bf16[272,128]{1,0:T(8,128)(2,1)S(1)}, u32[]{:S(2)}, u32[]{:S(2)}) collective-permute-start(bf16[272,128]{1,0:T(8,128)(2,1)S(1)} %copy-done.20), channel_id=1, source_target_pairs={{0,12},{4,8},{8,4},{12,0},{16,28},{20,24},{24,20},{28,16},{1,13},{... | collective-permute-start | bytes 208904 | tf_op jit(solution)/shard_map/ppermute | solution.py:399
  44.3 2.9 %collective-permute-start.19 = (bf16[272,128]{1,0:T(8,128)(2,1)S(1)}, bf16[272,128]{1,0:T(8,128)(2,1)S(1)}, u32[]{:S(2)}, u32[]{:S(2)}) collective-permute-start(bf16[272,128]{1,0:T(8,128)(2,1)S(1)} %copy-done.19), channel_id=1, source_target_pairs={{0,16},{4,20},{8,24},{12,28},{16,0},{20,4},{24,8},{28,12},{1,17},{... | collective-permute-start | bytes 208904 | tf_op jit(solution)/shard_map/ppermute | solution.py:399
  47.2 1.1 %collective-permute-start.20 = (bf16[272,128]{1,0:T(8,128)(2,1)S(1)}, bf16[272,128]{1,0:T(8,128)(2,1)S(1)}, u32[]{:S(2)}, u32[]{:S(2)}) collective-permute-start(bf16[272,128]{1,0:T(8,128)(2,1)S(1)} %copy-done.18), channel_id=1, source_target_pairs={{0,20},{4,16},{8,28},{12,24},{16,4},{20,0},{24,12},{28,8},{1,21},{... | collective-permute-start | bytes 208904 | tf_op jit(solution)/shard_map/ppermute | solution.py:399
  48.3 3.7 %collective-permute-start.21 = (bf16[272,128]{1,0:T(8,128)(2,1)S(1)}, bf16[272,128]{1,0:T(8,128)(2,1)S(1)}, u32[]{:S(2)}, u32[]{:S(2)}) collective-permute-start(bf16[272,128]{1,0:T(8,128)(2,1)S(1)} %copy-done.17), channel_id=1, source_target_pairs={{0,24},{4,28},{8,16},{12,20},{16,8},{20,12},{24,0},{28,4},{1,25},{... | collective-permute-start | bytes 208904 | tf_op jit(solution)/shard_map/ppermute | solution.py:399
  52.2 5.0 %collective-permute-done.20 = bf16[272,128]{1,0:T(8,128)(2,1)S(1)} collective-permute-done((bf16[272,128]{1,0:T(8,128)(2,1)S(1)}, bf16[272,128]{1,0:T(8,128)(2,1)S(1)}, u32[]{:S(2)}, u32[]{:S(2)}) %collective-permute-start.20) | collective-permute-done | bytes 69664 | tf_op jit(solution)/shard_map/ppermute | solution.py:399
  57.2 2.0 %collective-permute-done.22 = bf16[272,128]{1,0:T(8,128)(2,1)S(1)} collective-permute-done((bf16[272,128]{1,0:T(8,128)(2,1)S(1)}, bf16[272,128]{1,0:T(8,128)(2,1)S(1)}, u32[]{:S(2)}, u32[]{:S(2)}) %collective-permute-start.22) | collective-permute-done | bytes 69664 | tf_op jit(solution)/shard_map/ppermute | solution.py:399
  59.8 3.2 %finish.1 = (f32[128,128]{1,0:T(8,128)}, f32[16,4096]{1,0:T(8,128)}) custom-call(bf16[128,128]{1,0:T(8,128)(2,1)} %get-tuple-element.41.refs_0_, bf16[64,128]{1,0:T(8,128)(2,1)} %get-tuple-element.42.refs_1_, bf16[64,128]{1,0:T(8,128)(2,1)} %copy-done.9, bf16[64,128]{1,0:T(8,128)(2,1)} %copy-done.8, bf16[64,128]{1,0:T(8,128)(2,1)} %copy-done.7, ...), custom_call_target="tpu_custom_call" | custom-call | tf_op jit(solution)/shard_map/finish/pallas_call | solution.py:516
  (82 shorter events, 4.4 us)
Async XLA Ops:
  0.6 8.4 %collective-permute-start.4 = (bf16[64,128]{1,0:T(8,128)(2,1)}, bf16[64,128]{1,0:T(8,128)(2,1)S(1)}, u32[]{:S(2)}, u32[]{:S(2)}) collective-permute-start(bf16[64,128]{1,0:T(8,128)(2,1)} %refs_4_.1), channel_id=1, source_target_pairs={{0,2},{1,3},{2,0},{3,1},{4,6},{5,7},{6,4},{7,5},{8,10},{9,11},{10,... | collective-permute-start | bytes 49160 | tf_op jit(solution)/shard_map/ppermute | solution.py:389
  3.6 5.5 %collective-permute-start.3 = (bf16[64,128]{1,0:T(8,128)(2,1)}, bf16[64,128]{1,0:T(8,128)(2,1)S(1)}, u32[]{:S(2)}, u32[]{:S(2)}) collective-permute-start(bf16[64,128]{1,0:T(8,128)(2,1)} %refs_4_.1), channel_id=1, source_target_pairs={{0,1},{1,0},{2,3},{3,2},{4,5},{5,4},{6,7},{7,6},{8,9},{9,8},{10,11... | collective-permute-start | bytes 49160 | tf_op jit(solution)/shard_map/ppermute | solution.py:389
  3.6 5.5 %collective-permute-start.5 = (bf16[64,128]{1,0:T(8,128)(2,1)}, bf16[64,128]{1,0:T(8,128)(2,1)S(1)}, u32[]{:S(2)}, u32[]{:S(2)}) collective-permute-start(bf16[64,128]{1,0:T(8,128)(2,1)} %refs_4_.1), channel_id=1, source_target_pairs={{0,3},{1,2},{2,1},{3,0},{4,7},{5,6},{6,5},{7,4},{8,11},{9,10},{10,... | collective-permute-start | bytes 49160 | tf_op jit(solution)/shard_map/ppermute | solution.py:389
  3.8 3.2 %collective-permute-start.2 = (s32[1,64]{1,0:T(1,128)}, s32[1,64]{1,0:T(1,128)S(1)}, u32[]{:S(2)}, u32[]{:S(2)}) collective-permute-start(s32[1,64]{1,0:T(1,128)} %bitcast.19), channel_id=1, source_target_pairs={{0,3},{1,2},{2,1},{3,0},{4,7},{5,6},{6,5},{7,4},{8,11},{9,10},{10,... | collective-permute-start | bytes 776 | tf_op jit(solution)/shard_map/ppermute | solution.py:389
  5.4 3.7 %collective-permute-start.1 = (s32[1,64]{1,0:T(1,128)}, s32[1,64]{1,0:T(1,128)S(1)}, u32[]{:S(2)}, u32[]{:S(2)}) collective-permute-start(s32[1,64]{1,0:T(1,128)} %bitcast.20), channel_id=1, source_target_pairs={{0,2},{1,3},{2,0},{3,1},{4,6},{5,7},{6,4},{7,5},{8,10},{9,11},{10,... | collective-permute-start | bytes 776 | tf_op jit(solution)/shard_map/ppermute | solution.py:389
  7.1 2.0 %collective-permute-start = (s32[1,64]{1,0:T(1,128)}, s32[1,64]{1,0:T(1,128)S(1)}, u32[]{:S(2)}, u32[]{:S(2)}) collective-permute-start(s32[1,64]{1,0:T(1,128)} %bitcast.21), channel_id=1, source_target_pairs={{0,1},{1,0},{2,3},{3,2},{4,5},{5,4},{6,7},{7,6},{8,9},{9,8},{10,11... | collective-permute-start | bytes 776 | tf_op jit(solution)/shard_map/ppermute | solution.py:389
  12.4 7.4 %collective-permute-start.6 = (bf16[64,128]{1,0:T(8,128)(2,1)}, bf16[64,128]{1,0:T(8,128)(2,1)S(1)}, u32[]{:S(2)}, u32[]{:S(2)}) collective-permute-start(bf16[64,128]{1,0:T(8,128)(2,1)} %get-tuple-element.33), channel_id=1, source_target_pairs={{0,4},{4,0},{8,12},{12,8},{16,20},{20,16},{24,28},{28,24},{1,5},{5... | collective-permute-start | bytes 49160 | tf_op jit(solution)/shard_map/ppermute | solution.py:399
  14.0 9.5 %collective-permute-start.7 = (bf16[64,128]{1,0:T(8,128)(2,1)}, bf16[64,128]{1,0:T(8,128)(2,1)S(1)}, u32[]{:S(2)}, u32[]{:S(2)}) collective-permute-start(bf16[64,128]{1,0:T(8,128)(2,1)} %get-tuple-element.34), channel_id=1, source_target_pairs={{0,8},{4,12},{8,0},{12,4},{16,24},{20,28},{24,16},{28,20},{1,9},{5... | collective-permute-start | bytes 49160 | tf_op jit(solution)/shard_map/ppermute | solution.py:399
  15.6 11.8 %collective-permute-start.8 = (bf16[64,128]{1,0:T(8,128)(2,1)}, bf16[64,128]{1,0:T(8,128)(2,1)S(1)}, u32[]{:S(2)}, u32[]{:S(2)}) collective-permute-start(bf16[64,128]{1,0:T(8,128)(2,1)} %get-tuple-element.35), channel_id=1, source_target_pairs={{0,12},{4,8},{8,4},{12,0},{16,28},{20,24},{24,20},{28,16},{1,13},{... | collective-permute-start | bytes 49160 | tf_op jit(solution)/shard_map/ppermute | solution.py:399
  16.0 13.0 %collective-permute-start.9 = (bf16[64,128]{1,0:T(8,128)(2,1)}, bf16[64,128]{1,0:T(8,128)(2,1)S(1)}, u32[]{:S(2)}, u32[]{:S(2)}) collective-permute-start(bf16[64,128]{1,0:T(8,128)(2,1)} %get-tuple-element.36), channel_id=1, source_target_pairs={{0,16},{4,20},{8,24},{12,28},{16,0},{20,4},{24,8},{28,12},{1,17},{... | collective-permute-start | bytes 49160 | tf_op jit(solution)/shard_map/ppermute | solution.py:399
  18.6 10.4 %collective-permute-start.10 = (bf16[64,128]{1,0:T(8,128)(2,1)}, bf16[64,128]{1,0:T(8,128)(2,1)S(1)}, u32[]{:S(2)}, u32[]{:S(2)}) collective-permute-start(bf16[64,128]{1,0:T(8,128)(2,1)} %get-tuple-element.37), channel_id=1, source_target_pairs={{0,20},{4,16},{8,28},{12,24},{16,4},{20,0},{24,12},{28,8},{1,21},{... | collective-permute-start | bytes 49160 | tf_op jit(solution)/shard_map/ppermute | solution.py:399
  19.9 9.2 %collective-permute-start.11 = (bf16[64,128]{1,0:T(8,128)(2,1)}, bf16[64,128]{1,0:T(8,128)(2,1)S(1)}, u32[]{:S(2)}, u32[]{:S(2)}) collective-permute-start(bf16[64,128]{1,0:T(8,128)(2,1)} %get-tuple-element.38), channel_id=1, source_target_pairs={{0,24},{4,28},{8,16},{12,20},{16,8},{20,12},{24,0},{28,4},{1,25},{... | collective-permute-start | bytes 49160 | tf_op jit(solution)/shard_map/ppermute | solution.py:399
  23.5 6.8 %collective-permute-start.12 = (bf16[64,128]{1,0:T(8,128)(2,1)}, bf16[64,128]{1,0:T(8,128)(2,1)S(1)}, u32[]{:S(2)}, u32[]{:S(2)}) collective-permute-start(bf16[64,128]{1,0:T(8,128)(2,1)} %get-tuple-element.39), channel_id=1, source_target_pairs={{0,28},{4,24},{8,20},{12,16},{16,12},{20,8},{24,4},{28,0},{1,29},{... | collective-permute-start | bytes 49160 | tf_op jit(solution)/shard_map/ppermute | solution.py:399
  27.4 20.9 %collective-permute-start.16 = (bf16[272,128]{1,0:T(8,128)(2,1)}, bf16[272,128]{1,0:T(8,128)(2,1)S(1)}, u32[]{:S(2)}, u32[]{:S(2)}) collective-permute-start(bf16[272,128]{1,0:T(8,128)(2,1)} %get-tuple-element.52), channel_id=1, source_target_pairs={{0,4},{4,0},{8,12},{12,8},{16,20},{20,16},{24,28},{28,24},{1,5},{5... | collective-permute-start | bytes 208904 | tf_op jit(solution)/shard_map/ppermute | solution.py:399
  29.0 23.0 %collective-permute-start.17 = (bf16[272,128]{1,0:T(8,128)(2,1)}, bf16[272,128]{1,0:T(8,128)(2,1)S(1)}, u32[]{:S(2)}, u32[]{:S(2)}) collective-permute-start(bf16[272,128]{1,0:T(8,128)(2,1)} %get-tuple-element.53), channel_id=1, source_target_pairs={{0,8},{4,12},{8,0},{12,4},{16,24},{20,28},{24,16},{28,20},{1,9},{5... | collective-permute-start | bytes 208904 | tf_op jit(solution)/shard_map/ppermute | solution.py:399
  30.9 21.1 %copy-start.16 = (bf16[272,128]{1,0:T(8,128)(2,1)S(1)}, bf16[272,128]{1,0:T(8,128)(2,1)}, u32[]{:S(2)}) copy-start(bf16[272,128]{1,0:T(8,128)(2,1)} %get-tuple-element.58) | copy-start | bytes 208900
  40.1 3.4 %collective-permute-start.15 = (bf16[64,128]{1,0:T(8,128)(2,1)}, bf16[64,128]{1,0:T(8,128)(2,1)S(1)}, u32[]{:S(2)}, u32[]{:S(2)}) collective-permute-start(bf16[64,128]{1,0:T(8,128)(2,1)} %get-tuple-element.42.refs_1_), channel_id=1, source_target_pairs={{0,3},{1,2},{2,1},{3,0},{4,7},{5,6},{6,5},{7,4},{8,11},{9,10},{10,... | collective-permute-start | bytes 49160 | tf_op jit(solution)/shard_map/ppermute | solution.py:389
  40.1 4.1 %collective-permute-start.14 = (bf16[64,128]{1,0:T(8,128)(2,1)}, bf16[64,128]{1,0:T(8,128)(2,1)S(1)}, u32[]{:S(2)}, u32[]{:S(2)}) collective-permute-start(bf16[64,128]{1,0:T(8,128)(2,1)} %get-tuple-element.42.refs_1_), channel_id=1, source_target_pairs={{0,2},{1,3},{2,0},{3,1},{4,6},{5,7},{6,4},{7,5},{8,10},{9,11},{10,... | collective-permute-start | bytes 49160 | tf_op jit(solution)/shard_map/ppermute | solution.py:389
  41.3 5.9 %collective-permute-start.13 = (bf16[64,128]{1,0:T(8,128)(2,1)}, bf16[64,128]{1,0:T(8,128)(2,1)S(1)}, u32[]{:S(2)}, u32[]{:S(2)}) collective-permute-start(bf16[64,128]{1,0:T(8,128)(2,1)} %get-tuple-element.42.refs_1_), channel_id=1, source_target_pairs={{0,1},{1,0},{2,3},{3,2},{4,5},{5,4},{6,7},{7,6},{8,9},{9,8},{10,11... | collective-permute-start | bytes 49160 | tf_op jit(solution)/shard_map/ppermute | solution.py:389
  43.5 8.7 %collective-permute-start.18 = (bf16[272,128]{1,0:T(8,128)(2,1)S(1)}, bf16[272,128]{1,0:T(8,128)(2,1)S(1)}, u32[]{:S(2)}, u32[]{:S(2)}) collective-permute-start(bf16[272,128]{1,0:T(8,128)(2,1)S(1)} %copy-done.20), channel_id=1, source_target_pairs={{0,12},{4,8},{8,4},{12,0},{16,28},{20,24},{24,20},{28,16},{1,13},{... | collective-permute-start | bytes 208904 | tf_op jit(solution)/shard_map/ppermute | solution.py:399
  44.3 7.9 %collective-permute-start.19 = (bf16[272,128]{1,0:T(8,128)(2,1)S(1)}, bf16[272,128]{1,0:T(8,128)(2,1)S(1)}, u32[]{:S(2)}, u32[]{:S(2)}) collective-permute-start(bf16[272,128]{1,0:T(8,128)(2,1)S(1)} %copy-done.19), channel_id=1, source_target_pairs={{0,16},{4,20},{8,24},{12,28},{16,0},{20,4},{24,8},{28,12},{1,17},{... | collective-permute-start | bytes 208904 | tf_op jit(solution)/shard_map/ppermute | solution.py:399
  47.2 10.0 %collective-permute-start.20 = (bf16[272,128]{1,0:T(8,128)(2,1)S(1)}, bf16[272,128]{1,0:T(8,128)(2,1)S(1)}, u32[]{:S(2)}, u32[]{:S(2)}) collective-permute-start(bf16[272,128]{1,0:T(8,128)(2,1)S(1)} %copy-done.18), channel_id=1, source_target_pairs={{0,20},{4,16},{8,28},{12,24},{16,4},{20,0},{24,12},{28,8},{1,21},{... | collective-permute-start | bytes 208904 | tf_op jit(solution)/shard_map/ppermute | solution.py:399
  48.3 8.9 %collective-permute-start.21 = (bf16[272,128]{1,0:T(8,128)(2,1)S(1)}, bf16[272,128]{1,0:T(8,128)(2,1)S(1)}, u32[]{:S(2)}, u32[]{:S(2)}) collective-permute-start(bf16[272,128]{1,0:T(8,128)(2,1)S(1)} %copy-done.17), channel_id=1, source_target_pairs={{0,24},{4,28},{8,16},{12,20},{16,8},{20,12},{24,0},{28,4},{1,25},{... | collective-permute-start | bytes 208904 | tf_op jit(solution)/shard_map/ppermute | solution.py:399
  52.0 7.2 %collective-permute-start.22 = (bf16[272,128]{1,0:T(8,128)(2,1)S(1)}, bf16[272,128]{1,0:T(8,128)(2,1)S(1)}, u32[]{:S(2)}, u32[]{:S(2)}) collective-permute-start(bf16[272,128]{1,0:T(8,128)(2,1)S(1)} %copy-done.16), channel_id=1, source_target_pairs={{0,28},{4,24},{8,20},{12,16},{16,12},{20,8},{24,4},{28,0},{1,29},{... | collective-permute-start | bytes 208904 | tf_op jit(solution)/shard_map/ppermute | solution.py:399
  (27 other events, 168.4 us)

commit v6 on v4

v6 whole, which is shorter than its diff:
```python
import functools

import jax
import jax.numpy as jnp
from jax import lax
from jax.experimental import pallas as pl
from jax.experimental.pallas import tpu as pltpu
from jax.sharding import PartitionSpec as P

FACE_COEFFS = 128
FACES_PER_ELEM = 3
MROW = 64
MCOL = 96
NC = 16
HALF = MROW // 2
LANES = 128
DENSE = HALF * MROW // LANES
OWNER_ROWS = NC * (DENSE + 1)
PER_FACE = 16
NAMED = FACES_PER_ELEM * PER_FACE
SHARE_ROWS = NAMED + 16
SLOT_BASE = 16
CHUNK = 16
EARLY = 5
BIG = 62 << 20
PITCH = MROW + 8

BF16 = jnp.bfloat16
F32 = jnp.float32
I32 = jnp.int32

NT = (((1,), (1,)), ((), ()))
TN = (((0,), (0,)), ((), ()))


def iota(shape, dim):
    return lax.broadcasted_iota(I32, shape, dim)


def dot(left, right, dims=(((1,), (0,)), ((), ()))):
    return lax.dot_general(left, right, dims, preferred_element_type=F32)


def place_kernel(elem_count, face_count, capacity, owner_hbm, trace_hbm, placed_ref, *refs):
    owner_ref, trace_ref, sems = refs
    copies = [
        pltpu.make_async_copy(owner_hbm, owner_ref, sems.at[0]),
        pltpu.make_async_copy(trace_hbm, trace_ref, sems.at[1]),
    ]
    for copy in copies:
        copy.start()
    slots, rows = placed_ref.shape[0], trace_ref.shape[0]
    earlier = (iota((rows, rows), 0) < iota((rows, rows), 1)).astype(BF16)
    slot = iota((slots, rows), 0)
    wanted = lax.div(slot, elem_count * capacity) * capacity + lax.rem(slot, capacity)
    for copy in copies:
        copy.wait()
    owners = owner_ref[...]
    hot = (iota((face_count, rows), 0) == owners).astype(F32)
    rank = jnp.sum(hot * dot(hot.astype(BF16), earlier), axis=0, keepdims=True).astype(I32)
    place = (wanted == owners * capacity + rank).astype(BF16)
    placed_ref[...] = dot(place, trace_ref[...]).astype(BF16)


class Element:
    def __init__(self, hbm, vmem, sems, turned, product, rhs_turned_ref):
        self.inverse_hbm, self.coupling_hbm = hbm
        self.inverse_ref, self.coupling_ref = vmem
        self.sems, self.turned, self.product = sems, turned, product
        self.rhs_turned_ref = rhs_turned_ref

    def coupling_copy(self, e, k):
        return pltpu.make_async_copy(
            self.coupling_hbm.at[e], self.coupling_ref.at[k], self.sems.at[0, k]
        )

    def inverse_copy(self, e, k):
        return pltpu.make_async_copy(
            self.inverse_hbm.at[e], self.inverse_ref.at[k], self.sems.at[1, k]
        )

    def turn(self, k):
        self.turned[k % 2][...] = self.coupling_ref[k].T

    def first(self, k):
        product = dot(self.turned[k % 2][...], self.inverse_ref[k])
        self.product[k % 2][...] = product.astype(BF16)

    def second(self, k):
        wide = jnp.concatenate([self.coupling_ref[k], self.rhs_turned_ref[...]], axis=1)
        return dot(self.product[k % 2][...], wide)


def turn_rhs(rhs_ref, wide_ref, rhs_turned_ref):
    wide_ref[...] = jnp.zeros_like(wide_ref)
    wide_ref[0 : rhs_ref.shape[0], :] = rhs_ref[...].astype(F32)
    rhs_turned_ref[...] = wide_ref[...].T.astype(BF16)


def gram_kernel(
    face_count,
    owner_hbm,
    coarse_hbm,
    tiles_hbm,
    rhs_hbm,
    inverse_hbm,
    coupling_hbm,
    out_ref,
    schur_hbm,
    solved_ref,
    owner_ref,
    coarse_ref,
    tiles_ref,
    rows_ref,
    acc_a_ref,
    acc_b_ref,
    diag_a_ref,
    diag_b_ref,
    rhs_ref,
    wide_ref,
    rhs_turned_ref,
    inverse_ref,
    coupling_ref,
    schur_ref,
    turned_a_ref,
    turned_b_ref,
    product_a_ref,
    product_b_ref,
    sems,
    block_sems,
    schur_sems,
):
    accs, diags = (acc_a_ref, acc_b_ref), (diag_a_ref, diag_b_ref)
    tiles = tiles_ref.shape[0]
    early, trace = schur_ref.shape[:2]
    element = Element(
        (inverse_hbm, coupling_hbm),
        (inverse_ref, coupling_ref),
        block_sems,
        (turned_a_ref, turned_b_ref),
        (product_a_ref, product_b_ref),
        rhs_turned_ref,
    )
    copies = [
        pltpu.make_async_copy(owner_hbm, owner_ref, sems.at[0]),
        pltpu.make_async_copy(coarse_hbm, coarse_ref, sems.at[1]),
        pltpu.make_async_copy(rhs_hbm, rhs_ref, sems.at[2]),
        pltpu.make_async_copy(tiles_hbm, tiles_ref, sems.at[3]),
    ]
    for copy in copies:
        copy.start()
    for e in range(2):
        element.coupling_copy(e, e).start()
        element.inverse_copy(e, e).start()
    element.coupling_copy(2, 2).start()
    for ref in (*accs, *diags, solved_ref):
        ref[...] = jnp.zeros_like(ref)
    for copy in copies:
        copy.wait()
    turn_rhs(rhs_ref, wide_ref, rhs_turned_ref)

    def leave(e):
        return pltpu.make_async_copy(schur_ref.at[e], schur_hbm.at[e], schur_sems.at[e])

    def solve(step):
        if step + 1 < early:
            element.turn(step + 1)
        if step < early:
            element.first(step)
        if 0 <= step - 1 < early:
            e = step - 1
            condensed = element.second(e)
            schur_ref[e] = (-condensed[:, :trace]).astype(BF16)
            solved_ref[...] = jnp.where(
                iota((trace, LANES), 1) == e, condensed[:, trace:], solved_ref[...]
            )

    lane = iota((CHUNK, LANES), 1)
    inside = lane < MCOL
    row = iota((HALF, LANES), 0)
    column = lax.rem(iota((HALF, LANES), 1), MROW)
    swapped = (column > row) & (column < HALF)
    diagonal = column == row
    low = iota((DENSE, LANES), 1) < MROW
    low_wide = iota((MROW, LANES), 1) < MROW
    low_row = iota((1, LANES), 1) < MROW

    element.coupling_copy(0, 0).wait()
    element.turn(0)
    for chunk in range(tiles // CHUNK):
        if chunk + 2 < early:
            element.inverse_copy(chunk + 2, chunk + 2).start()
        if chunk + 3 < early:
            element.coupling_copy(chunk + 3, chunk + 3).start()
        if chunk + 1 < early:
            element.coupling_copy(chunk + 1, chunk + 1).wait()
        if chunk < early:
            element.inverse_copy(chunk, chunk).wait()
        if 0 <= chunk - 2 < early:
            leave(chunk - 2).start()
        solve(chunk)
        first_tile = chunk * CHUNK
        for group in range(MROW // 4):
            base = group * 3 * LANES
            one, two, three = (
                tiles_ref[
                    first_tile : first_tile + CHUNK, base + k * LANES : base + (k + 1) * LANES
                ].astype(F32)
                for k in range(3)
            )
            rolled = (
                one,
                pltpu.roll(jnp.where(lane < 64, two, one), 32, 1),
                pltpu.roll(jnp.where(lane < 32, three, two), 64, 1),
                pltpu.roll(three, 96, 1),
            )
            for k in range(4):
                rows_ref[pl.ds(first_tile * PITCH + 4 * group + k, CHUNK, stride=PITCH), :] = (
                    jnp.where(inside, rolled[k], 0.0)
                )
        for tile in range(first_tile, first_tile + CHUNK, 2):
            both = jnp.concatenate(
                [
                    rows_ref[t * PITCH : t * PITCH + MROW, :].astype(BF16)
                    for t in (tile, tile + 1)
                ],
                axis=0,
            )
            gram = dot(both, both, NT)
            side = jnp.where(low_wide, gram[:MROW], gram[MROW:])
            lower = pltpu.roll(side[HALF:], LANES - HALF, 1)
            packed = jnp.where(swapped, lower, side[:HALF])
            diag = jnp.sum(jnp.where(diagonal, lower, 0.0), axis=0, keepdims=True)
            turned = pltpu.roll(packed, MROW, 1)
            dense = (
                jnp.where(low, packed[:DENSE], turned[DENSE:]),
                jnp.where(low, turned[:DENSE], packed[DENSE:]),
            )
            own = (jnp.where(low_row, diag, 0.0), jnp.where(low_row, 0.0, diag))
            for k in range(2):
                block = owner_ref[tile + k] * NC + coarse_ref[tile + k]
                here = pl.ds(pl.multiple_of(block * DENSE, DENSE), DENSE)
                accs[k][here, :] += dense[k]
                diags[k][pl.ds(block, 1), :] += own[k]
    size = NC * DENSE
    for owner in range(face_count):
        start = owner * OWNER_ROWS
        here = slice(owner * size, (owner + 1) * size)
        out_ref[start : start + size, :] = (accs[0][here, :] + accs[1][here, :]).astype(BF16)
        here = slice(owner * NC, (owner + 1) * NC)
        out_ref[start + size : start + size + NC, :] = (
            diags[0][here, :] + diags[1][here, :]
        ).astype(BF16)
    for e in range(max(tiles // CHUNK - 2, 0), early):
        leave(e).start()
    for e in range(early):
        leave(e).wait()


def main_kernel(
    elem_count,
    face_count,
    table_hbm,
    conn_hbm,
    rhs_hbm,
    inverse_hbm,
    coupling_hbm,
    schur_in_hbm,
    solved_hbm,
    schur_hbm,
    share_ref,
    own_ref,
    conn_ref,
    rhs_ref,
    table_ref,
    inverse_ref,
    coupling_ref,
    schur_ref,
    wide_ref,
    rhs_turned_ref,
    vector_ref,
    sum_ref,
    turned_a_ref,
    turned_b_ref,
    product_a_ref,
    product_b_ref,
    sems,
    block_sems,
    early_sems,
    schur_sems,
):
    elements = rhs_ref.shape[0]
    late = inverse_ref.shape[0]
    early = elements - late
    trace = FACES_PER_ELEM * FACE_COEFFS
    slots = table_ref.shape[0]
    own = own_ref.shape[0]
    capacity = own // face_count
    my_elem = lax.axis_index("elem")
    element = Element(
        (inverse_hbm, coupling_hbm),
        (inverse_ref, coupling_ref),
        block_sems,
        (turned_a_ref, turned_b_ref),
        (product_a_ref, product_b_ref),
        rhs_turned_ref,
    )
    copies = [
        pltpu.make_async_copy(rhs_hbm, rhs_ref, sems.at[0]),
        pltpu.make_async_copy(conn_hbm, conn_ref, sems.at[1]),
        pltpu.make_async_copy(table_hbm, table_ref, sems.at[2]),
        pltpu.make_async_copy(solved_hbm, sum_ref, sems.at[3]),
    ]

    def known(e):
        return pltpu.make_async_copy(schur_in_hbm.at[e], schur_ref.at[e], early_sems.at[e])

    def leave(k):
        e = early + k
        return pltpu.make_async_copy(schur_ref.at[e], schur_hbm.at[e], schur_sems.at[k])

    element.coupling_copy(early, 0).start()
    for copy in copies:
        copy.start()
    element.inverse_copy(early, 0).start()
    for k in range(1, late):
        element.coupling_copy(early + k, k).start()
        element.inverse_copy(early + k, k).start()
    for e in range(early):
        known(e).start()

    row = iota((PER_FACE, LANES), 0)
    lane = iota((PER_FACE, LANES), 1)
    first_lane = iota((1, LANES), 1)
    wide_lane = iota((trace, LANES), 1)
    for copy in copies:
        copy.wait()
    turn_rhs(rhs_ref, wide_ref, rhs_turned_ref)

    def position(elem, inner):
        face = lax.div(inner, capacity)
        return (face * elem_count + elem) * capacity + lax.rem(inner, capacity)

    high = jnp.full((1, LANES), -1, I32)
    rest = jnp.zeros((1, LANES), I32)
    for a in range(FACES_PER_ELEM):
        positions = jnp.full((PER_FACE, LANES), -1, I32)
        for e in range(elements):
            slot = conn_ref[a, e]
            here = position(lax.div(slot, own), lax.rem(slot, own))
            positions = jnp.where(row == e, here, positions)
            high = jnp.where(first_lane == a * PER_FACE + e, lax.div(slot, SLOT_BASE), high)
            rest = jnp.where(first_lane == a * PER_FACE + e, lax.rem(slot, SLOT_BASE), rest)
        hot = jnp.concatenate([positions == lane + k for k in range(0, slots, LANES)], axis=1)
        vector_ref[:, a * LANES : (a + 1) * LANES] = dot(hot.astype(BF16), table_ref[...])
    names = jnp.where(row == 0, high, jnp.where(row == 1, rest, 0))
    share_ref[NAMED:, :] = names.astype(F32).astype(BF16)
    place = position(my_elem, iota((own, slots), 0))
    pick = (iota((own, slots), 1) == place).astype(BF16)
    own_ref[...] = dot(pick, table_ref[...]).astype(BF16)

    def add(e, schur):
        total = schur * vector_ref[e : e + 1, :]
        total = sum(total[:, a * LANES : (a + 1) * LANES] for a in range(FACES_PER_ELEM))
        sums = jnp.sum(total, axis=1, keepdims=True)
        sum_ref[...] = sum_ref[...] + jnp.where(wide_lane == e, sums, 0.0)

    element.coupling_copy(early, 0).wait()
    element.turn(0)
    for step in range(late + 1):
        if step + 1 < late:
            element.coupling_copy(early + step + 1, step + 1).wait()
            element.turn(step + 1)
        if step < late:
            element.inverse_copy(early + step, step).wait()
            element.first(step)
        for e in range(step * early // (late + 1), (step + 1) * early // (late + 1)):
            known(e).wait()
            add(e, schur_ref[e].astype(F32))
        if step >= 1:
            k = step - 1
            e = early + k
            condensed = element.second(k)
            schur = -condensed[:, :trace]
            schur_ref[e] = schur.astype(BF16)
            leave(k).start()
            sum_ref[...] = jnp.where(wide_lane == e, condensed[:, trace:], sum_ref[...])
            add(e, schur)

    for a in range(FACES_PER_ELEM):
        shares = sum_ref[a * LANES : (a + 1) * LANES, :].T
        share_ref[a * PER_FACE : (a + 1) * PER_FACE, :] = shares[:PER_FACE].astype(BF16)
    for k in range(late):
        leave(k).wait()


def residual_kernel(elem_count, *refs):
    ins, (residual_ref, own_ref, shares_ref, sems) = refs[:-4], refs[-4:]
    places = [own_ref] + [shares_ref.at[k] for k in range(elem_count)]
    copies = [pltpu.make_async_copy(ins[k], places[k], sems.at[k]) for k in range(len(ins))]
    for copy in copies:
        copy.start()
    own = residual_ref.shape[0]
    mine = lax.axis_index("elem")
    slot = (iota((own, SHARE_ROWS), 0) + mine * own).astype(F32)
    for copy in copies:
        copy.wait()
    left = own_ref[...].astype(F32)
    for k in range(elem_count):
        names = shares_ref[k, NAMED:, :].astype(F32)
        named = (names[0:1] * SLOT_BASE + names[1:2])[:, :SHARE_ROWS]
        left = left - dot((slot == named).astype(BF16), shares_ref[k])
    residual_ref[...] = left


def coarse_kernel(got_hbm, out_ref, got_ref, sum_ref, full_ref, sem):
    copy = pltpu.make_async_copy(got_hbm, got_ref, sem)
    copy.start()
    copy.wait()
    total = got_ref[0].astype(F32)
    for k in range(1, got_ref.shape[0]):
        total = total + got_ref[k].astype(F32)
    sum_ref[...] = total

    lane = iota((HALF, LANES), 1)
    row = iota((HALF, LANES), 0)
    wide_row = iota((MROW, LANES), 0)
    wide_lane = iota((MROW, LANES), 1)
    top = wide_row < HALF
    held = (top & ((wide_lane <= wide_row) | (wide_lane >= HALF))) | (
        (~top) & (wide_lane >= wide_row)
    )
    for block in range(NC):
        dense = sum_ref[block * DENSE : (block + 1) * DENSE, :]
        upper = jnp.concatenate([dense, pltpu.roll(dense, MROW, 1)], axis=0)
        diag = sum_ref[NC * DENSE + block : NC * DENSE + block + 1, :]
        diag = pltpu.roll(diag + pltpu.roll(diag, MROW, 1), HALF, 1)
        lower = jnp.where(lane == row + HALF, diag, pltpu.roll(upper, HALF, 1))
        given = jnp.concatenate([upper, lower], axis=0)
        turned = jnp.concatenate([given, given], axis=0).T[:MROW]
        full_ref[block * MROW : (block + 1) * MROW, :] = jnp.where(held, given, turned)
    low = iota((NC, LANES), 1) < MROW
    for chunk in range(HALF):
        left = full_ref[pl.ds(2 * chunk, NC, stride=MROW), :]
        right = full_ref[pl.ds(2 * chunk + 1, NC, stride=MROW), :]
        out_ref[:, chunk * LANES : (chunk + 1) * LANES] = jnp.where(
            low, left, pltpu.roll(right, MROW, 1)
        )


ANY = pl.BlockSpec(memory_space=pl.ANY)
VMEM = pl.BlockSpec(memory_space=pltpu.VMEM)


def params(limit):
    return pltpu.CompilerParams(vmem_limit_bytes=limit)


def around(block, axis):
    count = lax.axis_size(axis)
    return [block] + [
        lax.ppermute(block, axis, [(i, i ^ k) for i in range(count)]) for k in range(1, count)
    ]


def shards(
    trace_old,
    new_owner,
    mortar_tiles,
    mortar_owner,
    mortar_coarse,
    interior_rhs,
    local_inverse,
    coupling,
    connectivity,
):
    face_count = lax.axis_size("face")
    elem_count = lax.axis_size("elem")
    row_count = trace_old.shape[0]
    tile_count = mortar_tiles.shape[0]
    elements, modes = interior_rhs.shape
    trace = FACES_PER_ELEM * FACE_COEFFS
    capacity = max(2, 2 * row_count // face_count)
    own = face_count * capacity

    slots = own * elem_count
    devices = face_count * elem_count
    early = min(EARLY, elements - 2)
    late = elements - early

    placed = pl.pallas_call(
        functools.partial(place_kernel, elem_count, face_count, capacity),
        out_shape=jax.ShapeDtypeStruct((slots, FACE_COEFFS), BF16),
        in_specs=[ANY, ANY],
        out_specs=VMEM,
        scratch_shapes=[
            pltpu.VMEM((1, row_count), I32),
            pltpu.VMEM(trace_old.shape, BF16),
            pltpu.SemaphoreType.DMA((2,)),
        ],
        compiler_params=params(BIG),
        name="place",
    )(new_owner.reshape(1, row_count), trace_old)
    table = lax.all_to_all(
        placed.reshape(devices, capacity, FACE_COEFFS), ("face", "elem"), 0, 0, tiled=True
    ).reshape(slots, FACE_COEFFS)

    stages = [
        pltpu.VMEM((trace, modes), BF16),
        pltpu.VMEM((trace, modes), BF16),
        pltpu.VMEM((trace, modes), BF16),
        pltpu.VMEM((trace, modes), BF16),
    ]
    blocks = face_count * NC
    sums_shape = (blocks * DENSE, LANES)
    schur_shape = jax.ShapeDtypeStruct((elements, trace, trace), BF16)
    half_grams, schur_early, solved = pl.pallas_call(
        functools.partial(gram_kernel, face_count),
        out_shape=(
            jax.ShapeDtypeStruct((blocks * (DENSE + 1), LANES), BF16),
            schur_shape,
            jax.ShapeDtypeStruct((trace, LANES), F32),
        ),
        in_specs=[ANY] * 6,
        out_specs=(VMEM, ANY, VMEM),
        scratch_shapes=[
            pltpu.SMEM((tile_count,), I32),
            pltpu.SMEM((tile_count,), I32),
            pltpu.VMEM(mortar_tiles.shape, BF16),
            pltpu.VMEM((tile_count * PITCH, LANES), F32),
            pltpu.VMEM(sums_shape, F32),
            pltpu.VMEM(sums_shape, F32),
            pltpu.VMEM((blocks, LANES), F32),
            pltpu.VMEM((blocks, LANES), F32),
            pltpu.VMEM((elements, modes), BF16),
            pltpu.VMEM((LANES, modes), F32),
            pltpu.VMEM((modes, LANES), BF16),
            pltpu.VMEM((early, modes, modes), BF16),
            pltpu.VMEM((early, modes, trace), BF16),
            pltpu.VMEM((early, trace, trace), BF16),
            *stages,
            pltpu.SemaphoreType.DMA((4,)),
            pltpu.SemaphoreType.DMA((2, early)),
            pltpu.SemaphoreType.DMA((early,)),
        ],
        compiler_params=params(BIG),
        cost_estimate=pl.CostEstimate(
            flops=2 * early * modes * trace * (modes + trace),
            bytes_accessed=16 << 20,
            transcendentals=0,
        ),
        name="gram",
    )(
        mortar_owner.reshape(tile_count),
        mortar_coarse,
        mortar_tiles,
        interior_rhs,
        local_inverse,
        coupling,
    )
    got = lax.all_to_all(
        half_grams.reshape(face_count, OWNER_ROWS, LANES), "face", 0, 0, tiled=True
    )

    schur_blocks, shares, own_rows = pl.pallas_call(
        functools.partial(main_kernel, elem_count, face_count),
        out_shape=(
            schur_shape,
            jax.ShapeDtypeStruct((SHARE_ROWS, LANES), BF16),
            jax.ShapeDtypeStruct((own, FACE_COEFFS), BF16),
        ),
        in_specs=[ANY] * 7,
        out_specs=(ANY, VMEM, VMEM),
        input_output_aliases={5: 0},
        scratch_shapes=[
            pltpu.SMEM((FACES_PER_ELEM, elements), I32),
            pltpu.VMEM((elements, modes), BF16),
            pltpu.VMEM((slots, FACE_COEFFS), BF16),
            pltpu.VMEM((late, modes, modes), BF16),
            pltpu.VMEM((late, modes, trace), BF16),
            pltpu.VMEM((elements, trace, trace), BF16),
            pltpu.VMEM((LANES, modes), F32),
            pltpu.VMEM((modes, LANES), BF16),
            pltpu.VMEM((PER_FACE, trace), F32),
            pltpu.VMEM((trace, LANES), F32),
            *stages,
            pltpu.SemaphoreType.DMA((4,)),
            pltpu.SemaphoreType.DMA((2, late)),
            pltpu.SemaphoreType.DMA((early,)),
            pltpu.SemaphoreType.DMA((late,)),
        ],
        compiler_params=params(BIG),
        cost_estimate=pl.CostEstimate(
            flops=2 * late * modes * trace * (modes + trace),
            bytes_accessed=16 << 20,
            transcendentals=0,
        ),
        name="condense",
    )(
        table,
        connectivity.T,
        interior_rhs,
        local_inverse,
        coupling,
        schur_early,
        solved,
    )

    all_shares = around(shares, "elem")
    coarse_blocks = pl.pallas_call(
        coarse_kernel,
        out_shape=jax.ShapeDtypeStruct((NC, MROW * MROW), F32),
        in_specs=[ANY],
        out_specs=VMEM,
        scratch_shapes=[
            pltpu.VMEM((face_count, OWNER_ROWS, LANES), BF16),
            pltpu.VMEM((OWNER_ROWS, LANES), F32),
            pltpu.VMEM((NC * MROW, LANES), F32),
            pltpu.SemaphoreType.DMA,
        ],
        compiler_params=params(BIG),
        name="coarse",
    )(got)
    own_rows, coarse_blocks = lax.optimization_barrier((own_rows, coarse_blocks))

    slot_residual = pl.pallas_call(
        functools.partial(residual_kernel, elem_count),
        out_shape=jax.ShapeDtypeStruct((own, FACE_COEFFS), F32),
        in_specs=[ANY] * (1 + elem_count),
        out_specs=VMEM,
        scratch_shapes=[
            pltpu.VMEM((own, FACE_COEFFS), BF16),
            pltpu.VMEM((elem_count, SHARE_ROWS, LANES), BF16),
            pltpu.SemaphoreType.DMA((1 + elem_count,)),
        ],
        compiler_params=params(BIG),
        name="residual",
    )(own_rows, *all_shares)
    return schur_blocks, slot_residual, coarse_blocks


def solution(mesh):
    return jax.shard_map(
        shards,
        mesh=mesh,
        in_specs=(
            P(("face", "elem"), None),
            P(("face", "elem"), None),
            P(("face", "elem"), None),
            P(("face", "elem"), None),
            P(("face", "elem")),
            P(("face", "elem"), None),
            P(("face", "elem"), None, None),
            P(("face", "elem"), None, None),
            P(("face", "elem"), None),
        ),
        out_specs=(
            P(("face", "elem"), None, None),
            P(("face", "elem"), None),
            P(("face", "elem"), None),
        ),
        check_vma=False,
    )
```

time: 46.5 us -> 46.5 us (level)
  waiting for transfers between devices: 9.2 us -> 5.4 us
  Pallas kernels: 19.7 us -> 22.9 us
  starting transfers between devices: 14.4 us -> 15.1 us
    ppermute x6 -> x3, waiting for transfers between devices: 6.37 us -> 0.01 us  [around(): lax.ppermute(block, axis, [(i, i ^ k) for i in range(count)])]
    all_to_all x1, waiting for transfers between devices: 0.01 us -> 5.39 us  [shards(): lax.all_to_all(half_grams.reshape(face_count, OWNER_ROWS, LANES), 'face',...]
    pallas_call x4 -> x5, Pallas kernels: 19.7 us -> 22.9 us  [the longest x1 8.49 us: shards(): pl.pallas_call(functools.partial(gram_kernel, face_count), out_shape=(jax...]
    all_to_all x1, waiting for transfers between devices: 2.83 us -> 0.01 us  [shards(): lax.all_to_all(placed.reshape(devices, capacity, FACE_COEFFS), ('face', '...]
    all_to_all x1, starting transfers between devices: 3.54 us -> 5.84 us  [shards(): lax.all_to_all(half_grams.reshape(face_count, OWNER_ROWS, LANES), 'face',...]
    ppermute x6 -> x3, starting transfers between devices: 3.56 us -> 1.93 us  [around(): lax.ppermute(block, axis, [(i, i ^ k) for i in range(count)])]
    unnamed x16 -> x10, local copies, waits for them, and re-layouts: 2.02 us -> 1.99 us
  transfers between devices with their start and end apart: 8 -> 5, of which waited for: 5 -> 1; matrix products, arithmetic and copies ran while one was open for 0% -> 0% of each run, Pallas kernels for 33% -> 42%
where the time goes in v6:
time: 46.5 us; the launch traced here: 46.1 us
  Pallas kernels  22.9 us (49%)
  starting transfers between devices  15.1 us (32%)
  waiting for transfers between devices  5.4 us (12%)
  local copies, waits for them, and re-layouts  1.99 us (4%)
  between operations  0.73 us (2%)
    pallas_call x1, Pallas kernels, shards(): pl.pallas_call(functools.partial(gram_kernel, face_count), out_shape=(jax...  8.49 us
    pallas_call x1, Pallas kernels, shards(): pl.pallas_call(functools.partial(main_kernel, elem_count, face_count), ou...  8.17 us
    all_to_all x1, starting transfers between devices, shards(): lax.all_to_all(placed.reshape(devices, capacity, FACE_COEFFS), ('face', '...  7.3 us
    all_to_all x1, starting transfers between devices, shards(): lax.all_to_all(half_grams.reshape(face_count, OWNER_ROWS, LANES), 'face',...  5.84 us
    all_to_all x1, waiting for transfers between devices, shards(): lax.all_to_all(half_grams.reshape(face_count, OWNER_ROWS, LANES), 'face',...  5.39 us
    pallas_call x1, Pallas kernels, shards(): pl.pallas_call(coarse_kernel, out_shape=jax.ShapeDtypeStruct((NC, MROW *...  2.91 us
    unnamed x10, local copies, waits for them, and re-layouts  1.99 us
    ppermute x3, starting transfers between devices, around(): lax.ppermute(block, axis, [(i, i ^ k) for i in range(count)])  1.93 us
  transfers between devices with their start and end apart: 5, of which 1 were waited for; matrix products, arithmetic and copies ran while one was open for 0% of the time, Pallas kernels for 42%

profile of v6, /device:TPU:0, one launch (start us, length us, event | category | flops | bytes accessed | tf_op | source)
XLA Modules:
  0.0 46.1 jit_solution(2964895375390347915)
XLA Ops:
  0.6 1.7 %place.1 = bf16[512,128]{1,0:T(8,128)(2,1)} custom-call(s32[1,64]{1,0:T(1,128)} %bitcast.10, bf16[64,128]{1,0:T(8,128)(2,1)} %trace_hbm.1), custom_call_target="tpu_custom_call" | custom-call | tf_op jit(solution)/shard_map/place/pallas_call | solution.py:491
  2.3 7.3 %all-to-all-start = ((bf16[32,16,128]{2,1,0:T(8,128)(2,1)}), bf16[32,16,128]{2,1,0:T(8,128)(2,1)S(1)}, u32[]{:S(2)}, u32[]{:S(2)}) async-start(bf16[32,16,128]{2,1,0:T(8,128)(2,1)} %bitcast.8), calls=%async_computation | async-start | bytes 262144 | tf_op jit(solution)/shard_map/all_to_all | solution.py:504
  9.7 8.5 %gram.1 = (bf16[2176,128]{1,0:T(8,128)(2,1)}, bf16[9,384,384]{2,1,0:T(8,128)(2,1)}, f32[384,128]{1,0:T(8,128)}) custom-call(s32[96]{0:T(128)} %bitcast.11, s32[96]{0:T(128)} %coarse_hbm.1, bf16[96,6144]{1,0:T(8,128)(2,1)} %tiles_hbm.1, bf16[9,512]{1,0:T(8,128)(2,1)} %rhs_hbm.3, bf16[9,512,512]{2,1,0:T(8,128)(2,1)} %inverse_hbm.3, ...), custom_call_target="tpu_custom_call" | custom-call | flops 1761607680 | bytes 16777216 | tf_op jit(solution)/shard_map/gram/pallas_call | solution.py:517
  18.1 0.0 all-to-all-done
  18.2 0.0 copy-start.1
  18.2 5.8 %all-to-all-start.1 = ((bf16[8,272,128]{2,1,0:T(8,128)(2,1)}), bf16[8,272,128]{2,1,0:T(8,128)(2,1)S(1)}, u32[]{:S(2)}, u32[]{:S(2)}) async-start(bf16[8,272,128]{2,1,0:T(8,128)(2,1)} %bitcast.6), calls=%async_computation.1 | async-start | bytes 1114112 | tf_op jit(solution)/shard_map/all_to_all | solution.py:561
  24.0 0.0 copy-done.1
  24.0 8.2 %condense.1 = (bf16[9,384,384]{2,1,0:T(8,128)(2,1)}, bf16[64,128]{1,0:T(8,128)(2,1)}, bf16[128,128]{1,0:T(8,128)(2,1)}) custom-call(bf16[512,128]{1,0:T(8,128)(2,1)} %bitcast.7, s32[3,9]{1,0:T(4,128)} %bitcast.9, bf16[9,512]{1,0:T(8,128)(2,1)} %rhs_hbm.3, bf16[9,512,512]{2,1,0:T(8,128)(2,1)} %inverse_hbm.3, ...), custom_call_target="tpu_custom_call", output_to_operand_aliasing={{0}: (5, {})} | custom-call | flops 1409286144 | bytes 16777216 | tf_op jit(solution)/shard_map/condense/pallas_call | solution.py:565
  32.2 1.0 %collective-permute-start.2 = (bf16[64,128]{1,0:T(8,128)(2,1)}, bf16[64,128]{1,0:T(8,128)(2,1)S(1)}, u32[]{:S(2)}, u32[]{:S(2)}) collective-permute-start(bf16[64,128]{1,0:T(8,128)(2,1)} %get-tuple-element.17.refs_1_), channel_id=1, source_target_pairs={{0,3},{1,2},{2,1},{3,0},{4,7},{5,6},{6,5},{7,4},{8,11},{9,10},{10,... | collective-permute-start | bytes 49160 | tf_op jit(solution)/shard_map/ppermute | solution.py:462
  33.2 0.6 %collective-permute-start.1 = (bf16[64,128]{1,0:T(8,128)(2,1)}, bf16[64,128]{1,0:T(8,128)(2,1)S(1)}, u32[]{:S(2)}, u32[]{:S(2)}) collective-permute-start(bf16[64,128]{1,0:T(8,128)(2,1)} %get-tuple-element.17.refs_1_), channel_id=1, source_target_pairs={{0,2},{1,3},{2,0},{3,1},{4,6},{5,7},{6,4},{7,5},{8,10},{9,11},{10,... | collective-permute-start | bytes 49160 | tf_op jit(solution)/shard_map/ppermute | solution.py:462
  33.8 0.3 collective-permute-start
  34.1 5.4 %all-to-all-done.1.got_hbm = bf16[8,272,128]{2,1,0:T(8,128)(2,1)S(1)} async-done(((bf16[8,272,128]{2,1,0:T(8,128)(2,1)}), bf16[8,272,128]{2,1,0:T(8,128)(2,1)S(1)}, u32[]{:S(2)}, u32[]{:S(2)}) %all-to-all-start.1) | async-done | bytes 557088 | tf_op jit(solution)/shard_map/all_to_all | solution.py:561
  39.5 0.0 copy-start
  39.5 0.8 %copy-done = bf16[8,272,128]{2,1,0:T(8,128)(2,1)} copy-done((bf16[8,272,128]{2,1,0:T(8,128)(2,1)}, bf16[8,272,128]{2,1,0:T(8,128)(2,1)S(1)}, u32[]{:S(2)}) %copy-start) | copy-done | bytes 557080
  40.3 2.9 %coarse.1 = f32[16,4096]{1,0:T(8,128)} custom-call(bf16[8,272,128]{2,1,0:T(8,128)(2,1)} %copy-done), custom_call_target="tpu_custom_call" | custom-call | tf_op jit(solution)/shard_map/coarse/pallas_call | solution.py:610
  43.2 0.0 collective-permute-done.2.refs_4_
  43.2 0.0 copy-start.2
  43.3 0.0 collective-permute-done.1.refs_3_
  43.3 0.0 copy-start.3
  43.3 0.0 collective-permute-done.refs_2_
  43.3 0.6 %copy-done.2 = bf16[64,128]{1,0:T(8,128)(2,1)} copy-done((bf16[64,128]{1,0:T(8,128)(2,1)}, bf16[64,128]{1,0:T(8,128)(2,1)S(1)}, u32[]{:S(2)}) %copy-start.2) | copy-done | bytes 16408
  43.8 0.0 copy-done.3
  43.9 0.6 %copy-done.4 = bf16[64,128]{1,0:T(8,128)(2,1)} copy-done((bf16[64,128]{1,0:T(8,128)(2,1)}, bf16[64,128]{1,0:T(8,128)(2,1)S(1)}, u32[]{:S(2)}) %copy-start.4) | copy-done | bytes 16408
  44.5 1.6 %residual.1 = f32[128,128]{1,0:T(8,128)} custom-call(bf16[128,128]{1,0:T(8,128)(2,1)} %get-tuple-element.16.refs_0_, bf16[64,128]{1,0:T(8,128)(2,1)} %get-tuple-element.17.refs_1_, bf16[64,128]{1,0:T(8,128)(2,1)} %copy-done.4, bf16[64,128]{1,0:T(8,128)(2,1)} %copy-done.3, bf16[64,128]{1,0:T(8,128)(2,1)} %copy-done.2), custom_call_target="tpu_custom_call" | custom-call | tf_op jit(solution)/shard_map/residual/pallas_call | solution.py:626
  (1 shorter events, 0.0 us)
Async XLA Ops:
  2.3 15.8 %all-to-all-start = ((bf16[32,16,128]{2,1,0:T(8,128)(2,1)}), bf16[32,16,128]{2,1,0:T(8,128)(2,1)S(1)}, u32[]{:S(2)}, u32[]{:S(2)}) async-start(bf16[32,16,128]{2,1,0:T(8,128)(2,1)} %bitcast.8), calls=%async_computation | async-start | bytes 262144 | tf_op jit(solution)/shard_map/all_to_all | solution.py:504
  18.2 5.9 %copy-start.1 = (bf16[32,16,128]{2,1,0:T(8,128)(2,1)}, bf16[32,16,128]{2,1,0:T(8,128)(2,1)S(1)}, u32[]{:S(2)}) copy-start(bf16[32,16,128]{2,1,0:T(8,128)(2,1)S(1)} %all-to-all-done) | copy-start | bytes 393220
  18.2 21.3 %all-to-all-start.1 = ((bf16[8,272,128]{2,1,0:T(8,128)(2,1)}), bf16[8,272,128]{2,1,0:T(8,128)(2,1)S(1)}, u32[]{:S(2)}, u32[]{:S(2)}) async-start(bf16[8,272,128]{2,1,0:T(8,128)(2,1)} %bitcast.6), calls=%async_computation.1 | async-start | bytes 1114112 | tf_op jit(solution)/shard_map/all_to_all | solution.py:561
  32.2 11.0 %collective-permute-start.2 = (bf16[64,128]{1,0:T(8,128)(2,1)}, bf16[64,128]{1,0:T(8,128)(2,1)S(1)}, u32[]{:S(2)}, u32[]{:S(2)}) collective-permute-start(bf16[64,128]{1,0:T(8,128)(2,1)} %get-tuple-element.17.refs_1_), channel_id=1, source_target_pairs={{0,3},{1,2},{2,1},{3,0},{4,7},{5,6},{6,5},{7,4},{8,11},{9,10},{10,... | collective-permute-start | bytes 49160 | tf_op jit(solution)/shard_map/ppermute | solution.py:462
  33.2 10.0 %collective-permute-start.1 = (bf16[64,128]{1,0:T(8,128)(2,1)}, bf16[64,128]{1,0:T(8,128)(2,1)S(1)}, u32[]{:S(2)}, u32[]{:S(2)}) collective-permute-start(bf16[64,128]{1,0:T(8,128)(2,1)} %get-tuple-element.17.refs_1_), channel_id=1, source_target_pairs={{0,2},{1,3},{2,0},{3,1},{4,6},{5,7},{6,4},{7,5},{8,10},{9,11},{10,... | collective-permute-start | bytes 49160 | tf_op jit(solution)/shard_map/ppermute | solution.py:462
  33.8 9.5 %collective-permute-start = (bf16[64,128]{1,0:T(8,128)(2,1)}, bf16[64,128]{1,0:T(8,128)(2,1)S(1)}, u32[]{:S(2)}, u32[]{:S(2)}) collective-permute-start(bf16[64,128]{1,0:T(8,128)(2,1)} %get-tuple-element.17.refs_1_), channel_id=1, source_target_pairs={{0,1},{1,0},{2,3},{3,2},{4,5},{5,4},{6,7},{7,6},{8,9},{9,8},{10,11... | collective-permute-start | bytes 49160 | tf_op jit(solution)/shard_map/ppermute | solution.py:462
  39.5 0.8 %copy-start = (bf16[8,272,128]{2,1,0:T(8,128)(2,1)}, bf16[8,272,128]{2,1,0:T(8,128)(2,1)S(1)}, u32[]{:S(2)}) copy-start(bf16[8,272,128]{2,1,0:T(8,128)(2,1)S(1)} %all-to-all-done.1.got_hbm) | copy-start | bytes 1671172
  43.2 0.6 %copy-start.2 = (bf16[64,128]{1,0:T(8,128)(2,1)}, bf16[64,128]{1,0:T(8,128)(2,1)S(1)}, u32[]{:S(2)}) copy-start(bf16[64,128]{1,0:T(8,128)(2,1)S(1)} %collective-permute-done.2.refs_4_) | copy-start | bytes 49156
  43.3 0.6 %copy-start.3 = (bf16[64,128]{1,0:T(8,128)(2,1)}, bf16[64,128]{1,0:T(8,128)(2,1)S(1)}, u32[]{:S(2)}) copy-start(bf16[64,128]{1,0:T(8,128)(2,1)S(1)} %collective-permute-done.1.refs_3_) | copy-start | bytes 49156
  43.9 0.6 %copy-start.4 = (bf16[64,128]{1,0:T(8,128)(2,1)}, bf16[64,128]{1,0:T(8,128)(2,1)S(1)}, u32[]{:S(2)}) copy-start(bf16[64,128]{1,0:T(8,128)(2,1)S(1)} %collective-permute-done.refs_2_) | copy-start | bytes 49156

commit v7 on v5

v7 whole, which is shorter than its diff:
```python
import functools

import jax
import jax.numpy as jnp
from jax import lax
from jax.experimental import pallas as pl
from jax.experimental.pallas import tpu as pltpu
from jax.sharding import PartitionSpec as P

FACE_COEFFS = 128
FACES_PER_ELEM = 3
MROW = 64
MCOL = 96
NC = 16
HALF = MROW // 2
LANES = 128
DENSE = HALF * MROW // LANES
OWNER_ROWS = NC * (DENSE + 1)
PER_FACE = 16
NAMED = FACES_PER_ELEM * PER_FACE
SHARE_ROWS = NAMED + 16
SLOT_BASE = 16
CHUNK = 16
BIG = 62 << 20
SMALL = 12 << 20
PITCH = MROW + 8

BF16 = jnp.bfloat16
F32 = jnp.float32
I32 = jnp.int32

NT = (((1,), (1,)), ((), ()))
TN = (((0,), (0,)), ((), ()))


def iota(shape, dim):
    return lax.broadcasted_iota(I32, shape, dim)


def dot(left, right, dims=(((1,), (0,)), ((), ()))):
    return lax.dot_general(left, right, dims, preferred_element_type=F32)


def divided(value, by):
    shift = by.bit_length() - 1
    assert by == 1 << shift
    return value >> shift, value & (by - 1)


def place_kernel(elem_count, face_count, capacity, owner_hbm, trace_hbm, placed_ref, *refs):
    owner_ref, trace_ref, sems = refs
    copies = [
        pltpu.make_async_copy(owner_hbm, owner_ref, sems.at[0]),
        pltpu.make_async_copy(trace_hbm, trace_ref, sems.at[1]),
    ]
    for copy in copies:
        copy.start()
    slots, rows = placed_ref.shape[0], trace_ref.shape[0]
    earlier = (iota((rows, rows), 0) < iota((rows, rows), 1)).astype(BF16)
    slot = iota((slots, rows), 0)
    wanted = divided(slot, elem_count * capacity)[0] * capacity + divided(slot, capacity)[1]
    for copy in copies:
        copy.wait()
    owners = owner_ref[...]
    hot = (iota((face_count, rows), 0) == owners).astype(F32)
    rank = jnp.sum(hot * dot(hot.astype(BF16), earlier), axis=0, keepdims=True).astype(I32)
    place = (wanted == owners * capacity + rank).astype(BF16)
    placed_ref[...] = dot(place, trace_ref[...]).astype(BF16)


def turn_rhs(rhs_ref, wide_ref, rhs_turned_ref):
    wide_ref[...] = jnp.zeros_like(wide_ref)
    wide_ref[0 : rhs_ref.shape[0], :] = rhs_ref[...].astype(F32)
    rhs_turned_ref[...] = wide_ref[...].T.astype(BF16)


def gram_kernel(
    face_count,
    owner_hbm,
    coarse_hbm,
    tiles_hbm,
    out_ref,
    owner_ref,
    coarse_ref,
    tiles_ref,
    rows_ref,
    acc_a_ref,
    acc_b_ref,
    diag_a_ref,
    diag_b_ref,
    sems,
):
    accs, diags = (acc_a_ref, acc_b_ref), (diag_a_ref, diag_b_ref)
    tiles = tiles_ref.shape[0]
    copies = [
        pltpu.make_async_copy(owner_hbm, owner_ref, sems.at[0]),
        pltpu.make_async_copy(coarse_hbm, coarse_ref, sems.at[1]),
    ]
    chunks = []
    for chunk in range(tiles // CHUNK):
        here = pl.ds(chunk * CHUNK, CHUNK)
        chunks.append(
            pltpu.make_async_copy(tiles_hbm.at[here], tiles_ref.at[here], sems.at[2 + chunk])
        )
    for copy in copies + chunks:
        copy.start()
    for ref in (*accs, *diags):
        ref[...] = jnp.zeros_like(ref)
    for copy in copies:
        copy.wait()

    lane = iota((CHUNK, LANES), 1)
    inside = lane < MCOL
    row = iota((HALF, LANES), 0)
    column = divided(iota((HALF, LANES), 1), MROW)[1]
    swapped = (column > row) & (column < HALF)
    diagonal = column == row
    low = iota((DENSE, LANES), 1) < MROW
    low_wide = iota((MROW, LANES), 1) < MROW
    low_row = iota((1, LANES), 1) < MROW

    for chunk in range(tiles // CHUNK):
        chunks[chunk].wait()
        first_tile = chunk * CHUNK
        for group in range(MROW // 4):
            base = group * 3 * LANES
            one, two, three = (
                tiles_ref[
                    first_tile : first_tile + CHUNK, base + k * LANES : base + (k + 1) * LANES
                ].astype(F32)
                for k in range(3)
            )
            rolled = (
                one,
                pltpu.roll(jnp.where(lane < 64, two, one), 32, 1),
                pltpu.roll(jnp.where(lane < 32, three, two), 64, 1),
                pltpu.roll(three, 96, 1),
            )
            for k in range(4):
                rows_ref[pl.ds(first_tile * PITCH + 4 * group + k, CHUNK, stride=PITCH), :] = (
                    jnp.where(inside, rolled[k], 0.0)
                )
        for tile in range(first_tile, first_tile + CHUNK, 2):
            both = jnp.concatenate(
                [
                    rows_ref[t * PITCH : t * PITCH + MROW, :].astype(BF16)
                    for t in (tile, tile + 1)
                ],
                axis=0,
            )
            gram = dot(both, both, NT)
            side = jnp.where(low_wide, gram[:MROW], gram[MROW:])
            lower = pltpu.roll(side[HALF:], LANES - HALF, 1)
            packed = jnp.where(swapped, lower, side[:HALF])
            diag = jnp.sum(jnp.where(diagonal, lower, 0.0), axis=0, keepdims=True)
            turned = pltpu.roll(packed, MROW, 1)
            dense = (
                jnp.where(low, packed[:DENSE], turned[DENSE:]),
                jnp.where(low, turned[:DENSE], packed[DENSE:]),
            )
            own = (jnp.where(low_row, diag, 0.0), jnp.where(low_row, 0.0, diag))
            for k in range(2):
                block = owner_ref[tile + k] * NC + coarse_ref[tile + k]
                here = pl.ds(pl.multiple_of(block * DENSE, DENSE), DENSE)
                accs[k][here, :] += dense[k]
                diags[k][pl.ds(block, 1), :] += own[k]
    size = NC * DENSE
    for owner in range(face_count):
        start = owner * OWNER_ROWS
        here = slice(owner * size, (owner + 1) * size)
        out_ref[start : start + size, :] = (accs[0][here, :] + accs[1][here, :]).astype(BF16)
        here = slice(owner * NC, (owner + 1) * NC)
        out_ref[start + size : start + size + NC, :] = (
            diags[0][here, :] + diags[1][here, :]
        ).astype(BF16)


def main_kernel(
    elem_count,
    face_count,
    table_hbm,
    conn_hbm,
    rhs_hbm,
    inverse_hbm,
    coupling_hbm,
    schur_hbm,
    share_ref,
    own_ref,
    conn_ref,
    rhs_ref,
    table_ref,
    inverse_ref,
    coupling_ref,
    schur_ref,
    wide_ref,
    rhs_turned_ref,
    vector_ref,
    sum_ref,
    turned_a_ref,
    turned_b_ref,
    product_a_ref,
    product_b_ref,
    small_sems,
    block_sems,
    schur_sems,
):
    elements = rhs_ref.shape[0]
    trace = FACES_PER_ELEM * FACE_COEFFS
    slots = table_ref.shape[0]
    own = own_ref.shape[0]
    capacity = own // face_count
    my_elem = lax.axis_index("elem")
    small = [
        pltpu.make_async_copy(rhs_hbm, rhs_ref, small_sems.at[0]),
        pltpu.make_async_copy(conn_hbm, conn_ref, small_sems.at[1]),
        pltpu.make_async_copy(table_hbm, table_ref, small_sems.at[2]),
    ]

    def coupling_copy(e):
        return pltpu.make_async_copy(coupling_hbm.at[e], coupling_ref.at[e], block_sems.at[0, e])

    def inverse_copy(e):
        return pltpu.make_async_copy(inverse_hbm.at[e], inverse_ref.at[e], block_sems.at[1, e])

    def leave(e):
        return pltpu.make_async_copy(schur_ref.at[e], schur_hbm.at[e], schur_sems.at[e])

    coupling_copy(0).start()
    for copy in small:
        copy.start()
    inverse_copy(0).start()
    coupling_copy(1).start()
    inverse_copy(1).start()
    coupling_copy(2).start()

    def turn(e, turned_ref):
        turned_ref[...] = coupling_ref[e].T

    def first(e, turned_ref, product_ref):
        product_ref[...] = dot(turned_ref[...], inverse_ref[e]).astype(BF16)

    def second(e, product_ref):
        wide = jnp.concatenate([coupling_ref[e], rhs_turned_ref[...]], axis=1)
        condensed = dot(product_ref[...], wide)
        schur_ref[e] = (-condensed[:, :trace]).astype(BF16)
        total = condensed * vector_ref[pl.ds(e, 1), :]
        total = sum(total[:, k * LANES : (k + 1) * LANES] for k in range(FACES_PER_ELEM + 1))
        sums = jnp.sum(total, axis=1, keepdims=True)
        sum_ref[...] = jnp.where(iota((trace, LANES), 1) == e, sums, sum_ref[...])

    turned = (turned_a_ref, turned_b_ref)
    product = (product_a_ref, product_b_ref)

    def advance(e, parity, turning=True, finishing=True):
        if turning:
            @pl.when(e + 2 < elements)
            def _():
                inverse_copy(e + 2).start()

            @pl.when(e + 3 < elements)
            def _():
                coupling_copy(e + 3).start()

            coupling_copy(e + 1).wait()
        inverse_copy(e).wait()
        if turning:
            turn(e + 1, turned[1 - parity])
        first(e, turned[parity], product[parity])
        if finishing:
            second(e - 1, product[1 - parity])
            leave(e - 1).start()

    coupling_copy(0).wait()
    turn(0, turned[0])
    for copy in small:
        copy.wait()
    sum_ref[...] = jnp.zeros_like(sum_ref)
    turn_rhs(rhs_ref, wide_ref, rhs_turned_ref)
    row = iota((PER_FACE, LANES), 0)
    lane = iota((PER_FACE, LANES), 1)

    def position(elem, inner):
        face, rank = divided(inner, capacity)
        return (face * elem_count + elem) * capacity + rank

    first_lane = iota((1, LANES), 1)
    high = jnp.full((1, LANES), -1, I32)
    rest = jnp.zeros((1, LANES), I32)
    for a in range(FACES_PER_ELEM):
        positions = jnp.full((PER_FACE, LANES), -1, I32)
        for e in range(elements):
            slot = conn_ref[a, e]
            positions = jnp.where(row == e, position(*divided(slot, own)), positions)
            here = first_lane == a * PER_FACE + e
            quotient, remainder = divided(slot, SLOT_BASE)
            high = jnp.where(here, quotient, high)
            rest = jnp.where(here, remainder, rest)
        hot = jnp.concatenate([positions == lane + k for k in range(0, slots, LANES)], axis=1)
        lam = dot(hot.astype(BF16), table_ref[...])
        vector_ref[:, a * LANES : (a + 1) * LANES] = -lam
    vector_ref[:, trace:] = (row == lane).astype(F32)
    names = jnp.where(row == 0, high, jnp.where(row == 1, rest, 0))
    share_ref[NAMED:, :] = names.astype(F32).astype(BF16)
    place = position(my_elem, iota((own, slots), 0))
    pick = (iota((own, slots), 1) == place).astype(BF16)
    own_ref[...] = dot(pick, table_ref[...]).astype(BF16)

    advance(0, 0, finishing=False)

    def two(index, carry):
        advance(2 * index + 1, 1)
        advance(2 * index + 2, 0)
        return carry

    pairs = (elements - 2) // 2
    lax.fori_loop(0, pairs, two, 0)
    for e in range(2 * pairs + 1, elements):
        advance(e, e % 2, turning=e + 1 < elements)
    second(elements - 1, product[(elements - 1) % 2])
    leave(elements - 1).start()

    for a in range(FACES_PER_ELEM):
        shares = sum_ref[a * LANES : (a + 1) * LANES, :].T
        share_ref[a * PER_FACE : (a + 1) * PER_FACE, :] = shares[:PER_FACE].astype(BF16)
    for e in range(elements):
        leave(e).wait()


def residual_kernel(elem_count, *refs):
    ins, (residual_ref, own_ref, shares_ref, sems) = refs[:-4], refs[-4:]
    places = [own_ref] + [shares_ref.at[k] for k in range(elem_count)]
    copies = [pltpu.make_async_copy(ins[k], places[k], sems.at[k]) for k in range(len(ins))]
    for copy in copies:
        copy.start()
    own = residual_ref.shape[0]
    mine = lax.axis_index("elem")
    slot = (iota((own, SHARE_ROWS), 0) + mine * own).astype(F32)
    for copy in copies:
        copy.wait()
    left = own_ref[...].astype(F32)
    for k in range(elem_count):
        names = shares_ref[k, NAMED:, :].astype(F32)
        named = (names[0:1] * SLOT_BASE + names[1:2])[:, :SHARE_ROWS]
        left = left - dot((slot == named).astype(BF16), shares_ref[k])
    residual_ref[...] = left


def coarse_kernel(got_ref, out_ref, sum_ref, full_ref):
    total = got_ref[0].astype(F32)
    for k in range(1, got_ref.shape[0]):
        total = total + got_ref[k].astype(F32)
    sum_ref[...] = total

    lane = iota((HALF, LANES), 1)
    row = iota((HALF, LANES), 0)
    wide_row = iota((MROW, LANES), 0)
    wide_lane = iota((MROW, LANES), 1)
    top = wide_row < HALF
    held = (top & ((wide_lane <= wide_row) | (wide_lane >= HALF))) | (
        (~top) & (wide_lane >= wide_row)
    )
    for block in range(NC):
        dense = sum_ref[block * DENSE : (block + 1) * DENSE, :]
        upper = jnp.concatenate([dense, pltpu.roll(dense, MROW, 1)], axis=0)
        diag = sum_ref[NC * DENSE + block : NC * DENSE + block + 1, :]
        diag = pltpu.roll(diag + pltpu.roll(diag, MROW, 1), HALF, 1)
        lower = jnp.where(lane == row + HALF, diag, pltpu.roll(upper, HALF, 1))
        given = jnp.concatenate([upper, lower], axis=0)
        turned = jnp.concatenate([given, given], axis=0).T[:MROW]
        full_ref[block * MROW : (block + 1) * MROW, :] = jnp.where(held, given, turned)
    low = iota((NC, LANES), 1) < MROW
    for chunk in range(HALF):
        left = full_ref[pl.ds(2 * chunk, NC, stride=MROW), :]
        right = full_ref[pl.ds(2 * chunk + 1, NC, stride=MROW), :]
        out_ref[:, chunk * LANES : (chunk + 1) * LANES] = jnp.where(
            low, left, pltpu.roll(right, MROW, 1)
        )


ANY = pl.BlockSpec(memory_space=pl.ANY)
VMEM = pl.BlockSpec(memory_space=pltpu.VMEM)


def params(limit):
    return pltpu.CompilerParams(vmem_limit_bytes=limit)


def around(block, axis):
    count = lax.axis_size(axis)
    return [block] + [
        lax.ppermute(block, axis, [(i, i ^ k) for i in range(count)]) for k in range(1, count)
    ]


def shards(
    trace_old,
    new_owner,
    mortar_tiles,
    mortar_owner,
    mortar_coarse,
    interior_rhs,
    local_inverse,
    coupling,
    connectivity,
):
    face_count = lax.axis_size("face")
    elem_count = lax.axis_size("elem")
    row_count = trace_old.shape[0]
    tile_count = mortar_tiles.shape[0]
    elements, modes = interior_rhs.shape
    trace = FACES_PER_ELEM * FACE_COEFFS
    capacity = max(2, 2 * row_count // face_count)
    own = face_count * capacity

    slots = own * elem_count
    devices = face_count * elem_count

    placed = pl.pallas_call(
        functools.partial(place_kernel, elem_count, face_count, capacity),
        out_shape=jax.ShapeDtypeStruct((slots, FACE_COEFFS), BF16),
        in_specs=[ANY, ANY],
        out_specs=VMEM,
        scratch_shapes=[
            pltpu.VMEM((1, row_count), I32),
            pltpu.VMEM(trace_old.shape, BF16),
            pltpu.SemaphoreType.DMA((2,)),
        ],
        compiler_params=params(BIG),
        name="place",
    )(new_owner.reshape(1, row_count), trace_old)
    table = lax.all_to_all(
        placed.reshape(devices, capacity, FACE_COEFFS), ("face", "elem"), 0, 0, tiled=True
    ).reshape(slots, FACE_COEFFS)

    blocks = face_count * NC
    sums_shape = (blocks * DENSE, LANES)
    half_grams = pl.pallas_call(
        functools.partial(gram_kernel, face_count),
        out_shape=jax.ShapeDtypeStruct((blocks * (DENSE + 1), LANES), BF16),
        in_specs=[ANY] * 3,
        out_specs=VMEM,
        scratch_shapes=[
            pltpu.SMEM((tile_count,), I32),
            pltpu.SMEM((tile_count,), I32),
            pltpu.VMEM(mortar_tiles.shape, BF16),
            pltpu.VMEM((tile_count * PITCH, LANES), F32),
            pltpu.VMEM(sums_shape, F32),
            pltpu.VMEM(sums_shape, F32),
            pltpu.VMEM((blocks, LANES), F32),
            pltpu.VMEM((blocks, LANES), F32),
            pltpu.SemaphoreType.DMA((2 + tile_count // CHUNK,)),
        ],
        compiler_params=params(BIG),
        cost_estimate=pl.CostEstimate(
            flops=4 * tile_count * MROW * MROW * LANES, bytes_accessed=12 << 20, transcendentals=0
        ),
        name="gram",
    )(mortar_owner.reshape(tile_count), mortar_coarse, mortar_tiles)
    got = lax.all_to_all(
        half_grams.reshape(face_count, OWNER_ROWS, LANES), "face", 0, 0, tiled=True
    )

    slots_named, _ = lax.optimization_barrier((connectivity.T, half_grams))
    schur_blocks, shares, own_rows = pl.pallas_call(
        functools.partial(main_kernel, elem_count, face_count),
        out_shape=(
            jax.ShapeDtypeStruct((elements, trace, trace), BF16),
            jax.ShapeDtypeStruct((SHARE_ROWS, LANES), BF16),
            jax.ShapeDtypeStruct((own, FACE_COEFFS), BF16),
        ),
        in_specs=[ANY] * 5,
        out_specs=(ANY, VMEM, VMEM),
        scratch_shapes=[
            pltpu.SMEM((FACES_PER_ELEM, elements), I32),
            pltpu.VMEM((elements, modes), BF16),
            pltpu.VMEM((slots, FACE_COEFFS), BF16),
            pltpu.VMEM((elements, modes, modes), BF16),
            pltpu.VMEM((elements, modes, trace), BF16),
            pltpu.VMEM((elements, trace, trace), BF16),
            pltpu.VMEM((LANES, modes), F32),
            pltpu.VMEM((modes, LANES), BF16),
            pltpu.VMEM((PER_FACE, trace + LANES), F32),
            pltpu.VMEM((trace, LANES), F32),
            pltpu.VMEM((trace, modes), BF16),
            pltpu.VMEM((trace, modes), BF16),
            pltpu.VMEM((trace, modes), BF16),
            pltpu.VMEM((trace, modes), BF16),
            pltpu.SemaphoreType.DMA((3,)),
            pltpu.SemaphoreType.DMA((2, elements)),
            pltpu.SemaphoreType.DMA((elements,)),
        ],
        compiler_params=params(BIG),
        cost_estimate=pl.CostEstimate(
            flops=2 * elements * modes * trace * (modes + trace),
            bytes_accessed=2 * elements * (modes * (modes + trace) + trace * trace),
            transcendentals=0,
        ),
        name="condense",
    )(table, slots_named, interior_rhs, local_inverse, coupling)

    slot_residual = pl.pallas_call(
        functools.partial(residual_kernel, elem_count),
        out_shape=jax.ShapeDtypeStruct((own, FACE_COEFFS), F32),
        in_specs=[ANY] * (1 + elem_count),
        out_specs=VMEM,
        scratch_shapes=[
            pltpu.VMEM((own, FACE_COEFFS), BF16),
            pltpu.VMEM((elem_count, SHARE_ROWS, LANES), BF16),
            pltpu.SemaphoreType.DMA((1 + elem_count,)),
        ],
        compiler_params=params(SMALL),
        name="residual",
    )(own_rows, *around(shares, "elem"))

    got, slot_residual = lax.optimization_barrier((got, slot_residual))
    coarse_blocks = pl.pallas_call(
        coarse_kernel,
        out_shape=jax.ShapeDtypeStruct((NC, MROW * MROW), F32),
        in_specs=[VMEM],
        out_specs=VMEM,
        scratch_shapes=[
            pltpu.VMEM((OWNER_ROWS, LANES), F32),
            pltpu.VMEM((NC * MROW, LANES), F32),
        ],
        compiler_params=params(SMALL),
        name="coarse",
    )(got)
    return schur_blocks, slot_residual, coarse_blocks


def solution(mesh):
    return jax.shard_map(
        shards,
        mesh=mesh,
        in_specs=(
            P(("face", "elem"), None),
            P(("face", "elem"), None),
            P(("face", "elem"), None),
            P(("face", "elem"), None),
            P(("face", "elem")),
            P(("face", "elem"), None),
            P(("face", "elem"), None, None),
            P(("face", "elem"), None, None),
            P(("face", "elem"), None),
        ),
        out_specs=(
            P(("face", "elem"), None, None),
            P(("face", "elem"), None),
            P(("face", "elem"), None),
        ),
        check_vma=False,
    )
```

time: 63.3 us -> 39.6 us (0.63)
  starting transfers between devices: 29.1 us -> 12.8 us
  waiting for transfers between devices: 12.4 us -> 5.36 us
  local copies, waits for them, and re-layouts: 2.38 us -> 1.48 us
    ppermute x14 -> x0, starting transfers between devices: 21.5 us -> none  [exchange(): lax.ppermute(blocks[k], 'face', [(i, i ^ k) for i in range(face_count)])]
    all_to_all x0 -> x2, starting transfers between devices: none -> 10.8 us  [the longest x1 7.3 us: shards(): lax.all_to_all(placed.reshape(devices, capacity, FACE_COEFFS), ('face', '...]
    ppermute x14 -> x0, waiting for transfers between devices: 8.13 us -> none  [exchange(): lax.ppermute(blocks[k], 'face', [(i, i ^ k) for i in range(face_count)])]
    ppermute x9 -> x3, starting transfers between devices: 7.62 us -> 1.93 us  [around(): lax.ppermute(block, axis, [(i, i ^ k) for i in range(count)])]
    all_to_all x0 -> x2, waiting for transfers between devices: none -> 3.03 us  [the longest x1 3.03 us: shards(): lax.all_to_all(placed.reshape(devices, capacity, FACE_COEFFS), ('face', '...]
    ppermute x9 -> x3, waiting for transfers between devices: 4.25 us -> 2.33 us  [around(): lax.ppermute(block, axis, [(i, i ^ k) for i in range(count)])]
    pallas_call x3 -> x4, Pallas kernels: 16.1 us -> 17.1 us  [the longest x1 9.07 us: shards(): pl.pallas_call(functools.partial(main_kernel, elem_count, face_count), ou...]
    unnamed x56 -> x6, local copies, waits for them, and re-layouts: 2.38 us -> 1.48 us
  transfers between devices with their start and end apart: 23 -> 5, of which waited for: 6 -> 3; matrix products, arithmetic and copies ran while one was open for 0% -> 0% of each run, Pallas kernels for 20% -> 39%
where the time goes in v7:
time: 39.6 us; the launch traced here: 39.1 us
  Pallas kernels  18.8 us (47%)
  starting transfers between devices  12.8 us (32%)
  waiting for transfers between devices  5.36 us (14%)
  local copies, waits for them, and re-layouts  1.48 us (4%)
  between operations  0.7 us (2%)
    pallas_call x1, Pallas kernels, shards(): pl.pallas_call(functools.partial(main_kernel, elem_count, face_count), ou...  9.07 us
    all_to_all x1, starting transfers between devices, shards(): lax.all_to_all(placed.reshape(devices, capacity, FACE_COEFFS), ('face', '...  7.3 us
    pallas_call x1, Pallas kernels, shards(): pl.pallas_call(functools.partial(gram_kernel, face_count), out_shape=jax....  5.2 us
    all_to_all x1, starting transfers between devices, shards(): lax.all_to_all(half_grams.reshape(face_count, OWNER_ROWS, LANES), 'face',...  3.54 us
    all_to_all x1, waiting for transfers between devices, shards(): lax.all_to_all(placed.reshape(devices, capacity, FACE_COEFFS), ('face', '...  3.03 us
    ppermute x3, waiting for transfers between devices, around(): lax.ppermute(block, axis, [(i, i ^ k) for i in range(count)])  2.33 us
    ppermute x3, starting transfers between devices, around(): lax.ppermute(block, axis, [(i, i ^ k) for i in range(count)])  1.93 us
    pallas_call x1, Pallas kernels, shards(): pl.pallas_call(coarse_kernel, out_shape=jax.ShapeDtypeStruct((NC, MROW *...  1.85 us
  transfers between devices with their start and end apart: 5, of which 3 were waited for; matrix products, arithmetic and copies ran while one was open for 0% of the time, Pallas kernels for 39%

profile of v7, /device:TPU:0, one launch (start us, length us, event | category | flops | bytes accessed | tf_op | source)
XLA Modules:
  0.0 39.1 jit_solution(10254684275338548426)
XLA Ops:
  0.6 1.7 %place.1 = bf16[512,128]{1,0:T(8,128)(2,1)} custom-call(s32[1,64]{1,0:T(1,128)} %bitcast.9, bf16[64,128]{1,0:T(8,128)(2,1)} %trace_hbm.1), custom_call_target="tpu_custom_call" | custom-call | tf_op jit(solution)/shard_map/place/pallas_call | solution.py:418
  2.3 7.3 %all-to-all-start = ((bf16[32,16,128]{2,1,0:T(8,128)(2,1)}), bf16[32,16,128]{2,1,0:T(8,128)(2,1)S(1)}, u32[]{:S(2)}, u32[]{:S(2)}) async-start(bf16[32,16,128]{2,1,0:T(8,128)(2,1)} %bitcast.7), calls=%async_computation | async-start | bytes 262144 | tf_op jit(solution)/shard_map/all_to_all | solution.py:431
  9.7 5.2 %gram.1 = bf16[2176,128]{1,0:T(8,128)(2,1)} custom-call(s32[96]{0:T(128)} %bitcast.10, s32[96]{0:T(128)} %coarse_hbm.1, bf16[96,6144]{1,0:T(8,128)(2,1)} %tiles_hbm.1), custom_call_target="tpu_custom_call" | custom-call | flops 201326592 | bytes 12582912 | tf_op jit(solution)/shard_map/gram/pallas_call | solution.py:437
  14.9 3.0 %all-to-all-done = bf16[32,16,128]{2,1,0:T(8,128)(2,1)S(1)} async-done(((bf16[32,16,128]{2,1,0:T(8,128)(2,1)}), bf16[32,16,128]{2,1,0:T(8,128)(2,1)S(1)}, u32[]{:S(2)}, u32[]{:S(2)}) %all-to-all-start) | async-done | bytes 131104 | tf_op jit(solution)/shard_map/all_to_all | solution.py:431
  17.9 0.0 copy-start.2
  17.9 3.5 %all-to-all-start.1 = ((bf16[8,272,128]{2,1,0:T(8,128)(2,1)}), bf16[8,272,128]{2,1,0:T(8,128)(2,1)S(1)}, u32[]{:S(2)}, u32[]{:S(2)}) async-start(bf16[8,272,128]{2,1,0:T(8,128)(2,1)} %bitcast.6), calls=%async_computation.1 | async-start | bytes 1114112 | tf_op jit(solution)/shard_map/all_to_all | solution.py:459
  21.4 0.0 copy-done.2
  21.4 9.1 %condense.1 = (bf16[9,384,384]{2,1,0:T(8,128)(2,1)}, bf16[64,128]{1,0:T(8,128)(2,1)}, bf16[128,128]{1,0:T(8,128)(2,1)}) custom-call(bf16[512,128]{1,0:T(8,128)(2,1)} %bitcast.8, s32[3,9]{1,0:T(4,128)} %bitcast.11, bf16[9,512]{1,0:T(8,128)(2,1)} %rhs_hbm.1, bf16[9,512,512]{2,1,0:T(8,128)(2,1)} %inverse_hbm.1, bf16[9,512,384]{2,1,0:T(8,128)(2,1)} %coupling_hbm.1), custom_call_target="tpu_custom_call" | custom-call | flops 3170893824 | bytes 10911744 | tf_op jit(solution)/shard_map/condense/pallas_call | solution.py:464
  30.5 0.3 collective-permute-start.2
  30.8 1.6 %collective-permute-start.1 = (bf16[64,128]{1,0:T(8,128)(2,1)}, bf16[64,128]{1,0:T(8,128)(2,1)S(1)}, u32[]{:S(2)}, u32[]{:S(2)}) collective-permute-start(bf16[64,128]{1,0:T(8,128)(2,1)} %get-tuple-element.12.refs_1_), channel_id=1, source_target_pairs={{0,2},{1,3},{2,0},{3,1},{4,6},{5,7},{6,4},{7,5},{8,10},{9,11},{10,... | collective-permute-start | bytes 49160 | tf_op jit(solution)/shard_map/ppermute | solution.py:391
  32.4 0.0 collective-permute-start
  32.4 1.5 %collective-permute-done.2.refs_4_ = bf16[64,128]{1,0:T(8,128)(2,1)S(1)} collective-permute-done((bf16[64,128]{1,0:T(8,128)(2,1)}, bf16[64,128]{1,0:T(8,128)(2,1)S(1)}, u32[]{:S(2)}, u32[]{:S(2)}) %collective-permute-start.2) | collective-permute-done | bytes 16416 | tf_op jit(solution)/shard_map/ppermute | solution.py:391
  34.0 0.8 %collective-permute-done.1.refs_3_ = bf16[64,128]{1,0:T(8,128)(2,1)S(1)} collective-permute-done((bf16[64,128]{1,0:T(8,128)(2,1)}, bf16[64,128]{1,0:T(8,128)(2,1)S(1)}, u32[]{:S(2)}, u32[]{:S(2)}) %collective-permute-start.1) | collective-permute-done | bytes 16416 | tf_op jit(solution)/shard_map/ppermute | solution.py:391
  34.8 0.0 collective-permute-done.refs_2_
  34.8 0.0 copy-start
  34.8 0.8 %copy-done = bf16[128,128]{1,0:T(8,128)(2,1)S(1)} copy-done((bf16[128,128]{1,0:T(8,128)(2,1)S(1)}, bf16[128,128]{1,0:T(8,128)(2,1)}, u32[]{:S(2)}) %copy-start) | copy-done | bytes 32792
  35.5 0.0 copy-start.1
  35.5 0.7 %copy-done.1 = bf16[64,128]{1,0:T(8,128)(2,1)S(1)} copy-done((bf16[64,128]{1,0:T(8,128)(2,1)S(1)}, bf16[64,128]{1,0:T(8,128)(2,1)}, u32[]{:S(2)}) %copy-start.1) | copy-done | bytes 16408
  36.3 1.0 %residual.1 = f32[128,128]{1,0:T(8,128)} custom-call(bf16[128,128]{1,0:T(8,128)(2,1)S(1)} %copy-done, bf16[64,128]{1,0:T(8,128)(2,1)S(1)} %copy-done.1, bf16[64,128]{1,0:T(8,128)(2,1)S(1)} %collective-permute-done.refs_2_, bf16[64,128]{1,0:T(8,128)(2,1)S(1)} %collective-permute-done.1.refs_3_, bf16[64,128]{1,0:T(8,128)(2,1)S(1)} %collective-permute-done.2.refs_4_), custom_call_target="tpu_custom_call" | custom-call | tf_op jit(solution)/shard_map/residual/pallas_call | solution.py:501
  37.2 0.0 all-to-all-done.1.got_ref
  37.2 1.9 %coarse.1 = f32[16,4096]{1,0:T(8,128)} custom-call(bf16[8,272,128]{2,1,0:T(8,128)(2,1)S(1)} %all-to-all-done.1.got_ref), custom_call_target="tpu_custom_call" | custom-call | tf_op jit(solution)/shard_map/coarse/pallas_call | solution.py:516
Async XLA Ops:
  2.3 15.5 %all-to-all-start = ((bf16[32,16,128]{2,1,0:T(8,128)(2,1)}), bf16[32,16,128]{2,1,0:T(8,128)(2,1)S(1)}, u32[]{:S(2)}, u32[]{:S(2)}) async-start(bf16[32,16,128]{2,1,0:T(8,128)(2,1)} %bitcast.7), calls=%async_computation | async-start | bytes 262144 | tf_op jit(solution)/shard_map/all_to_all | solution.py:431
  17.9 3.5 %copy-start.2 = (bf16[32,16,128]{2,1,0:T(8,128)(2,1)}, bf16[32,16,128]{2,1,0:T(8,128)(2,1)S(1)}, u32[]{:S(2)}) copy-start(bf16[32,16,128]{2,1,0:T(8,128)(2,1)S(1)} %all-to-all-done) | copy-start | bytes 393220
  17.9 19.3 %all-to-all-start.1 = ((bf16[8,272,128]{2,1,0:T(8,128)(2,1)}), bf16[8,272,128]{2,1,0:T(8,128)(2,1)S(1)}, u32[]{:S(2)}, u32[]{:S(2)}) async-start(bf16[8,272,128]{2,1,0:T(8,128)(2,1)} %bitcast.6), calls=%async_computation.1 | async-start | bytes 1114112 | tf_op jit(solution)/shard_map/all_to_all | solution.py:459
  30.5 3.4 %collective-permute-start.2 = (bf16[64,128]{1,0:T(8,128)(2,1)}, bf16[64,128]{1,0:T(8,128)(2,1)S(1)}, u32[]{:S(2)}, u32[]{:S(2)}) collective-permute-start(bf16[64,128]{1,0:T(8,128)(2,1)} %get-tuple-element.12.refs_1_), channel_id=1, source_target_pairs={{0,3},{1,2},{2,1},{3,0},{4,7},{5,6},{6,5},{7,4},{8,11},{9,10},{10,... | collective-permute-start | bytes 49160 | tf_op jit(solution)/shard_map/ppermute | solution.py:391
  30.8 3.9 %collective-permute-start.1 = (bf16[64,128]{1,0:T(8,128)(2,1)}, bf16[64,128]{1,0:T(8,128)(2,1)S(1)}, u32[]{:S(2)}, u32[]{:S(2)}) collective-permute-start(bf16[64,128]{1,0:T(8,128)(2,1)} %get-tuple-element.12.refs_1_), channel_id=1, source_target_pairs={{0,2},{1,3},{2,0},{3,1},{4,6},{5,7},{6,4},{7,5},{8,10},{9,11},{10,... | collective-permute-start | bytes 49160 | tf_op jit(solution)/shard_map/ppermute | solution.py:391
  32.4 2.3 %collective-permute-start = (bf16[64,128]{1,0:T(8,128)(2,1)}, bf16[64,128]{1,0:T(8,128)(2,1)S(1)}, u32[]{:S(2)}, u32[]{:S(2)}) collective-permute-start(bf16[64,128]{1,0:T(8,128)(2,1)} %get-tuple-element.12.refs_1_), channel_id=1, source_target_pairs={{0,1},{1,0},{2,3},{3,2},{4,5},{5,4},{6,7},{7,6},{8,9},{9,8},{10,11... | collective-permute-start | bytes 49160 | tf_op jit(solution)/shard_map/ppermute | solution.py:391
  34.8 0.8 %copy-start = (bf16[128,128]{1,0:T(8,128)(2,1)S(1)}, bf16[128,128]{1,0:T(8,128)(2,1)}, u32[]{:S(2)}) copy-start(bf16[128,128]{1,0:T(8,128)(2,1)} %get-tuple-element.11.refs_0_) | copy-start | bytes 98308
  35.5 0.7 %copy-start.1 = (bf16[64,128]{1,0:T(8,128)(2,1)S(1)}, bf16[64,128]{1,0:T(8,128)(2,1)}, u32[]{:S(2)}) copy-start(bf16[64,128]{1,0:T(8,128)(2,1)} %get-tuple-element.12.refs_1_) | copy-start | bytes 49156

commit v8 on v7

--- a/solution.py
+++ b/solution.py
@@ -21,6 +21,7 @@
 SHARE_ROWS = NAMED + 16
 SLOT_BASE = 16
 CHUNK = 16
+MOST_PAIRED = 8
 BIG = 62 << 20
 SMALL = 12 << 20
 PITCH = MROW + 8
@@ -74,35 +75,24 @@
     rhs_turned_ref[...] = wide_ref[...].T.astype(BF16)
 
 
-def gram_kernel(
-    face_count,
-    owner_hbm,
-    coarse_hbm,
-    tiles_hbm,
-    out_ref,
-    owner_ref,
-    coarse_ref,
-    tiles_ref,
-    rows_ref,
-    acc_a_ref,
-    acc_b_ref,
-    diag_a_ref,
-    diag_b_ref,
-    sems,
-):
-    accs, diags = (acc_a_ref, acc_b_ref), (diag_a_ref, diag_b_ref)
+def gram_kernel(face_count, paired, owner_hbm, coarse_hbm, tiles_hbm, *refs):
+    out_refs, refs = refs[:-9], refs[-9:]
+    owner_ref, coarse_ref, tiles_ref, rows_ref = refs[:4]
+    accs, diags, sems = refs[4:6], refs[6:8], refs[8]
+
+    def place_of(owner):
+        if not paired:
+            return owner
+        other = owner ^ lax.axis_index("face")
+        return (other & 1) * (face_count // 2) + (other >> 1)
+
     tiles = tiles_ref.shape[0]
     copies = [
         pltpu.make_async_copy(owner_hbm, owner_ref, sems.at[0]),
         pltpu.make_async_copy(coarse_hbm, coarse_ref, sems.at[1]),
     ]
-    chunks = []
-    for chunk in range(tiles // CHUNK):
-        here = pl.ds(chunk * CHUNK, CHUNK)
-        chunks.append(
-            pltpu.make_async_copy(tiles_hbm.at[here], tiles_ref.at[here], sems.at[2 + chunk])
-        )
-    for copy in copies + chunks:
+    copies.append(pltpu.make_async_copy(tiles_hbm, tiles_ref, sems.at[2]))
+    for copy in copies:
         copy.start()
     for ref in (*accs, *diags):
         ref[...] = jnp.zeros_like(ref)
@@ -120,7 +110,6 @@
     low_row = iota((1, LANES), 1) < MROW
 
     for chunk in range(tiles // CHUNK):
-        chunks[chunk].wait()
         first_tile = chunk * CHUNK
         for group in range(MROW // 4):
             base = group * 3 * LANES
@@ -160,13 +149,14 @@
             )
             own = (jnp.where(low_row, diag, 0.0), jnp.where(low_row, 0.0, diag))
             for k in range(2):
-                block = owner_ref[tile + k] * NC + coarse_ref[tile + k]
+                block = place_of(owner_ref[tile + k]) * NC + coarse_ref[tile + k]
                 here = pl.ds(pl.multiple_of(block * DENSE, DENSE), DENSE)
                 accs[k][here, :] += dense[k]
                 diags[k][pl.ds(block, 1), :] += own[k]
     size = NC * DENSE
+    each = face_count // len(out_refs)
     for owner in range(face_count):
-        start = owner * OWNER_ROWS
+        out_ref, start = out_refs[owner // each], owner % each * OWNER_ROWS
         here = slice(owner * size, (owner + 1) * size)
         out_ref[start : start + size, :] = (accs[0][here, :] + accs[1][here, :]).astype(BF16)
         here = slice(owner * NC, (owner + 1) * NC)
@@ -175,46 +165,37 @@
         ).astype(BF16)
 
 
+def join_kernel(kept_ref, came_ref, *out_refs):
+    for k, out_ref in enumerate(out_refs):
+        here = slice(k * OWNER_ROWS, (k + 1) * OWNER_ROWS)
+        total = kept_ref[here, :].astype(F32) + came_ref[here, :].astype(F32)
+        out_ref[...] = total.astype(BF16)
+
+
 def main_kernel(
-    elem_count,
-    face_count,
-    table_hbm,
-    conn_hbm,
     rhs_hbm,
     inverse_hbm,
     coupling_hbm,
     schur_hbm,
-    share_ref,
-    own_ref,
-    conn_ref,
+    solved_ref,
     rhs_ref,
-    table_ref,
     inverse_ref,
     coupling_ref,
     schur_ref,
     wide_ref,
     rhs_turned_ref,
-    vector_ref,
-    sum_ref,
     turned_a_ref,
     turned_b_ref,
     product_a_ref,
     product_b_ref,
-    small_sems,
+    small_sem,
     block_sems,
     schur_sems,
 ):
     elements = rhs_ref.shape[0]
     trace = FACES_PER_ELEM * FACE_COEFFS
-    slots = table_ref.shape[0]
-    own = own_ref.shape[0]
-    capacity = own // face_count
-    my_elem = lax.axis_index("elem")
-    small = [
-        pltpu.make_async_copy(rhs_hbm, rhs_ref, small_sems.at[0]),
-        pltpu.make_async_copy(conn_hbm, conn_ref, small_sems.at[1]),
-        pltpu.make_async_copy(table_hbm, table_ref, small_sems.at[2]),
-    ]
+    wide_lane = iota((trace, LANES), 1)
+    small = pltpu.make_async_copy(rhs_hbm, rhs_ref, small_sem)
 
     def coupling_copy(e):
         return pltpu.make_async_copy(coupling_hbm.at[e], coupling_ref.at[e], block_sems.at[0, e])
@@ -226,8 +207,7 @@
         return pltpu.make_async_copy(schur_ref.at[e], schur_hbm.at[e], schur_sems.at[e])
 
     coupling_copy(0).start()
-    for copy in small:
-        copy.start()
+    small.start()
     inverse_copy(0).start()
     coupling_copy(1).start()
     inverse_copy(1).start()
@@ -243,16 +223,14 @@
         wide = jnp.concatenate([coupling_ref[e], rhs_turned_ref[...]], axis=1)
         condensed = dot(product_ref[...], wide)
         schur_ref[e] = (-condensed[:, :trace]).astype(BF16)
-        total = condensed * vector_ref[pl.ds(e, 1), :]
-        total = sum(total[:, k * LANES : (k + 1) * LANES] for k in range(FACES_PER_ELEM + 1))
-        sums = jnp.sum(total, axis=1, keepdims=True)
-        sum_ref[...] = jnp.where(iota((trace, LANES), 1) == e, sums, sum_ref[...])
+        solved_ref[...] = jnp.where(wide_lane == e, condensed[:, trace:], solved_ref[...])
 
     turned = (turned_a_ref, turned_b_ref)
     product = (product_a_ref, product_b_ref)
 
     def advance(e, parity, turning=True, finishing=True):
         if turning:
+
             @pl.when(e + 2 < elements)
             def _():
                 inverse_copy(e + 2).start()
@@ -270,20 +248,74 @@
             second(e - 1, product[1 - parity])
             leave(e - 1).start()
 
+    solved_ref[...] = jnp.zeros_like(solved_ref)
     coupling_copy(0).wait()
+    small.wait()
     turn(0, turned[0])
-    for copy in small:
+    turn_rhs(rhs_ref, wide_ref, rhs_turned_ref)
+    advance(0, 0, finishing=False)
+
+    def two(index, carry):
+        advance(2 * index + 1, 1)
+        advance(2 * index + 2, 0)
+        return carry
+
+    pairs = (elements - 2) // 2
+    lax.fori_loop(0, pairs, two, 0)
+    for e in range(2 * pairs + 1, elements):
+        advance(e, e % 2, turning=e + 1 < elements)
+    second(elements - 1, product[(elements - 1) % 2])
+    leave(elements - 1).start()
+    for e in range(elements):
+        leave(e).wait()
+
+
+def share_kernel(
+    elem_count,
+    face_count,
+    table_hbm,
+    conn_hbm,
+    schur_hbm,
+    solved_hbm,
+    share_ref,
+    own_ref,
+    table_ref,
+    conn_ref,
+    schur_ref,
+    vector_ref,
+    sum_ref,
+    sems,
+    schur_sems,
+):
+    elements = schur_ref.shape[0]
+    trace = FACES_PER_ELEM * FACE_COEFFS
+    slots = table_ref.shape[0]
+    own = own_ref.shape[0]
+    capacity = own // face_count
+    my_elem = lax.axis_index("elem")
+    copies = [
+        pltpu.make_async_copy(conn_hbm, conn_ref, sems.at[0]),
+        pltpu.make_async_copy(table_hbm, table_ref, sems.at[1]),
+        pltpu.make_async_copy(solved_hbm, sum_ref, sems.at[2]),
+    ]
+    parts = [
+        pltpu.make_async_copy(schur_hbm.at[e], schur_ref.at[e], schur_sems.at[e])
+        for e in range(elements)
+    ]
+    for copy in copies + parts:
+        copy.start()
+    for copy in copies:
         copy.wait()
-    sum_ref[...] = jnp.zeros_like(sum_ref)
-    turn_rhs(rhs_ref, wide_ref, rhs_turned_ref)
+
     row = iota((PER_FACE, LANES), 0)
     lane = iota((PER_FACE, LANES), 1)
+    first_lane = iota((1, LANES), 1)
+    wide_lane = iota((trace, LANES), 1)
 
     def position(elem, inner):
         face, rank = divided(inner, capacity)
         return (face * elem_count + elem) * capacity + rank
 
-    first_lane = iota((1, LANES), 1)
     high = jnp.full((1, LANES), -1, I32)
     rest = jnp.zeros((1, LANES), I32)
     for a in range(FACES_PER_ELEM):
@@ -296,60 +328,53 @@
             high = jnp.where(here, quotient, high)
             rest = jnp.where(here, remainder, rest)
         hot = jnp.concatenate([positions == lane + k for k in range(0, slots, LANES)], axis=1)
-        lam = dot(hot.astype(BF16), table_ref[...])
-        vector_ref[:, a * LANES : (a + 1) * LANES] = -lam
-    vector_ref[:, trace:] = (row == lane).astype(F32)
+        vector_ref[:, a * LANES : (a + 1) * LANES] = dot(hot.astype(BF16), table_ref[...])
     names = jnp.where(row == 0, high, jnp.where(row == 1, rest, 0))
     share_ref[NAMED:, :] = names.astype(F32).astype(BF16)
     place = position(my_elem, iota((own, slots), 0))
     pick = (iota((own, slots), 1) == place).astype(BF16)
     own_ref[...] = dot(pick, table_ref[...]).astype(BF16)
 
-    advance(0, 0, finishing=False)
-
-    def two(index, carry):
-        advance(2 * index + 1, 1)
-        advance(2 * index + 2, 0)
-        return carry
-
-    pairs = (elements - 2) // 2
-    lax.fori_loop(0, pairs, two, 0)
-    for e in range(2 * pairs + 1, elements):
-        advance(e, e % 2, turning=e + 1 < elements)
-    second(elements - 1, product[(elements - 1) % 2])
-    leave(elements - 1).start()
-
+    for copy in parts:
+        copy.wait()
+    columns = sum_ref[...]
+    for e in range(elements):
+        total = sum(
+            schur_ref[e, :, a * LANES : (a + 1) * LANES].astype(F32)
+            * vector_ref[e : e + 1, a * LANES : (a + 1) * LANES]
+            for a in range(FACES_PER_ELEM)
+        )
+        sums = jnp.sum(total, axis=1, keepdims=True)
+        columns = columns + jnp.where(wide_lane == e, sums, 0.0)
     for a in range(FACES_PER_ELEM):
-        shares = sum_ref[a * LANES : (a + 1) * LANES, :].T
+        shares = columns[a * LANES : (a + 1) * LANES, :].T
         share_ref[a * PER_FACE : (a + 1) * PER_FACE, :] = shares[:PER_FACE].astype(BF16)
-    for e in range(elements):
-        leave(e).wait()
-
-
-def residual_kernel(elem_count, *refs):
-    ins, (residual_ref, own_ref, shares_ref, sems) = refs[:-4], refs[-4:]
-    places = [own_ref] + [shares_ref.at[k] for k in range(elem_count)]
-    copies = [pltpu.make_async_copy(ins[k], places[k], sems.at[k]) for k in range(len(ins))]
-    for copy in copies:
-        copy.start()
-    own = residual_ref.shape[0]
-    mine = lax.axis_index("elem")
-    slot = (iota((own, SHARE_ROWS), 0) + mine * own).astype(F32)
-    for copy in copies:
-        copy.wait()
-    left = own_ref[...].astype(F32)
-    for k in range(elem_count):
-        names = shares_ref[k, NAMED:, :].astype(F32)
-        named = (names[0:1] * SLOT_BASE + names[1:2])[:, :SHARE_ROWS]
-        left = left - dot((slot == named).astype(BF16), shares_ref[k])
+
+
+def less_shares(left, share_ref):
+    own = left.shape[0]
+    slot = (iota((own, SHARE_ROWS), 0) + lax.axis_index("elem") * own).astype(F32)
+    names = share_ref[NAMED:, :].astype(F32)
+    named = (names[0:1] * SLOT_BASE + names[1:2])[:, :SHARE_ROWS]
+    return left - dot((slot == named).astype(BF16), share_ref[...])
+
+
+def residual_kernel(left_ref, *refs):
+    share_refs, residual_ref = refs[:-1], refs[-1]
+    left = left_ref[...]
+    for share_ref in share_refs:
+        left = less_shares(left, share_ref)
     residual_ref[...] = left
 
 
-def coarse_kernel(got_ref, out_ref, sum_ref, full_ref):
-    total = got_ref[0].astype(F32)
-    for k in range(1, got_ref.shape[0]):
-        total = total + got_ref[k].astype(F32)
-    sum_ref[...] = total
+def coarse_kernel(own_ref, share_ref, *refs):
+    got_refs, (left_ref, out_ref, sum_ref, full_ref) = refs[:-4], refs[-4:]
+    left_ref[...] = less_shares(own_ref[...].astype(F32), share_ref)
+    sum_ref[...] = sum(
+        got_ref[k : k + OWNER_ROWS, :].astype(F32)
+        for got_ref in got_refs
+        for k in range(0, got_ref.shape[0], OWNER_ROWS)
+    )
 
     lane = iota((HALF, LANES), 1)
     row = iota((HALF, LANES), 0)
@@ -381,6 +406,10 @@
 VMEM = pl.BlockSpec(memory_space=pltpu.VMEM)
 
 
+def cost(flops, bytes_accessed):
+    return pl.CostEstimate(flops=flops, bytes_accessed=bytes_accessed, transcendentals=0)
+
+
 def params(limit):
     return pltpu.CompilerParams(vmem_limit_bytes=limit)
 
@@ -414,7 +443,35 @@
 
     slots = own * elem_count
     devices = face_count * elem_count
-
+    paired = face_count <= MOST_PAIRED
+    sides = 2 if paired else 1
+
+    blocks = face_count * NC
+    sums_shape = (blocks * DENSE, LANES)
+    half_grams = pl.pallas_call(
+        functools.partial(gram_kernel, face_count, paired),
+        out_shape=[jax.ShapeDtypeStruct((blocks * (DENSE + 1) // sides, LANES), BF16)] * sides,
+        in_specs=[ANY] * 3,
+        out_specs=[VMEM] * sides,
+        scratch_shapes=[
+            pltpu.SMEM((tile_count,), I32),
+            pltpu.SMEM((tile_count,), I32),
+            pltpu.VMEM(mortar_tiles.shape, BF16),
+            pltpu.VMEM((tile_count * PITCH, LANES), F32),
+            pltpu.VMEM(sums_shape, F32),
+            pltpu.VMEM(sums_shape, F32),
+            pltpu.VMEM((blocks, LANES), F32),
+            pltpu.VMEM((blocks, LANES), F32),
+            pltpu.SemaphoreType.DMA((3,)),
+        ],
+        compiler_params=params(BIG),
+        cost_estimate=cost(4 * tile_count * MROW * MROW * LANES, 12 << 20),
+        name="gram",
+    )(mortar_owner.reshape(tile_count), mortar_coarse, mortar_tiles)
+    if paired:
+        came = lax.ppermute(half_grams[1], "face", [(i, i ^ 1) for i in range(face_count)])
+
+    owners, _ = lax.optimization_barrier((new_owner.reshape(1, row_count), half_grams[0]))
     placed = pl.pallas_call(
         functools.partial(place_kernel, elem_count, face_count, capacity),
         out_shape=jax.ShapeDtypeStruct((slots, FACE_COEFFS), BF16),
@@ -427,104 +484,111 @@
         ],
         compiler_params=params(BIG),
         name="place",
-    )(new_owner.reshape(1, row_count), trace_old)
+    )(owners, trace_old)
     table = lax.all_to_all(
         placed.reshape(devices, capacity, FACE_COEFFS), ("face", "elem"), 0, 0, tiled=True
     ).reshape(slots, FACE_COEFFS)
 
-    blocks = face_count * NC
-    sums_shape = (blocks * DENSE, LANES)
-    half_grams = pl.pallas_call(
-        functools.partial(gram_kernel, face_count),
-        out_shape=jax.ShapeDtypeStruct((blocks * (DENSE + 1), LANES), BF16),
-        in_specs=[ANY] * 3,
-        out_specs=VMEM,
-        scratch_shapes=[
-            pltpu.SMEM((tile_count,), I32),
-            pltpu.SMEM((tile_count,), I32),
-            pltpu.VMEM(mortar_tiles.shape, BF16),
-            pltpu.VMEM((tile_count * PITCH, LANES), F32),
-            pltpu.VMEM(sums_shape, F32),
-            pltpu.VMEM(sums_shape, F32),
-            pltpu.VMEM((blocks, LANES), F32),
-            pltpu.VMEM((blocks, LANES), F32),
-            pltpu.SemaphoreType.DMA((2 + tile_count // CHUNK,)),
-        ],
-        compiler_params=params(BIG),
-        cost_estimate=pl.CostEstimate(
-            flops=4 * tile_count * MROW * MROW * LANES, bytes_accessed=12 << 20, transcendentals=0
-        ),
-        name="gram",
-    )(mortar_owner.reshape(tile_count), mortar_coarse, mortar_tiles)
-    got = lax.all_to_all(
-        half_grams.reshape(face_count, OWNER_ROWS, LANES), "face", 0, 0, tiled=True
-    )
-
-    slots_named, _ = lax.optimization_barrier((connectivity.T, half_grams))
-    schur_blocks, shares, own_rows = pl.pallas_call(
-        functools.partial(main_kernel, elem_count, face_count),
+    if paired:
+        kept, _ = lax.optimization_barrier((half_grams[0], placed))
+        joined = pl.pallas_call(
+            join_kernel,
+            out_shape=[jax.ShapeDtypeStruct((OWNER_ROWS, LANES), BF16)] * (face_count // 2),
+            in_specs=[VMEM] * 2,
+            out_specs=[VMEM] * (face_count // 2),
+            compiler_params=params(SMALL),
+            cost_estimate=cost(0, 4 << 20),
+            name="join",
+        )(kept, came)
+        got = [joined[0]] + [
+            lax.ppermute(joined[k], "face", [(i, i ^ (2 * k)) for i in range(face_count)])
+            for k in range(1, face_count // 2)
+        ]
+        before = joined[0]
+    else:
+        blocked = half_grams[0].reshape(face_count, OWNER_ROWS, LANES)
+        got = [lax.all_to_all(blocked, "face", 0, 0, tiled=True).reshape(-1, LANES)]
+        before = half_grams[0]
+
+    rhs, _ = lax.optimization_barrier((interior_rhs, before))
+    schur_blocks, solved = pl.pallas_call(
+        main_kernel,
         out_shape=(
             jax.ShapeDtypeStruct((elements, trace, trace), BF16),
-            jax.ShapeDtypeStruct((SHARE_ROWS, LANES), BF16),
-            jax.ShapeDtypeStruct((own, FACE_COEFFS), BF16),
+            jax.ShapeDtypeStruct((trace, LANES), F32),
         ),
-        in_specs=[ANY] * 5,
-        out_specs=(ANY, VMEM, VMEM),
+        in_specs=[ANY] * 3,
+        out_specs=(ANY, VMEM),
         scratch_shapes=[
-            pltpu.SMEM((FACES_PER_ELEM, elements), I32),
             pltpu.VMEM((elements, modes), BF16),
-            pltpu.VMEM((slots, FACE_COEFFS), BF16),
             pltpu.VMEM((elements, modes, modes), BF16),
             pltpu.VMEM((elements, modes, trace), BF16),
             pltpu.VMEM((elements, trace, trace), BF16),
             pltpu.VMEM((LANES, modes), F32),
             pltpu.VMEM((modes, LANES), BF16),
-            pltpu.VMEM((PER_FACE, trace + LANES), F32),
-            pltpu.VMEM((trace, LANES), F32),
             pltpu.VMEM((trace, modes), BF16),
             pltpu.VMEM((trace, modes), BF16),
             pltpu.VMEM((trace, modes), BF16),
             pltpu.VMEM((trace, modes), BF16),
-            pltpu.SemaphoreType.DMA((3,)),
+            pltpu.SemaphoreType.DMA,
             pltpu.SemaphoreType.DMA((2, elements)),
             pltpu.SemaphoreType.DMA((elements,)),
         ],
         compiler_params=params(BIG),
-        cost_estimate=pl.CostEstimate(
-            flops=2 * elements * modes * trace * (modes + trace),
-            bytes_accessed=2 * elements * (modes * (modes + trace) + trace * trace),
-            transcendentals=0,
+        cost_estimate=cost(
+            2 * elements * modes * trace * (modes + trace),
+            2 * elements * (modes * (modes + trace) + trace * trace),
         ),
         name="condense",
-    )(table, slots_named, interior_rhs, local_inverse, coupling)
-
-    slot_residual = pl.pallas_call(
-        functools.partial(residual_kernel, elem_count),
-        out_shape=jax.ShapeDtypeStruct((own, FACE_COEFFS), F32),
-        in_specs=[ANY] * (1 + elem_count),
-        out_specs=VMEM,
+    )(rhs, local_inverse, coupling)
+
+    shares, own_rows = pl.pallas_call(
+        functools.partial(share_kernel, elem_count, face_count),
+        out_shape=(
+            jax.ShapeDtypeStruct((SHARE_ROWS, LANES), BF16),
+            jax.ShapeDtypeStruct((own, FACE_COEFFS), BF16),
+        ),
+        in_specs=[ANY] * 4,
+        out_specs=(VMEM, VMEM),
         scratch_shapes=[
-            pltpu.VMEM((own, FACE_COEFFS), BF16),
-            pltpu.VMEM((elem_count, SHARE_ROWS, LANES), BF16),
-            pltpu.SemaphoreType.DMA((1 + elem_count,)),
+            pltpu.VMEM((slots, FACE_COEFFS), BF16),
+            pltpu.SMEM((FACES_PER_ELEM, elements), I32),
+            pltpu.VMEM((elements, trace, trace), BF16),
+            pltpu.VMEM((PER_FACE, trace), F32),
+            pltpu.VMEM((trace, LANES), F32),
+            pltpu.SemaphoreType.DMA((3,)),
+            pltpu.SemaphoreType.DMA((elements,)),
         ],
-        compiler_params=params(SMALL),
-        name="residual",
-    )(own_rows, *around(shares, "elem"))
-
-    got, slot_residual = lax.optimization_barrier((got, slot_residual))
-    coarse_blocks = pl.pallas_call(
+        compiler_params=params(BIG),
+        cost_estimate=cost(0, 8 << 20),
+        name="share",
+    )(table, connectivity.T, schur_blocks, solved)
+
+    all_shares = around(shares, "elem")
+    left, coarse_blocks = pl.pallas_call(
         coarse_kernel,
-        out_shape=jax.ShapeDtypeStruct((NC, MROW * MROW), F32),
-        in_specs=[VMEM],
-        out_specs=VMEM,
+        out_shape=(
+            jax.ShapeDtypeStruct((own, FACE_COEFFS), F32),
+            jax.ShapeDtypeStruct((NC, MROW * MROW), F32),
+        ),
+        in_specs=[VMEM] * (2 + len(got)),
+        out_specs=(VMEM, VMEM),
         scratch_shapes=[
             pltpu.VMEM((OWNER_ROWS, LANES), F32),
             pltpu.VMEM((NC * MROW, LANES), F32),
         ],
         compiler_params=params(SMALL),
+        cost_estimate=cost(0, 8 << 20),
         name="coarse",
-    )(got)
+    )(own_rows, shares, *got)
+    slot_residual = pl.pallas_call(
+        residual_kernel,
+        out_shape=jax.ShapeDtypeStruct((own, FACE_COEFFS), F32),
+        in_specs=[VMEM] * elem_count,
+        out_specs=VMEM,
+        compiler_params=params(SMALL),
+        name="residual",
+    )(left, *all_shares[1:])
     return schur_blocks, slot_residual, coarse_blocks
 
 

time: 39.6 us -> 39.1 us (0.987)
  waiting for transfers between devices: 5.36 us -> 0.27 us
  local copies, waits for them, and re-layouts: 1.48 us -> 3.08 us
  starting transfers between devices: 12.8 us -> 14.3 us
  Pallas kernels: 18.8 us -> 20.2 us
    ppermute x0 -> x4, starting transfers between devices: none -> 7.49 us  [the longest x3 4.46 us: shards(): lax.ppermute(joined[k], 'face', [(i, i ^ 2 * k) for i in range(face_count)])]
    all_to_all x1 -> x0, starting transfers between devices: 3.54 us -> none  [shards(): lax.all_to_all(half_grams.reshape(face_count, OWNER_ROWS, LANES), 'face',...]
    all_to_all x1, waiting for transfers between devices: 3.03 us -> 0.01 us  [shards(): lax.all_to_all(placed.reshape(devices, capacity, FACE_COEFFS), ('face', '...]
    all_to_all x1, starting transfers between devices: 7.3 us -> 4.89 us  [shards(): lax.all_to_all(placed.reshape(devices, capacity, FACE_COEFFS), ('face', '...]
    ppermute x3, waiting for transfers between devices: 2.33 us -> 0.01 us  [around(): lax.ppermute(block, axis, [(i, i ^ k) for i in range(count)])]
    unnamed x6 -> x8, local copies, waits for them, and re-layouts: 1.48 us -> 3.08 us
    pallas_call x4 -> x6, Pallas kernels: 17.1 us -> 18.5 us  [the longest x1 8.59 us: shards(): pl.pallas_call(main_kernel, out_shape=(jax.ShapeDtypeStruct((elements, tr...]
  transfers between devices with their start and end apart: 5 -> 8, of which waited for: 3 -> 1; matrix products, arithmetic and copies ran while one was open for 0% -> 0% of each run, Pallas kernels for 39% -> 40%
where the time goes in v8:
time: 39.1 us; the launch traced here: 38.6 us
  Pallas kernels  20.2 us (52%)
  starting transfers between devices  14.3 us (37%)
  local copies, waits for them, and re-layouts  3.08 us (8%)
  between operations  0.71 us (2%)
    pallas_call x1, Pallas kernels, shards(): pl.pallas_call(main_kernel, out_shape=(jax.ShapeDtypeStruct((elements, tr...  8.59 us
    all_to_all x1, starting transfers between devices, shards(): lax.all_to_all(placed.reshape(devices, capacity, FACE_COEFFS), ('face', '...  4.89 us
    ppermute x3, starting transfers between devices, shards(): lax.ppermute(joined[k], 'face', [(i, i ^ 2 * k) for i in range(face_count)])  4.46 us
    pallas_call x1, Pallas kernels, shards(): pl.pallas_call(functools.partial(gram_kernel, face_count, paired), out_sh...  3.79 us
    pallas_call x1, Pallas kernels, shards(): pl.pallas_call(functools.partial(share_kernel, elem_count, face_count), o...  3.38 us
    unnamed x8, local copies, waits for them, and re-layouts  3.08 us
    ppermute x1, starting transfers between devices, shards(): lax.ppermute(half_grams[1], 'face', [(i, i ^ 1) for i in range(face_count)])  3.03 us
    ppermute x3, starting transfers between devices, around(): lax.ppermute(block, axis, [(i, i ^ k) for i in range(count)])  1.94 us
  transfers between devices with their start and end apart: 8, of which 1 were waited for; matrix products, arithmetic and copies ran while one was open for 0% of the time, Pallas kernels for 40%

profile of v8, /device:TPU:0, one launch (start us, length us, event | category | flops | bytes accessed | tf_op | source)
XLA Modules:
  0.0 38.6 jit_solution(5215050847810798292)
XLA Ops:
  0.6 3.8 %gram.1 = (bf16[1088,128]{1,0:T(8,128)(2,1)}, bf16[1088,128]{1,0:T(8,128)(2,1)}) custom-call(s32[96]{0:T(128)} %bitcast.8, s32[96]{0:T(128)} %coarse_hbm.1, bf16[96,6144]{1,0:T(8,128)(2,1)} %tiles_hbm.1), custom_call_target="tpu_custom_call" | custom-call | flops 201326592 | bytes 12582912 | tf_op jit(solution)/shard_map/gram/pallas_call | solution.py:451
  4.4 3.0 %collective-permute-start = (bf16[1088,128]{1,0:T(8,128)(2,1)}, bf16[1088,128]{1,0:T(8,128)(2,1)S(1)}, u32[]{:S(2)}, u32[]{:S(2)}) collective-permute-start(bf16[1088,128]{1,0:T(8,128)(2,1)} %get-tuple-element.21), channel_id=1, source_target_pairs={{0,4},{4,0},{8,12},{12,8},{16,20},{20,16},{24,28},{28,24},{1,5},{5... | collective-permute-start | bytes 835592 | tf_op jit(solution)/shard_map/ppermute | solution.py:472
  7.5 1.7 %place.1 = bf16[512,128]{1,0:T(8,128)(2,1)} custom-call(s32[1,64]{1,0:T(1,128)} %bitcast.9, bf16[64,128]{1,0:T(8,128)(2,1)} %trace_hbm.1), custom_call_target="tpu_custom_call" | custom-call | tf_op jit(solution)/shard_map/place/pallas_call | solution.py:475
  9.2 4.9 %all-to-all-start = ((bf16[32,16,128]{2,1,0:T(8,128)(2,1)}), bf16[32,16,128]{2,1,0:T(8,128)(2,1)S(1)}, u32[]{:S(2)}, u32[]{:S(2)}) async-start(bf16[32,16,128]{2,1,0:T(8,128)(2,1)} %bitcast.6), calls=%async_computation | async-start | bytes 262144 | tf_op jit(solution)/shard_map/all_to_all | solution.py:488
  14.1 0.3 collective-permute-done.came_ref
  14.3 1.0 %copy-done = bf16[1088,128]{1,0:T(8,128)(2,1)S(1)} copy-done((bf16[1088,128]{1,0:T(8,128)(2,1)S(1)}, bf16[1088,128]{1,0:T(8,128)(2,1)}, u32[]{:S(2)}) %copy-start) | copy-done | bytes 278552
  15.3 0.1 join.1
  15.3 1.9 %collective-permute-start.1 = (bf16[272,128]{1,0:T(8,128)(2,1)S(1)}, bf16[272,128]{1,0:T(8,128)(2,1)S(1)}, u32[]{:S(2)}, u32[]{:S(2)}) collective-permute-start(bf16[272,128]{1,0:T(8,128)(2,1)S(1)} %get-tuple-element.28), channel_id=1, source_target_pairs={{0,8},{4,12},{8,0},{12,4},{16,24},{20,28},{24,16},{28,20},{1,9},{5... | collective-permute-start | bytes 208904 | tf_op jit(solution)/shard_map/ppermute | solution.py:504
  17.2 2.6 %collective-permute-start.2 = (bf16[272,128]{1,0:T(8,128)(2,1)S(1)}, bf16[272,128]{1,0:T(8,128)(2,1)S(1)}, u32[]{:S(2)}, u32[]{:S(2)}) collective-permute-start(bf16[272,128]{1,0:T(8,128)(2,1)S(1)} %get-tuple-element.29), channel_id=1, source_target_pairs={{0,16},{4,20},{8,24},{12,28},{16,0},{20,4},{24,8},{28,12},{1,17},{... | collective-permute-start | bytes 208904 | tf_op jit(solution)/shard_map/ppermute | solution.py:504
  19.8 0.0 collective-permute-start.3
  19.8 8.6 %condense.1 = (bf16[9,384,384]{2,1,0:T(8,128)(2,1)}, f32[384,128]{1,0:T(8,128)}) custom-call(bf16[9,512]{1,0:T(8,128)(2,1)} %rhs_hbm, bf16[9,512,512]{2,1,0:T(8,128)(2,1)} %inverse_hbm.1, bf16[9,512,384]{2,1,0:T(8,128)(2,1)} %coupling_hbm.1), custom_call_target="tpu_custom_call" | custom-call | flops 3170893824 | bytes 10911744 | tf_op jit(solution)/shard_map/condense/pallas_call | solution.py:514
  28.4 0.0 all-to-all-done
  28.4 0.6 %copy-done.3 = bf16[32,16,128]{2,1,0:T(8,128)(2,1)} copy-done((bf16[32,16,128]{2,1,0:T(8,128)(2,1)}, bf16[32,16,128]{2,1,0:T(8,128)(2,1)S(1)}, u32[]{:S(2)}) %copy-start.3) | copy-done | bytes 131096
  29.1 3.4 %share.1 = (bf16[64,128]{1,0:T(8,128)(2,1)}, bf16[128,128]{1,0:T(8,128)(2,1)}) custom-call(bf16[512,128]{1,0:T(8,128)(2,1)} %bitcast.5, s32[3,9]{1,0:T(4,128)} %bitcast.7, bf16[9,384,384]{2,1,0:T(8,128)(2,1)} %get-tuple-element.15.schur_hbm, f32[384,128]{1,0:T(8,128)} %get-tuple-element.25.solved_hbm), custom_call_target="tpu_custom_call" | custom-call | bytes 8388608 | tf_op jit(solution)/shard_map/share/pallas_call | solution.py:545
  32.5 0.5 %collective-permute-start.6 = (bf16[64,128]{1,0:T(8,128)(2,1)}, bf16[64,128]{1,0:T(8,128)(2,1)S(1)}, u32[]{:S(2)}, u32[]{:S(2)}) collective-permute-start(bf16[64,128]{1,0:T(8,128)(2,1)} %get-tuple-element.27.share_ref), channel_id=1, source_target_pairs={{0,3},{1,2},{2,1},{3,0},{4,7},{5,6},{6,5},{7,4},{8,11},{9,10},{10,... | collective-permute-start | bytes 49160 | tf_op jit(solution)/shard_map/ppermute | solution.py:420
  33.0 1.4 %collective-permute-start.5 = (bf16[64,128]{1,0:T(8,128)(2,1)}, bf16[64,128]{1,0:T(8,128)(2,1)S(1)}, u32[]{:S(2)}, u32[]{:S(2)}) collective-permute-start(bf16[64,128]{1,0:T(8,128)(2,1)} %get-tuple-element.27.share_ref), channel_id=1, source_target_pairs={{0,2},{1,3},{2,0},{3,1},{4,6},{5,7},{6,4},{7,5},{8,10},{9,11},{10,... | collective-permute-start | bytes 49160 | tf_op jit(solution)/shard_map/ppermute | solution.py:420
  34.3 0.0 collective-permute-done.1.refs_1_
  34.3 0.1 collective-permute-start.4
  34.4 0.0 collective-permute-done.2.refs_2_
  34.4 0.0 collective-permute-done.3.refs_3_
  34.4 0.8 %copy-done.1 = bf16[128,128]{1,0:T(8,128)(2,1)S(1)} copy-done((bf16[128,128]{1,0:T(8,128)(2,1)S(1)}, bf16[128,128]{1,0:T(8,128)(2,1)}, u32[]{:S(2)}) %copy-start.1) | copy-done | bytes 32792
  35.2 0.7 %copy-done.2 = bf16[64,128]{1,0:T(8,128)(2,1)S(1)} copy-done((bf16[64,128]{1,0:T(8,128)(2,1)S(1)}, bf16[64,128]{1,0:T(8,128)(2,1)}, u32[]{:S(2)}) %copy-start.2) | copy-done | bytes 16408
  35.9 1.9 %coarse.1 = (f32[128,128]{1,0:T(8,128)S(1)}, f32[16,4096]{1,0:T(8,128)}) custom-call(bf16[128,128]{1,0:T(8,128)(2,1)S(1)} %copy-done.1, bf16[64,128]{1,0:T(8,128)(2,1)S(1)} %copy-done.2, bf16[272,128]{1,0:T(8,128)(2,1)S(1)} %get-tuple-element.22.refs_0_, bf16[272,128]{1,0:T(8,128)(2,1)S(1)} %collective-permute-done.1.refs_1_, ...), custom_call_target="tpu_custom_call" | custom-call | bytes 8388608 | tf_op jit(solution)/shard_map/coarse/pallas_call | solution.py:568
  37.8 0.8 %residual.1 = f32[128,128]{1,0:T(8,128)} custom-call(f32[128,128]{1,0:T(8,128)S(1)} %get-tuple-element.31.left_ref, bf16[64,128]{1,0:T(8,128)(2,1)S(1)} %collective-permute-done.4.refs_0_, bf16[64,128]{1,0:T(8,128)(2,1)S(1)} %collective-permute-done.5.refs_1_, bf16[64,128]{1,0:T(8,128)(2,1)S(1)} %collective-permute-done.6.refs_2_), custom_call_target="tpu_custom_call" | custom-call | tf_op jit(solution)/shard_map/residual/pallas_call | solution.py:584
  (7 shorter events, 0.0 us)
Async XLA Ops:
  4.4 9.9 %collective-permute-start = (bf16[1088,128]{1,0:T(8,128)(2,1)}, bf16[1088,128]{1,0:T(8,128)(2,1)S(1)}, u32[]{:S(2)}, u32[]{:S(2)}) collective-permute-start(bf16[1088,128]{1,0:T(8,128)(2,1)} %get-tuple-element.21), channel_id=1, source_target_pairs={{0,4},{4,0},{8,12},{12,8},{16,20},{20,16},{24,28},{28,24},{1,5},{5... | collective-permute-start | bytes 835592 | tf_op jit(solution)/shard_map/ppermute | solution.py:472
  9.2 19.2 %all-to-all-start = ((bf16[32,16,128]{2,1,0:T(8,128)(2,1)}), bf16[32,16,128]{2,1,0:T(8,128)(2,1)S(1)}, u32[]{:S(2)}, u32[]{:S(2)}) async-start(bf16[32,16,128]{2,1,0:T(8,128)(2,1)} %bitcast.6), calls=%async_computation | async-start | bytes 262144 | tf_op jit(solution)/shard_map/all_to_all | solution.py:488
  14.3 1.0 %copy-start = (bf16[1088,128]{1,0:T(8,128)(2,1)S(1)}, bf16[1088,128]{1,0:T(8,128)(2,1)}, u32[]{:S(2)}) copy-start(bf16[1088,128]{1,0:T(8,128)(2,1)} %get-tuple-element.20.kept_ref) | copy-start | bytes 835588
  15.3 19.0 %collective-permute-start.1 = (bf16[272,128]{1,0:T(8,128)(2,1)S(1)}, bf16[272,128]{1,0:T(8,128)(2,1)S(1)}, u32[]{:S(2)}, u32[]{:S(2)}) collective-permute-start(bf16[272,128]{1,0:T(8,128)(2,1)S(1)} %get-tuple-element.28), channel_id=1, source_target_pairs={{0,8},{4,12},{8,0},{12,4},{16,24},{20,28},{24,16},{28,20},{1,9},{5... | collective-permute-start | bytes 208904 | tf_op jit(solution)/shard_map/ppermute | solution.py:504
  17.2 17.2 %collective-permute-start.2 = (bf16[272,128]{1,0:T(8,128)(2,1)S(1)}, bf16[272,128]{1,0:T(8,128)(2,1)S(1)}, u32[]{:S(2)}, u32[]{:S(2)}) collective-permute-start(bf16[272,128]{1,0:T(8,128)(2,1)S(1)} %get-tuple-element.29), channel_id=1, source_target_pairs={{0,16},{4,20},{8,24},{12,28},{16,0},{20,4},{24,8},{28,12},{1,17},{... | collective-permute-start | bytes 208904 | tf_op jit(solution)/shard_map/ppermute | solution.py:504
  19.8 14.6 %collective-permute-start.3 = (bf16[272,128]{1,0:T(8,128)(2,1)S(1)}, bf16[272,128]{1,0:T(8,128)(2,1)S(1)}, u32[]{:S(2)}, u32[]{:S(2)}) collective-permute-start(bf16[272,128]{1,0:T(8,128)(2,1)S(1)} %get-tuple-element.30), channel_id=1, source_target_pairs={{0,24},{4,28},{8,16},{12,20},{16,8},{20,12},{24,0},{28,4},{1,25},{... | collective-permute-start | bytes 208904 | tf_op jit(solution)/shard_map/ppermute | solution.py:504
  28.4 0.7 %copy-start.3 = (bf16[32,16,128]{2,1,0:T(8,128)(2,1)}, bf16[32,16,128]{2,1,0:T(8,128)(2,1)S(1)}, u32[]{:S(2)}) copy-start(bf16[32,16,128]{2,1,0:T(8,128)(2,1)S(1)} %all-to-all-done) | copy-start | bytes 393220
  32.5 5.3 %collective-permute-start.6 = (bf16[64,128]{1,0:T(8,128)(2,1)}, bf16[64,128]{1,0:T(8,128)(2,1)S(1)}, u32[]{:S(2)}, u32[]{:S(2)}) collective-permute-start(bf16[64,128]{1,0:T(8,128)(2,1)} %get-tuple-element.27.share_ref), channel_id=1, source_target_pairs={{0,3},{1,2},{2,1},{3,0},{4,7},{5,6},{6,5},{7,4},{8,11},{9,10},{10,... | collective-permute-start | bytes 49160 | tf_op jit(solution)/shard_map/ppermute | solution.py:420
  33.0 4.8 %collective-permute-start.5 = (bf16[64,128]{1,0:T(8,128)(2,1)}, bf16[64,128]{1,0:T(8,128)(2,1)S(1)}, u32[]{:S(2)}, u32[]{:S(2)}) collective-permute-start(bf16[64,128]{1,0:T(8,128)(2,1)} %get-tuple-element.27.share_ref), channel_id=1, source_target_pairs={{0,2},{1,3},{2,0},{3,1},{4,6},{5,7},{6,4},{7,5},{8,10},{9,11},{10,... | collective-permute-start | bytes 49160 | tf_op jit(solution)/shard_map/ppermute | solution.py:420
  34.3 3.5 %collective-permute-start.4 = (bf16[64,128]{1,0:T(8,128)(2,1)}, bf16[64,128]{1,0:T(8,128)(2,1)S(1)}, u32[]{:S(2)}, u32[]{:S(2)}) collective-permute-start(bf16[64,128]{1,0:T(8,128)(2,1)} %get-tuple-element.27.share_ref), channel_id=1, source_target_pairs={{0,1},{1,0},{2,3},{3,2},{4,5},{5,4},{6,7},{7,6},{8,9},{9,8},{10,11... | collective-permute-start | bytes 49160 | tf_op jit(solution)/shard_map/ppermute | solution.py:420
  34.4 0.8 %copy-start.1 = (bf16[128,128]{1,0:T(8,128)(2,1)S(1)}, bf16[128,128]{1,0:T(8,128)(2,1)}, u32[]{:S(2)}) copy-start(bf16[128,128]{1,0:T(8,128)(2,1)} %get-tuple-element.26.own_ref) | copy-start | bytes 98308
  35.2 0.7 %copy-start.2 = (bf16[64,128]{1,0:T(8,128)(2,1)S(1)}, bf16[64,128]{1,0:T(8,128)(2,1)}, u32[]{:S(2)}) copy-start(bf16[64,128]{1,0:T(8,128)(2,1)} %get-tuple-element.27.share_ref) | copy-start | bytes 49156

commit v9 on v7

--- a/solution.py
+++ b/solution.py
@@ -21,6 +21,7 @@
 SHARE_ROWS = NAMED + 16
 SLOT_BASE = 16
 CHUNK = 16
+MOST_PAIRED = 8
 BIG = 62 << 20
 SMALL = 12 << 20
 PITCH = MROW + 8
@@ -47,25 +48,15 @@
     return value >> shift, value & (by - 1)
 
 
-def place_kernel(elem_count, face_count, capacity, owner_hbm, trace_hbm, placed_ref, *refs):
-    owner_ref, trace_ref, sems = refs
-    copies = [
-        pltpu.make_async_copy(owner_hbm, owner_ref, sems.at[0]),
-        pltpu.make_async_copy(trace_hbm, trace_ref, sems.at[1]),
-    ]
-    for copy in copies:
-        copy.start()
-    slots, rows = placed_ref.shape[0], trace_ref.shape[0]
+def place_rows(elem_count, face_count, capacity, owners, trace, slots):
+    rows = owners.shape[1]
     earlier = (iota((rows, rows), 0) < iota((rows, rows), 1)).astype(BF16)
+    hot = (iota((face_count, rows), 0) == owners).astype(F32)
+    rank = jnp.sum(hot * dot(hot.astype(BF16), earlier), axis=0, keepdims=True).astype(I32)
     slot = iota((slots, rows), 0)
     wanted = divided(slot, elem_count * capacity)[0] * capacity + divided(slot, capacity)[1]
-    for copy in copies:
-        copy.wait()
-    owners = owner_ref[...]
-    hot = (iota((face_count, rows), 0) == owners).astype(F32)
-    rank = jnp.sum(hot * dot(hot.astype(BF16), earlier), axis=0, keepdims=True).astype(I32)
     place = (wanted == owners * capacity + rank).astype(BF16)
-    placed_ref[...] = dot(place, trace_ref[...]).astype(BF16)
+    return dot(place, trace).astype(BF16)
 
 
 def turn_rhs(rhs_ref, wide_ref, rhs_turned_ref):
@@ -75,39 +66,46 @@
 
 
 def gram_kernel(
+    elem_count,
     face_count,
+    capacity,
+    paired,
     owner_hbm,
     coarse_hbm,
     tiles_hbm,
-    out_ref,
-    owner_ref,
-    coarse_ref,
-    tiles_ref,
-    rows_ref,
-    acc_a_ref,
-    acc_b_ref,
-    diag_a_ref,
-    diag_b_ref,
-    sems,
+    new_owner_hbm,
+    trace_hbm,
+    placed_ref,
+    *refs,
 ):
-    accs, diags = (acc_a_ref, acc_b_ref), (diag_a_ref, diag_b_ref)
+    out_refs, refs = refs[:-11], refs[-11:]
+    owner_ref, coarse_ref, tiles_ref, rows_ref = refs[:4]
+    accs, diags = refs[4:6], refs[6:8]
+    new_owner_ref, trace_ref, sems = refs[8:]
+
+    def place_of(owner):
+        if not paired:
+            return owner
+        other = owner ^ lax.axis_index("face")
+        return (other & 1) * (face_count // 2) + (other >> 1)
+
     tiles = tiles_ref.shape[0]
     copies = [
         pltpu.make_async_copy(owner_hbm, owner_ref, sems.at[0]),
         pltpu.make_async_copy(coarse_hbm, coarse_ref, sems.at[1]),
+        pltpu.make_async_copy(new_owner_hbm, new_owner_ref, sems.at[2]),
+        pltpu.make_async_copy(trace_hbm, trace_ref, sems.at[3]),
+        pltpu.make_async_copy(tiles_hbm, tiles_ref, sems.at[4]),
     ]
-    chunks = []
-    for chunk in range(tiles // CHUNK):
-        here = pl.ds(chunk * CHUNK, CHUNK)
-        chunks.append(
-            pltpu.make_async_copy(tiles_hbm.at[here], tiles_ref.at[here], sems.at[2 + chunk])
-        )
-    for copy in copies + chunks:
+    for copy in copies:
         copy.start()
     for ref in (*accs, *diags):
         ref[...] = jnp.zeros_like(ref)
     for copy in copies:
         copy.wait()
+    placed_ref[...] = place_rows(
+        elem_count, face_count, capacity, new_owner_ref[...], trace_ref[...], placed_ref.shape[0]
+    )
 
     lane = iota((CHUNK, LANES), 1)
     inside = lane < MCOL
@@ -120,7 +118,6 @@
     low_row = iota((1, LANES), 1) < MROW
 
     for chunk in range(tiles // CHUNK):
-        chunks[chunk].wait()
         first_tile = chunk * CHUNK
         for group in range(MROW // 4):
             base = group * 3 * LANES
@@ -160,19 +157,27 @@
             )
             own = (jnp.where(low_row, diag, 0.0), jnp.where(low_row, 0.0, diag))
             for k in range(2):
-                block = owner_ref[tile + k] * NC + coarse_ref[tile + k]
+                block = place_of(owner_ref[tile + k]) * NC + coarse_ref[tile + k]
                 here = pl.ds(pl.multiple_of(block * DENSE, DENSE), DENSE)
                 accs[k][here, :] += dense[k]
                 diags[k][pl.ds(block, 1), :] += own[k]
     size = NC * DENSE
+    each = face_count // len(out_refs)
     for owner in range(face_count):
-        start = owner * OWNER_ROWS
+        out_ref, start = out_refs[owner // each], owner % each * OWNER_ROWS
         here = slice(owner * size, (owner + 1) * size)
         out_ref[start : start + size, :] = (accs[0][here, :] + accs[1][here, :]).astype(BF16)
         here = slice(owner * NC, (owner + 1) * NC)
         out_ref[start + size : start + size + NC, :] = (
             diags[0][here, :] + diags[1][here, :]
         ).astype(BF16)
+
+
+def join_kernel(kept_ref, came_ref, *out_refs):
+    for k, out_ref in enumerate(out_refs):
+        here = slice(k * OWNER_ROWS, (k + 1) * OWNER_ROWS)
+        total = kept_ref[here, :].astype(F32) + came_ref[here, :].astype(F32)
+        out_ref[...] = total.astype(BF16)
 
 
 def main_kernel(
@@ -185,7 +190,7 @@
     coupling_hbm,
     schur_hbm,
     share_ref,
-    own_ref,
+    left_ref,
     conn_ref,
     rhs_ref,
     table_ref,
@@ -205,9 +210,10 @@
     schur_sems,
 ):
     elements = rhs_ref.shape[0]
+    modes = rhs_ref.shape[1]
     trace = FACES_PER_ELEM * FACE_COEFFS
     slots = table_ref.shape[0]
-    own = own_ref.shape[0]
+    own = left_ref.shape[0]
     capacity = own // face_count
     my_elem = lax.axis_index("elem")
     small = [
@@ -237,14 +243,21 @@
         turned_ref[...] = coupling_ref[e].T
 
     def first(e, turned_ref, product_ref):
-        product_ref[...] = dot(turned_ref[...], inverse_ref[e]).astype(BF16)
+        for half in range(2):
+            here = slice(half * modes // 2, (half + 1) * modes // 2)
+            product_ref[:, here] = dot(turned_ref[...], inverse_ref[e, :, here]).astype(BF16)
 
     def second(e, product_ref):
-        wide = jnp.concatenate([coupling_ref[e], rhs_turned_ref[...]], axis=1)
-        condensed = dot(product_ref[...], wide)
-        schur_ref[e] = (-condensed[:, :trace]).astype(BF16)
-        total = condensed * vector_ref[pl.ds(e, 1), :]
-        total = sum(total[:, k * LANES : (k + 1) * LANES] for k in range(FACES_PER_ELEM + 1))
+        split = 2 * LANES
+        one = dot(product_ref[...], coupling_ref[e, :, :split])
+        wide = jnp.concatenate([coupling_ref[e, :, split:], rhs_turned_ref[...]], axis=1)
+        two = dot(product_ref[...], wide)
+        schur_ref[e, :, :split] = (-one).astype(BF16)
+        schur_ref[e, :, split:] = (-two[:, : trace - split]).astype(BF16)
+        vector = vector_ref[pl.ds(e, 1), :]
+        one = one * vector[:, :split]
+        two = two * vector[:, split:]
+        total = (one[:, :LANES] + one[:, LANES:]) + (two[:, :LANES] + two[:, LANES:])
         sums = jnp.sum(total, axis=1, keepdims=True)
         sum_ref[...] = jnp.where(iota((trace, LANES), 1) == e, sums, sum_ref[...])
 
@@ -303,7 +316,7 @@
     share_ref[NAMED:, :] = names.astype(F32).astype(BF16)
     place = position(my_elem, iota((own, slots), 0))
     pick = (iota((own, slots), 1) == place).astype(BF16)
-    own_ref[...] = dot(pick, table_ref[...]).astype(BF16)
+    left_ref[...] = dot(pick, table_ref[...])
 
     advance(0, 0, finishing=False)
 
@@ -322,34 +335,34 @@
     for a in range(FACES_PER_ELEM):
         shares = sum_ref[a * LANES : (a + 1) * LANES, :].T
         share_ref[a * PER_FACE : (a + 1) * PER_FACE, :] = shares[:PER_FACE].astype(BF16)
+    left_ref[...] = less_shares(left_ref[...], share_ref)
     for e in range(elements):
         leave(e).wait()
 
 
-def residual_kernel(elem_count, *refs):
-    ins, (residual_ref, own_ref, shares_ref, sems) = refs[:-4], refs[-4:]
-    places = [own_ref] + [shares_ref.at[k] for k in range(elem_count)]
-    copies = [pltpu.make_async_copy(ins[k], places[k], sems.at[k]) for k in range(len(ins))]
-    for copy in copies:
-        copy.start()
-    own = residual_ref.shape[0]
-    mine = lax.axis_index("elem")
-    slot = (iota((own, SHARE_ROWS), 0) + mine * own).astype(F32)
-    for copy in copies:
-        copy.wait()
-    left = own_ref[...].astype(F32)
-    for k in range(elem_count):
-        names = shares_ref[k, NAMED:, :].astype(F32)
-        named = (names[0:1] * SLOT_BASE + names[1:2])[:, :SHARE_ROWS]
-        left = left - dot((slot == named).astype(BF16), shares_ref[k])
+def less_shares(left, share_ref):
+    own = left.shape[0]
+    slot = (iota((own, SHARE_ROWS), 0) + lax.axis_index("elem") * own).astype(F32)
+    names = share_ref[NAMED:, :].astype(F32)
+    named = (names[0:1] * SLOT_BASE + names[1:2])[:, :SHARE_ROWS]
+    return left - dot((slot == named).astype(BF16), share_ref[...])
+
+
+def residual_kernel(left_ref, *refs):
+    share_refs, residual_ref = refs[:-1], refs[-1]
+    left = left_ref[...]
+    for share_ref in share_refs:
+        left = less_shares(left, share_ref)
     residual_ref[...] = left
 
 
-def coarse_kernel(got_ref, out_ref, sum_ref, full_ref):
-    total = got_ref[0].astype(F32)
-    for k in range(1, got_ref.shape[0]):
-        total = total + got_ref[k].astype(F32)
-    sum_ref[...] = total
+def coarse_kernel(*refs):
+    got_refs, (out_ref, sum_ref, full_ref) = refs[:-3], refs[-3:]
+    sum_ref[...] = sum(
+        got_ref[k : k + OWNER_ROWS, :].astype(F32)
+        for got_ref in got_refs
+        for k in range(0, got_ref.shape[0], OWNER_ROWS)
+    )
 
     lane = iota((HALF, LANES), 1)
     row = iota((HALF, LANES), 0)
@@ -381,6 +394,10 @@
 VMEM = pl.BlockSpec(memory_space=pltpu.VMEM)
 
 
+def cost(flops, bytes_accessed):
+    return pl.CostEstimate(flops=flops, bytes_accessed=bytes_accessed, transcendentals=0)
+
+
 def params(limit):
     return pltpu.CompilerParams(vmem_limit_bytes=limit)
 
@@ -414,31 +431,17 @@
 
     slots = own * elem_count
     devices = face_count * elem_count
-
-    placed = pl.pallas_call(
-        functools.partial(place_kernel, elem_count, face_count, capacity),
-        out_shape=jax.ShapeDtypeStruct((slots, FACE_COEFFS), BF16),
-        in_specs=[ANY, ANY],
-        out_specs=VMEM,
-        scratch_shapes=[
-            pltpu.VMEM((1, row_count), I32),
-            pltpu.VMEM(trace_old.shape, BF16),
-            pltpu.SemaphoreType.DMA((2,)),
-        ],
-        compiler_params=params(BIG),
-        name="place",
-    )(new_owner.reshape(1, row_count), trace_old)
-    table = lax.all_to_all(
-        placed.reshape(devices, capacity, FACE_COEFFS), ("face", "elem"), 0, 0, tiled=True
-    ).reshape(slots, FACE_COEFFS)
+    paired = face_count <= MOST_PAIRED
+    sides = 2 if paired else 1
 
     blocks = face_count * NC
     sums_shape = (blocks * DENSE, LANES)
-    half_grams = pl.pallas_call(
-        functools.partial(gram_kernel, face_count),
-        out_shape=jax.ShapeDtypeStruct((blocks * (DENSE + 1), LANES), BF16),
-        in_specs=[ANY] * 3,
-        out_specs=VMEM,
+    placed, *half_grams = pl.pallas_call(
+        functools.partial(gram_kernel, elem_count, face_count, capacity, paired),
+        out_shape=[jax.ShapeDtypeStruct((slots, FACE_COEFFS), BF16)]
+        + [jax.ShapeDtypeStruct((blocks * (DENSE + 1) // sides, LANES), BF16)] * sides,
+        in_specs=[ANY] * 5,
+        out_specs=[VMEM] * (1 + sides),
         scratch_shapes=[
             pltpu.SMEM((tile_count,), I32),
             pltpu.SMEM((tile_count,), I32),
@@ -448,25 +451,53 @@
             pltpu.VMEM(sums_shape, F32),
             pltpu.VMEM((blocks, LANES), F32),
             pltpu.VMEM((blocks, LANES), F32),
-            pltpu.SemaphoreType.DMA((2 + tile_count // CHUNK,)),
+            pltpu.VMEM((1, row_count), I32),
+            pltpu.VMEM(trace_old.shape, BF16),
+            pltpu.SemaphoreType.DMA((5,)),
         ],
         compiler_params=params(BIG),
-        cost_estimate=pl.CostEstimate(
-            flops=4 * tile_count * MROW * MROW * LANES, bytes_accessed=12 << 20, transcendentals=0
-        ),
+        cost_estimate=cost(4 * tile_count * MROW * MROW * LANES, 12 << 20),
         name="gram",
-    )(mortar_owner.reshape(tile_count), mortar_coarse, mortar_tiles)
-    got = lax.all_to_all(
-        half_grams.reshape(face_count, OWNER_ROWS, LANES), "face", 0, 0, tiled=True
+    )(
+        mortar_owner.reshape(tile_count),
+        mortar_coarse,
+        mortar_tiles,
+        new_owner.reshape(1, row_count),
+        trace_old,
     )
-
-    slots_named, _ = lax.optimization_barrier((connectivity.T, half_grams))
-    schur_blocks, shares, own_rows = pl.pallas_call(
+    if paired:
+        came = lax.ppermute(half_grams[1], "face", [(i, i ^ 1) for i in range(face_count)])
+    table = lax.all_to_all(
+        placed.reshape(devices, capacity, FACE_COEFFS), ("face", "elem"), 0, 0, tiled=True
+    ).reshape(slots, FACE_COEFFS)
+
+    if paired:
+        joined = pl.pallas_call(
+            join_kernel,
+            out_shape=[jax.ShapeDtypeStruct((OWNER_ROWS, LANES), BF16)] * (face_count // 2),
+            in_specs=[VMEM] * 2,
+            out_specs=[VMEM] * (face_count // 2),
+            compiler_params=params(SMALL),
+            cost_estimate=cost(0, 4 << 20),
+            name="join",
+        )(half_grams[0], came)
+        got = [joined[0]] + [
+            lax.ppermute(joined[k], "face", [(i, i ^ (2 * k)) for i in range(face_count)])
+            for k in range(1, face_count // 2)
+        ]
+        before = joined[0]
+    else:
+        blocked = half_grams[0].reshape(face_count, OWNER_ROWS, LANES)
+        got = [lax.all_to_all(blocked, "face", 0, 0, tiled=True).reshape(-1, LANES)]
+        before = half_grams[0]
+
+    rhs, _ = lax.optimization_barrier((interior_rhs, before))
+    schur_blocks, shares, left = pl.pallas_call(
         functools.partial(main_kernel, elem_count, face_count),
         out_shape=(
             jax.ShapeDtypeStruct((elements, trace, trace), BF16),
             jax.ShapeDtypeStruct((SHARE_ROWS, LANES), BF16),
-            jax.ShapeDtypeStruct((own, FACE_COEFFS), BF16),
+            jax.ShapeDtypeStruct((own, FACE_COEFFS), F32),
         ),
         in_specs=[ANY] * 5,
         out_specs=(ANY, VMEM, VMEM),
@@ -490,41 +521,36 @@
             pltpu.SemaphoreType.DMA((elements,)),
         ],
         compiler_params=params(BIG),
-        cost_estimate=pl.CostEstimate(
-            flops=2 * elements * modes * trace * (modes + trace),
-            bytes_accessed=2 * elements * (modes * (modes + trace) + trace * trace),
-            transcendentals=0,
+        cost_estimate=cost(
+            2 * elements * modes * trace * (modes + trace),
+            2 * elements * (modes * (modes + trace) + trace * trace),
         ),
         name="condense",
-    )(table, slots_named, interior_rhs, local_inverse, coupling)
-
-    slot_residual = pl.pallas_call(
-        functools.partial(residual_kernel, elem_count),
-        out_shape=jax.ShapeDtypeStruct((own, FACE_COEFFS), F32),
-        in_specs=[ANY] * (1 + elem_count),
-        out_specs=VMEM,
-        scratch_shapes=[
-            pltpu.VMEM((own, FACE_COEFFS), BF16),
-            pltpu.VMEM((elem_count, SHARE_ROWS, LANES), BF16),
-            pltpu.SemaphoreType.DMA((1 + elem_count,)),
-        ],
-        compiler_params=params(SMALL),
-        name="residual",
-    )(own_rows, *around(shares, "elem"))
-
-    got, slot_residual = lax.optimization_barrier((got, slot_residual))
+    )(table, connectivity.T, rhs, local_inverse, coupling)
+
+    all_shares = around(shares, "elem")
     coarse_blocks = pl.pallas_call(
         coarse_kernel,
         out_shape=jax.ShapeDtypeStruct((NC, MROW * MROW), F32),
-        in_specs=[VMEM],
+        in_specs=[VMEM] * len(got),
         out_specs=VMEM,
         scratch_shapes=[
             pltpu.VMEM((OWNER_ROWS, LANES), F32),
             pltpu.VMEM((NC * MROW, LANES), F32),
         ],
         compiler_params=params(SMALL),
+        cost_estimate=cost(0, 8 << 20),
         name="coarse",
-    )(got)
+    )(*got)
+    left, coarse_blocks = lax.optimization_barrier((left, coarse_blocks))
+    slot_residual = pl.pallas_call(
+        residual_kernel,
+        out_shape=jax.ShapeDtypeStruct((own, FACE_COEFFS), F32),
+        in_specs=[VMEM] * elem_count,
+        out_specs=VMEM,
+        compiler_params=params(SMALL),
+        name="residual",
+    )(left, *all_shares[1:])
     return schur_blocks, slot_residual, coarse_blocks
 
 

time: 39.6 us -> 36.5 us (0.922)
  Pallas kernels: 18.8 us -> 15.5 us
  waiting for transfers between devices: 5.36 us -> 3.21 us
  starting transfers between devices: 12.8 us -> 14.3 us
  local copies, waits for them, and re-layouts: 1.48 us -> 2.45 us
    ppermute x0 -> x4, starting transfers between devices: none -> 7.5 us  [the longest x3 4.46 us: shards(): lax.ppermute(joined[k], 'face', [(i, i ^ 2 * k) for i in range(face_count)])]
    all_to_all x1 -> x0, starting transfers between devices: 3.54 us -> none  [shards(): lax.all_to_all(half_grams.reshape(face_count, OWNER_ROWS, LANES), 'face',...]
    pallas_call x3, Pallas kernels: 7.86 us -> 4.6 us  [the longest x1 3.74 us: shards(): pl.pallas_call(functools.partial(gram_kernel, elem_count, face_count, cap...]
    all_to_all x1, starting transfers between devices: 7.3 us -> 4.89 us  [shards(): lax.all_to_all(placed.reshape(devices, capacity, FACE_COEFFS), ('face', '...]
    all_to_all x1, waiting for transfers between devices: 3.03 us -> 0.78 us  [shards(): lax.all_to_all(placed.reshape(devices, capacity, FACE_COEFFS), ('face', '...]
    ppermute x0 -> x4, waiting for transfers between devices: none -> 1.97 us  [the longest x1 1.96 us: shards(): lax.ppermute(half_grams[1], 'face', [(i, i ^ 1) for i in range(face_count)])]
    ppermute x3, waiting for transfers between devices: 2.33 us -> 0.46 us  [around(): lax.ppermute(block, axis, [(i, i ^ k) for i in range(count)])]
    unnamed x6, local copies, waits for them, and re-layouts: 1.48 us -> 2.45 us
  transfers between devices with their start and end apart: 5 -> 8, of which waited for: 3 -> 3; matrix products, arithmetic and copies ran while one was open for 0% -> 0% of each run, Pallas kernels for 39% -> 30%
where the time goes in v9:
time: 36.5 us; the launch traced here: 36.2 us
  Pallas kernels  15.5 us (42%)
  starting transfers between devices  14.3 us (39%)
  waiting for transfers between devices  3.21 us (9%)
  local copies, waits for them, and re-layouts  2.45 us (7%)
  between operations  0.67 us (2%)
    pallas_call x1, Pallas kernels, shards(): pl.pallas_call(functools.partial(main_kernel, elem_count, face_count), ou...  9.07 us
    all_to_all x1, starting transfers between devices, shards(): lax.all_to_all(placed.reshape(devices, capacity, FACE_COEFFS), ('face', '...  4.89 us
    ppermute x3, starting transfers between devices, shards(): lax.ppermute(joined[k], 'face', [(i, i ^ 2 * k) for i in range(face_count)])  4.46 us
    pallas_call x1, Pallas kernels, shards(): pl.pallas_call(functools.partial(gram_kernel, elem_count, face_count, cap...  3.74 us
    ppermute x1, starting transfers between devices, shards(): lax.ppermute(half_grams[1], 'face', [(i, i ^ 1) for i in range(face_count)])  3.04 us
    unnamed x6, local copies, waits for them, and re-layouts  2.45 us
    ppermute x1, waiting for transfers between devices, shards(): lax.ppermute(half_grams[1], 'face', [(i, i ^ 1) for i in range(face_count)])  1.96 us
    ppermute x3, starting transfers between devices, around(): lax.ppermute(block, axis, [(i, i ^ k) for i in range(count)])  1.93 us
  transfers between devices with their start and end apart: 8, of which 3 were waited for; matrix products, arithmetic and copies ran while one was open for 0% of the time, Pallas kernels for 30%

profile of v9, /device:TPU:0, one launch (start us, length us, event | category | flops | bytes accessed | tf_op | source)
XLA Modules:
  0.0 36.2 jit_solution(6585040996550960233)
XLA Ops:
  0.6 3.7 %gram.1 = (bf16[512,128]{1,0:T(8,128)(2,1)}, bf16[1088,128]{1,0:T(8,128)(2,1)}, bf16[1088,128]{1,0:T(8,128)(2,1)}) custom-call(s32[96]{0:T(128)} %bitcast.7, s32[96]{0:T(128)} %coarse_hbm.1, bf16[96,6144]{1,0:T(8,128)(2,1)} %tiles_hbm.1, s32[1,64]{1,0:T(1,128)} %bitcast.8, bf16[64,128]{1,0:T(8,128)(2,1)} %trace_hbm.1), custom_call_target="tpu_custom_call" | custom-call | flops 201326592 | bytes 12582912 | tf_op jit(solution)/shard_map/gram/pallas_call | solution.py:439
  4.4 3.0 %collective-permute-start = (bf16[1088,128]{1,0:T(8,128)(2,1)}, bf16[1088,128]{1,0:T(8,128)(2,1)S(1)}, u32[]{:S(2)}, u32[]{:S(2)}) collective-permute-start(bf16[1088,128]{1,0:T(8,128)(2,1)} %get-tuple-element.18), channel_id=1, source_target_pairs={{0,4},{4,0},{8,12},{12,8},{16,20},{20,16},{24,28},{28,24},{1,5},{5... | collective-permute-start | bytes 835592 | tf_op jit(solution)/shard_map/ppermute | solution.py:469
  7.4 4.9 %all-to-all-start = ((bf16[32,16,128]{2,1,0:T(8,128)(2,1)}), bf16[32,16,128]{2,1,0:T(8,128)(2,1)S(1)}, u32[]{:S(2)}, u32[]{:S(2)}) async-start(bf16[32,16,128]{2,1,0:T(8,128)(2,1)} %bitcast.6), calls=%async_computation | async-start | bytes 262144 | tf_op jit(solution)/shard_map/all_to_all | solution.py:470
  12.3 2.0 %collective-permute-done.came_ref = bf16[1088,128]{1,0:T(8,128)(2,1)S(1)} collective-permute-done((bf16[1088,128]{1,0:T(8,128)(2,1)}, bf16[1088,128]{1,0:T(8,128)(2,1)S(1)}, u32[]{:S(2)}, u32[]{:S(2)}) %collective-permute-start) | collective-permute-done | bytes 278560 | tf_op jit(solution)/shard_map/ppermute | solution.py:469
  14.3 1.0 %copy-done = bf16[1088,128]{1,0:T(8,128)(2,1)S(1)} copy-done((bf16[1088,128]{1,0:T(8,128)(2,1)S(1)}, bf16[1088,128]{1,0:T(8,128)(2,1)}, u32[]{:S(2)}) %copy-start) | copy-done | bytes 278552
  15.2 0.1 join.1
  15.3 1.9 %collective-permute-start.1 = (bf16[272,128]{1,0:T(8,128)(2,1)S(1)}, bf16[272,128]{1,0:T(8,128)(2,1)S(1)}, u32[]{:S(2)}, u32[]{:S(2)}) collective-permute-start(bf16[272,128]{1,0:T(8,128)(2,1)S(1)} %get-tuple-element.23), channel_id=1, source_target_pairs={{0,8},{4,12},{8,0},{12,4},{16,24},{20,28},{24,16},{28,20},{1,9},{5... | collective-permute-start | bytes 208904 | tf_op jit(solution)/shard_map/ppermute | solution.py:485
  17.2 2.6 %collective-permute-start.2 = (bf16[272,128]{1,0:T(8,128)(2,1)S(1)}, bf16[272,128]{1,0:T(8,128)(2,1)S(1)}, u32[]{:S(2)}, u32[]{:S(2)}) collective-permute-start(bf16[272,128]{1,0:T(8,128)(2,1)S(1)} %get-tuple-element.24), channel_id=1, source_target_pairs={{0,16},{4,20},{8,24},{12,28},{16,0},{20,4},{24,8},{28,12},{1,17},{... | collective-permute-start | bytes 208904 | tf_op jit(solution)/shard_map/ppermute | solution.py:485
  19.8 0.0 collective-permute-start.3
  19.8 0.8 %all-to-all-done = bf16[32,16,128]{2,1,0:T(8,128)(2,1)S(1)} async-done(((bf16[32,16,128]{2,1,0:T(8,128)(2,1)}), bf16[32,16,128]{2,1,0:T(8,128)(2,1)S(1)}, u32[]{:S(2)}, u32[]{:S(2)}) %all-to-all-start) | async-done | bytes 131104 | tf_op jit(solution)/shard_map/all_to_all | solution.py:470
  20.5 0.7 %copy-done.2 = bf16[32,16,128]{2,1,0:T(8,128)(2,1)} copy-done((bf16[32,16,128]{2,1,0:T(8,128)(2,1)}, bf16[32,16,128]{2,1,0:T(8,128)(2,1)S(1)}, u32[]{:S(2)}) %copy-start.2) | copy-done | bytes 131096
  21.2 9.1 %condense.1 = (bf16[9,384,384]{2,1,0:T(8,128)(2,1)}, bf16[64,128]{1,0:T(8,128)(2,1)}, f32[128,128]{1,0:T(8,128)}) custom-call(bf16[512,128]{1,0:T(8,128)(2,1)} %bitcast.5, s32[3,9]{1,0:T(4,128)} %bitcast.9, bf16[9,512]{1,0:T(8,128)(2,1)} %rhs_hbm, bf16[9,512,512]{2,1,0:T(8,128)(2,1)} %inverse_hbm.1, bf16[9,512,384]{2,1,0:T(8,128)(2,1)} %coupling_hbm.1), custom_call_target="tpu_custom_call" | custom-call | flops 3170893824 | bytes 10911744 | tf_op jit(solution)/shard_map/condense/pallas_call | solution.py:495
  30.3 0.2 collective-permute-start.6
  30.5 1.7 %collective-permute-start.5 = (bf16[64,128]{1,0:T(8,128)(2,1)}, bf16[64,128]{1,0:T(8,128)(2,1)S(1)}, u32[]{:S(2)}, u32[]{:S(2)}) collective-permute-start(bf16[64,128]{1,0:T(8,128)(2,1)} %get-tuple-element.27), channel_id=1, source_target_pairs={{0,2},{1,3},{2,0},{3,1},{4,6},{5,7},{6,4},{7,5},{8,10},{9,11},{10,... | collective-permute-start | bytes 49160 | tf_op jit(solution)/shard_map/ppermute | solution.py:408
  32.2 0.0 collective-permute-done.1.refs_1_
  32.2 0.0 collective-permute-start.4
  32.2 0.0 collective-permute-done.2.refs_2_
  32.2 0.0 collective-permute-done.3.refs_3_
  32.2 1.9 %coarse.1 = f32[16,4096]{1,0:T(8,128)} custom-call(bf16[272,128]{1,0:T(8,128)(2,1)S(1)} %get-tuple-element.19.refs_0_, bf16[272,128]{1,0:T(8,128)(2,1)S(1)} %collective-permute-done.1.refs_1_, bf16[272,128]{1,0:T(8,128)(2,1)S(1)} %collective-permute-done.2.refs_2_, bf16[272,128]{1,0:T(8,128)(2,1)S(1)} %collective-permute-done.3.refs_3_), custom_call_target="tpu_custom_call" | custom-call | bytes 8388608 | tf_op jit(solution)/shard_map/coarse/pallas_call | solution.py:532
  34.1 0.0 collective-permute-done.6.refs_2_
  34.1 0.5 %collective-permute-done.5.refs_1_ = bf16[64,128]{1,0:T(8,128)(2,1)S(1)} collective-permute-done((bf16[64,128]{1,0:T(8,128)(2,1)}, bf16[64,128]{1,0:T(8,128)(2,1)S(1)}, u32[]{:S(2)}, u32[]{:S(2)}) %collective-permute-start.5) | collective-permute-done | bytes 16416 | tf_op jit(solution)/shard_map/ppermute | solution.py:408
  34.5 0.0 collective-permute-done.4.refs_0_
  34.6 0.8 %copy-done.1 = f32[128,128]{1,0:T(8,128)S(1)} copy-done((f32[128,128]{1,0:T(8,128)S(1)}, f32[128,128]{1,0:T(8,128)}, u32[]{:S(2)}) %copy-start.1) | copy-done | bytes 65560
  35.4 0.8 %residual.1 = f32[128,128]{1,0:T(8,128)} custom-call(f32[128,128]{1,0:T(8,128)S(1)} %copy-done.1, bf16[64,128]{1,0:T(8,128)(2,1)S(1)} %collective-permute-done.4.refs_0_, bf16[64,128]{1,0:T(8,128)(2,1)S(1)} %collective-permute-done.5.refs_1_, bf16[64,128]{1,0:T(8,128)(2,1)S(1)} %collective-permute-done.6.refs_2_), custom_call_target="tpu_custom_call" | custom-call | tf_op jit(solution)/shard_map/residual/pallas_call | solution.py:546
  (3 shorter events, 0.0 us)
Async XLA Ops:
  4.4 9.9 %collective-permute-start = (bf16[1088,128]{1,0:T(8,128)(2,1)}, bf16[1088,128]{1,0:T(8,128)(2,1)S(1)}, u32[]{:S(2)}, u32[]{:S(2)}) collective-permute-start(bf16[1088,128]{1,0:T(8,128)(2,1)} %get-tuple-element.18), channel_id=1, source_target_pairs={{0,4},{4,0},{8,12},{12,8},{16,20},{20,16},{24,28},{28,24},{1,5},{5... | collective-permute-start | bytes 835592 | tf_op jit(solution)/shard_map/ppermute | solution.py:469
  7.4 13.1 %all-to-all-start = ((bf16[32,16,128]{2,1,0:T(8,128)(2,1)}), bf16[32,16,128]{2,1,0:T(8,128)(2,1)S(1)}, u32[]{:S(2)}, u32[]{:S(2)}) async-start(bf16[32,16,128]{2,1,0:T(8,128)(2,1)} %bitcast.6), calls=%async_computation | async-start | bytes 262144 | tf_op jit(solution)/shard_map/all_to_all | solution.py:470
  14.3 1.0 %copy-start = (bf16[1088,128]{1,0:T(8,128)(2,1)S(1)}, bf16[1088,128]{1,0:T(8,128)(2,1)}, u32[]{:S(2)}) copy-start(bf16[1088,128]{1,0:T(8,128)(2,1)} %get-tuple-element.17.kept_ref) | copy-start | bytes 835588
  15.3 16.9 %collective-permute-start.1 = (bf16[272,128]{1,0:T(8,128)(2,1)S(1)}, bf16[272,128]{1,0:T(8,128)(2,1)S(1)}, u32[]{:S(2)}, u32[]{:S(2)}) collective-permute-start(bf16[272,128]{1,0:T(8,128)(2,1)S(1)} %get-tuple-element.23), channel_id=1, source_target_pairs={{0,8},{4,12},{8,0},{12,4},{16,24},{20,28},{24,16},{28,20},{1,9},{5... | collective-permute-start | bytes 208904 | tf_op jit(solution)/shard_map/ppermute | solution.py:485
  17.2 15.0 %collective-permute-start.2 = (bf16[272,128]{1,0:T(8,128)(2,1)S(1)}, bf16[272,128]{1,0:T(8,128)(2,1)S(1)}, u32[]{:S(2)}, u32[]{:S(2)}) collective-permute-start(bf16[272,128]{1,0:T(8,128)(2,1)S(1)} %get-tuple-element.24), channel_id=1, source_target_pairs={{0,16},{4,20},{8,24},{12,28},{16,0},{20,4},{24,8},{28,12},{1,17},{... | collective-permute-start | bytes 208904 | tf_op jit(solution)/shard_map/ppermute | solution.py:485
  19.8 12.5 %collective-permute-start.3 = (bf16[272,128]{1,0:T(8,128)(2,1)S(1)}, bf16[272,128]{1,0:T(8,128)(2,1)S(1)}, u32[]{:S(2)}, u32[]{:S(2)}) collective-permute-start(bf16[272,128]{1,0:T(8,128)(2,1)S(1)} %get-tuple-element.25), channel_id=1, source_target_pairs={{0,24},{4,28},{8,16},{12,20},{16,8},{20,12},{24,0},{28,4},{1,25},{... | collective-permute-start | bytes 208904 | tf_op jit(solution)/shard_map/ppermute | solution.py:485
  20.5 0.7 %copy-start.2 = (bf16[32,16,128]{2,1,0:T(8,128)(2,1)}, bf16[32,16,128]{2,1,0:T(8,128)(2,1)S(1)}, u32[]{:S(2)}) copy-start(bf16[32,16,128]{2,1,0:T(8,128)(2,1)S(1)} %all-to-all-done) | copy-start | bytes 393220
  30.3 3.8 %collective-permute-start.6 = (bf16[64,128]{1,0:T(8,128)(2,1)}, bf16[64,128]{1,0:T(8,128)(2,1)S(1)}, u32[]{:S(2)}, u32[]{:S(2)}) collective-permute-start(bf16[64,128]{1,0:T(8,128)(2,1)} %get-tuple-element.27), channel_id=1, source_target_pairs={{0,3},{1,2},{2,1},{3,0},{4,7},{5,6},{6,5},{7,4},{8,11},{9,10},{10,... | collective-permute-start | bytes 49160 | tf_op jit(solution)/shard_map/ppermute | solution.py:408
  30.5 4.0 %collective-permute-start.5 = (bf16[64,128]{1,0:T(8,128)(2,1)}, bf16[64,128]{1,0:T(8,128)(2,1)S(1)}, u32[]{:S(2)}, u32[]{:S(2)}) collective-permute-start(bf16[64,128]{1,0:T(8,128)(2,1)} %get-tuple-element.27), channel_id=1, source_target_pairs={{0,2},{1,3},{2,0},{3,1},{4,6},{5,7},{6,4},{7,5},{8,10},{9,11},{10,... | collective-permute-start | bytes 49160 | tf_op jit(solution)/shard_map/ppermute | solution.py:408
  32.2 2.4 %collective-permute-start.4 = (bf16[64,128]{1,0:T(8,128)(2,1)}, bf16[64,128]{1,0:T(8,128)(2,1)S(1)}, u32[]{:S(2)}, u32[]{:S(2)}) collective-permute-start(bf16[64,128]{1,0:T(8,128)(2,1)} %get-tuple-element.27), channel_id=1, source_target_pairs={{0,1},{1,0},{2,3},{3,2},{4,5},{5,4},{6,7},{7,6},{8,9},{9,8},{10,11... | collective-permute-start | bytes 49160 | tf_op jit(solution)/shard_map/ppermute | solution.py:408
  34.5 0.8 %copy-start.1 = (f32[128,128]{1,0:T(8,128)S(1)}, f32[128,128]{1,0:T(8,128)}, u32[]{:S(2)}) copy-start(f32[128,128]{1,0:T(8,128)} %get-tuple-element.26.left_ref) | copy-start | bytes 196612

commit v10 on v9

--- a/solution.py
+++ b/solution.py
@@ -21,6 +21,7 @@
 SHARE_ROWS = NAMED + 16
 SLOT_BASE = 16
 CHUNK = 16
+AHEAD = 5
 MOST_PAIRED = 8
 BIG = 62 << 20
 SMALL = 12 << 20
@@ -231,13 +232,16 @@
     def leave(e):
         return pltpu.make_async_copy(schur_ref.at[e], schur_hbm.at[e], schur_sems.at[e])
 
+    def bring(first, last):
+        for e in range(first, min(last, elements)):
+            coupling_copy(e).start()
+            inverse_copy(e).start()
+
     coupling_copy(0).start()
     for copy in small:
         copy.start()
     inverse_copy(0).start()
-    coupling_copy(1).start()
-    inverse_copy(1).start()
-    coupling_copy(2).start()
+    bring(1, 2)
 
     def turn(e, turned_ref):
         turned_ref[...] = coupling_ref[e].T
@@ -266,13 +270,11 @@
 
     def advance(e, parity, turning=True, finishing=True):
         if turning:
-            @pl.when(e + 2 < elements)
+
+            @pl.when(e + AHEAD < elements)
             def _():
-                inverse_copy(e + 2).start()
-
-            @pl.when(e + 3 < elements)
-            def _():
-                coupling_copy(e + 3).start()
+                coupling_copy(e + AHEAD).start()
+                inverse_copy(e + AHEAD).start()
 
             coupling_copy(e + 1).wait()
         inverse_copy(e).wait()
@@ -284,9 +286,11 @@
             leave(e - 1).start()
 
     coupling_copy(0).wait()
+    bring(2, 3)
     turn(0, turned[0])
     for copy in small:
         copy.wait()
+    bring(3, AHEAD)
     sum_ref[...] = jnp.zeros_like(sum_ref)
     turn_rhs(rhs_ref, wide_ref, rhs_turned_ref)
     row = iota((PER_FACE, LANES), 0)

time: 36.5 us -> 36.5 us (level)
  no operation moved by 1% of the time
where the time goes in v10:
time: 36.5 us; the launch traced here: 36.2 us
  Pallas kernels  15.6 us (43%)
  starting transfers between devices  14.3 us (39%)
  waiting for transfers between devices  3.22 us (9%)
  local copies, waits for them, and re-layouts  2.45 us (7%)
  between operations  0.67 us (2%)
    pallas_call x1, Pallas kernels, shards(): pl.pallas_call(functools.partial(main_kernel, elem_count, face_count), ou...  9.08 us
    all_to_all x1, starting transfers between devices, shards(): lax.all_to_all(placed.reshape(devices, capacity, FACE_COEFFS), ('face', '...  4.89 us
    ppermute x3, starting transfers between devices, shards(): lax.ppermute(joined[k], 'face', [(i, i ^ 2 * k) for i in range(face_count)])  4.46 us
    pallas_call x1, Pallas kernels, shards(): pl.pallas_call(functools.partial(gram_kernel, elem_count, face_count, cap...  3.75 us
    ppermute x1, starting transfers between devices, shards(): lax.ppermute(half_grams[1], 'face', [(i, i ^ 1) for i in range(face_count)])  3.03 us
    unnamed x6, local copies, waits for them, and re-layouts  2.45 us
    ppermute x1, waiting for transfers between devices, shards(): lax.ppermute(half_grams[1], 'face', [(i, i ^ 1) for i in range(face_count)])  1.96 us
    ppermute x3, starting transfers between devices, around(): lax.ppermute(block, axis, [(i, i ^ k) for i in range(count)])  1.93 us
  transfers between devices with their start and end apart: 8, of which 3 were waited for; matrix products, arithmetic and copies ran while one was open for 0% of the time, Pallas kernels for 30%

profile of v10, /device:TPU:0, one launch (start us, length us, event | category | flops | bytes accessed | tf_op | source)
XLA Modules:
  0.0 36.2 jit_solution(11628116143877837823)
XLA Ops:
  0.6 3.7 %gram.1 = (bf16[512,128]{1,0:T(8,128)(2,1)}, bf16[1088,128]{1,0:T(8,128)(2,1)}, bf16[1088,128]{1,0:T(8,128)(2,1)}) custom-call(s32[96]{0:T(128)} %bitcast.7, s32[96]{0:T(128)} %coarse_hbm.1, bf16[96,6144]{1,0:T(8,128)(2,1)} %tiles_hbm.1, s32[1,64]{1,0:T(1,128)} %bitcast.8, bf16[64,128]{1,0:T(8,128)(2,1)} %trace_hbm.1), custom_call_target="tpu_custom_call" | custom-call | flops 201326592 | bytes 12582912 | tf_op jit(solution)/shard_map/gram/pallas_call | solution.py:443
  4.4 3.0 %collective-permute-start = (bf16[1088,128]{1,0:T(8,128)(2,1)}, bf16[1088,128]{1,0:T(8,128)(2,1)S(1)}, u32[]{:S(2)}, u32[]{:S(2)}) collective-permute-start(bf16[1088,128]{1,0:T(8,128)(2,1)} %get-tuple-element.18), channel_id=1, source_target_pairs={{0,4},{4,0},{8,12},{12,8},{16,20},{20,16},{24,28},{28,24},{1,5},{5... | collective-permute-start | bytes 835592 | tf_op jit(solution)/shard_map/ppermute | solution.py:473
  7.4 4.9 %all-to-all-start = ((bf16[32,16,128]{2,1,0:T(8,128)(2,1)}), bf16[32,16,128]{2,1,0:T(8,128)(2,1)S(1)}, u32[]{:S(2)}, u32[]{:S(2)}) async-start(bf16[32,16,128]{2,1,0:T(8,128)(2,1)} %bitcast.6), calls=%async_computation | async-start | bytes 262144 | tf_op jit(solution)/shard_map/all_to_all | solution.py:474
  12.3 2.0 %collective-permute-done.came_ref = bf16[1088,128]{1,0:T(8,128)(2,1)S(1)} collective-permute-done((bf16[1088,128]{1,0:T(8,128)(2,1)}, bf16[1088,128]{1,0:T(8,128)(2,1)S(1)}, u32[]{:S(2)}, u32[]{:S(2)}) %collective-permute-start) | collective-permute-done | bytes 278560 | tf_op jit(solution)/shard_map/ppermute | solution.py:473
  14.3 1.0 %copy-done = bf16[1088,128]{1,0:T(8,128)(2,1)S(1)} copy-done((bf16[1088,128]{1,0:T(8,128)(2,1)S(1)}, bf16[1088,128]{1,0:T(8,128)(2,1)}, u32[]{:S(2)}) %copy-start) | copy-done | bytes 278552
  15.2 0.1 join.1
  15.3 1.9 %collective-permute-start.1 = (bf16[272,128]{1,0:T(8,128)(2,1)S(1)}, bf16[272,128]{1,0:T(8,128)(2,1)S(1)}, u32[]{:S(2)}, u32[]{:S(2)}) collective-permute-start(bf16[272,128]{1,0:T(8,128)(2,1)S(1)} %get-tuple-element.23), channel_id=1, source_target_pairs={{0,8},{4,12},{8,0},{12,4},{16,24},{20,28},{24,16},{28,20},{1,9},{5... | collective-permute-start | bytes 208904 | tf_op jit(solution)/shard_map/ppermute | solution.py:489
  17.2 2.6 %collective-permute-start.2 = (bf16[272,128]{1,0:T(8,128)(2,1)S(1)}, bf16[272,128]{1,0:T(8,128)(2,1)S(1)}, u32[]{:S(2)}, u32[]{:S(2)}) collective-permute-start(bf16[272,128]{1,0:T(8,128)(2,1)S(1)} %get-tuple-element.24), channel_id=1, source_target_pairs={{0,16},{4,20},{8,24},{12,28},{16,0},{20,4},{24,8},{28,12},{1,17},{... | collective-permute-start | bytes 208904 | tf_op jit(solution)/shard_map/ppermute | solution.py:489
  19.8 0.0 collective-permute-start.3
  19.8 0.8 %all-to-all-done = bf16[32,16,128]{2,1,0:T(8,128)(2,1)S(1)} async-done(((bf16[32,16,128]{2,1,0:T(8,128)(2,1)}), bf16[32,16,128]{2,1,0:T(8,128)(2,1)S(1)}, u32[]{:S(2)}, u32[]{:S(2)}) %all-to-all-start) | async-done | bytes 131104 | tf_op jit(solution)/shard_map/all_to_all | solution.py:474
  20.5 0.7 %copy-done.2 = bf16[32,16,128]{2,1,0:T(8,128)(2,1)} copy-done((bf16[32,16,128]{2,1,0:T(8,128)(2,1)}, bf16[32,16,128]{2,1,0:T(8,128)(2,1)S(1)}, u32[]{:S(2)}) %copy-start.2) | copy-done | bytes 131096
  21.2 9.1 %condense.1 = (bf16[9,384,384]{2,1,0:T(8,128)(2,1)}, bf16[64,128]{1,0:T(8,128)(2,1)}, f32[128,128]{1,0:T(8,128)}) custom-call(bf16[512,128]{1,0:T(8,128)(2,1)} %bitcast.5, s32[3,9]{1,0:T(4,128)} %bitcast.9, bf16[9,512]{1,0:T(8,128)(2,1)} %rhs_hbm, bf16[9,512,512]{2,1,0:T(8,128)(2,1)} %inverse_hbm.1, bf16[9,512,384]{2,1,0:T(8,128)(2,1)} %coupling_hbm.1), custom_call_target="tpu_custom_call" | custom-call | flops 3170893824 | bytes 10911744 | tf_op jit(solution)/shard_map/condense/pallas_call | solution.py:499
  30.3 0.2 collective-permute-start.6
  30.5 1.7 %collective-permute-start.5 = (bf16[64,128]{1,0:T(8,128)(2,1)}, bf16[64,128]{1,0:T(8,128)(2,1)S(1)}, u32[]{:S(2)}, u32[]{:S(2)}) collective-permute-start(bf16[64,128]{1,0:T(8,128)(2,1)} %get-tuple-element.27), channel_id=1, source_target_pairs={{0,2},{1,3},{2,0},{3,1},{4,6},{5,7},{6,4},{7,5},{8,10},{9,11},{10,... | collective-permute-start | bytes 49160 | tf_op jit(solution)/shard_map/ppermute | solution.py:412
  32.2 0.0 collective-permute-done.1.refs_1_
  32.2 0.0 collective-permute-start.4
  32.2 0.0 collective-permute-done.2.refs_2_
  32.2 0.0 collective-permute-done.3.refs_3_
  32.2 1.9 %coarse.1 = f32[16,4096]{1,0:T(8,128)} custom-call(bf16[272,128]{1,0:T(8,128)(2,1)S(1)} %get-tuple-element.19.refs_0_, bf16[272,128]{1,0:T(8,128)(2,1)S(1)} %collective-permute-done.1.refs_1_, bf16[272,128]{1,0:T(8,128)(2,1)S(1)} %collective-permute-done.2.refs_2_, bf16[272,128]{1,0:T(8,128)(2,1)S(1)} %collective-permute-done.3.refs_3_), custom_call_target="tpu_custom_call" | custom-call | bytes 8388608 | tf_op jit(solution)/shard_map/coarse/pallas_call | solution.py:536
  34.1 0.0 collective-permute-done.6.refs_2_
  34.1 0.5 %collective-permute-done.5.refs_1_ = bf16[64,128]{1,0:T(8,128)(2,1)S(1)} collective-permute-done((bf16[64,128]{1,0:T(8,128)(2,1)}, bf16[64,128]{1,0:T(8,128)(2,1)S(1)}, u32[]{:S(2)}, u32[]{:S(2)}) %collective-permute-start.5) | collective-permute-done | bytes 16416 | tf_op jit(solution)/shard_map/ppermute | solution.py:412
  34.6 0.0 collective-permute-done.4.refs_0_
  34.6 0.8 %copy-done.1 = f32[128,128]{1,0:T(8,128)S(1)} copy-done((f32[128,128]{1,0:T(8,128)S(1)}, f32[128,128]{1,0:T(8,128)}, u32[]{:S(2)}) %copy-start.1) | copy-done | bytes 65560
  35.4 0.8 %residual.1 = f32[128,128]{1,0:T(8,128)} custom-call(f32[128,128]{1,0:T(8,128)S(1)} %copy-done.1, bf16[64,128]{1,0:T(8,128)(2,1)S(1)} %collective-permute-done.4.refs_0_, bf16[64,128]{1,0:T(8,128)(2,1)S(1)} %collective-permute-done.5.refs_1_, bf16[64,128]{1,0:T(8,128)(2,1)S(1)} %collective-permute-done.6.refs_2_), custom_call_target="tpu_custom_call" | custom-call | tf_op jit(solution)/shard_map/residual/pallas_call | solution.py:550
  (3 shorter events, 0.0 us)
Async XLA Ops:
  4.4 9.9 %collective-permute-start = (bf16[1088,128]{1,0:T(8,128)(2,1)}, bf16[1088,128]{1,0:T(8,128)(2,1)S(1)}, u32[]{:S(2)}, u32[]{:S(2)}) collective-permute-start(bf16[1088,128]{1,0:T(8,128)(2,1)} %get-tuple-element.18), channel_id=1, source_target_pairs={{0,4},{4,0},{8,12},{12,8},{16,20},{20,16},{24,28},{28,24},{1,5},{5... | collective-permute-start | bytes 835592 | tf_op jit(solution)/shard_map/ppermute | solution.py:473
  7.4 13.1 %all-to-all-start = ((bf16[32,16,128]{2,1,0:T(8,128)(2,1)}), bf16[32,16,128]{2,1,0:T(8,128)(2,1)S(1)}, u32[]{:S(2)}, u32[]{:S(2)}) async-start(bf16[32,16,128]{2,1,0:T(8,128)(2,1)} %bitcast.6), calls=%async_computation | async-start | bytes 262144 | tf_op jit(solution)/shard_map/all_to_all | solution.py:474
  14.3 1.0 %copy-start = (bf16[1088,128]{1,0:T(8,128)(2,1)S(1)}, bf16[1088,128]{1,0:T(8,128)(2,1)}, u32[]{:S(2)}) copy-start(bf16[1088,128]{1,0:T(8,128)(2,1)} %get-tuple-element.17.kept_ref) | copy-start | bytes 835588
  15.3 16.9 %collective-permute-start.1 = (bf16[272,128]{1,0:T(8,128)(2,1)S(1)}, bf16[272,128]{1,0:T(8,128)(2,1)S(1)}, u32[]{:S(2)}, u32[]{:S(2)}) collective-permute-start(bf16[272,128]{1,0:T(8,128)(2,1)S(1)} %get-tuple-element.23), channel_id=1, source_target_pairs={{0,8},{4,12},{8,0},{12,4},{16,24},{20,28},{24,16},{28,20},{1,9},{5... | collective-permute-start | bytes 208904 | tf_op jit(solution)/shard_map/ppermute | solution.py:489
  17.2 15.0 %collective-permute-start.2 = (bf16[272,128]{1,0:T(8,128)(2,1)S(1)}, bf16[272,128]{1,0:T(8,128)(2,1)S(1)}, u32[]{:S(2)}, u32[]{:S(2)}) collective-permute-start(bf16[272,128]{1,0:T(8,128)(2,1)S(1)} %get-tuple-element.24), channel_id=1, source_target_pairs={{0,16},{4,20},{8,24},{12,28},{16,0},{20,4},{24,8},{28,12},{1,17},{... | collective-permute-start | bytes 208904 | tf_op jit(solution)/shard_map/ppermute | solution.py:489
  19.8 12.5 %collective-permute-start.3 = (bf16[272,128]{1,0:T(8,128)(2,1)S(1)}, bf16[272,128]{1,0:T(8,128)(2,1)S(1)}, u32[]{:S(2)}, u32[]{:S(2)}) collective-permute-start(bf16[272,128]{1,0:T(8,128)(2,1)S(1)} %get-tuple-element.25), channel_id=1, source_target_pairs={{0,24},{4,28},{8,16},{12,20},{16,8},{20,12},{24,0},{28,4},{1,25},{... | collective-permute-start | bytes 208904 | tf_op jit(solution)/shard_map/ppermute | solution.py:489
  20.5 0.7 %copy-start.2 = (bf16[32,16,128]{2,1,0:T(8,128)(2,1)}, bf16[32,16,128]{2,1,0:T(8,128)(2,1)S(1)}, u32[]{:S(2)}) copy-start(bf16[32,16,128]{2,1,0:T(8,128)(2,1)S(1)} %all-to-all-done) | copy-start | bytes 393220
  30.3 3.8 %collective-permute-start.6 = (bf16[64,128]{1,0:T(8,128)(2,1)}, bf16[64,128]{1,0:T(8,128)(2,1)S(1)}, u32[]{:S(2)}, u32[]{:S(2)}) collective-permute-start(bf16[64,128]{1,0:T(8,128)(2,1)} %get-tuple-element.27), channel_id=1, source_target_pairs={{0,3},{1,2},{2,1},{3,0},{4,7},{5,6},{6,5},{7,4},{8,11},{9,10},{10,... | collective-permute-start | bytes 49160 | tf_op jit(solution)/shard_map/ppermute | solution.py:412
  30.5 4.0 %collective-permute-start.5 = (bf16[64,128]{1,0:T(8,128)(2,1)}, bf16[64,128]{1,0:T(8,128)(2,1)S(1)}, u32[]{:S(2)}, u32[]{:S(2)}) collective-permute-start(bf16[64,128]{1,0:T(8,128)(2,1)} %get-tuple-element.27), channel_id=1, source_target_pairs={{0,2},{1,3},{2,0},{3,1},{4,6},{5,7},{6,4},{7,5},{8,10},{9,11},{10,... | collective-permute-start | bytes 49160 | tf_op jit(solution)/shard_map/ppermute | solution.py:412
  32.2 2.4 %collective-permute-start.4 = (bf16[64,128]{1,0:T(8,128)(2,1)}, bf16[64,128]{1,0:T(8,128)(2,1)S(1)}, u32[]{:S(2)}, u32[]{:S(2)}) collective-permute-start(bf16[64,128]{1,0:T(8,128)(2,1)} %get-tuple-element.27), channel_id=1, source_target_pairs={{0,1},{1,0},{2,3},{3,2},{4,5},{5,4},{6,7},{7,6},{8,9},{9,8},{10,11... | collective-permute-start | bytes 49160 | tf_op jit(solution)/shard_map/ppermute | solution.py:412
  34.6 0.8 %copy-start.1 = (f32[128,128]{1,0:T(8,128)S(1)}, f32[128,128]{1,0:T(8,128)}, u32[]{:S(2)}) copy-start(f32[128,128]{1,0:T(8,128)} %get-tuple-element.26.left_ref) | copy-start | bytes 196612

commit v11 on v8

--- a/solution.py
+++ b/solution.py
@@ -48,25 +48,15 @@
     return value >> shift, value & (by - 1)
 
 
-def place_kernel(elem_count, face_count, capacity, owner_hbm, trace_hbm, placed_ref, *refs):
-    owner_ref, trace_ref, sems = refs
-    copies = [
-        pltpu.make_async_copy(owner_hbm, owner_ref, sems.at[0]),
-        pltpu.make_async_copy(trace_hbm, trace_ref, sems.at[1]),
-    ]
-    for copy in copies:
-        copy.start()
-    slots, rows = placed_ref.shape[0], trace_ref.shape[0]
+def place_rows(elem_count, face_count, capacity, owners, trace, slots):
+    rows = owners.shape[1]
     earlier = (iota((rows, rows), 0) < iota((rows, rows), 1)).astype(BF16)
+    hot = (iota((face_count, rows), 0) == owners).astype(F32)
+    rank = jnp.sum(hot * dot(hot.astype(BF16), earlier), axis=0, keepdims=True).astype(I32)
     slot = iota((slots, rows), 0)
     wanted = divided(slot, elem_count * capacity)[0] * capacity + divided(slot, capacity)[1]
-    for copy in copies:
-        copy.wait()
-    owners = owner_ref[...]
-    hot = (iota((face_count, rows), 0) == owners).astype(F32)
-    rank = jnp.sum(hot * dot(hot.astype(BF16), earlier), axis=0, keepdims=True).astype(I32)
     place = (wanted == owners * capacity + rank).astype(BF16)
-    placed_ref[...] = dot(place, trace_ref[...]).astype(BF16)
+    return dot(place, trace).astype(BF16)
 
 
 def turn_rhs(rhs_ref, wide_ref, rhs_turned_ref):
@@ -75,29 +65,48 @@
     rhs_turned_ref[...] = wide_ref[...].T.astype(BF16)
 
 
-def gram_kernel(face_count, paired, owner_hbm, coarse_hbm, tiles_hbm, *refs):
-    out_refs, refs = refs[:-9], refs[-9:]
+def gram_kernel(
+    elem_count,
+    face_count,
+    capacity,
+    paired,
+    owner_hbm,
+    coarse_hbm,
+    tiles_hbm,
+    new_owner_hbm,
+    trace_hbm,
+    placed_ref,
+    *refs,
+):
+    out_refs, refs = refs[:-11], refs[-11:]
     owner_ref, coarse_ref, tiles_ref, rows_ref = refs[:4]
-    accs, diags, sems = refs[4:6], refs[6:8], refs[8]
+    accs, diags = refs[4:6], refs[6:8]
+    new_owner_ref, trace_ref, sems = refs[8:]
 
     def place_of(owner):
         if not paired:
             return owner
         other = owner ^ lax.axis_index("face")
-        return (other & 1) * (face_count // 2) + (other >> 1)
+        bits = face_count.bit_length() - 1
+        return sum(((other >> k) & 1) << (bits - 1 - k) for k in range(bits))
 
     tiles = tiles_ref.shape[0]
     copies = [
         pltpu.make_async_copy(owner_hbm, owner_ref, sems.at[0]),
         pltpu.make_async_copy(coarse_hbm, coarse_ref, sems.at[1]),
+        pltpu.make_async_copy(new_owner_hbm, new_owner_ref, sems.at[2]),
+        pltpu.make_async_copy(trace_hbm, trace_ref, sems.at[3]),
+        pltpu.make_async_copy(tiles_hbm, tiles_ref, sems.at[4]),
     ]
-    copies.append(pltpu.make_async_copy(tiles_hbm, tiles_ref, sems.at[2]))
     for copy in copies:
         copy.start()
     for ref in (*accs, *diags):
         ref[...] = jnp.zeros_like(ref)
     for copy in copies:
         copy.wait()
+    placed_ref[...] = place_rows(
+        elem_count, face_count, capacity, new_owner_ref[...], trace_ref[...], placed_ref.shape[0]
+    )
 
     lane = iota((CHUNK, LANES), 1)
     inside = lane < MCOL
@@ -165,9 +174,9 @@
         ).astype(BF16)
 
 
-def join_kernel(kept_ref, came_ref, *out_refs):
-    for k, out_ref in enumerate(out_refs):
-        here = slice(k * OWNER_ROWS, (k + 1) * OWNER_ROWS)
+def join_kernel(kept_ref, came_ref, keep_ref, send_ref):
+    half = keep_ref.shape[0]
+    for out_ref, here in ((keep_ref, slice(0, half)), (send_ref, slice(half, 2 * half))):
         total = kept_ref[here, :].astype(F32) + came_ref[here, :].astype(F32)
         out_ref[...] = total.astype(BF16)
 
@@ -278,7 +287,7 @@
     schur_hbm,
     solved_hbm,
     share_ref,
-    own_ref,
+    left_ref,
     table_ref,
     conn_ref,
     schur_ref,
@@ -290,7 +299,7 @@
     elements = schur_ref.shape[0]
     trace = FACES_PER_ELEM * FACE_COEFFS
     slots = table_ref.shape[0]
-    own = own_ref.shape[0]
+    own = left_ref.shape[0]
     capacity = own // face_count
     my_elem = lax.axis_index("elem")
     copies = [
@@ -304,8 +313,7 @@
     ]
     for copy in copies + parts:
         copy.start()
-    for copy in copies:
-        copy.wait()
+    copies[0].wait()
 
     row = iota((PER_FACE, LANES), 0)
     lane = iota((PER_FACE, LANES), 1)
@@ -318,6 +326,7 @@
 
     high = jnp.full((1, LANES), -1, I32)
     rest = jnp.zeros((1, LANES), I32)
+    hots = []
     for a in range(FACES_PER_ELEM):
         positions = jnp.full((PER_FACE, LANES), -1, I32)
         for e in range(elements):
@@ -328,27 +337,31 @@
             high = jnp.where(here, quotient, high)
             rest = jnp.where(here, remainder, rest)
         hot = jnp.concatenate([positions == lane + k for k in range(0, slots, LANES)], axis=1)
-        vector_ref[:, a * LANES : (a + 1) * LANES] = dot(hot.astype(BF16), table_ref[...])
+        hots.append(hot.astype(BF16))
     names = jnp.where(row == 0, high, jnp.where(row == 1, rest, 0))
     share_ref[NAMED:, :] = names.astype(F32).astype(BF16)
     place = position(my_elem, iota((own, slots), 0))
     pick = (iota((own, slots), 1) == place).astype(BF16)
-    own_ref[...] = dot(pick, table_ref[...]).astype(BF16)
-
-    for copy in parts:
+    for copy in copies[1:]:
         copy.wait()
+    for a, hot in enumerate(hots):
+        vector_ref[:, a * LANES : (a + 1) * LANES] = dot(hot, table_ref[...])
+    left_ref[...] = dot(pick, table_ref[...])
+
     columns = sum_ref[...]
     for e in range(elements):
+        parts[e].wait()
         total = sum(
             schur_ref[e, :, a * LANES : (a + 1) * LANES].astype(F32)
             * vector_ref[e : e + 1, a * LANES : (a + 1) * LANES]
             for a in range(FACES_PER_ELEM)
         )
         sums = jnp.sum(total, axis=1, keepdims=True)
-        columns = columns + jnp.where(wide_lane == e, sums, 0.0)
+        columns = jnp.where(wide_lane == e, columns + sums, columns)
     for a in range(FACES_PER_ELEM):
         shares = columns[a * LANES : (a + 1) * LANES, :].T
         share_ref[a * PER_FACE : (a + 1) * PER_FACE, :] = shares[:PER_FACE].astype(BF16)
+    left_ref[...] = less_shares(left_ref[...], share_ref)
 
 
 def less_shares(left, share_ref):
@@ -367,9 +380,8 @@
     residual_ref[...] = left
 
 
-def coarse_kernel(own_ref, share_ref, *refs):
-    got_refs, (left_ref, out_ref, sum_ref, full_ref) = refs[:-4], refs[-4:]
-    left_ref[...] = less_shares(own_ref[...].astype(F32), share_ref)
+def coarse_kernel(*refs):
+    got_refs, (out_ref, sum_ref, full_ref) = refs[:-3], refs[-3:]
     sum_ref[...] = sum(
         got_ref[k : k + OWNER_ROWS, :].astype(F32)
         for got_ref in got_refs
@@ -421,6 +433,24 @@
     ]
 
 
+def trade(block, distance):
+    count = lax.axis_size("face")
+    return lax.ppermute(block, "face", [(i, i ^ distance) for i in range(count)])
+
+
+def join(kept, came):
+    half = jax.ShapeDtypeStruct((kept.shape[0] // 2, LANES), BF16)
+    return pl.pallas_call(
+        join_kernel,
+        out_shape=(half, half),
+        in_specs=[VMEM] * 2,
+        out_specs=(VMEM, VMEM),
+        compiler_params=params(SMALL),
+        cost_estimate=cost(0, 4 << 20),
+        name="join",
+    )(kept, came)
+
+
 def shards(
     trace_old,
     new_owner,
@@ -448,11 +478,12 @@
 
     blocks = face_count * NC
     sums_shape = (blocks * DENSE, LANES)
-    half_grams = pl.pallas_call(
-        functools.partial(gram_kernel, face_count, paired),
-        out_shape=[jax.ShapeDtypeStruct((blocks * (DENSE + 1) // sides, LANES), BF16)] * sides,
-        in_specs=[ANY] * 3,
-        out_specs=[VMEM] * sides,
+    placed, *half_grams = pl.pallas_call(
+        functools.partial(gram_kernel, elem_count, face_count, capacity, paired),
+        out_shape=[jax.ShapeDtypeStruct((slots, FACE_COEFFS), BF16)]
+        + [jax.ShapeDtypeStruct((blocks * (DENSE + 1) // sides, LANES), BF16)] * sides,
+        in_specs=[ANY] * 5,
+        out_specs=[VMEM] * (1 + sides),
         scratch_shapes=[
             pltpu.SMEM((tile_count,), I32),
             pltpu.SMEM((tile_count,), I32),
@@ -462,55 +493,31 @@
             pltpu.VMEM(sums_shape, F32),
             pltpu.VMEM((blocks, LANES), F32),
             pltpu.VMEM((blocks, LANES), F32),
-            pltpu.SemaphoreType.DMA((3,)),
+            pltpu.VMEM((1, row_count), I32),
+            pltpu.VMEM(trace_old.shape, BF16),
+            pltpu.SemaphoreType.DMA((5,)),
         ],
         compiler_params=params(BIG),
         cost_estimate=cost(4 * tile_count * MROW * MROW * LANES, 12 << 20),
         name="gram",
-    )(mortar_owner.reshape(tile_count), mortar_coarse, mortar_tiles)
+    )(
+        mortar_owner.reshape(tile_count),
+        mortar_coarse,
+        mortar_tiles,
+        new_owner.reshape(1, row_count),
+        trace_old,
+    )
     if paired:
-        came = lax.ppermute(half_grams[1], "face", [(i, i ^ 1) for i in range(face_count)])
-
-    owners, _ = lax.optimization_barrier((new_owner.reshape(1, row_count), half_grams[0]))
-    placed = pl.pallas_call(
-        functools.partial(place_kernel, elem_count, face_count, capacity),
-        out_shape=jax.ShapeDtypeStruct((slots, FACE_COEFFS), BF16),
-        in_specs=[ANY, ANY],
-        out_specs=VMEM,
-        scratch_shapes=[
-            pltpu.VMEM((1, row_count), I32),
-            pltpu.VMEM(trace_old.shape, BF16),
-            pltpu.SemaphoreType.DMA((2,)),
-        ],
-        compiler_params=params(BIG),
-        name="place",
-    )(owners, trace_old)
+        kept, came = half_grams[0], trade(half_grams[1], 1)
     table = lax.all_to_all(
         placed.reshape(devices, capacity, FACE_COEFFS), ("face", "elem"), 0, 0, tiled=True
     ).reshape(slots, FACE_COEFFS)
 
-    if paired:
-        kept, _ = lax.optimization_barrier((half_grams[0], placed))
-        joined = pl.pallas_call(
-            join_kernel,
-            out_shape=[jax.ShapeDtypeStruct((OWNER_ROWS, LANES), BF16)] * (face_count // 2),
-            in_specs=[VMEM] * 2,
-            out_specs=[VMEM] * (face_count // 2),
-            compiler_params=params(SMALL),
-            cost_estimate=cost(0, 4 << 20),
-            name="join",
-        )(kept, came)
-        got = [joined[0]] + [
-            lax.ppermute(joined[k], "face", [(i, i ^ (2 * k)) for i in range(face_count)])
-            for k in range(1, face_count // 2)
-        ]
-        before = joined[0]
-    else:
+    if not paired:
         blocked = half_grams[0].reshape(face_count, OWNER_ROWS, LANES)
         got = [lax.all_to_all(blocked, "face", 0, 0, tiled=True).reshape(-1, LANES)]
-        before = half_grams[0]
-
-    rhs, _ = lax.optimization_barrier((interior_rhs, before))
+
+    rhs, _ = lax.optimization_barrier((interior_rhs, half_grams[0]))
     schur_blocks, solved = pl.pallas_call(
         main_kernel,
         out_shape=(
@@ -542,11 +549,17 @@
         name="condense",
     )(rhs, local_inverse, coupling)
 
-    shares, own_rows = pl.pallas_call(
+    names = connectivity.T
+    if paired and face_count > 2:
+        kept, _ = lax.optimization_barrier((kept, solved))
+        kept, sent = join(kept, came)
+        came = trade(sent, 2)
+        names, kept = lax.optimization_barrier((names, kept))
+    shares, left = pl.pallas_call(
         functools.partial(share_kernel, elem_count, face_count),
         out_shape=(
             jax.ShapeDtypeStruct((SHARE_ROWS, LANES), BF16),
-            jax.ShapeDtypeStruct((own, FACE_COEFFS), BF16),
+            jax.ShapeDtypeStruct((own, FACE_COEFFS), F32),
         ),
         in_specs=[ANY] * 4,
         out_specs=(VMEM, VMEM),
@@ -562,25 +575,16 @@
         compiler_params=params(BIG),
         cost_estimate=cost(0, 8 << 20),
         name="share",
-    )(table, connectivity.T, schur_blocks, solved)
+    )(table, names, schur_blocks, solved)
+
+    if paired:
+        for distance in (1 << k for k in range(2, face_count.bit_length() - 1)):
+            kept, _ = lax.optimization_barrier((kept, shares))
+            kept, sent = join(kept, came)
+            came = trade(sent, distance)
+        got = [kept, came]
 
     all_shares = around(shares, "elem")
-    left, coarse_blocks = pl.pallas_call(
-        coarse_kernel,
-        out_shape=(
-            jax.ShapeDtypeStruct((own, FACE_COEFFS), F32),
-            jax.ShapeDtypeStruct((NC, MROW * MROW), F32),
-        ),
-        in_specs=[VMEM] * (2 + len(got)),
-        out_specs=(VMEM, VMEM),
-        scratch_shapes=[
-            pltpu.VMEM((OWNER_ROWS, LANES), F32),
-            pltpu.VMEM((NC * MROW, LANES), F32),
-        ],
-        compiler_params=params(SMALL),
-        cost_estimate=cost(0, 8 << 20),
-        name="coarse",
-    )(own_rows, shares, *got)
     slot_residual = pl.pallas_call(
         residual_kernel,
         out_shape=jax.ShapeDtypeStruct((own, FACE_COEFFS), F32),
@@ -589,6 +593,21 @@
         compiler_params=params(SMALL),
         name="residual",
     )(left, *all_shares[1:])
+
+    first, slot_residual = lax.optimization_barrier((got[0], slot_residual))
+    coarse_blocks = pl.pallas_call(
+        coarse_kernel,
+        out_shape=jax.ShapeDtypeStruct((NC, MROW * MROW), F32),
+        in_specs=[VMEM] * len(got),
+        out_specs=VMEM,
+        scratch_shapes=[
+            pltpu.VMEM((OWNER_ROWS, LANES), F32),
+            pltpu.VMEM((NC * MROW, LANES), F32),
+        ],
+        compiler_params=params(SMALL),
+        cost_estimate=cost(0, 8 << 20),
+        name="coarse",
+    )(first, *got[1:])
     return schur_blocks, slot_residual, coarse_blocks
 
 

time: 39.1 us -> 39.3 us (level)
  waiting for transfers between devices: 0.27 us -> 2.49 us
  local copies, waits for them, and re-layouts: 3.08 us -> 1.5 us
  Pallas kernels: 20.2 us -> 19.2 us
  starting transfers between devices: 14.3 us -> 15 us
    ppermute x3, waiting for transfers between devices: 0.01 us -> 2.48 us  [around(): lax.ppermute(block, axis, [(i, i ^ k) for i in range(count)])]
    all_to_all x1, starting transfers between devices: 4.89 us -> 7.3 us  [shards(): lax.all_to_all(placed.reshape(devices, capacity, FACE_COEFFS), ('face', '...]
    pallas_call x4, Pallas kernels: 7.43 us -> 5.72 us  [the longest x1 3.74 us: shards(): pl.pallas_call(functools.partial(gram_kernel, elem_count, face_count, cap...]
    ppermute x4 -> x3, starting transfers between devices: 7.49 us -> 5.88 us  [trade(): lax.ppermute(block, 'face', [(i, i ^ distance) for i in range(count)])]
    unnamed x8 -> x6, local copies, waits for them, and re-layouts: 3.08 us -> 1.5 us
    pallas_call x1, Pallas kernels: 3.38 us -> 4.01 us  [shards(): pl.pallas_call(functools.partial(share_kernel, elem_count, face_count), o...]
  transfers between devices with their start and end apart: 8 -> 7, of which waited for: 1 -> 2; matrix products, arithmetic and copies ran while one was open for 0% -> 0% of each run, Pallas kernels for 40% -> 35%
where the time goes in v11:
time: 39.3 us; the launch traced here: 38.9 us
  Pallas kernels  19.2 us (49%)
  starting transfers between devices  15 us (38%)
  waiting for transfers between devices  2.49 us (6%)
  local copies, waits for them, and re-layouts  1.5 us (4%)
  between operations  0.71 us (2%)
    pallas_call x1, Pallas kernels, shards(): pl.pallas_call(main_kernel, out_shape=(jax.ShapeDtypeStruct((elements, tr...  8.63 us
    all_to_all x1, starting transfers between devices, shards(): lax.all_to_all(placed.reshape(devices, capacity, FACE_COEFFS), ('face', '...  7.3 us
    ppermute x3, starting transfers between devices, trade(): lax.ppermute(block, 'face', [(i, i ^ distance) for i in range(count)])  5.88 us
    pallas_call x1, Pallas kernels, shards(): pl.pallas_call(functools.partial(share_kernel, elem_count, face_count), o...  4.01 us
    pallas_call x1, Pallas kernels, shards(): pl.pallas_call(functools.partial(gram_kernel, elem_count, face_count, cap...  3.74 us
    ppermute x3, waiting for transfers between devices, around(): lax.ppermute(block, axis, [(i, i ^ k) for i in range(count)])  2.48 us
    pallas_call x1, Pallas kernels, shards(): pl.pallas_call(coarse_kernel, out_shape=jax.ShapeDtypeStruct((NC, MROW *...  1.87 us
    ppermute x3, starting transfers between devices, around(): lax.ppermute(block, axis, [(i, i ^ k) for i in range(count)])  1.86 us
  transfers between devices with their start and end apart: 7, of which 2 were waited for; matrix products, arithmetic and copies ran while one was open for 0% of the time, Pallas kernels for 35%

profile of v11, /device:TPU:0, one launch (start us, length us, event | category | flops | bytes accessed | tf_op | source)
XLA Modules:
  0.0 38.9 jit_solution(109151566632371268)
XLA Ops:
  0.6 3.7 %gram.1 = (bf16[512,128]{1,0:T(8,128)(2,1)}, bf16[1088,128]{1,0:T(8,128)(2,1)}, bf16[1088,128]{1,0:T(8,128)(2,1)}) custom-call(s32[96]{0:T(128)} %bitcast.8, s32[96]{0:T(128)} %coarse_hbm.1, bf16[96,6144]{1,0:T(8,128)(2,1)} %tiles_hbm.1, s32[1,64]{1,0:T(1,128)} %bitcast.9, bf16[64,128]{1,0:T(8,128)(2,1)} %trace_hbm.1), custom_call_target="tpu_custom_call" | custom-call | flops 201326592 | bytes 12582912 | tf_op jit(solution)/shard_map/gram/pallas_call | solution.py:481
  4.4 7.3 %all-to-all-start = ((bf16[32,16,128]{2,1,0:T(8,128)(2,1)}), bf16[32,16,128]{2,1,0:T(8,128)(2,1)S(1)}, u32[]{:S(2)}, u32[]{:S(2)}) async-start(bf16[32,16,128]{2,1,0:T(8,128)(2,1)} %bitcast.6), calls=%async_computation | async-start | bytes 262144 | tf_op jit(solution)/shard_map/all_to_all | solution.py:512
  11.7 1.8 %collective-permute-start = (bf16[1088,128]{1,0:T(8,128)(2,1)}, bf16[1088,128]{1,0:T(8,128)(2,1)S(1)}, u32[]{:S(2)}, u32[]{:S(2)}) collective-permute-start(bf16[1088,128]{1,0:T(8,128)(2,1)} %get-tuple-element.26), channel_id=1, source_target_pairs={{0,4},{4,0},{8,12},{12,8},{16,20},{20,16},{24,28},{28,24},{1,5},{5... | collective-permute-start | bytes 835592 | tf_op jit(solution)/shard_map/ppermute | solution.py:438
  13.5 0.0 copy-start
  13.5 8.6 %condense.1 = (bf16[9,384,384]{2,1,0:T(8,128)(2,1)}, f32[384,128]{1,0:T(8,128)}) custom-call(bf16[9,512]{1,0:T(8,128)(2,1)} %rhs_hbm, bf16[9,512,512]{2,1,0:T(8,128)(2,1)} %inverse_hbm.1, bf16[9,512,384]{2,1,0:T(8,128)(2,1)} %coupling_hbm.1), custom_call_target="tpu_custom_call" | custom-call | flops 3170893824 | bytes 10911744 | tf_op jit(solution)/shard_map/condense/pallas_call | solution.py:521
  22.2 0.0 collective-permute-done.came_ref
  22.2 0.0 copy-done
  22.2 0.1 join.2
  22.3 1.6 %collective-permute-start.1 = (bf16[544,128]{1,0:T(8,128)(2,1)S(1)}, bf16[544,128]{1,0:T(8,128)(2,1)S(1)}, u32[]{:S(2)}, u32[]{:S(2)}) collective-permute-start(bf16[544,128]{1,0:T(8,128)(2,1)S(1)} %get-tuple-element.33), channel_id=1, source_target_pairs={{0,8},{4,12},{8,0},{12,4},{16,24},{20,28},{24,16},{28,20},{1,9},{5... | collective-permute-start | bytes 417800 | tf_op jit(solution)/shard_map/ppermute | solution.py:438
  23.9 0.0 all-to-all-done
  23.9 0.7 %copy-done.2 = bf16[32,16,128]{2,1,0:T(8,128)(2,1)} copy-done((bf16[32,16,128]{2,1,0:T(8,128)(2,1)}, bf16[32,16,128]{2,1,0:T(8,128)(2,1)S(1)}, u32[]{:S(2)}) %copy-start.2) | copy-done | bytes 131096
  24.5 4.0 %share.1 = (bf16[64,128]{1,0:T(8,128)(2,1)}, f32[128,128]{1,0:T(8,128)}) custom-call(bf16[512,128]{1,0:T(8,128)(2,1)} %bitcast.5, s32[3,9]{1,0:T(4,128)} %bitcast.7, bf16[9,384,384]{2,1,0:T(8,128)(2,1)} %get-tuple-element.18.schur_hbm, f32[384,128]{1,0:T(8,128)} %get-tuple-element.24.solved_hbm), custom_call_target="tpu_custom_call" | custom-call | bytes 8388608 | tf_op jit(solution)/shard_map/share/pallas_call | solution.py:558
  28.5 0.0 collective-permute-done.1.came_ref
  28.6 2.4 %collective-permute-start.5 = (bf16[272,128]{1,0:T(8,128)(2,1)S(1)}, bf16[272,128]{1,0:T(8,128)(2,1)S(1)}, u32[]{:S(2)}, u32[]{:S(2)}) collective-permute-start(bf16[272,128]{1,0:T(8,128)(2,1)S(1)} %get-tuple-element.38), channel_id=1, source_target_pairs={{0,16},{4,20},{8,24},{12,28},{16,0},{20,4},{24,8},{28,12},{1,17},{... | collective-permute-start | bytes 208904 | tf_op jit(solution)/shard_map/ppermute | solution.py:438
  31.0 0.4 %collective-permute-start.4 = (bf16[64,128]{1,0:T(8,128)(2,1)}, bf16[64,128]{1,0:T(8,128)(2,1)S(1)}, u32[]{:S(2)}, u32[]{:S(2)}) collective-permute-start(bf16[64,128]{1,0:T(8,128)(2,1)} %get-tuple-element.31), channel_id=1, source_target_pairs={{0,3},{1,2},{2,1},{3,0},{4,7},{5,6},{6,5},{7,4},{8,11},{9,10},{10,... | collective-permute-start | bytes 49160 | tf_op jit(solution)/shard_map/ppermute | solution.py:432
  31.4 1.1 %collective-permute-start.3 = (bf16[64,128]{1,0:T(8,128)(2,1)}, bf16[64,128]{1,0:T(8,128)(2,1)S(1)}, u32[]{:S(2)}, u32[]{:S(2)}) collective-permute-start(bf16[64,128]{1,0:T(8,128)(2,1)} %get-tuple-element.31), channel_id=1, source_target_pairs={{0,2},{1,3},{2,0},{3,1},{4,6},{5,7},{6,4},{7,5},{8,10},{9,11},{10,... | collective-permute-start | bytes 49160 | tf_op jit(solution)/shard_map/ppermute | solution.py:432
  32.6 0.3 collective-permute-start.2
  32.9 1.7 %collective-permute-done.4.refs_2_ = bf16[64,128]{1,0:T(8,128)(2,1)S(1)} collective-permute-done((bf16[64,128]{1,0:T(8,128)(2,1)}, bf16[64,128]{1,0:T(8,128)(2,1)S(1)}, u32[]{:S(2)}, u32[]{:S(2)}) %collective-permute-start.4) | collective-permute-done | bytes 16416 | tf_op jit(solution)/shard_map/ppermute | solution.py:432
  34.6 0.8 %collective-permute-done.3.refs_1_ = bf16[64,128]{1,0:T(8,128)(2,1)S(1)} collective-permute-done((bf16[64,128]{1,0:T(8,128)(2,1)}, bf16[64,128]{1,0:T(8,128)(2,1)S(1)}, u32[]{:S(2)}, u32[]{:S(2)}) %collective-permute-start.3) | collective-permute-done | bytes 16416 | tf_op jit(solution)/shard_map/ppermute | solution.py:432
  35.4 0.0 collective-permute-done.2.refs_0_
  35.4 0.8 %copy-done.1 = f32[128,128]{1,0:T(8,128)S(1)} copy-done((f32[128,128]{1,0:T(8,128)S(1)}, f32[128,128]{1,0:T(8,128)}, u32[]{:S(2)}) %copy-start.1) | copy-done | bytes 65560
  36.2 0.8 %residual.1 = f32[128,128]{1,0:T(8,128)} custom-call(f32[128,128]{1,0:T(8,128)S(1)} %copy-done.1, bf16[64,128]{1,0:T(8,128)(2,1)S(1)} %collective-permute-done.2.refs_0_, bf16[64,128]{1,0:T(8,128)(2,1)S(1)} %collective-permute-done.3.refs_1_, bf16[64,128]{1,0:T(8,128)(2,1)S(1)} %collective-permute-done.4.refs_2_), custom_call_target="tpu_custom_call" | custom-call | tf_op jit(solution)/shard_map/residual/pallas_call | solution.py:588
  37.0 0.0 collective-permute-done.5.refs_1_
  37.0 1.9 %coarse.1 = f32[16,4096]{1,0:T(8,128)} custom-call(bf16[272,128]{1,0:T(8,128)(2,1)S(1)} %get-tuple-element.37.refs_0_, bf16[272,128]{1,0:T(8,128)(2,1)S(1)} %collective-permute-done.5.refs_1_), custom_call_target="tpu_custom_call" | custom-call | bytes 8388608 | tf_op jit(solution)/shard_map/coarse/pallas_call | solution.py:598
  (3 shorter events, 0.0 us)
Async XLA Ops:
  4.4 19.5 %all-to-all-start = ((bf16[32,16,128]{2,1,0:T(8,128)(2,1)}), bf16[32,16,128]{2,1,0:T(8,128)(2,1)S(1)}, u32[]{:S(2)}, u32[]{:S(2)}) async-start(bf16[32,16,128]{2,1,0:T(8,128)(2,1)} %bitcast.6), calls=%async_computation | async-start | bytes 262144 | tf_op jit(solution)/shard_map/all_to_all | solution.py:512
  11.7 10.5 %collective-permute-start = (bf16[1088,128]{1,0:T(8,128)(2,1)}, bf16[1088,128]{1,0:T(8,128)(2,1)S(1)}, u32[]{:S(2)}, u32[]{:S(2)}) collective-permute-start(bf16[1088,128]{1,0:T(8,128)(2,1)} %get-tuple-element.26), channel_id=1, source_target_pairs={{0,4},{4,0},{8,12},{12,8},{16,20},{20,16},{24,28},{28,24},{1,5},{5... | collective-permute-start | bytes 835592 | tf_op jit(solution)/shard_map/ppermute | solution.py:438
  13.5 8.7 %copy-start = (bf16[1088,128]{1,0:T(8,128)(2,1)S(1)}, bf16[1088,128]{1,0:T(8,128)(2,1)}, u32[]{:S(2)}) copy-start(bf16[1088,128]{1,0:T(8,128)(2,1)} %get-tuple-element.25.kept_ref) | copy-start | bytes 835588
  22.3 6.3 %collective-permute-start.1 = (bf16[544,128]{1,0:T(8,128)(2,1)S(1)}, bf16[544,128]{1,0:T(8,128)(2,1)S(1)}, u32[]{:S(2)}, u32[]{:S(2)}) collective-permute-start(bf16[544,128]{1,0:T(8,128)(2,1)S(1)} %get-tuple-element.33), channel_id=1, source_target_pairs={{0,8},{4,12},{8,0},{12,4},{16,24},{20,28},{24,16},{28,20},{1,9},{5... | collective-permute-start | bytes 417800 | tf_op jit(solution)/shard_map/ppermute | solution.py:438
  23.9 0.7 %copy-start.2 = (bf16[32,16,128]{2,1,0:T(8,128)(2,1)}, bf16[32,16,128]{2,1,0:T(8,128)(2,1)S(1)}, u32[]{:S(2)}) copy-start(bf16[32,16,128]{2,1,0:T(8,128)(2,1)S(1)} %all-to-all-done) | copy-start | bytes 393220
  28.6 8.4 %collective-permute-start.5 = (bf16[272,128]{1,0:T(8,128)(2,1)S(1)}, bf16[272,128]{1,0:T(8,128)(2,1)S(1)}, u32[]{:S(2)}, u32[]{:S(2)}) collective-permute-start(bf16[272,128]{1,0:T(8,128)(2,1)S(1)} %get-tuple-element.38), channel_id=1, source_target_pairs={{0,16},{4,20},{8,24},{12,28},{16,0},{20,4},{24,8},{28,12},{1,17},{... | collective-permute-start | bytes 208904 | tf_op jit(solution)/shard_map/ppermute | solution.py:438
  31.0 3.5 %collective-permute-start.4 = (bf16[64,128]{1,0:T(8,128)(2,1)}, bf16[64,128]{1,0:T(8,128)(2,1)S(1)}, u32[]{:S(2)}, u32[]{:S(2)}) collective-permute-start(bf16[64,128]{1,0:T(8,128)(2,1)} %get-tuple-element.31), channel_id=1, source_target_pairs={{0,3},{1,2},{2,1},{3,0},{4,7},{5,6},{6,5},{7,4},{8,11},{9,10},{10,... | collective-permute-start | bytes 49160 | tf_op jit(solution)/shard_map/ppermute | solution.py:432
  31.4 3.9 %collective-permute-start.3 = (bf16[64,128]{1,0:T(8,128)(2,1)}, bf16[64,128]{1,0:T(8,128)(2,1)S(1)}, u32[]{:S(2)}, u32[]{:S(2)}) collective-permute-start(bf16[64,128]{1,0:T(8,128)(2,1)} %get-tuple-element.31), channel_id=1, source_target_pairs={{0,2},{1,3},{2,0},{3,1},{4,6},{5,7},{6,4},{7,5},{8,10},{9,11},{10,... | collective-permute-start | bytes 49160 | tf_op jit(solution)/shard_map/ppermute | solution.py:432
  32.6 2.8 %collective-permute-start.2 = (bf16[64,128]{1,0:T(8,128)(2,1)}, bf16[64,128]{1,0:T(8,128)(2,1)S(1)}, u32[]{:S(2)}, u32[]{:S(2)}) collective-permute-start(bf16[64,128]{1,0:T(8,128)(2,1)} %get-tuple-element.31), channel_id=1, source_target_pairs={{0,1},{1,0},{2,3},{3,2},{4,5},{5,4},{6,7},{7,6},{8,9},{9,8},{10,11... | collective-permute-start | bytes 49160 | tf_op jit(solution)/shard_map/ppermute | solution.py:432
  35.4 0.8 %copy-start.1 = (f32[128,128]{1,0:T(8,128)S(1)}, f32[128,128]{1,0:T(8,128)}, u32[]{:S(2)}) copy-start(f32[128,128]{1,0:T(8,128)} %get-tuple-element.35.left_ref) | copy-start | bytes 196612

commit v12 on v9

--- a/solution.py
+++ b/solution.py
@@ -87,7 +87,12 @@
         if not paired:
             return owner
         other = owner ^ lax.axis_index("face")
-        return (other & 1) * (face_count // 2) + (other >> 1)
+        bits = face_count.bit_length() - 1
+        odd = lax.axis_index("elem") & 1
+        place = [(other >> k) & 1 for k in range(bits)]
+        if bits > 1:
+            place[:2] = (jnp.where(odd == 1, place[1 - k], place[k]) for k in range(2))
+        return sum(bit << (bits - 1 - k) for k, bit in enumerate(place))
 
     tiles = tiles_ref.shape[0]
     copies = [
@@ -173,9 +178,9 @@
         ).astype(BF16)
 
 
-def join_kernel(kept_ref, came_ref, *out_refs):
-    for k, out_ref in enumerate(out_refs):
-        here = slice(k * OWNER_ROWS, (k + 1) * OWNER_ROWS)
+def join_kernel(kept_ref, came_ref, keep_ref, send_ref):
+    half = keep_ref.shape[0]
+    for out_ref, here in ((keep_ref, slice(0, half)), (send_ref, slice(half, 2 * half))):
         total = kept_ref[here, :].astype(F32) + came_ref[here, :].astype(F32)
         out_ref[...] = total.astype(BF16)
 
@@ -409,6 +414,31 @@
     ]
 
 
+def trade(block, stage):
+    face_count, elem_count = lax.axis_size("face"), lax.axis_size("elem")
+    bits = face_count.bit_length() - 1
+    pairs = []
+    for face in range(face_count):
+        for elem in range(elem_count):
+            swapped = bits > 1 and elem % 2 == 1 and stage < 2
+            other = face ^ (1 << (1 - stage if swapped else stage))
+            pairs.append((face * elem_count + elem, other * elem_count + elem))
+    return lax.ppermute(block, ("face", "elem"), pairs)
+
+
+def join(kept, came):
+    half = jax.ShapeDtypeStruct((kept.shape[0] // 2, LANES), BF16)
+    return pl.pallas_call(
+        join_kernel,
+        out_shape=(half, half),
+        in_specs=[VMEM] * 2,
+        out_specs=(VMEM, VMEM),
+        compiler_params=params(SMALL),
+        cost_estimate=cost(0, 4 << 20),
+        name="join",
+    )(kept, came)
+
+
 def shards(
     trace_old,
     new_owner,
@@ -466,32 +496,22 @@
         trace_old,
     )
     if paired:
-        came = lax.ppermute(half_grams[1], "face", [(i, i ^ 1) for i in range(face_count)])
+        kept, came = half_grams[0], trade(half_grams[1], 0)
     table = lax.all_to_all(
         placed.reshape(devices, capacity, FACE_COEFFS), ("face", "elem"), 0, 0, tiled=True
     ).reshape(slots, FACE_COEFFS)
 
     if paired:
-        joined = pl.pallas_call(
-            join_kernel,
-            out_shape=[jax.ShapeDtypeStruct((OWNER_ROWS, LANES), BF16)] * (face_count // 2),
-            in_specs=[VMEM] * 2,
-            out_specs=[VMEM] * (face_count // 2),
-            compiler_params=params(SMALL),
-            cost_estimate=cost(0, 4 << 20),
-            name="join",
-        )(half_grams[0], came)
-        got = [joined[0]] + [
-            lax.ppermute(joined[k], "face", [(i, i ^ (2 * k)) for i in range(face_count)])
-            for k in range(1, face_count // 2)
-        ]
-        before = joined[0]
+        for stage in range(1, face_count.bit_length() - 1):
+            kept, sent = join(kept, came)
+            came = trade(sent, stage)
+        got = [kept, came]
     else:
         blocked = half_grams[0].reshape(face_count, OWNER_ROWS, LANES)
         got = [lax.all_to_all(blocked, "face", 0, 0, tiled=True).reshape(-1, LANES)]
-        before = half_grams[0]
-
-    rhs, _ = lax.optimization_barrier((interior_rhs, before))
+        kept = half_grams[0]
+
+    rhs, _ = lax.optimization_barrier((interior_rhs, kept))
     schur_blocks, shares, left = pl.pallas_call(
         functools.partial(main_kernel, elem_count, face_count),
         out_shape=(

time: 36.5 us -> 37.7 us (1.033)
  waiting for transfers between devices: 3.21 us -> 4.82 us
  starting transfers between devices: 14.3 us -> 13.8 us
    ppermute x4 -> x3, waiting for transfers between devices: 1.97 us -> 4.14 us  [trade(): return lax.ppermute(block, ('face', 'elem'), pairs)]
    all_to_all x1, waiting for transfers between devices: 0.78 us -> 0.01 us  [shards(): lax.all_to_all(placed.reshape(devices, capacity, FACE_COEFFS), ('face', '...]
    ppermute x4 -> x3, starting transfers between devices: 7.5 us -> 6.99 us  [trade(): return lax.ppermute(block, ('face', 'elem'), pairs)]
  transfers between devices with their start and end apart: 8 -> 7, of which waited for: 3 -> 2; matrix products, arithmetic and copies ran while one was open for 0% -> 0% of each run, Pallas kernels for 30% -> 30%
where the time goes in v12:
time: 37.7 us; the launch traced here: 37.3 us
  Pallas kernels  15.6 us (41%)
  starting transfers between devices  13.8 us (37%)
  waiting for transfers between devices  4.82 us (13%)
  local copies, waits for them, and re-layouts  2.45 us (6%)
  between operations  0.69 us (2%)
    pallas_call x1, Pallas kernels, shards(): pl.pallas_call(functools.partial(main_kernel, elem_count, face_count), ou...  9.07 us
    ppermute x3, starting transfers between devices, trade(): return lax.ppermute(block, ('face', 'elem'), pairs)  6.99 us
    all_to_all x1, starting transfers between devices, shards(): lax.all_to_all(placed.reshape(devices, capacity, FACE_COEFFS), ('face', '...  4.9 us
    ppermute x3, waiting for transfers between devices, trade(): return lax.ppermute(block, ('face', 'elem'), pairs)  4.14 us
    pallas_call x1, Pallas kernels, shards(): pl.pallas_call(functools.partial(gram_kernel, elem_count, face_count, cap...  3.72 us
    unnamed x6, local copies, waits for them, and re-layouts  2.45 us
    ppermute x3, starting transfers between devices, around(): lax.ppermute(block, axis, [(i, i ^ k) for i in range(count)])  1.93 us
    pallas_call x1, Pallas kernels, shards(): pl.pallas_call(coarse_kernel, out_shape=jax.ShapeDtypeStruct((NC, MROW *...  1.87 us
  transfers between devices with their start and end apart: 7, of which 2 were waited for; matrix products, arithmetic and copies ran while one was open for 0% of the time, Pallas kernels for 30%

profile of v12, /device:TPU:0, one launch (start us, length us, event | category | flops | bytes accessed | tf_op | source)
XLA Modules:
  0.0 37.3 jit_solution(5901659638294750283)
XLA Ops:
  0.6 3.7 %gram.1 = (bf16[512,128]{1,0:T(8,128)(2,1)}, bf16[1088,128]{1,0:T(8,128)(2,1)}, bf16[1088,128]{1,0:T(8,128)(2,1)}) custom-call(s32[96]{0:T(128)} %bitcast.7, s32[96]{0:T(128)} %coarse_hbm.1, bf16[96,6144]{1,0:T(8,128)(2,1)} %tiles_hbm.1, s32[1,64]{1,0:T(1,128)} %bitcast.8, bf16[64,128]{1,0:T(8,128)(2,1)} %trace_hbm.1), custom_call_target="tpu_custom_call" | custom-call | flops 201326592 | bytes 12582912 | tf_op jit(solution)/shard_map/gram/pallas_call | solution.py:469
  4.4 3.0 %collective-permute-start = (bf16[1088,128]{1,0:T(8,128)(2,1)}, bf16[1088,128]{1,0:T(8,128)(2,1)S(1)}, u32[]{:S(2)}, u32[]{:S(2)}) collective-permute-start(bf16[1088,128]{1,0:T(8,128)(2,1)} %get-tuple-element.18), channel_id=1, source_target_pairs={{0,4},{1,9},{2,6},{3,11},{4,0},{5,13},{6,2},{7,15},{8,12},{9,1},{1... | collective-permute-start | bytes 835592 | tf_op jit(solution)/shard_map/ppermute | solution.py:426
  7.4 4.9 %all-to-all-start = ((bf16[32,16,128]{2,1,0:T(8,128)(2,1)}), bf16[32,16,128]{2,1,0:T(8,128)(2,1)S(1)}, u32[]{:S(2)}, u32[]{:S(2)}) async-start(bf16[32,16,128]{2,1,0:T(8,128)(2,1)} %bitcast.6), calls=%async_computation | async-start | bytes 262144 | tf_op jit(solution)/shard_map/all_to_all | solution.py:500
  12.3 0.0 collective-permute-done.came_ref
  12.3 0.0 copy-start
  12.3 0.9 %copy-done = bf16[1088,128]{1,0:T(8,128)(2,1)S(1)} copy-done((bf16[1088,128]{1,0:T(8,128)(2,1)S(1)}, bf16[1088,128]{1,0:T(8,128)(2,1)}, u32[]{:S(2)}) %copy-start) | copy-done | bytes 278552
  13.3 0.1 join.2
  13.3 2.0 %collective-permute-start.1 = (bf16[544,128]{1,0:T(8,128)(2,1)S(1)}, bf16[544,128]{1,0:T(8,128)(2,1)S(1)}, u32[]{:S(2)}, u32[]{:S(2)}) collective-permute-start(bf16[544,128]{1,0:T(8,128)(2,1)S(1)} %get-tuple-element.20), channel_id=1, source_target_pairs={{0,8},{1,5},{2,10},{3,7},{4,12},{5,1},{6,14},{7,3},{8,0},{9,13},{1... | collective-permute-start | bytes 417800 | tf_op jit(solution)/shard_map/ppermute | solution.py:426
  15.3 4.1 %collective-permute-done.1.came_ref = bf16[544,128]{1,0:T(8,128)(2,1)S(1)} collective-permute-done((bf16[544,128]{1,0:T(8,128)(2,1)S(1)}, bf16[544,128]{1,0:T(8,128)(2,1)S(1)}, u32[]{:S(2)}, u32[]{:S(2)}) %collective-permute-start.1) | collective-permute-done | bytes 139296 | tf_op jit(solution)/shard_map/ppermute | solution.py:426
  19.5 2.0 %collective-permute-start.2 = (bf16[272,128]{1,0:T(8,128)(2,1)S(1)}, bf16[272,128]{1,0:T(8,128)(2,1)S(1)}, u32[]{:S(2)}, u32[]{:S(2)}) collective-permute-start(bf16[272,128]{1,0:T(8,128)(2,1)S(1)} %get-tuple-element.25), channel_id=1, source_target_pairs={{0,16},{1,17},{2,18},{3,19},{4,20},{5,21},{6,22},{7,23},{8,24},{9,... | collective-permute-start | bytes 208904 | tf_op jit(solution)/shard_map/ppermute | solution.py:426
  21.5 0.0 all-to-all-done
  21.5 0.0 copy-start.2
  21.5 0.7 %copy-done.2 = bf16[32,16,128]{2,1,0:T(8,128)(2,1)} copy-done((bf16[32,16,128]{2,1,0:T(8,128)(2,1)}, bf16[32,16,128]{2,1,0:T(8,128)(2,1)S(1)}, u32[]{:S(2)}) %copy-start.2) | copy-done | bytes 131096
  22.1 9.1 %condense.1 = (bf16[9,384,384]{2,1,0:T(8,128)(2,1)}, bf16[64,128]{1,0:T(8,128)(2,1)}, f32[128,128]{1,0:T(8,128)}) custom-call(bf16[512,128]{1,0:T(8,128)(2,1)} %bitcast.5, s32[3,9]{1,0:T(4,128)} %bitcast.9, bf16[9,512]{1,0:T(8,128)(2,1)} %rhs_hbm, bf16[9,512,512]{2,1,0:T(8,128)(2,1)} %inverse_hbm.1, bf16[9,512,384]{2,1,0:T(8,128)(2,1)} %coupling_hbm.1), custom_call_target="tpu_custom_call" | custom-call | flops 3170893824 | bytes 10911744 | tf_op jit(solution)/shard_map/condense/pallas_call | solution.py:515
  31.2 0.5 %collective-permute-start.5 = (bf16[64,128]{1,0:T(8,128)(2,1)}, bf16[64,128]{1,0:T(8,128)(2,1)S(1)}, u32[]{:S(2)}, u32[]{:S(2)}) collective-permute-start(bf16[64,128]{1,0:T(8,128)(2,1)} %get-tuple-element.27), channel_id=1, source_target_pairs={{0,3},{1,2},{2,1},{3,0},{4,7},{5,6},{6,5},{7,4},{8,11},{9,10},{10,... | collective-permute-start | bytes 49160 | tf_op jit(solution)/shard_map/ppermute | solution.py:413
  31.7 1.1 %collective-permute-start.4 = (bf16[64,128]{1,0:T(8,128)(2,1)}, bf16[64,128]{1,0:T(8,128)(2,1)S(1)}, u32[]{:S(2)}, u32[]{:S(2)}) collective-permute-start(bf16[64,128]{1,0:T(8,128)(2,1)} %get-tuple-element.27), channel_id=1, source_target_pairs={{0,2},{1,3},{2,0},{3,1},{4,6},{5,7},{6,4},{7,5},{8,10},{9,11},{10,... | collective-permute-start | bytes 49160 | tf_op jit(solution)/shard_map/ppermute | solution.py:413
  32.8 0.3 collective-permute-start.3
  33.1 0.0 collective-permute-done.2.refs_1_
  33.1 1.9 %coarse.1 = f32[16,4096]{1,0:T(8,128)} custom-call(bf16[272,128]{1,0:T(8,128)(2,1)S(1)} %get-tuple-element.21.refs_0_, bf16[272,128]{1,0:T(8,128)(2,1)S(1)} %collective-permute-done.2.refs_1_), custom_call_target="tpu_custom_call" | custom-call | bytes 8388608 | tf_op jit(solution)/shard_map/coarse/pallas_call | solution.py:552
  35.0 0.0 collective-permute-done.5.refs_2_
  35.0 0.7 %collective-permute-done.4.refs_1_ = bf16[64,128]{1,0:T(8,128)(2,1)S(1)} collective-permute-done((bf16[64,128]{1,0:T(8,128)(2,1)}, bf16[64,128]{1,0:T(8,128)(2,1)S(1)}, u32[]{:S(2)}, u32[]{:S(2)}) %collective-permute-start.4) | collective-permute-done | bytes 16416 | tf_op jit(solution)/shard_map/ppermute | solution.py:413
  35.7 0.0 collective-permute-done.3.refs_0_
  35.7 0.8 %copy-done.1 = f32[128,128]{1,0:T(8,128)S(1)} copy-done((f32[128,128]{1,0:T(8,128)S(1)}, f32[128,128]{1,0:T(8,128)}, u32[]{:S(2)}) %copy-start.1) | copy-done | bytes 65560
  36.5 0.8 %residual.1 = f32[128,128]{1,0:T(8,128)} custom-call(f32[128,128]{1,0:T(8,128)S(1)} %copy-done.1, bf16[64,128]{1,0:T(8,128)(2,1)S(1)} %collective-permute-done.3.refs_0_, bf16[64,128]{1,0:T(8,128)(2,1)S(1)} %collective-permute-done.4.refs_1_, bf16[64,128]{1,0:T(8,128)(2,1)S(1)} %collective-permute-done.5.refs_2_), custom_call_target="tpu_custom_call" | custom-call | tf_op jit(solution)/shard_map/residual/pallas_call | solution.py:566
  (2 shorter events, 0.0 us)
Async XLA Ops:
  4.4 7.9 %collective-permute-start = (bf16[1088,128]{1,0:T(8,128)(2,1)}, bf16[1088,128]{1,0:T(8,128)(2,1)S(1)}, u32[]{:S(2)}, u32[]{:S(2)}) collective-permute-start(bf16[1088,128]{1,0:T(8,128)(2,1)} %get-tuple-element.18), channel_id=1, source_target_pairs={{0,4},{1,9},{2,6},{3,11},{4,0},{5,13},{6,2},{7,15},{8,12},{9,1},{1... | collective-permute-start | bytes 835592 | tf_op jit(solution)/shard_map/ppermute | solution.py:426
  7.4 14.1 %all-to-all-start = ((bf16[32,16,128]{2,1,0:T(8,128)(2,1)}), bf16[32,16,128]{2,1,0:T(8,128)(2,1)S(1)}, u32[]{:S(2)}, u32[]{:S(2)}) async-start(bf16[32,16,128]{2,1,0:T(8,128)(2,1)} %bitcast.6), calls=%async_computation | async-start | bytes 262144 | tf_op jit(solution)/shard_map/all_to_all | solution.py:500
  12.3 1.0 %copy-start = (bf16[1088,128]{1,0:T(8,128)(2,1)S(1)}, bf16[1088,128]{1,0:T(8,128)(2,1)}, u32[]{:S(2)}) copy-start(bf16[1088,128]{1,0:T(8,128)(2,1)} %get-tuple-element.17.kept_ref) | copy-start | bytes 835588
  13.3 6.1 %collective-permute-start.1 = (bf16[544,128]{1,0:T(8,128)(2,1)S(1)}, bf16[544,128]{1,0:T(8,128)(2,1)S(1)}, u32[]{:S(2)}, u32[]{:S(2)}) collective-permute-start(bf16[544,128]{1,0:T(8,128)(2,1)S(1)} %get-tuple-element.20), channel_id=1, source_target_pairs={{0,8},{1,5},{2,10},{3,7},{4,12},{5,1},{6,14},{7,3},{8,0},{9,13},{1... | collective-permute-start | bytes 417800 | tf_op jit(solution)/shard_map/ppermute | solution.py:426
  19.5 13.7 %collective-permute-start.2 = (bf16[272,128]{1,0:T(8,128)(2,1)S(1)}, bf16[272,128]{1,0:T(8,128)(2,1)S(1)}, u32[]{:S(2)}, u32[]{:S(2)}) collective-permute-start(bf16[272,128]{1,0:T(8,128)(2,1)S(1)} %get-tuple-element.25), channel_id=1, source_target_pairs={{0,16},{1,17},{2,18},{3,19},{4,20},{5,21},{6,22},{7,23},{8,24},{9,... | collective-permute-start | bytes 208904 | tf_op jit(solution)/shard_map/ppermute | solution.py:426
  21.5 0.7 %copy-start.2 = (bf16[32,16,128]{2,1,0:T(8,128)(2,1)}, bf16[32,16,128]{2,1,0:T(8,128)(2,1)S(1)}, u32[]{:S(2)}) copy-start(bf16[32,16,128]{2,1,0:T(8,128)(2,1)S(1)} %all-to-all-done) | copy-start | bytes 393220
  31.2 3.8 %collective-permute-start.5 = (bf16[64,128]{1,0:T(8,128)(2,1)}, bf16[64,128]{1,0:T(8,128)(2,1)S(1)}, u32[]{:S(2)}, u32[]{:S(2)}) collective-permute-start(bf16[64,128]{1,0:T(8,128)(2,1)} %get-tuple-element.27), channel_id=1, source_target_pairs={{0,3},{1,2},{2,1},{3,0},{4,7},{5,6},{6,5},{7,4},{8,11},{9,10},{10,... | collective-permute-start | bytes 49160 | tf_op jit(solution)/shard_map/ppermute | solution.py:413
  31.7 3.9 %collective-permute-start.4 = (bf16[64,128]{1,0:T(8,128)(2,1)}, bf16[64,128]{1,0:T(8,128)(2,1)S(1)}, u32[]{:S(2)}, u32[]{:S(2)}) collective-permute-start(bf16[64,128]{1,0:T(8,128)(2,1)} %get-tuple-element.27), channel_id=1, source_target_pairs={{0,2},{1,3},{2,0},{3,1},{4,6},{5,7},{6,4},{7,5},{8,10},{9,11},{10,... | collective-permute-start | bytes 49160 | tf_op jit(solution)/shard_map/ppermute | solution.py:413
  32.8 2.8 %collective-permute-start.3 = (bf16[64,128]{1,0:T(8,128)(2,1)}, bf16[64,128]{1,0:T(8,128)(2,1)S(1)}, u32[]{:S(2)}, u32[]{:S(2)}) collective-permute-start(bf16[64,128]{1,0:T(8,128)(2,1)} %get-tuple-element.27), channel_id=1, source_target_pairs={{0,1},{1,0},{2,3},{3,2},{4,5},{5,4},{6,7},{7,6},{8,9},{9,8},{10,11... | collective-permute-start | bytes 49160 | tf_op jit(solution)/shard_map/ppermute | solution.py:413
  35.7 0.8 %copy-start.1 = (f32[128,128]{1,0:T(8,128)S(1)}, f32[128,128]{1,0:T(8,128)}, u32[]{:S(2)}) copy-start(f32[128,128]{1,0:T(8,128)} %get-tuple-element.26.left_ref) | copy-start | bytes 196612

commit v13 on v9

--- a/solution.py
+++ b/solution.py
@@ -87,7 +87,12 @@
         if not paired:
             return owner
         other = owner ^ lax.axis_index("face")
-        return (other & 1) * (face_count // 2) + (other >> 1)
+        bits = face_count.bit_length() - 1
+        odd = lax.axis_index("elem") & 1
+        place = [(other >> k) & 1 for k in range(bits)]
+        if bits > 1:
+            place[:2] = (jnp.where(odd == 1, place[1 - k], place[k]) for k in range(2))
+        return sum(bit << (bits - 1 - k) for k, bit in enumerate(place))
 
     tiles = tiles_ref.shape[0]
     copies = [
@@ -235,9 +240,6 @@
     for copy in small:
         copy.start()
     inverse_copy(0).start()
-    coupling_copy(1).start()
-    inverse_copy(1).start()
-    coupling_copy(2).start()
 
     def turn(e, turned_ref):
         turned_ref[...] = coupling_ref[e].T
@@ -284,6 +286,9 @@
             leave(e - 1).start()
 
     coupling_copy(0).wait()
+    coupling_copy(1).start()
+    inverse_copy(1).start()
+    coupling_copy(2).start()
     turn(0, turned[0])
     for copy in small:
         copy.wait()
@@ -407,6 +412,21 @@
     return [block] + [
         lax.ppermute(block, axis, [(i, i ^ k) for i in range(count)]) for k in range(1, count)
     ]
+
+
+def trade(block, place, face_count):
+    elem_count = lax.axis_size("elem")
+    bits = face_count.bit_length() - 1
+    pairs = []
+    for face in range(face_count):
+        for elem in range(elem_count):
+            other = face
+            for k in range(bits):
+                swapped = bits > 1 and elem % 2 == 1 and k < 2
+                if place >> (bits - 1 - k) & 1:
+                    other ^= 1 << (1 - k if swapped else k)
+            pairs.append((face * elem_count + elem, other * elem_count + elem))
+    return lax.ppermute(block, ("face", "elem"), pairs)
 
 
 def shards(
@@ -466,7 +486,7 @@
         trace_old,
     )
     if paired:
-        came = lax.ppermute(half_grams[1], "face", [(i, i ^ 1) for i in range(face_count)])
+        came = trade(half_grams[1], face_count // 2, face_count)
     table = lax.all_to_all(
         placed.reshape(devices, capacity, FACE_COEFFS), ("face", "elem"), 0, 0, tiled=True
     ).reshape(slots, FACE_COEFFS)
@@ -482,8 +502,7 @@
             name="join",
         )(half_grams[0], came)
         got = [joined[0]] + [
-            lax.ppermute(joined[k], "face", [(i, i ^ (2 * k)) for i in range(face_count)])
-            for k in range(1, face_count // 2)
+            trade(joined[k], k, face_count) for k in range(face_count // 2 - 1, 0, -1)
         ]
         before = joined[0]
     else:

time: 36.5 us -> 37.3 us (1.022)
  starting transfers between devices: 14.3 us -> 14.9 us
  Pallas kernels: 15.5 us -> 15.9 us
    ppermute x4, waiting for transfers between devices: 1.97 us -> 0.01 us  [trade(): return lax.ppermute(block, ('face', 'elem'), pairs)]
    all_to_all x1, waiting for transfers between devices: 0.78 us -> 2.6 us  [shards(): lax.all_to_all(placed.reshape(devices, capacity, FACE_COEFFS), ('face', '...]
    ppermute x3, starting transfers between devices: 1.93 us -> 2.31 us  [around(): lax.ppermute(block, axis, [(i, i ^ k) for i in range(count)])]
  transfers between devices with their start and end apart: 8 -> 8, of which waited for: 3 -> 2; matrix products, arithmetic and copies ran while one was open for 0% -> 0% of each run, Pallas kernels for 30% -> 31%
where the time goes in v13:
time: 37.3 us; the launch traced here: 37 us
  Pallas kernels  15.9 us (43%)
  starting transfers between devices  14.9 us (40%)
  waiting for transfers between devices  3.1 us (8%)
  local copies, waits for them, and re-layouts  2.45 us (7%)
  between operations  0.69 us (2%)
    pallas_call x1, Pallas kernels, shards(): pl.pallas_call(functools.partial(main_kernel, elem_count, face_count), ou...  9.4 us
    ppermute x4, starting transfers between devices, trade(): return lax.ppermute(block, ('face', 'elem'), pairs)  7.66 us
    all_to_all x1, starting transfers between devices, shards(): lax.all_to_all(placed.reshape(devices, capacity, FACE_COEFFS), ('face', '...  4.9 us
    pallas_call x1, Pallas kernels, shards(): pl.pallas_call(functools.partial(gram_kernel, elem_count, face_count, cap...  3.72 us
    all_to_all x1, waiting for transfers between devices, shards(): lax.all_to_all(placed.reshape(devices, capacity, FACE_COEFFS), ('face', '...  2.6 us
    unnamed x6, local copies, waits for them, and re-layouts  2.45 us
    ppermute x3, starting transfers between devices, around(): lax.ppermute(block, axis, [(i, i ^ k) for i in range(count)])  2.31 us
    pallas_call x1, Pallas kernels, shards(): pl.pallas_call(coarse_kernel, out_shape=jax.ShapeDtypeStruct((NC, MROW *...  1.87 us
  transfers between devices with their start and end apart: 8, of which 2 were waited for; matrix products, arithmetic and copies ran while one was open for 0% of the time, Pallas kernels for 31%

profile of v13, /device:TPU:0, one launch (start us, length us, event | category | flops | bytes accessed | tf_op | source)
XLA Modules:
  0.0 37.0 jit_solution(11081202614440245529)
XLA Ops:
  0.6 3.7 %gram.1 = (bf16[512,128]{1,0:T(8,128)(2,1)}, bf16[1088,128]{1,0:T(8,128)(2,1)}, bf16[1088,128]{1,0:T(8,128)(2,1)}) custom-call(s32[96]{0:T(128)} %bitcast.7, s32[96]{0:T(128)} %coarse_hbm.1, bf16[96,6144]{1,0:T(8,128)(2,1)} %tiles_hbm.1, s32[1,64]{1,0:T(1,128)} %bitcast.8, bf16[64,128]{1,0:T(8,128)(2,1)} %trace_hbm.1), custom_call_target="tpu_custom_call" | custom-call | flops 201326592 | bytes 12582912 | tf_op jit(solution)/shard_map/gram/pallas_call | solution.py:459
  4.4 3.0 %collective-permute-start = (bf16[1088,128]{1,0:T(8,128)(2,1)}, bf16[1088,128]{1,0:T(8,128)(2,1)S(1)}, u32[]{:S(2)}, u32[]{:S(2)}) collective-permute-start(bf16[1088,128]{1,0:T(8,128)(2,1)} %get-tuple-element.18), channel_id=1, source_target_pairs={{0,4},{1,9},{2,6},{3,11},{4,0},{5,13},{6,2},{7,15},{8,12},{9,1},{1... | collective-permute-start | bytes 835592 | tf_op jit(solution)/shard_map/ppermute | solution.py:429
  7.4 4.9 %all-to-all-start = ((bf16[32,16,128]{2,1,0:T(8,128)(2,1)}), bf16[32,16,128]{2,1,0:T(8,128)(2,1)S(1)}, u32[]{:S(2)}, u32[]{:S(2)}) async-start(bf16[32,16,128]{2,1,0:T(8,128)(2,1)} %bitcast.6), calls=%async_computation | async-start | bytes 262144 | tf_op jit(solution)/shard_map/all_to_all | solution.py:490
  12.3 0.0 collective-permute-done.came_ref
  12.3 0.0 copy-start
  12.3 0.9 %copy-done = bf16[1088,128]{1,0:T(8,128)(2,1)S(1)} copy-done((bf16[1088,128]{1,0:T(8,128)(2,1)S(1)}, bf16[1088,128]{1,0:T(8,128)(2,1)}, u32[]{:S(2)}) %copy-start) | copy-done | bytes 278552
  13.3 0.1 join.1
  13.3 4.0 %collective-permute-start.1 = (bf16[272,128]{1,0:T(8,128)(2,1)S(1)}, bf16[272,128]{1,0:T(8,128)(2,1)S(1)}, u32[]{:S(2)}, u32[]{:S(2)}) collective-permute-start(bf16[272,128]{1,0:T(8,128)(2,1)S(1)} %get-tuple-element.23), channel_id=1, source_target_pairs={{0,24},{1,21},{2,26},{3,23},{4,28},{5,17},{6,30},{7,19},{8,16},{9,... | collective-permute-start | bytes 208904 | tf_op jit(solution)/shard_map/ppermute | solution.py:429
  17.3 0.0 collective-permute-start.2
  17.3 0.6 %collective-permute-start.3 = (bf16[272,128]{1,0:T(8,128)(2,1)S(1)}, bf16[272,128]{1,0:T(8,128)(2,1)S(1)}, u32[]{:S(2)}, u32[]{:S(2)}) collective-permute-start(bf16[272,128]{1,0:T(8,128)(2,1)S(1)} %get-tuple-element.25), channel_id=1, source_target_pairs={{0,16},{1,17},{2,18},{3,19},{4,20},{5,21},{6,22},{7,23},{8,24},{9,... | collective-permute-start | bytes 208904 | tf_op jit(solution)/shard_map/ppermute | solution.py:429
  18.0 2.6 %all-to-all-done = bf16[32,16,128]{2,1,0:T(8,128)(2,1)S(1)} async-done(((bf16[32,16,128]{2,1,0:T(8,128)(2,1)}), bf16[32,16,128]{2,1,0:T(8,128)(2,1)S(1)}, u32[]{:S(2)}, u32[]{:S(2)}) %all-to-all-start) | async-done | bytes 131104 | tf_op jit(solution)/shard_map/all_to_all | solution.py:490
  20.6 0.7 %copy-done.2 = bf16[32,16,128]{2,1,0:T(8,128)(2,1)} copy-done((bf16[32,16,128]{2,1,0:T(8,128)(2,1)}, bf16[32,16,128]{2,1,0:T(8,128)(2,1)S(1)}, u32[]{:S(2)}) %copy-start.2) | copy-done | bytes 131096
  21.2 9.4 %condense.1 = (bf16[9,384,384]{2,1,0:T(8,128)(2,1)}, bf16[64,128]{1,0:T(8,128)(2,1)}, f32[128,128]{1,0:T(8,128)}) custom-call(bf16[512,128]{1,0:T(8,128)(2,1)} %bitcast.5, s32[3,9]{1,0:T(4,128)} %bitcast.9, bf16[9,512]{1,0:T(8,128)(2,1)} %rhs_hbm, bf16[9,512,512]{2,1,0:T(8,128)(2,1)} %inverse_hbm.1, bf16[9,512,384]{2,1,0:T(8,128)(2,1)} %coupling_hbm.1), custom_call_target="tpu_custom_call" | custom-call | flops 3170893824 | bytes 10911744 | tf_op jit(solution)/shard_map/condense/pallas_call | solution.py:514
  30.6 0.7 %collective-permute-start.6 = (bf16[64,128]{1,0:T(8,128)(2,1)}, bf16[64,128]{1,0:T(8,128)(2,1)S(1)}, u32[]{:S(2)}, u32[]{:S(2)}) collective-permute-start(bf16[64,128]{1,0:T(8,128)(2,1)} %get-tuple-element.27), channel_id=1, source_target_pairs={{0,3},{1,2},{2,1},{3,0},{4,7},{5,6},{6,5},{7,4},{8,11},{9,10},{10,... | collective-permute-start | bytes 49160 | tf_op jit(solution)/shard_map/ppermute | solution.py:413
  31.4 1.6 %collective-permute-start.5 = (bf16[64,128]{1,0:T(8,128)(2,1)}, bf16[64,128]{1,0:T(8,128)(2,1)S(1)}, u32[]{:S(2)}, u32[]{:S(2)}) collective-permute-start(bf16[64,128]{1,0:T(8,128)(2,1)} %get-tuple-element.27), channel_id=1, source_target_pairs={{0,2},{1,3},{2,0},{3,1},{4,6},{5,7},{6,4},{7,5},{8,10},{9,11},{10,... | collective-permute-start | bytes 49160 | tf_op jit(solution)/shard_map/ppermute | solution.py:413
  32.9 0.0 collective-permute-done.1.refs_1_
  32.9 0.0 collective-permute-start.4
  32.9 0.0 collective-permute-done.2.refs_2_
  32.9 0.0 collective-permute-done.3.refs_3_
  33.0 1.9 %coarse.1 = f32[16,4096]{1,0:T(8,128)} custom-call(bf16[272,128]{1,0:T(8,128)(2,1)S(1)} %get-tuple-element.19.refs_0_, bf16[272,128]{1,0:T(8,128)(2,1)S(1)} %collective-permute-done.1.refs_1_, bf16[272,128]{1,0:T(8,128)(2,1)S(1)} %collective-permute-done.2.refs_2_, bf16[272,128]{1,0:T(8,128)(2,1)S(1)} %collective-permute-done.3.refs_3_), custom_call_target="tpu_custom_call" | custom-call | bytes 8388608 | tf_op jit(solution)/shard_map/coarse/pallas_call | solution.py:551
  34.8 0.5 %collective-permute-done.5.refs_1_ = bf16[64,128]{1,0:T(8,128)(2,1)S(1)} collective-permute-done((bf16[64,128]{1,0:T(8,128)(2,1)}, bf16[64,128]{1,0:T(8,128)(2,1)S(1)}, u32[]{:S(2)}, u32[]{:S(2)}) %collective-permute-start.5) | collective-permute-done | bytes 16416 | tf_op jit(solution)/shard_map/ppermute | solution.py:413
  35.3 0.0 collective-permute-done.4.refs_0_
  35.3 0.8 %copy-done.1 = f32[128,128]{1,0:T(8,128)S(1)} copy-done((f32[128,128]{1,0:T(8,128)S(1)}, f32[128,128]{1,0:T(8,128)}, u32[]{:S(2)}) %copy-start.1) | copy-done | bytes 65560
  36.2 0.8 %residual.1 = f32[128,128]{1,0:T(8,128)} custom-call(f32[128,128]{1,0:T(8,128)S(1)} %copy-done.1, bf16[64,128]{1,0:T(8,128)(2,1)S(1)} %collective-permute-done.4.refs_0_, bf16[64,128]{1,0:T(8,128)(2,1)S(1)} %collective-permute-done.5.refs_1_, bf16[64,128]{1,0:T(8,128)(2,1)S(1)} %collective-permute-done.6.refs_2_), custom_call_target="tpu_custom_call" | custom-call | tf_op jit(solution)/shard_map/residual/pallas_call | solution.py:565
  (3 shorter events, 0.0 us)
Async XLA Ops:
  4.4 7.9 %collective-permute-start = (bf16[1088,128]{1,0:T(8,128)(2,1)}, bf16[1088,128]{1,0:T(8,128)(2,1)S(1)}, u32[]{:S(2)}, u32[]{:S(2)}) collective-permute-start(bf16[1088,128]{1,0:T(8,128)(2,1)} %get-tuple-element.18), channel_id=1, source_target_pairs={{0,4},{1,9},{2,6},{3,11},{4,0},{5,13},{6,2},{7,15},{8,12},{9,1},{1... | collective-permute-start | bytes 835592 | tf_op jit(solution)/shard_map/ppermute | solution.py:429
  7.4 13.2 %all-to-all-start = ((bf16[32,16,128]{2,1,0:T(8,128)(2,1)}), bf16[32,16,128]{2,1,0:T(8,128)(2,1)S(1)}, u32[]{:S(2)}, u32[]{:S(2)}) async-start(bf16[32,16,128]{2,1,0:T(8,128)(2,1)} %bitcast.6), calls=%async_computation | async-start | bytes 262144 | tf_op jit(solution)/shard_map/all_to_all | solution.py:490
  12.3 1.0 %copy-start = (bf16[1088,128]{1,0:T(8,128)(2,1)S(1)}, bf16[1088,128]{1,0:T(8,128)(2,1)}, u32[]{:S(2)}) copy-start(bf16[1088,128]{1,0:T(8,128)(2,1)} %get-tuple-element.17.kept_ref) | copy-start | bytes 835588
  13.3 19.6 %collective-permute-start.1 = (bf16[272,128]{1,0:T(8,128)(2,1)S(1)}, bf16[272,128]{1,0:T(8,128)(2,1)S(1)}, u32[]{:S(2)}, u32[]{:S(2)}) collective-permute-start(bf16[272,128]{1,0:T(8,128)(2,1)S(1)} %get-tuple-element.23), channel_id=1, source_target_pairs={{0,24},{1,21},{2,26},{3,23},{4,28},{5,17},{6,30},{7,19},{8,16},{9,... | collective-permute-start | bytes 208904 | tf_op jit(solution)/shard_map/ppermute | solution.py:429
  17.3 15.6 %collective-permute-start.2 = (bf16[272,128]{1,0:T(8,128)(2,1)S(1)}, bf16[272,128]{1,0:T(8,128)(2,1)S(1)}, u32[]{:S(2)}, u32[]{:S(2)}) collective-permute-start(bf16[272,128]{1,0:T(8,128)(2,1)S(1)} %get-tuple-element.24), channel_id=1, source_target_pairs={{0,8},{1,5},{2,10},{3,7},{4,12},{5,1},{6,14},{7,3},{8,0},{9,13},{1... | collective-permute-start | bytes 208904 | tf_op jit(solution)/shard_map/ppermute | solution.py:429
  17.3 15.6 %collective-permute-start.3 = (bf16[272,128]{1,0:T(8,128)(2,1)S(1)}, bf16[272,128]{1,0:T(8,128)(2,1)S(1)}, u32[]{:S(2)}, u32[]{:S(2)}) collective-permute-start(bf16[272,128]{1,0:T(8,128)(2,1)S(1)} %get-tuple-element.25), channel_id=1, source_target_pairs={{0,16},{1,17},{2,18},{3,19},{4,20},{5,21},{6,22},{7,23},{8,24},{9,... | collective-permute-start | bytes 208904 | tf_op jit(solution)/shard_map/ppermute | solution.py:429
  20.6 0.7 %copy-start.2 = (bf16[32,16,128]{2,1,0:T(8,128)(2,1)}, bf16[32,16,128]{2,1,0:T(8,128)(2,1)S(1)}, u32[]{:S(2)}) copy-start(bf16[32,16,128]{2,1,0:T(8,128)(2,1)S(1)} %all-to-all-done) | copy-start | bytes 393220
  30.6 4.2 %collective-permute-start.6 = (bf16[64,128]{1,0:T(8,128)(2,1)}, bf16[64,128]{1,0:T(8,128)(2,1)S(1)}, u32[]{:S(2)}, u32[]{:S(2)}) collective-permute-start(bf16[64,128]{1,0:T(8,128)(2,1)} %get-tuple-element.27), channel_id=1, source_target_pairs={{0,3},{1,2},{2,1},{3,0},{4,7},{5,6},{6,5},{7,4},{8,11},{9,10},{10,... | collective-permute-start | bytes 49160 | tf_op jit(solution)/shard_map/ppermute | solution.py:413
  31.4 3.9 %collective-permute-start.5 = (bf16[64,128]{1,0:T(8,128)(2,1)}, bf16[64,128]{1,0:T(8,128)(2,1)S(1)}, u32[]{:S(2)}, u32[]{:S(2)}) collective-permute-start(bf16[64,128]{1,0:T(8,128)(2,1)} %get-tuple-element.27), channel_id=1, source_target_pairs={{0,2},{1,3},{2,0},{3,1},{4,6},{5,7},{6,4},{7,5},{8,10},{9,11},{10,... | collective-permute-start | bytes 49160 | tf_op jit(solution)/shard_map/ppermute | solution.py:413
  32.9 2.4 %collective-permute-start.4 = (bf16[64,128]{1,0:T(8,128)(2,1)}, bf16[64,128]{1,0:T(8,128)(2,1)S(1)}, u32[]{:S(2)}, u32[]{:S(2)}) collective-permute-start(bf16[64,128]{1,0:T(8,128)(2,1)} %get-tuple-element.27), channel_id=1, source_target_pairs={{0,1},{1,0},{2,3},{3,2},{4,5},{5,4},{6,7},{7,6},{8,9},{9,8},{10,11... | collective-permute-start | bytes 49160 | tf_op jit(solution)/shard_map/ppermute | solution.py:413
  35.3 0.8 %copy-start.1 = (f32[128,128]{1,0:T(8,128)S(1)}, f32[128,128]{1,0:T(8,128)}, u32[]{:S(2)}) copy-start(f32[128,128]{1,0:T(8,128)} %get-tuple-element.26.left_ref) | copy-start | bytes 196612

commit v14 on v13

--- a/solution.py
+++ b/solution.py
@@ -59,6 +59,35 @@
     return dot(place, trace).astype(BF16)
 
 
+def position(elem, inner, elem_count, capacity):
+    face, rank = divided(inner, capacity)
+    return (face * elem_count + elem) * capacity + rank
+
+
+def name_slots(elem_count, face_count, capacity, conn_ref, named_ref):
+    elements = conn_ref.shape[1]
+    slots = named_ref.shape[1]
+    row = iota((PER_FACE, LANES), 0)
+    lane = iota((PER_FACE, LANES), 1)
+    first_lane = iota((1, LANES), 1)
+    high = jnp.full((1, LANES), -1, I32)
+    rest = jnp.zeros((1, LANES), I32)
+    for a in range(FACES_PER_ELEM):
+        positions = jnp.full((PER_FACE, LANES), -1, I32)
+        for e in range(elements):
+            slot = conn_ref[a, e]
+            place = position(*divided(slot, face_count * capacity), elem_count, capacity)
+            positions = jnp.where(row == e, place, positions)
+            here = first_lane == a * PER_FACE + e
+            quotient, remainder = divided(slot, SLOT_BASE)
+            high = jnp.where(here, quotient, high)
+            rest = jnp.where(here, remainder, rest)
+        hot = jnp.concatenate([positions == lane + k for k in range(0, slots, LANES)], axis=1)
+        named_ref[a * PER_FACE : (a + 1) * PER_FACE, :] = hot.astype(BF16)
+    names = jnp.where(row == 0, high, jnp.where(row == 1, rest, 0)).astype(F32)
+    named_ref[NAMED:, :] = jnp.concatenate([names] * (slots // LANES), axis=1).astype(BF16)
+
+
 def turn_rhs(rhs_ref, wide_ref, rhs_turned_ref):
     wide_ref[...] = jnp.zeros_like(wide_ref)
     wide_ref[0 : rhs_ref.shape[0], :] = rhs_ref[...].astype(F32)
@@ -75,13 +104,15 @@
     tiles_hbm,
     new_owner_hbm,
     trace_hbm,
+    conn_hbm,
     placed_ref,
+    named_ref,
     *refs,
 ):
-    out_refs, refs = refs[:-11], refs[-11:]
+    out_refs, refs = refs[:-12], refs[-12:]
     owner_ref, coarse_ref, tiles_ref, rows_ref = refs[:4]
     accs, diags = refs[4:6], refs[6:8]
-    new_owner_ref, trace_ref, sems = refs[8:]
+    new_owner_ref, trace_ref, conn_ref, sems = refs[8:]
 
     def place_of(owner):
         if not paired:
@@ -102,10 +133,14 @@
         pltpu.make_async_copy(trace_hbm, trace_ref, sems.at[3]),
         pltpu.make_async_copy(tiles_hbm, tiles_ref, sems.at[4]),
     ]
+    names = pltpu.make_async_copy(conn_hbm, conn_ref, sems.at[5])
+    names.start()
     for copy in copies:
         copy.start()
     for ref in (*accs, *diags):
         ref[...] = jnp.zeros_like(ref)
+    names.wait()
+    name_slots(elem_count, face_count, capacity, conn_ref, named_ref)
     for copy in copies:
         copy.wait()
     placed_ref[...] = place_rows(
@@ -189,14 +224,14 @@
     elem_count,
     face_count,
     table_hbm,
-    conn_hbm,
+    named_hbm,
     rhs_hbm,
     inverse_hbm,
     coupling_hbm,
     schur_hbm,
     share_ref,
     left_ref,
-    conn_ref,
+    named_ref,
     rhs_ref,
     table_ref,
     inverse_ref,
@@ -223,7 +258,7 @@
     my_elem = lax.axis_index("elem")
     small = [
         pltpu.make_async_copy(rhs_hbm, rhs_ref, small_sems.at[0]),
-        pltpu.make_async_copy(conn_hbm, conn_ref, small_sems.at[1]),
+        pltpu.make_async_copy(named_hbm, named_ref, small_sems.at[1]),
         pltpu.make_async_copy(table_hbm, table_ref, small_sems.at[2]),
     ]
 
@@ -240,6 +275,9 @@
     for copy in small:
         copy.start()
     inverse_copy(0).start()
+    coupling_copy(1).start()
+    inverse_copy(1).start()
+    coupling_copy(2).start()
 
     def turn(e, turned_ref):
         turned_ref[...] = coupling_ref[e].T
@@ -286,9 +324,6 @@
             leave(e - 1).start()
 
     coupling_copy(0).wait()
-    coupling_copy(1).start()
-    inverse_copy(1).start()
-    coupling_copy(2).start()
     turn(0, turned[0])
     for copy in small:
         copy.wait()
@@ -297,29 +332,12 @@
     row = iota((PER_FACE, LANES), 0)
     lane = iota((PER_FACE, LANES), 1)
 
-    def position(elem, inner):
-        face, rank = divided(inner, capacity)
-        return (face * elem_count + elem) * capacity + rank
-
-    first_lane = iota((1, LANES), 1)
-    high = jnp.full((1, LANES), -1, I32)
-    rest = jnp.zeros((1, LANES), I32)
     for a in range(FACES_PER_ELEM):
-        positions = jnp.full((PER_FACE, LANES), -1, I32)
-        for e in range(elements):
-            slot = conn_ref[a, e]
-            positions = jnp.where(row == e, position(*divided(slot, own)), positions)
-            here = first_lane == a * PER_FACE + e
-            quotient, remainder = divided(slot, SLOT_BASE)
-            high = jnp.where(here, quotient, high)
-            rest = jnp.where(here, remainder, rest)
-        hot = jnp.concatenate([positions == lane + k for k in range(0, slots, LANES)], axis=1)
-        lam = dot(hot.astype(BF16), table_ref[...])
-        vector_ref[:, a * LANES : (a + 1) * LANES] = -lam
+        hot = named_ref[a * PER_FACE : (a + 1) * PER_FACE, :]
+        vector_ref[:, a * LANES : (a + 1) * LANES] = -dot(hot, table_ref[...])
     vector_ref[:, trace:] = (row == lane).astype(F32)
-    names = jnp.where(row == 0, high, jnp.where(row == 1, rest, 0))
-    share_ref[NAMED:, :] = names.astype(F32).astype(BF16)
-    place = position(my_elem, iota((own, slots), 0))
+    share_ref[NAMED:, :] = named_ref[NAMED:, :LANES]
+    place = position(my_elem, iota((own, slots), 0), elem_count, capacity)
     pick = (iota((own, slots), 1) == place).astype(BF16)
     left_ref[...] = dot(pick, table_ref[...])
 
@@ -456,12 +474,15 @@
 
     blocks = face_count * NC
     sums_shape = (blocks * DENSE, LANES)
-    placed, *half_grams = pl.pallas_call(
+    placed, named, *half_grams = pl.pallas_call(
         functools.partial(gram_kernel, elem_count, face_count, capacity, paired),
-        out_shape=[jax.ShapeDtypeStruct((slots, FACE_COEFFS), BF16)]
+        out_shape=[
+            jax.ShapeDtypeStruct((slots, FACE_COEFFS), BF16),
+            jax.ShapeDtypeStruct((SHARE_ROWS, slots), BF16),
+        ]
         + [jax.ShapeDtypeStruct((blocks * (DENSE + 1) // sides, LANES), BF16)] * sides,
-        in_specs=[ANY] * 5,
-        out_specs=[VMEM] * (1 + sides),
+        in_specs=[ANY] * 6,
+        out_specs=[VMEM] * (2 + sides),
         scratch_shapes=[
             pltpu.SMEM((tile_count,), I32),
             pltpu.SMEM((tile_count,), I32),
@@ -473,7 +494,8 @@
             pltpu.VMEM((blocks, LANES), F32),
             pltpu.VMEM((1, row_count), I32),
             pltpu.VMEM(trace_old.shape, BF16),
-            pltpu.SemaphoreType.DMA((5,)),
+            pltpu.SMEM((FACES_PER_ELEM, elements), I32),
+            pltpu.SemaphoreType.DMA((6,)),
         ],
         compiler_params=params(BIG),
         cost_estimate=cost(4 * tile_count * MROW * MROW * LANES, 12 << 20),
@@ -484,6 +506,7 @@
         mortar_tiles,
         new_owner.reshape(1, row_count),
         trace_old,
+        connectivity.T,
     )
     if paired:
         came = trade(half_grams[1], face_count // 2, face_count)
@@ -521,7 +544,7 @@
         in_specs=[ANY] * 5,
         out_specs=(ANY, VMEM, VMEM),
         scratch_shapes=[
-            pltpu.SMEM((FACES_PER_ELEM, elements), I32),
+            pltpu.VMEM((SHARE_ROWS, slots), BF16),
             pltpu.VMEM((elements, modes), BF16),
             pltpu.VMEM((slots, FACE_COEFFS), BF16),
             pltpu.VMEM((elements, modes, modes), BF16),
@@ -545,7 +568,7 @@
             2 * elements * (modes * (modes + trace) + trace * trace),
         ),
         name="condense",
-    )(table, connectivity.T, rhs, local_inverse, coupling)
+    )(table, named, rhs, local_inverse, coupling)
 
     all_shares = around(shares, "elem")
     coarse_blocks = pl.pallas_call(
@@ -561,7 +584,7 @@
         cost_estimate=cost(0, 8 << 20),
         name="coarse",
     )(*got)
-    left, coarse_blocks = lax.optimization_barrier((left, coarse_blocks))
+    last, coarse_blocks = lax.optimization_barrier((all_shares[-1], coarse_blocks))
     slot_residual = pl.pallas_call(
         residual_kernel,
         out_shape=jax.ShapeDtypeStruct((own, FACE_COEFFS), F32),
@@ -569,7 +592,7 @@
         out_specs=VMEM,
         compiler_params=params(SMALL),
         name="residual",
-    )(left, *all_shares[1:])
+    )(left, *all_shares[1:-1], last)
     return schur_blocks, slot_residual, coarse_blocks
 
 

time: 37.3 us -> 37 us (level)
  transfers between devices with their start and end apart: 8 -> 8, of which waited for: 2 -> 2; matrix products, arithmetic and copies ran while one was open for 0% -> 0% of each run, Pallas kernels for 31% -> 30%
where the time goes in v14:
time: 37 us; the launch traced here: 36.7 us
  Pallas kernels  15.6 us (42%)
  starting transfers between devices  14.9 us (40%)
  waiting for transfers between devices  3.1 us (8%)
  local copies, waits for them, and re-layouts  2.45 us (7%)
  between operations  0.69 us (2%)
    pallas_call x1, Pallas kernels, shards(): pl.pallas_call(functools.partial(main_kernel, elem_count, face_count), ou...  9.05 us
    ppermute x4, starting transfers between devices, trade(): return lax.ppermute(block, ('face', 'elem'), pairs)  7.67 us
    all_to_all x1, starting transfers between devices, shards(): lax.all_to_all(placed.reshape(devices, capacity, FACE_COEFFS), ('face', '...  4.89 us
    pallas_call x1, Pallas kernels, shards(): pl.pallas_call(functools.partial(gram_kernel, elem_count, face_count, cap...  3.8 us
    all_to_all x1, waiting for transfers between devices, shards(): lax.all_to_all(placed.reshape(devices, capacity, FACE_COEFFS), ('face', '...  2.59 us
    unnamed x6, local copies, waits for them, and re-layouts  2.45 us
    ppermute x3, starting transfers between devices, around(): lax.ppermute(block, axis, [(i, i ^ k) for i in range(count)])  2.31 us
    pallas_call x1, Pallas kernels, shards(): pl.pallas_call(coarse_kernel, out_shape=jax.ShapeDtypeStruct((NC, MROW *...  1.87 us
  transfers between devices with their start and end apart: 8, of which 2 were waited for; matrix products, arithmetic and copies ran while one was open for 0% of the time, Pallas kernels for 30%

profile of v14, /device:TPU:0, one launch (start us, length us, event | category | flops | bytes accessed | tf_op | source)
XLA Modules:
  0.0 36.7 jit_solution(13649381260878998361)
XLA Ops:
  0.6 3.8 %gram.1 = (bf16[512,128]{1,0:T(8,128)(2,1)}, bf16[64,512]{1,0:T(8,128)(2,1)}, bf16[1088,128]{1,0:T(8,128)(2,1)}, bf16[1088,128]{1,0:T(8,128)(2,1)}) custom-call(s32[96]{0:T(128)} %bitcast.8, s32[96]{0:T(128)} %coarse_hbm.1, bf16[96,6144]{1,0:T(8,128)(2,1)} %tiles_hbm.1, s32[1,64]{1,0:T(1,128)} %bitcast.9, bf16[64,128]{1,0:T(8,128)(2,1)} %trace_hbm.1, ...), custom_call_target="tpu_custom_call" | custom-call | flops 201326592 | bytes 12582912 | tf_op jit(solution)/shard_map/gram/pallas_call | solution.py:477
  4.4 3.0 %collective-permute-start = (bf16[1088,128]{1,0:T(8,128)(2,1)}, bf16[1088,128]{1,0:T(8,128)(2,1)S(1)}, u32[]{:S(2)}, u32[]{:S(2)}) collective-permute-start(bf16[1088,128]{1,0:T(8,128)(2,1)} %get-tuple-element.20), channel_id=1, source_target_pairs={{0,4},{1,9},{2,6},{3,11},{4,0},{5,13},{6,2},{7,15},{8,12},{9,1},{1... | collective-permute-start | bytes 835592 | tf_op jit(solution)/shard_map/ppermute | solution.py:447
  7.5 4.9 %all-to-all-start = ((bf16[32,16,128]{2,1,0:T(8,128)(2,1)}), bf16[32,16,128]{2,1,0:T(8,128)(2,1)S(1)}, u32[]{:S(2)}, u32[]{:S(2)}) async-start(bf16[32,16,128]{2,1,0:T(8,128)(2,1)} %bitcast.6), calls=%async_computation | async-start | bytes 262144 | tf_op jit(solution)/shard_map/all_to_all | solution.py:513
  12.4 0.0 collective-permute-done.came_ref
  12.4 0.0 copy-start
  12.4 0.9 %copy-done = bf16[1088,128]{1,0:T(8,128)(2,1)S(1)} copy-done((bf16[1088,128]{1,0:T(8,128)(2,1)S(1)}, bf16[1088,128]{1,0:T(8,128)(2,1)}, u32[]{:S(2)}) %copy-start) | copy-done | bytes 278552
  13.3 0.1 join.1
  13.4 4.0 %collective-permute-start.4 = (bf16[272,128]{1,0:T(8,128)(2,1)S(1)}, bf16[272,128]{1,0:T(8,128)(2,1)S(1)}, u32[]{:S(2)}, u32[]{:S(2)}) collective-permute-start(bf16[272,128]{1,0:T(8,128)(2,1)S(1)} %get-tuple-element.26), channel_id=1, source_target_pairs={{0,24},{1,21},{2,26},{3,23},{4,28},{5,17},{6,30},{7,19},{8,16},{9,... | collective-permute-start | bytes 208904 | tf_op jit(solution)/shard_map/ppermute | solution.py:447
  17.4 0.0 collective-permute-start.5
  17.4 0.6 %collective-permute-start.6 = (bf16[272,128]{1,0:T(8,128)(2,1)S(1)}, bf16[272,128]{1,0:T(8,128)(2,1)S(1)}, u32[]{:S(2)}, u32[]{:S(2)}) collective-permute-start(bf16[272,128]{1,0:T(8,128)(2,1)S(1)} %get-tuple-element.28), channel_id=1, source_target_pairs={{0,16},{1,17},{2,18},{3,19},{4,20},{5,21},{6,22},{7,23},{8,24},{9,... | collective-permute-start | bytes 208904 | tf_op jit(solution)/shard_map/ppermute | solution.py:447
  18.0 2.6 %all-to-all-done = bf16[32,16,128]{2,1,0:T(8,128)(2,1)S(1)} async-done(((bf16[32,16,128]{2,1,0:T(8,128)(2,1)}), bf16[32,16,128]{2,1,0:T(8,128)(2,1)S(1)}, u32[]{:S(2)}, u32[]{:S(2)}) %all-to-all-start) | async-done | bytes 131104 | tf_op jit(solution)/shard_map/all_to_all | solution.py:513
  20.6 0.7 %copy-done.2 = bf16[32,16,128]{2,1,0:T(8,128)(2,1)} copy-done((bf16[32,16,128]{2,1,0:T(8,128)(2,1)}, bf16[32,16,128]{2,1,0:T(8,128)(2,1)S(1)}, u32[]{:S(2)}) %copy-start.2) | copy-done | bytes 131096
  21.3 9.1 %condense.1 = (bf16[9,384,384]{2,1,0:T(8,128)(2,1)}, bf16[64,128]{1,0:T(8,128)(2,1)}, f32[128,128]{1,0:T(8,128)}) custom-call(bf16[512,128]{1,0:T(8,128)(2,1)} %bitcast.5, bf16[64,512]{1,0:T(8,128)(2,1)} %get-tuple-element.18.named_hbm, bf16[9,512]{1,0:T(8,128)(2,1)} %rhs_hbm, bf16[9,512,512]{2,1,0:T(8,128)(2,1)} %inverse_hbm.1, ...), custom_call_target="tpu_custom_call" | custom-call | flops 3170893824 | bytes 10911744 | tf_op jit(solution)/shard_map/condense/pallas_call | solution.py:537
  30.4 0.7 %collective-permute-start.3 = (bf16[64,128]{1,0:T(8,128)(2,1)}, bf16[64,128]{1,0:T(8,128)(2,1)S(1)}, u32[]{:S(2)}, u32[]{:S(2)}) collective-permute-start(bf16[64,128]{1,0:T(8,128)(2,1)} %get-tuple-element.25), channel_id=1, source_target_pairs={{0,3},{1,2},{2,1},{3,0},{4,7},{5,6},{6,5},{7,4},{8,11},{9,10},{10,... | collective-permute-start | bytes 49160 | tf_op jit(solution)/shard_map/ppermute | solution.py:431
  31.1 1.6 %collective-permute-start.2 = (bf16[64,128]{1,0:T(8,128)(2,1)}, bf16[64,128]{1,0:T(8,128)(2,1)S(1)}, u32[]{:S(2)}, u32[]{:S(2)}) collective-permute-start(bf16[64,128]{1,0:T(8,128)(2,1)} %get-tuple-element.25), channel_id=1, source_target_pairs={{0,2},{1,3},{2,0},{3,1},{4,6},{5,7},{6,4},{7,5},{8,10},{9,11},{10,... | collective-permute-start | bytes 49160 | tf_op jit(solution)/shard_map/ppermute | solution.py:431
  32.7 0.0 collective-permute-done.4.refs_1_
  32.7 0.0 collective-permute-start.1
  32.7 0.0 collective-permute-done.5.refs_2_
  32.7 0.0 collective-permute-done.6.refs_3_
  32.7 1.9 %coarse.1 = f32[16,4096]{1,0:T(8,128)} custom-call(bf16[272,128]{1,0:T(8,128)(2,1)S(1)} %get-tuple-element.21.refs_0_, bf16[272,128]{1,0:T(8,128)(2,1)S(1)} %collective-permute-done.4.refs_1_, bf16[272,128]{1,0:T(8,128)(2,1)S(1)} %collective-permute-done.5.refs_2_, bf16[272,128]{1,0:T(8,128)(2,1)S(1)} %collective-permute-done.6.refs_3_), custom_call_target="tpu_custom_call" | custom-call | bytes 8388608 | tf_op jit(solution)/shard_map/coarse/pallas_call | solution.py:574
  34.6 0.0 collective-permute-done.3.refs_2_
  34.6 0.5 %collective-permute-done.2.refs_1_ = bf16[64,128]{1,0:T(8,128)(2,1)S(1)} collective-permute-done((bf16[64,128]{1,0:T(8,128)(2,1)}, bf16[64,128]{1,0:T(8,128)(2,1)S(1)}, u32[]{:S(2)}, u32[]{:S(2)}) %collective-permute-start.2) | collective-permute-done | bytes 16416 | tf_op jit(solution)/shard_map/ppermute | solution.py:431
  35.1 0.8 %copy-done.1 = f32[128,128]{1,0:T(8,128)S(1)} copy-done((f32[128,128]{1,0:T(8,128)S(1)}, f32[128,128]{1,0:T(8,128)}, u32[]{:S(2)}) %copy-start.1) | copy-done | bytes 65560
  35.9 0.8 %residual.1 = f32[128,128]{1,0:T(8,128)} custom-call(f32[128,128]{1,0:T(8,128)S(1)} %copy-done.1, bf16[64,128]{1,0:T(8,128)(2,1)S(1)} %collective-permute-done.1.refs_0_, bf16[64,128]{1,0:T(8,128)(2,1)S(1)} %collective-permute-done.2.refs_1_, bf16[64,128]{1,0:T(8,128)(2,1)S(1)} %collective-permute-done.3.refs_2_), custom_call_target="tpu_custom_call" | custom-call | tf_op jit(solution)/shard_map/residual/pallas_call | solution.py:588
  (3 shorter events, 0.0 us)
Async XLA Ops:
  4.4 7.9 %collective-permute-start = (bf16[1088,128]{1,0:T(8,128)(2,1)}, bf16[1088,128]{1,0:T(8,128)(2,1)S(1)}, u32[]{:S(2)}, u32[]{:S(2)}) collective-permute-start(bf16[1088,128]{1,0:T(8,128)(2,1)} %get-tuple-element.20), channel_id=1, source_target_pairs={{0,4},{1,9},{2,6},{3,11},{4,0},{5,13},{6,2},{7,15},{8,12},{9,1},{1... | collective-permute-start | bytes 835592 | tf_op jit(solution)/shard_map/ppermute | solution.py:447
  7.5 13.2 %all-to-all-start = ((bf16[32,16,128]{2,1,0:T(8,128)(2,1)}), bf16[32,16,128]{2,1,0:T(8,128)(2,1)S(1)}, u32[]{:S(2)}, u32[]{:S(2)}) async-start(bf16[32,16,128]{2,1,0:T(8,128)(2,1)} %bitcast.6), calls=%async_computation | async-start | bytes 262144 | tf_op jit(solution)/shard_map/all_to_all | solution.py:513
  12.4 1.0 %copy-start = (bf16[1088,128]{1,0:T(8,128)(2,1)S(1)}, bf16[1088,128]{1,0:T(8,128)(2,1)}, u32[]{:S(2)}) copy-start(bf16[1088,128]{1,0:T(8,128)(2,1)} %get-tuple-element.19.kept_ref) | copy-start | bytes 835588
  13.4 19.3 %collective-permute-start.4 = (bf16[272,128]{1,0:T(8,128)(2,1)S(1)}, bf16[272,128]{1,0:T(8,128)(2,1)S(1)}, u32[]{:S(2)}, u32[]{:S(2)}) collective-permute-start(bf16[272,128]{1,0:T(8,128)(2,1)S(1)} %get-tuple-element.26), channel_id=1, source_target_pairs={{0,24},{1,21},{2,26},{3,23},{4,28},{5,17},{6,30},{7,19},{8,16},{9,... | collective-permute-start | bytes 208904 | tf_op jit(solution)/shard_map/ppermute | solution.py:447
  17.4 15.3 %collective-permute-start.5 = (bf16[272,128]{1,0:T(8,128)(2,1)S(1)}, bf16[272,128]{1,0:T(8,128)(2,1)S(1)}, u32[]{:S(2)}, u32[]{:S(2)}) collective-permute-start(bf16[272,128]{1,0:T(8,128)(2,1)S(1)} %get-tuple-element.27), channel_id=1, source_target_pairs={{0,8},{1,5},{2,10},{3,7},{4,12},{5,1},{6,14},{7,3},{8,0},{9,13},{1... | collective-permute-start | bytes 208904 | tf_op jit(solution)/shard_map/ppermute | solution.py:447
  17.4 15.3 %collective-permute-start.6 = (bf16[272,128]{1,0:T(8,128)(2,1)S(1)}, bf16[272,128]{1,0:T(8,128)(2,1)S(1)}, u32[]{:S(2)}, u32[]{:S(2)}) collective-permute-start(bf16[272,128]{1,0:T(8,128)(2,1)S(1)} %get-tuple-element.28), channel_id=1, source_target_pairs={{0,16},{1,17},{2,18},{3,19},{4,20},{5,21},{6,22},{7,23},{8,24},{9,... | collective-permute-start | bytes 208904 | tf_op jit(solution)/shard_map/ppermute | solution.py:447
  20.6 0.7 %copy-start.2 = (bf16[32,16,128]{2,1,0:T(8,128)(2,1)}, bf16[32,16,128]{2,1,0:T(8,128)(2,1)S(1)}, u32[]{:S(2)}) copy-start(bf16[32,16,128]{2,1,0:T(8,128)(2,1)S(1)} %all-to-all-done) | copy-start | bytes 393220
  30.4 4.2 %collective-permute-start.3 = (bf16[64,128]{1,0:T(8,128)(2,1)}, bf16[64,128]{1,0:T(8,128)(2,1)S(1)}, u32[]{:S(2)}, u32[]{:S(2)}) collective-permute-start(bf16[64,128]{1,0:T(8,128)(2,1)} %get-tuple-element.25), channel_id=1, source_target_pairs={{0,3},{1,2},{2,1},{3,0},{4,7},{5,6},{6,5},{7,4},{8,11},{9,10},{10,... | collective-permute-start | bytes 49160 | tf_op jit(solution)/shard_map/ppermute | solution.py:431
  31.1 3.9 %collective-permute-start.2 = (bf16[64,128]{1,0:T(8,128)(2,1)}, bf16[64,128]{1,0:T(8,128)(2,1)S(1)}, u32[]{:S(2)}, u32[]{:S(2)}) collective-permute-start(bf16[64,128]{1,0:T(8,128)(2,1)} %get-tuple-element.25), channel_id=1, source_target_pairs={{0,2},{1,3},{2,0},{3,1},{4,6},{5,7},{6,4},{7,5},{8,10},{9,11},{10,... | collective-permute-start | bytes 49160 | tf_op jit(solution)/shard_map/ppermute | solution.py:431
  32.7 2.4 %collective-permute-start.1 = (bf16[64,128]{1,0:T(8,128)(2,1)}, bf16[64,128]{1,0:T(8,128)(2,1)S(1)}, u32[]{:S(2)}, u32[]{:S(2)}) collective-permute-start(bf16[64,128]{1,0:T(8,128)(2,1)} %get-tuple-element.25), channel_id=1, source_target_pairs={{0,1},{1,0},{2,3},{3,2},{4,5},{5,4},{6,7},{7,6},{8,9},{9,8},{10,11... | collective-permute-start | bytes 49160 | tf_op jit(solution)/shard_map/ppermute | solution.py:431
  35.1 0.8 %copy-start.1 = (f32[128,128]{1,0:T(8,128)S(1)}, f32[128,128]{1,0:T(8,128)}, u32[]{:S(2)}) copy-start(f32[128,128]{1,0:T(8,128)} %get-tuple-element.24.left_ref) | copy-start | bytes 196612

commit v15 on v14

--- a/solution.py
+++ b/solution.py
@@ -23,6 +23,7 @@
 CHUNK = 16
 MOST_PAIRED = 8
 BIG = 62 << 20
+MIDDLE = 52 << 20
 SMALL = 12 << 20
 PITCH = MROW + 8
 
@@ -66,7 +67,7 @@
 
 def name_slots(elem_count, face_count, capacity, conn_ref, named_ref):
     elements = conn_ref.shape[1]
-    slots = named_ref.shape[1]
+    slots = elem_count * face_count * capacity
     row = iota((PER_FACE, LANES), 0)
     lane = iota((PER_FACE, LANES), 1)
     first_lane = iota((1, LANES), 1)
@@ -83,15 +84,9 @@
             high = jnp.where(here, quotient, high)
             rest = jnp.where(here, remainder, rest)
         hot = jnp.concatenate([positions == lane + k for k in range(0, slots, LANES)], axis=1)
-        named_ref[a * PER_FACE : (a + 1) * PER_FACE, :] = hot.astype(BF16)
+        named_ref[a * PER_FACE : (a + 1) * PER_FACE, :slots] = hot.astype(BF16)
     names = jnp.where(row == 0, high, jnp.where(row == 1, rest, 0)).astype(F32)
-    named_ref[NAMED:, :] = jnp.concatenate([names] * (slots // LANES), axis=1).astype(BF16)
-
-
-def turn_rhs(rhs_ref, wide_ref, rhs_turned_ref):
-    wide_ref[...] = jnp.zeros_like(wide_ref)
-    wide_ref[0 : rhs_ref.shape[0], :] = rhs_ref[...].astype(F32)
-    rhs_turned_ref[...] = wide_ref[...].T.astype(BF16)
+    named_ref[NAMED:SHARE_ROWS, :LANES] = names.astype(BF16)
 
 
 def gram_kernel(
@@ -105,14 +100,15 @@
     new_owner_hbm,
     trace_hbm,
     conn_hbm,
+    rhs_hbm,
     placed_ref,
     named_ref,
     *refs,
 ):
-    out_refs, refs = refs[:-12], refs[-12:]
+    out_refs, refs = refs[:-14], refs[-14:]
     owner_ref, coarse_ref, tiles_ref, rows_ref = refs[:4]
     accs, diags = refs[4:6], refs[6:8]
-    new_owner_ref, trace_ref, conn_ref, sems = refs[8:]
+    new_owner_ref, trace_ref, conn_ref, rhs_ref, wide_ref, sems = refs[8:]
 
     def place_of(owner):
         if not paired:
@@ -135,6 +131,7 @@
     ]
     names = pltpu.make_async_copy(conn_hbm, conn_ref, sems.at[5])
     names.start()
+    copies.append(pltpu.make_async_copy(rhs_hbm, rhs_ref, sems.at[6]))
     for copy in copies:
         copy.start()
     for ref in (*accs, *diags):
@@ -143,6 +140,9 @@
     name_slots(elem_count, face_count, capacity, conn_ref, named_ref)
     for copy in copies:
         copy.wait()
+    wide_ref[...] = jnp.zeros_like(wide_ref)
+    wide_ref[0 : rhs_ref.shape[0], :] = rhs_ref[...].astype(F32)
+    named_ref[SHARE_ROWS:, : wide_ref.shape[1]] = wide_ref[...].astype(BF16)
     placed_ref[...] = place_rows(
         elem_count, face_count, capacity, new_owner_ref[...], trace_ref[...], placed_ref.shape[0]
     )
@@ -225,14 +225,12 @@
     face_count,
     table_hbm,
     named_hbm,
-    rhs_hbm,
     inverse_hbm,
     coupling_hbm,
     schur_hbm,
     share_ref,
     left_ref,
     named_ref,
-    rhs_ref,
     table_ref,
     inverse_ref,
     coupling_ref,
@@ -249,17 +247,15 @@
     block_sems,
     schur_sems,
 ):
-    elements = rhs_ref.shape[0]
-    modes = rhs_ref.shape[1]
+    elements, modes = inverse_ref.shape[:2]
     trace = FACES_PER_ELEM * FACE_COEFFS
     slots = table_ref.shape[0]
     own = left_ref.shape[0]
     capacity = own // face_count
     my_elem = lax.axis_index("elem")
     small = [
-        pltpu.make_async_copy(rhs_hbm, rhs_ref, small_sems.at[0]),
-        pltpu.make_async_copy(named_hbm, named_ref, small_sems.at[1]),
-        pltpu.make_async_copy(table_hbm, table_ref, small_sems.at[2]),
+        pltpu.make_async_copy(named_hbm, named_ref, small_sems.at[0]),
+        pltpu.make_async_copy(table_hbm, table_ref, small_sems.at[1]),
     ]
 
     def coupling_copy(e):
@@ -328,15 +324,17 @@
     for copy in small:
         copy.wait()
     sum_ref[...] = jnp.zeros_like(sum_ref)
-    turn_rhs(rhs_ref, wide_ref, rhs_turned_ref)
+    wide_ref[...] = jnp.zeros_like(wide_ref)
+    wide_ref[0:PER_FACE, :] = named_ref[SHARE_ROWS:, :modes].astype(F32)
+    rhs_turned_ref[...] = wide_ref[...].T.astype(BF16)
     row = iota((PER_FACE, LANES), 0)
     lane = iota((PER_FACE, LANES), 1)
 
     for a in range(FACES_PER_ELEM):
-        hot = named_ref[a * PER_FACE : (a + 1) * PER_FACE, :]
+        hot = named_ref[a * PER_FACE : (a + 1) * PER_FACE, :slots]
         vector_ref[:, a * LANES : (a + 1) * LANES] = -dot(hot, table_ref[...])
     vector_ref[:, trace:] = (row == lane).astype(F32)
-    share_ref[NAMED:, :] = named_ref[NAMED:, :LANES]
+    share_ref[NAMED:, :] = named_ref[NAMED:SHARE_ROWS, :LANES]
     place = position(my_elem, iota((own, slots), 0), elem_count, capacity)
     pick = (iota((own, slots), 1) == place).astype(BF16)
     left_ref[...] = dot(pick, table_ref[...])
@@ -470,6 +468,7 @@
     slots = own * elem_count
     devices = face_count * elem_count
     paired = face_count <= MOST_PAIRED
+    named_shape = (SHARE_ROWS + PER_FACE, max(slots, modes))
     sides = 2 if paired else 1
 
     blocks = face_count * NC
@@ -478,10 +477,10 @@
         functools.partial(gram_kernel, elem_count, face_count, capacity, paired),
         out_shape=[
             jax.ShapeDtypeStruct((slots, FACE_COEFFS), BF16),
-            jax.ShapeDtypeStruct((SHARE_ROWS, slots), BF16),
+            jax.ShapeDtypeStruct(named_shape, BF16),
         ]
         + [jax.ShapeDtypeStruct((blocks * (DENSE + 1) // sides, LANES), BF16)] * sides,
-        in_specs=[ANY] * 6,
+        in_specs=[ANY] * 7,
         out_specs=[VMEM] * (2 + sides),
         scratch_shapes=[
             pltpu.SMEM((tile_count,), I32),
@@ -495,7 +494,9 @@
             pltpu.VMEM((1, row_count), I32),
             pltpu.VMEM(trace_old.shape, BF16),
             pltpu.SMEM((FACES_PER_ELEM, elements), I32),
-            pltpu.SemaphoreType.DMA((6,)),
+            pltpu.VMEM((elements, modes), BF16),
+            pltpu.VMEM((PER_FACE, modes), F32),
+            pltpu.SemaphoreType.DMA((7,)),
         ],
         compiler_params=params(BIG),
         cost_estimate=cost(4 * tile_count * MROW * MROW * LANES, 12 << 20),
@@ -507,6 +508,7 @@
         new_owner.reshape(1, row_count),
         trace_old,
         connectivity.T,
+        interior_rhs,
     )
     if paired:
         came = trade(half_grams[1], face_count // 2, face_count)
@@ -533,7 +535,7 @@
         got = [lax.all_to_all(blocked, "face", 0, 0, tiled=True).reshape(-1, LANES)]
         before = half_grams[0]
 
-    rhs, _ = lax.optimization_barrier((interior_rhs, before))
+    named, _ = lax.optimization_barrier((named, before))
     schur_blocks, shares, left = pl.pallas_call(
         functools.partial(main_kernel, elem_count, face_count),
         out_shape=(
@@ -541,11 +543,10 @@
             jax.ShapeDtypeStruct((SHARE_ROWS, LANES), BF16),
             jax.ShapeDtypeStruct((own, FACE_COEFFS), F32),
         ),
-        in_specs=[ANY] * 5,
+        in_specs=[ANY] * 4,
         out_specs=(ANY, VMEM, VMEM),
         scratch_shapes=[
-            pltpu.VMEM((SHARE_ROWS, slots), BF16),
-            pltpu.VMEM((elements, modes), BF16),
+            pltpu.VMEM(named_shape, BF16),
             pltpu.VMEM((slots, FACE_COEFFS), BF16),
             pltpu.VMEM((elements, modes, modes), BF16),
             pltpu.VMEM((elements, modes, trace), BF16),
@@ -558,17 +559,17 @@
             pltpu.VMEM((trace, modes), BF16),
             pltpu.VMEM((trace, modes), BF16),
             pltpu.VMEM((trace, modes), BF16),
-            pltpu.SemaphoreType.DMA((3,)),
+            pltpu.SemaphoreType.DMA((2,)),
             pltpu.SemaphoreType.DMA((2, elements)),
             pltpu.SemaphoreType.DMA((elements,)),
         ],
-        compiler_params=params(BIG),
+        compiler_params=params(MIDDLE),
         cost_estimate=cost(
             2 * elements * modes * trace * (modes + trace),
             2 * elements * (modes * (modes + trace) + trace * trace),
         ),
         name="condense",
-    )(table, named, rhs, local_inverse, coupling)
+    )(table, named, local_inverse, coupling)
 
     all_shares = around(shares, "elem")
     coarse_blocks = pl.pallas_call(

time: 37 us -> 35.3 us (0.954)
  Pallas kernels: 15.6 us -> 14.7 us
  local copies, waits for them, and re-layouts: 2.45 us -> 1.84 us
    pallas_call x1, Pallas kernels: 9.05 us -> 8.13 us  [shards(): pl.pallas_call(functools.partial(main_kernel, elem_count, face_count), ou...]
    unnamed x6 -> x4, local copies, waits for them, and re-layouts: 2.45 us -> 1.84 us
  transfers between devices with their start and end apart: 8 -> 8, of which waited for: 2 -> 2; matrix products, arithmetic and copies ran while one was open for 0% -> 0% of each run, Pallas kernels for 30% -> 29%
where the time goes in v15:
time: 35.3 us; the launch traced here: 35 us
  starting transfers between devices  14.9 us (42%)
  Pallas kernels  14.7 us (42%)
  waiting for transfers between devices  2.88 us (8%)
  local copies, waits for them, and re-layouts  1.84 us (5%)
  between operations  0.69 us (2%)
    pallas_call x1, Pallas kernels, shards(): pl.pallas_call(functools.partial(main_kernel, elem_count, face_count), ou...  8.13 us
    ppermute x4, starting transfers between devices, trade(): return lax.ppermute(block, ('face', 'elem'), pairs)  7.66 us
    all_to_all x1, starting transfers between devices, shards(): lax.all_to_all(placed.reshape(devices, capacity, FACE_COEFFS), ('face', '...  4.9 us
    pallas_call x1, Pallas kernels, shards(): pl.pallas_call(functools.partial(gram_kernel, elem_count, face_count, cap...  3.82 us
    all_to_all x1, waiting for transfers between devices, shards(): lax.all_to_all(placed.reshape(devices, capacity, FACE_COEFFS), ('face', '...  2.59 us
    ppermute x3, starting transfers between devices, around(): lax.ppermute(block, axis, [(i, i ^ k) for i in range(count)])  2.31 us
    pallas_call x1, Pallas kernels, shards(): pl.pallas_call(coarse_kernel, out_shape=jax.ShapeDtypeStruct((NC, MROW *...  1.87 us
    unnamed x4, local copies, waits for them, and re-layouts  1.84 us
  transfers between devices with their start and end apart: 8, of which 2 were waited for; matrix products, arithmetic and copies ran while one was open for 0% of the time, Pallas kernels for 29%

profile of v15, /device:TPU:0, one launch (start us, length us, event | category | flops | bytes accessed | tf_op | source)
XLA Modules:
  0.0 35.0 jit_solution(3580166308813282485)
XLA Ops:
  0.6 3.8 %gram.1 = (bf16[512,128]{1,0:T(8,128)(2,1)}, bf16[80,512]{1,0:T(8,128)(2,1)}, bf16[1088,128]{1,0:T(8,128)(2,1)}, bf16[1088,128]{1,0:T(8,128)(2,1)}) custom-call(s32[96]{0:T(128)} %bitcast.8, s32[96]{0:T(128)} %coarse_hbm.1, bf16[96,6144]{1,0:T(8,128)(2,1)} %tiles_hbm.1, s32[1,64]{1,0:T(1,128)} %bitcast.9, bf16[64,128]{1,0:T(8,128)(2,1)} %trace_hbm.1, ...), custom_call_target="tpu_custom_call" | custom-call | flops 201326592 | bytes 12582912 | tf_op jit(solution)/shard_map/gram/pallas_call | solution.py:476
  4.5 3.0 %collective-permute-start = (bf16[1088,128]{1,0:T(8,128)(2,1)}, bf16[1088,128]{1,0:T(8,128)(2,1)S(1)}, u32[]{:S(2)}, u32[]{:S(2)}) collective-permute-start(bf16[1088,128]{1,0:T(8,128)(2,1)} %get-tuple-element.20), channel_id=1, source_target_pairs={{0,4},{1,9},{2,6},{3,11},{4,0},{5,13},{6,2},{7,15},{8,12},{9,1},{1... | collective-permute-start | bytes 835592 | tf_op jit(solution)/shard_map/ppermute | solution.py:445
  7.5 4.9 %all-to-all-start = ((bf16[32,16,128]{2,1,0:T(8,128)(2,1)}), bf16[32,16,128]{2,1,0:T(8,128)(2,1)S(1)}, u32[]{:S(2)}, u32[]{:S(2)}) async-start(bf16[32,16,128]{2,1,0:T(8,128)(2,1)} %bitcast.6), calls=%async_computation | async-start | bytes 262144 | tf_op jit(solution)/shard_map/all_to_all | solution.py:515
  12.4 0.0 collective-permute-done.came_ref
  12.4 0.0 copy-start
  12.4 0.9 %copy-done = bf16[1088,128]{1,0:T(8,128)(2,1)S(1)} copy-done((bf16[1088,128]{1,0:T(8,128)(2,1)S(1)}, bf16[1088,128]{1,0:T(8,128)(2,1)}, u32[]{:S(2)}) %copy-start) | copy-done | bytes 278552
  13.4 0.1 join.1
  13.4 4.0 %collective-permute-start.4 = (bf16[272,128]{1,0:T(8,128)(2,1)S(1)}, bf16[272,128]{1,0:T(8,128)(2,1)S(1)}, u32[]{:S(2)}, u32[]{:S(2)}) collective-permute-start(bf16[272,128]{1,0:T(8,128)(2,1)S(1)} %get-tuple-element.26), channel_id=1, source_target_pairs={{0,24},{1,21},{2,26},{3,23},{4,28},{5,17},{6,30},{7,19},{8,16},{9,... | collective-permute-start | bytes 208904 | tf_op jit(solution)/shard_map/ppermute | solution.py:445
  17.4 0.0 collective-permute-start.5
  17.4 0.6 %collective-permute-start.6 = (bf16[272,128]{1,0:T(8,128)(2,1)S(1)}, bf16[272,128]{1,0:T(8,128)(2,1)S(1)}, u32[]{:S(2)}, u32[]{:S(2)}) collective-permute-start(bf16[272,128]{1,0:T(8,128)(2,1)S(1)} %get-tuple-element.28), channel_id=1, source_target_pairs={{0,16},{1,17},{2,18},{3,19},{4,20},{5,21},{6,22},{7,23},{8,24},{9,... | collective-permute-start | bytes 208904 | tf_op jit(solution)/shard_map/ppermute | solution.py:445
  18.1 2.6 %all-to-all-done = bf16[32,16,128]{2,1,0:T(8,128)(2,1)S(1)} async-done(((bf16[32,16,128]{2,1,0:T(8,128)(2,1)}), bf16[32,16,128]{2,1,0:T(8,128)(2,1)S(1)}, u32[]{:S(2)}, u32[]{:S(2)}) %all-to-all-start) | async-done | bytes 131104 | tf_op jit(solution)/shard_map/all_to_all | solution.py:515
  20.7 0.9 %copy-done.1 = bf16[80,512]{1,0:T(8,128)(2,1)S(1)} copy-done((bf16[80,512]{1,0:T(8,128)(2,1)S(1)}, bf16[80,512]{1,0:T(8,128)(2,1)}, u32[]{:S(2)}) %copy-start.1) | copy-done | bytes 81944
  21.5 8.1 %condense.1 = (bf16[9,384,384]{2,1,0:T(8,128)(2,1)}, bf16[64,128]{1,0:T(8,128)(2,1)S(1)}, f32[128,128]{1,0:T(8,128)S(1)}) custom-call(bf16[512,128]{1,0:T(8,128)(2,1)S(1)} %bitcast.5, bf16[80,512]{1,0:T(8,128)(2,1)S(1)} %copy-done.1, bf16[9,512,512]{2,1,0:T(8,128)(2,1)} %inverse_hbm.1, bf16[9,512,384]{2,1,0:T(8,128)(2,1)} %coupling_hbm.1), custom_call_target="tpu_custom_call" | custom-call | flops 3170893824 | bytes 10911744 | tf_op jit(solution)/shard_map/condense/pallas_call | solution.py:539
  29.7 0.7 %collective-permute-start.3 = (bf16[64,128]{1,0:T(8,128)(2,1)S(1)}, bf16[64,128]{1,0:T(8,128)(2,1)S(1)}, u32[]{:S(2)}, u32[]{:S(2)}) collective-permute-start(bf16[64,128]{1,0:T(8,128)(2,1)S(1)} %get-tuple-element.25), channel_id=1, source_target_pairs={{0,3},{1,2},{2,1},{3,0},{4,7},{5,6},{6,5},{7,4},{8,11},{9,10},{10,... | collective-permute-start | bytes 49160 | tf_op jit(solution)/shard_map/ppermute | solution.py:429
  30.4 1.6 %collective-permute-start.2 = (bf16[64,128]{1,0:T(8,128)(2,1)S(1)}, bf16[64,128]{1,0:T(8,128)(2,1)S(1)}, u32[]{:S(2)}, u32[]{:S(2)}) collective-permute-start(bf16[64,128]{1,0:T(8,128)(2,1)S(1)} %get-tuple-element.25), channel_id=1, source_target_pairs={{0,2},{1,3},{2,0},{3,1},{4,6},{5,7},{6,4},{7,5},{8,10},{9,11},{10,... | collective-permute-start | bytes 49160 | tf_op jit(solution)/shard_map/ppermute | solution.py:429
  32.0 0.0 collective-permute-done.4.refs_1_
  32.0 0.0 collective-permute-start.1
  32.0 0.0 collective-permute-done.5.refs_2_
  32.0 0.0 collective-permute-done.6.refs_3_
  32.0 1.9 %coarse.1 = f32[16,4096]{1,0:T(8,128)} custom-call(bf16[272,128]{1,0:T(8,128)(2,1)S(1)} %get-tuple-element.21.refs_0_, bf16[272,128]{1,0:T(8,128)(2,1)S(1)} %collective-permute-done.4.refs_1_, bf16[272,128]{1,0:T(8,128)(2,1)S(1)} %collective-permute-done.5.refs_2_, bf16[272,128]{1,0:T(8,128)(2,1)S(1)} %collective-permute-done.6.refs_3_), custom_call_target="tpu_custom_call" | custom-call | bytes 8388608 | tf_op jit(solution)/shard_map/coarse/pallas_call | solution.py:575
  33.9 0.0 collective-permute-done.3.refs_2_
  33.9 0.3 collective-permute-done.2.refs_1_
  34.2 0.0 collective-permute-done.1.refs_0_
  34.2 0.8 %residual.1 = f32[128,128]{1,0:T(8,128)} custom-call(f32[128,128]{1,0:T(8,128)S(1)} %get-tuple-element.24.left_ref, bf16[64,128]{1,0:T(8,128)(2,1)S(1)} %collective-permute-done.1.refs_0_, bf16[64,128]{1,0:T(8,128)(2,1)S(1)} %collective-permute-done.2.refs_1_, bf16[64,128]{1,0:T(8,128)(2,1)S(1)} %collective-permute-done.3.refs_2_), custom_call_target="tpu_custom_call" | custom-call | tf_op jit(solution)/shard_map/residual/pallas_call | solution.py:589
  (1 shorter events, 0.0 us)
Async XLA Ops:
  4.5 7.9 %collective-permute-start = (bf16[1088,128]{1,0:T(8,128)(2,1)}, bf16[1088,128]{1,0:T(8,128)(2,1)S(1)}, u32[]{:S(2)}, u32[]{:S(2)}) collective-permute-start(bf16[1088,128]{1,0:T(8,128)(2,1)} %get-tuple-element.20), channel_id=1, source_target_pairs={{0,4},{1,9},{2,6},{3,11},{4,0},{5,13},{6,2},{7,15},{8,12},{9,1},{1... | collective-permute-start | bytes 835592 | tf_op jit(solution)/shard_map/ppermute | solution.py:445
  7.5 13.2 %all-to-all-start = ((bf16[32,16,128]{2,1,0:T(8,128)(2,1)}), bf16[32,16,128]{2,1,0:T(8,128)(2,1)S(1)}, u32[]{:S(2)}, u32[]{:S(2)}) async-start(bf16[32,16,128]{2,1,0:T(8,128)(2,1)} %bitcast.6), calls=%async_computation | async-start | bytes 262144 | tf_op jit(solution)/shard_map/all_to_all | solution.py:515
  12.4 1.0 %copy-start = (bf16[1088,128]{1,0:T(8,128)(2,1)S(1)}, bf16[1088,128]{1,0:T(8,128)(2,1)}, u32[]{:S(2)}) copy-start(bf16[1088,128]{1,0:T(8,128)(2,1)} %get-tuple-element.19.kept_ref) | copy-start | bytes 835588
  13.4 18.6 %collective-permute-start.4 = (bf16[272,128]{1,0:T(8,128)(2,1)S(1)}, bf16[272,128]{1,0:T(8,128)(2,1)S(1)}, u32[]{:S(2)}, u32[]{:S(2)}) collective-permute-start(bf16[272,128]{1,0:T(8,128)(2,1)S(1)} %get-tuple-element.26), channel_id=1, source_target_pairs={{0,24},{1,21},{2,26},{3,23},{4,28},{5,17},{6,30},{7,19},{8,16},{9,... | collective-permute-start | bytes 208904 | tf_op jit(solution)/shard_map/ppermute | solution.py:445
  17.4 14.6 %collective-permute-start.5 = (bf16[272,128]{1,0:T(8,128)(2,1)S(1)}, bf16[272,128]{1,0:T(8,128)(2,1)S(1)}, u32[]{:S(2)}, u32[]{:S(2)}) collective-permute-start(bf16[272,128]{1,0:T(8,128)(2,1)S(1)} %get-tuple-element.27), channel_id=1, source_target_pairs={{0,8},{1,5},{2,10},{3,7},{4,12},{5,1},{6,14},{7,3},{8,0},{9,13},{1... | collective-permute-start | bytes 208904 | tf_op jit(solution)/shard_map/ppermute | solution.py:445
  17.4 14.6 %collective-permute-start.6 = (bf16[272,128]{1,0:T(8,128)(2,1)S(1)}, bf16[272,128]{1,0:T(8,128)(2,1)S(1)}, u32[]{:S(2)}, u32[]{:S(2)}) collective-permute-start(bf16[272,128]{1,0:T(8,128)(2,1)S(1)} %get-tuple-element.28), channel_id=1, source_target_pairs={{0,16},{1,17},{2,18},{3,19},{4,20},{5,21},{6,22},{7,23},{8,24},{9,... | collective-permute-start | bytes 208904 | tf_op jit(solution)/shard_map/ppermute | solution.py:445
  20.7 0.9 %copy-start.1 = (bf16[80,512]{1,0:T(8,128)(2,1)S(1)}, bf16[80,512]{1,0:T(8,128)(2,1)}, u32[]{:S(2)}) copy-start(bf16[80,512]{1,0:T(8,128)(2,1)} %get-tuple-element.22.named_hbm) | copy-start | bytes 245764
  29.7 4.2 %collective-permute-start.3 = (bf16[64,128]{1,0:T(8,128)(2,1)S(1)}, bf16[64,128]{1,0:T(8,128)(2,1)S(1)}, u32[]{:S(2)}, u32[]{:S(2)}) collective-permute-start(bf16[64,128]{1,0:T(8,128)(2,1)S(1)} %get-tuple-element.25), channel_id=1, source_target_pairs={{0,3},{1,2},{2,1},{3,0},{4,7},{5,6},{6,5},{7,4},{8,11},{9,10},{10,... | collective-permute-start | bytes 49160 | tf_op jit(solution)/shard_map/ppermute | solution.py:429
  30.4 3.7 %collective-permute-start.2 = (bf16[64,128]{1,0:T(8,128)(2,1)S(1)}, bf16[64,128]{1,0:T(8,128)(2,1)S(1)}, u32[]{:S(2)}, u32[]{:S(2)}) collective-permute-start(bf16[64,128]{1,0:T(8,128)(2,1)S(1)} %get-tuple-element.25), channel_id=1, source_target_pairs={{0,2},{1,3},{2,0},{3,1},{4,6},{5,7},{6,4},{7,5},{8,10},{9,11},{10,... | collective-permute-start | bytes 49160 | tf_op jit(solution)/shard_map/ppermute | solution.py:429
  32.0 2.2 %collective-permute-start.1 = (bf16[64,128]{1,0:T(8,128)(2,1)S(1)}, bf16[64,128]{1,0:T(8,128)(2,1)S(1)}, u32[]{:S(2)}, u32[]{:S(2)}) collective-permute-start(bf16[64,128]{1,0:T(8,128)(2,1)S(1)} %get-tuple-element.25), channel_id=1, source_target_pairs={{0,1},{1,0},{2,3},{3,2},{4,5},{5,4},{6,7},{7,6},{8,9},{9,8},{10,11... | collective-permute-start | bytes 49160 | tf_op jit(solution)/shard_map/ppermute | solution.py:429

commit v16 on v15

--- a/solution.py
+++ b/solution.py
@@ -102,9 +102,12 @@
     conn_hbm,
     rhs_hbm,
     placed_ref,
-    named_ref,
     *refs,
 ):
+    if paired:
+        *refs, named_ref = refs
+    else:
+        named_ref, *refs = refs
     out_refs, refs = refs[:-14], refs[-14:]
     owner_ref, coarse_ref, tiles_ref, rows_ref = refs[:4]
     accs, diags = refs[4:6], refs[6:8]
@@ -211,13 +214,22 @@
         out_ref[start + size : start + size + NC, :] = (
             diags[0][here, :] + diags[1][here, :]
         ).astype(BF16)
-
-
-def join_kernel(kept_ref, came_ref, *out_refs):
+    if paired:
+        rows = named_ref.shape[0]
+        for k in range(named_ref.shape[1] // LANES):
+            start = each * OWNER_ROWS + k * rows
+            out_refs[0][start : start + rows, :] = named_ref[:, k * LANES : (k + 1) * LANES]
+
+
+def join_kernel(kept_ref, came_ref, named_ref, *out_refs):
     for k, out_ref in enumerate(out_refs):
         here = slice(k * OWNER_ROWS, (k + 1) * OWNER_ROWS)
         total = kept_ref[here, :].astype(F32) + came_ref[here, :].astype(F32)
         out_ref[...] = total.astype(BF16)
+    rows = named_ref.shape[0]
+    for k in range(named_ref.shape[1] // LANES):
+        start = came_ref.shape[0] + k * rows
+        named_ref[:, k * LANES : (k + 1) * LANES] = kept_ref[start : start + rows, :]
 
 
 def main_kernel(
@@ -473,15 +485,18 @@
 
     blocks = face_count * NC
     sums_shape = (blocks * DENSE, LANES)
-    placed, named, *half_grams = pl.pallas_call(
+    half = (blocks * (DENSE + 1) // sides, LANES)
+    named_out = jax.ShapeDtypeStruct(named_shape, BF16)
+    if paired:
+        more = named_shape[0] * named_shape[1] // LANES
+        outs = [jax.ShapeDtypeStruct((half[0] + more, LANES), BF16), jax.ShapeDtypeStruct(half, BF16)]
+    else:
+        outs = [named_out, jax.ShapeDtypeStruct(half, BF16)]
+    placed, *half_grams = pl.pallas_call(
         functools.partial(gram_kernel, elem_count, face_count, capacity, paired),
-        out_shape=[
-            jax.ShapeDtypeStruct((slots, FACE_COEFFS), BF16),
-            jax.ShapeDtypeStruct(named_shape, BF16),
-        ]
-        + [jax.ShapeDtypeStruct((blocks * (DENSE + 1) // sides, LANES), BF16)] * sides,
+        out_shape=[jax.ShapeDtypeStruct((slots, FACE_COEFFS), BF16)] + outs,
         in_specs=[ANY] * 7,
-        out_specs=[VMEM] * (2 + sides),
+        out_specs=[VMEM] * (1 + len(outs)),
         scratch_shapes=[
             pltpu.SMEM((tile_count,), I32),
             pltpu.SMEM((tile_count,), I32),
@@ -497,7 +512,8 @@
             pltpu.VMEM((elements, modes), BF16),
             pltpu.VMEM((PER_FACE, modes), F32),
             pltpu.SemaphoreType.DMA((7,)),
-        ],
+        ]
+        + [pltpu.VMEM(named_shape, BF16)] * paired,
         compiler_params=params(BIG),
         cost_estimate=cost(4 * tile_count * MROW * MROW * LANES, 12 << 20),
         name="gram",
@@ -517,11 +533,12 @@
     ).reshape(slots, FACE_COEFFS)
 
     if paired:
-        joined = pl.pallas_call(
+        named, *joined = pl.pallas_call(
             join_kernel,
-            out_shape=[jax.ShapeDtypeStruct((OWNER_ROWS, LANES), BF16)] * (face_count // 2),
+            out_shape=[named_out]
+            + [jax.ShapeDtypeStruct((OWNER_ROWS, LANES), BF16)] * (face_count // 2),
             in_specs=[VMEM] * 2,
-            out_specs=[VMEM] * (face_count // 2),
+            out_specs=[VMEM] * (1 + face_count // 2),
             compiler_params=params(SMALL),
             cost_estimate=cost(0, 4 << 20),
             name="join",
@@ -529,13 +546,11 @@
         got = [joined[0]] + [
             trade(joined[k], k, face_count) for k in range(face_count // 2 - 1, 0, -1)
         ]
-        before = joined[0]
     else:
-        blocked = half_grams[0].reshape(face_count, OWNER_ROWS, LANES)
+        named, blocked = half_grams
+        blocked = blocked.reshape(face_count, OWNER_ROWS, LANES)
         got = [lax.all_to_all(blocked, "face", 0, 0, tiled=True).reshape(-1, LANES)]
-        before = half_grams[0]
-
-    named, _ = lax.optimization_barrier((named, before))
+
     schur_blocks, shares, left = pl.pallas_call(
         functools.partial(main_kernel, elem_count, face_count),
         out_shape=(

time: 35.3 us -> 34.4 us (0.975)
  local copies, waits for them, and re-layouts: 1.84 us -> 0.98 us
    unnamed x4 -> x2, local copies, waits for them, and re-layouts: 1.84 us -> 0.98 us
  transfers between devices with their start and end apart: 8 -> 8, of which waited for: 2 -> 2; matrix products, arithmetic and copies ran while one was open for 0% -> 0% of each run, Pallas kernels for 29% -> 30%
where the time goes in v16:
time: 34.4 us; the launch traced here: 34.1 us
  starting transfers between devices  14.9 us (43%)
  Pallas kernels  14.7 us (43%)
  waiting for transfers between devices  2.84 us (8%)
  local copies, waits for them, and re-layouts  0.98 us (3%)
  between operations  0.69 us (2%)
    pallas_call x1, Pallas kernels, shards(): pl.pallas_call(functools.partial(main_kernel, elem_count, face_count), ou...  8.13 us
    ppermute x4, starting transfers between devices, trade(): return lax.ppermute(block, ('face', 'elem'), pairs)  7.66 us
    all_to_all x1, starting transfers between devices, shards(): lax.all_to_all(placed.reshape(devices, capacity, FACE_COEFFS), ('face', '...  4.89 us
    pallas_call x1, Pallas kernels, shards(): pl.pallas_call(functools.partial(gram_kernel, elem_count, face_count, cap...  3.82 us
    all_to_all x1, waiting for transfers between devices, shards(): lax.all_to_all(placed.reshape(devices, capacity, FACE_COEFFS), ('face', '...  2.56 us
    ppermute x3, starting transfers between devices, around(): lax.ppermute(block, axis, [(i, i ^ k) for i in range(count)])  2.31 us
    pallas_call x1, Pallas kernels, shards(): pl.pallas_call(coarse_kernel, out_shape=jax.ShapeDtypeStruct((NC, MROW *...  1.87 us
    unnamed x2, local copies, waits for them, and re-layouts  0.98 us
  transfers between devices with their start and end apart: 8, of which 2 were waited for; matrix products, arithmetic and copies ran while one was open for 0% of the time, Pallas kernels for 30%

profile of v16, /device:TPU:0, one launch (start us, length us, event | category | flops | bytes accessed | tf_op | source)
XLA Modules:
  0.0 34.1 jit_solution(15865387435588533433)
XLA Ops:
  0.6 3.8 %gram.1 = (bf16[512,128]{1,0:T(8,128)(2,1)}, bf16[1408,128]{1,0:T(8,128)(2,1)}, bf16[1088,128]{1,0:T(8,128)(2,1)}) custom-call(s32[96]{0:T(128)} %bitcast.8, s32[96]{0:T(128)} %coarse_hbm.1, bf16[96,6144]{1,0:T(8,128)(2,1)} %tiles_hbm.1, s32[1,64]{1,0:T(1,128)} %bitcast.9, bf16[64,128]{1,0:T(8,128)(2,1)} %trace_hbm.1, s32[3,9]{1,0:T(4,128)} %bitcast.7, ...), custom_call_target="tpu_custom_call" | custom-call | flops 201326592 | bytes 12582912 | tf_op jit(solution)/shard_map/gram/pallas_call | solution.py:495
  4.5 3.0 %collective-permute-start = (bf16[1088,128]{1,0:T(8,128)(2,1)}, bf16[1088,128]{1,0:T(8,128)(2,1)S(1)}, u32[]{:S(2)}, u32[]{:S(2)}) collective-permute-start(bf16[1088,128]{1,0:T(8,128)(2,1)} %get-tuple-element.18), channel_id=1, source_target_pairs={{0,4},{1,9},{2,6},{3,11},{4,0},{5,13},{6,2},{7,15},{8,12},{9,1},{1... | collective-permute-start | bytes 835592 | tf_op jit(solution)/shard_map/ppermute | solution.py:457
  7.5 4.9 %all-to-all-start = ((bf16[32,16,128]{2,1,0:T(8,128)(2,1)}), bf16[32,16,128]{2,1,0:T(8,128)(2,1)S(1)}, u32[]{:S(2)}, u32[]{:S(2)}) async-start(bf16[32,16,128]{2,1,0:T(8,128)(2,1)} %bitcast.6), calls=%async_computation | async-start | bytes 262144 | tf_op jit(solution)/shard_map/all_to_all | solution.py:531
  12.4 0.0 collective-permute-done.came_ref
  12.4 0.0 copy-start
  12.4 1.0 %copy-done = bf16[1408,128]{1,0:T(8,128)(2,1)S(1)} copy-done((bf16[1408,128]{1,0:T(8,128)(2,1)S(1)}, bf16[1408,128]{1,0:T(8,128)(2,1)}, u32[]{:S(2)}) %copy-start) | copy-done | bytes 360472
  13.4 0.1 join.1
  13.5 4.0 %collective-permute-start.4 = (bf16[272,128]{1,0:T(8,128)(2,1)S(1)}, bf16[272,128]{1,0:T(8,128)(2,1)S(1)}, u32[]{:S(2)}, u32[]{:S(2)}) collective-permute-start(bf16[272,128]{1,0:T(8,128)(2,1)S(1)} %get-tuple-element.24), channel_id=1, source_target_pairs={{0,24},{1,21},{2,26},{3,23},{4,28},{5,17},{6,30},{7,19},{8,16},{9,... | collective-permute-start | bytes 208904 | tf_op jit(solution)/shard_map/ppermute | solution.py:457
  17.5 0.0 collective-permute-start.5
  17.5 0.6 %collective-permute-start.6 = (bf16[272,128]{1,0:T(8,128)(2,1)S(1)}, bf16[272,128]{1,0:T(8,128)(2,1)S(1)}, u32[]{:S(2)}, u32[]{:S(2)}) collective-permute-start(bf16[272,128]{1,0:T(8,128)(2,1)S(1)} %get-tuple-element.26), channel_id=1, source_target_pairs={{0,16},{1,17},{2,18},{3,19},{4,20},{5,21},{6,22},{7,23},{8,24},{9,... | collective-permute-start | bytes 208904 | tf_op jit(solution)/shard_map/ppermute | solution.py:457
  18.1 2.6 %all-to-all-done = bf16[32,16,128]{2,1,0:T(8,128)(2,1)S(1)} async-done(((bf16[32,16,128]{2,1,0:T(8,128)(2,1)}), bf16[32,16,128]{2,1,0:T(8,128)(2,1)S(1)}, u32[]{:S(2)}, u32[]{:S(2)}) %all-to-all-start) | async-done | bytes 131104 | tf_op jit(solution)/shard_map/all_to_all | solution.py:531
  20.7 8.1 %condense.1 = (bf16[9,384,384]{2,1,0:T(8,128)(2,1)}, bf16[64,128]{1,0:T(8,128)(2,1)S(1)}, f32[128,128]{1,0:T(8,128)S(1)}) custom-call(bf16[512,128]{1,0:T(8,128)(2,1)S(1)} %bitcast.5, bf16[80,512]{1,0:T(8,128)(2,1)S(1)} %get-tuple-element.19.named_hbm, bf16[9,512,512]{2,1,0:T(8,128)(2,1)} %inverse_hbm.1, bf16[9,512,384]{2,1,0:T(8,128)(2,1)} %coupling_hbm.1), custom_call_target="tpu_custom_call" | custom-call | flops 3170893824 | bytes 10911744 | tf_op jit(solution)/shard_map/condense/pallas_call | solution.py:554
  28.8 0.7 %collective-permute-start.3 = (bf16[64,128]{1,0:T(8,128)(2,1)S(1)}, bf16[64,128]{1,0:T(8,128)(2,1)S(1)}, u32[]{:S(2)}, u32[]{:S(2)}) collective-permute-start(bf16[64,128]{1,0:T(8,128)(2,1)S(1)} %get-tuple-element.22), channel_id=1, source_target_pairs={{0,3},{1,2},{2,1},{3,0},{4,7},{5,6},{6,5},{7,4},{8,11},{9,10},{10,... | collective-permute-start | bytes 49160 | tf_op jit(solution)/shard_map/ppermute | solution.py:441
  29.5 1.6 %collective-permute-start.2 = (bf16[64,128]{1,0:T(8,128)(2,1)S(1)}, bf16[64,128]{1,0:T(8,128)(2,1)S(1)}, u32[]{:S(2)}, u32[]{:S(2)}) collective-permute-start(bf16[64,128]{1,0:T(8,128)(2,1)S(1)} %get-tuple-element.22), channel_id=1, source_target_pairs={{0,2},{1,3},{2,0},{3,1},{4,6},{5,7},{6,4},{7,5},{8,10},{9,11},{10,... | collective-permute-start | bytes 49160 | tf_op jit(solution)/shard_map/ppermute | solution.py:441
  31.1 0.0 collective-permute-done.4.refs_1_
  31.1 0.0 collective-permute-start.1
  31.1 0.0 collective-permute-done.5.refs_2_
  31.1 0.0 collective-permute-done.6.refs_3_
  31.1 1.9 %coarse.1 = f32[16,4096]{1,0:T(8,128)} custom-call(bf16[272,128]{1,0:T(8,128)(2,1)S(1)} %get-tuple-element.23.refs_0_, bf16[272,128]{1,0:T(8,128)(2,1)S(1)} %collective-permute-done.4.refs_1_, bf16[272,128]{1,0:T(8,128)(2,1)S(1)} %collective-permute-done.5.refs_2_, bf16[272,128]{1,0:T(8,128)(2,1)S(1)} %collective-permute-done.6.refs_3_), custom_call_target="tpu_custom_call" | custom-call | bytes 8388608 | tf_op jit(solution)/shard_map/coarse/pallas_call | solution.py:590
  33.0 0.0 collective-permute-done.3.refs_2_
  33.0 0.3 collective-permute-done.2.refs_1_
  33.3 0.0 collective-permute-done.1.refs_0_
  33.3 0.8 %residual.1 = f32[128,128]{1,0:T(8,128)} custom-call(f32[128,128]{1,0:T(8,128)S(1)} %get-tuple-element.21.left_ref, bf16[64,128]{1,0:T(8,128)(2,1)S(1)} %collective-permute-done.1.refs_0_, bf16[64,128]{1,0:T(8,128)(2,1)S(1)} %collective-permute-done.2.refs_1_, bf16[64,128]{1,0:T(8,128)(2,1)S(1)} %collective-permute-done.3.refs_2_), custom_call_target="tpu_custom_call" | custom-call | tf_op jit(solution)/shard_map/residual/pallas_call | solution.py:604
Async XLA Ops:
  4.5 7.9 %collective-permute-start = (bf16[1088,128]{1,0:T(8,128)(2,1)}, bf16[1088,128]{1,0:T(8,128)(2,1)S(1)}, u32[]{:S(2)}, u32[]{:S(2)}) collective-permute-start(bf16[1088,128]{1,0:T(8,128)(2,1)} %get-tuple-element.18), channel_id=1, source_target_pairs={{0,4},{1,9},{2,6},{3,11},{4,0},{5,13},{6,2},{7,15},{8,12},{9,1},{1... | collective-permute-start | bytes 835592 | tf_op jit(solution)/shard_map/ppermute | solution.py:457
  7.5 13.2 %all-to-all-start = ((bf16[32,16,128]{2,1,0:T(8,128)(2,1)}), bf16[32,16,128]{2,1,0:T(8,128)(2,1)S(1)}, u32[]{:S(2)}, u32[]{:S(2)}) async-start(bf16[32,16,128]{2,1,0:T(8,128)(2,1)} %bitcast.6), calls=%async_computation | async-start | bytes 262144 | tf_op jit(solution)/shard_map/all_to_all | solution.py:531
  12.4 1.0 %copy-start = (bf16[1408,128]{1,0:T(8,128)(2,1)S(1)}, bf16[1408,128]{1,0:T(8,128)(2,1)}, u32[]{:S(2)}) copy-start(bf16[1408,128]{1,0:T(8,128)(2,1)} %get-tuple-element.17.kept_ref) | copy-start | bytes 1081348
  13.5 17.6 %collective-permute-start.4 = (bf16[272,128]{1,0:T(8,128)(2,1)S(1)}, bf16[272,128]{1,0:T(8,128)(2,1)S(1)}, u32[]{:S(2)}, u32[]{:S(2)}) collective-permute-start(bf16[272,128]{1,0:T(8,128)(2,1)S(1)} %get-tuple-element.24), channel_id=1, source_target_pairs={{0,24},{1,21},{2,26},{3,23},{4,28},{5,17},{6,30},{7,19},{8,16},{9,... | collective-permute-start | bytes 208904 | tf_op jit(solution)/shard_map/ppermute | solution.py:457
  17.5 13.7 %collective-permute-start.5 = (bf16[272,128]{1,0:T(8,128)(2,1)S(1)}, bf16[272,128]{1,0:T(8,128)(2,1)S(1)}, u32[]{:S(2)}, u32[]{:S(2)}) collective-permute-start(bf16[272,128]{1,0:T(8,128)(2,1)S(1)} %get-tuple-element.25), channel_id=1, source_target_pairs={{0,8},{1,5},{2,10},{3,7},{4,12},{5,1},{6,14},{7,3},{8,0},{9,13},{1... | collective-permute-start | bytes 208904 | tf_op jit(solution)/shard_map/ppermute | solution.py:457
  17.5 13.7 %collective-permute-start.6 = (bf16[272,128]{1,0:T(8,128)(2,1)S(1)}, bf16[272,128]{1,0:T(8,128)(2,1)S(1)}, u32[]{:S(2)}, u32[]{:S(2)}) collective-permute-start(bf16[272,128]{1,0:T(8,128)(2,1)S(1)} %get-tuple-element.26), channel_id=1, source_target_pairs={{0,16},{1,17},{2,18},{3,19},{4,20},{5,21},{6,22},{7,23},{8,24},{9,... | collective-permute-start | bytes 208904 | tf_op jit(solution)/shard_map/ppermute | solution.py:457
  28.8 4.2 %collective-permute-start.3 = (bf16[64,128]{1,0:T(8,128)(2,1)S(1)}, bf16[64,128]{1,0:T(8,128)(2,1)S(1)}, u32[]{:S(2)}, u32[]{:S(2)}) collective-permute-start(bf16[64,128]{1,0:T(8,128)(2,1)S(1)} %get-tuple-element.22), channel_id=1, source_target_pairs={{0,3},{1,2},{2,1},{3,0},{4,7},{5,6},{6,5},{7,4},{8,11},{9,10},{10,... | collective-permute-start | bytes 49160 | tf_op jit(solution)/shard_map/ppermute | solution.py:441
  29.5 3.7 %collective-permute-start.2 = (bf16[64,128]{1,0:T(8,128)(2,1)S(1)}, bf16[64,128]{1,0:T(8,128)(2,1)S(1)}, u32[]{:S(2)}, u32[]{:S(2)}) collective-permute-start(bf16[64,128]{1,0:T(8,128)(2,1)S(1)} %get-tuple-element.22), channel_id=1, source_target_pairs={{0,2},{1,3},{2,0},{3,1},{4,6},{5,7},{6,4},{7,5},{8,10},{9,11},{10,... | collective-permute-start | bytes 49160 | tf_op jit(solution)/shard_map/ppermute | solution.py:441
  31.1 2.2 %collective-permute-start.1 = (bf16[64,128]{1,0:T(8,128)(2,1)S(1)}, bf16[64,128]{1,0:T(8,128)(2,1)S(1)}, u32[]{:S(2)}, u32[]{:S(2)}) collective-permute-start(bf16[64,128]{1,0:T(8,128)(2,1)S(1)} %get-tuple-element.22), channel_id=1, source_target_pairs={{0,1},{1,0},{2,3},{3,2},{4,5},{5,4},{6,7},{7,6},{8,9},{9,8},{10,11... | collective-permute-start | bytes 49160 | tf_op jit(solution)/shard_map/ppermute | solution.py:441

commit v17 on v16

--- a/solution.py
+++ b/solution.py
@@ -20,6 +20,7 @@
 NAMED = FACES_PER_ELEM * PER_FACE
 SHARE_ROWS = NAMED + 16
 SLOT_BASE = 16
+ROWS = 8
 CHUNK = 16
 MOST_PAIRED = 8
 BIG = 62 << 20
@@ -390,7 +391,7 @@
 
 
 def coarse_kernel(*refs):
-    got_refs, (out_ref, sum_ref, full_ref) = refs[:-3], refs[-3:]
+    got_refs, (out_hbm, out_ref, sum_ref, full_ref, sems) = refs[:-5], refs[-5:]
     sum_ref[...] = sum(
         got_ref[k : k + OWNER_ROWS, :].astype(F32)
         for got_ref in got_refs
@@ -405,22 +406,32 @@
     held = (top & ((wide_lane <= wide_row) | (wide_lane >= HALF))) | (
         (~top) & (wide_lane >= wide_row)
     )
-    for block in range(NC):
-        dense = sum_ref[block * DENSE : (block + 1) * DENSE, :]
-        upper = jnp.concatenate([dense, pltpu.roll(dense, MROW, 1)], axis=0)
-        diag = sum_ref[NC * DENSE + block : NC * DENSE + block + 1, :]
-        diag = pltpu.roll(diag + pltpu.roll(diag, MROW, 1), HALF, 1)
-        lower = jnp.where(lane == row + HALF, diag, pltpu.roll(upper, HALF, 1))
-        given = jnp.concatenate([upper, lower], axis=0)
-        turned = jnp.concatenate([given, given], axis=0).T[:MROW]
-        full_ref[block * MROW : (block + 1) * MROW, :] = jnp.where(held, given, turned)
-    low = iota((NC, LANES), 1) < MROW
-    for chunk in range(HALF):
-        left = full_ref[pl.ds(2 * chunk, NC, stride=MROW), :]
-        right = full_ref[pl.ds(2 * chunk + 1, NC, stride=MROW), :]
-        out_ref[:, chunk * LANES : (chunk + 1) * LANES] = jnp.where(
-            low, left, pltpu.roll(right, MROW, 1)
+    low = iota((ROWS, LANES), 1) < MROW
+    copies = []
+    for start in range(0, NC, ROWS):
+        for block in range(start, start + ROWS):
+            dense = sum_ref[block * DENSE : (block + 1) * DENSE, :]
+            upper = jnp.concatenate([dense, pltpu.roll(dense, MROW, 1)], axis=0)
+            diag = sum_ref[NC * DENSE + block : NC * DENSE + block + 1, :]
+            diag = pltpu.roll(diag + pltpu.roll(diag, MROW, 1), HALF, 1)
+            lower = jnp.where(lane == row + HALF, diag, pltpu.roll(upper, HALF, 1))
+            given = jnp.concatenate([upper, lower], axis=0)
+            turned = jnp.concatenate([given, given], axis=0).T[:MROW]
+            full_ref[block * MROW : (block + 1) * MROW, :] = jnp.where(held, given, turned)
+        for chunk in range(HALF):
+            first = start * MROW + 2 * chunk
+            left = full_ref[pl.ds(first, ROWS, stride=MROW), :]
+            right = full_ref[pl.ds(first + 1, ROWS, stride=MROW), :]
+            out_ref[start : start + ROWS, chunk * LANES : (chunk + 1) * LANES] = jnp.where(
+                low, left, pltpu.roll(right, MROW, 1)
+            )
+        here = pl.ds(start, ROWS)
+        copies.append(
+            pltpu.make_async_copy(out_ref.at[here], out_hbm.at[here], sems.at[start // ROWS])
         )
+        copies[-1].start()
+    for copy in copies:
+        copy.wait()
 
 
 ANY = pl.BlockSpec(memory_space=pl.ANY)
@@ -591,10 +602,12 @@
         coarse_kernel,
         out_shape=jax.ShapeDtypeStruct((NC, MROW * MROW), F32),
         in_specs=[VMEM] * len(got),
-        out_specs=VMEM,
+        out_specs=ANY,
         scratch_shapes=[
+            pltpu.VMEM((NC, MROW * MROW), F32),
             pltpu.VMEM((OWNER_ROWS, LANES), F32),
             pltpu.VMEM((NC * MROW, LANES), F32),
+            pltpu.SemaphoreType.DMA((NC // ROWS,)),
         ],
         compiler_params=params(SMALL),
         cost_estimate=cost(0, 8 << 20),

time: 34.4 us -> 34.4 us (level)
  no operation moved by 1% of the time
where the time goes in v17:
time: 34.4 us; the launch traced here: 34.1 us
  starting transfers between devices  14.9 us (43%)
  Pallas kernels  14.7 us (43%)
  waiting for transfers between devices  2.79 us (8%)
  local copies, waits for them, and re-layouts  0.98 us (3%)
  between operations  0.71 us (2%)
    pallas_call x1, Pallas kernels, shards(): pl.pallas_call(functools.partial(main_kernel, elem_count, face_count), ou...  8.13 us
    ppermute x4, starting transfers between devices, trade(): return lax.ppermute(block, ('face', 'elem'), pairs)  7.66 us
    all_to_all x1, starting transfers between devices, shards(): lax.all_to_all(placed.reshape(devices, capacity, FACE_COEFFS), ('face', '...  4.9 us
    pallas_call x1, Pallas kernels, shards(): pl.pallas_call(functools.partial(gram_kernel, elem_count, face_count, cap...  3.82 us
    all_to_all x1, waiting for transfers between devices, shards(): lax.all_to_all(placed.reshape(devices, capacity, FACE_COEFFS), ('face', '...  2.56 us
    ppermute x3, starting transfers between devices, around(): lax.ppermute(block, axis, [(i, i ^ k) for i in range(count)])  2.31 us
    pallas_call x1, Pallas kernels, shards(): pl.pallas_call(coarse_kernel, out_shape=jax.ShapeDtypeStruct((NC, MROW *...  1.91 us
    unnamed x2, local copies, waits for them, and re-layouts  0.98 us
  transfers between devices with their start and end apart: 8, of which 2 were waited for; matrix products, arithmetic and copies ran while one was open for 0% of the time, Pallas kernels for 30%

profile of v17, /device:TPU:0, one launch (start us, length us, event | category | flops | bytes accessed | tf_op | source)
XLA Modules:
  0.0 34.1 jit_solution(5400958463127212348)
XLA Ops:
  0.6 3.8 %gram.1 = (bf16[512,128]{1,0:T(8,128)(2,1)}, bf16[1408,128]{1,0:T(8,128)(2,1)}, bf16[1088,128]{1,0:T(8,128)(2,1)}) custom-call(s32[96]{0:T(128)} %bitcast.8, s32[96]{0:T(128)} %coarse_hbm.1, bf16[96,6144]{1,0:T(8,128)(2,1)} %tiles_hbm.1, s32[1,64]{1,0:T(1,128)} %bitcast.9, bf16[64,128]{1,0:T(8,128)(2,1)} %trace_hbm.1, s32[3,9]{1,0:T(4,128)} %bitcast.7, ...), custom_call_target="tpu_custom_call" | custom-call | flops 201326592 | bytes 12582912 | tf_op jit(solution)/shard_map/gram/pallas_call | solution.py:506
  4.5 3.0 %collective-permute-start = (bf16[1088,128]{1,0:T(8,128)(2,1)}, bf16[1088,128]{1,0:T(8,128)(2,1)S(1)}, u32[]{:S(2)}, u32[]{:S(2)}) collective-permute-start(bf16[1088,128]{1,0:T(8,128)(2,1)} %get-tuple-element.18), channel_id=1, source_target_pairs={{0,4},{1,9},{2,6},{3,11},{4,0},{5,13},{6,2},{7,15},{8,12},{9,1},{1... | collective-permute-start | bytes 835592 | tf_op jit(solution)/shard_map/ppermute | solution.py:468
  7.5 4.9 %all-to-all-start = ((bf16[32,16,128]{2,1,0:T(8,128)(2,1)}), bf16[32,16,128]{2,1,0:T(8,128)(2,1)S(1)}, u32[]{:S(2)}, u32[]{:S(2)}) async-start(bf16[32,16,128]{2,1,0:T(8,128)(2,1)} %bitcast.6), calls=%async_computation | async-start | bytes 262144 | tf_op jit(solution)/shard_map/all_to_all | solution.py:542
  12.4 0.0 collective-permute-done.came_ref
  12.4 0.0 copy-start
  12.4 1.0 %copy-done = bf16[1408,128]{1,0:T(8,128)(2,1)S(1)} copy-done((bf16[1408,128]{1,0:T(8,128)(2,1)S(1)}, bf16[1408,128]{1,0:T(8,128)(2,1)}, u32[]{:S(2)}) %copy-start) | copy-done | bytes 360472
  13.4 0.1 join.1
  13.5 4.0 %collective-permute-start.4 = (bf16[272,128]{1,0:T(8,128)(2,1)S(1)}, bf16[272,128]{1,0:T(8,128)(2,1)S(1)}, u32[]{:S(2)}, u32[]{:S(2)}) collective-permute-start(bf16[272,128]{1,0:T(8,128)(2,1)S(1)} %get-tuple-element.24), channel_id=1, source_target_pairs={{0,24},{1,21},{2,26},{3,23},{4,28},{5,17},{6,30},{7,19},{8,16},{9,... | collective-permute-start | bytes 208904 | tf_op jit(solution)/shard_map/ppermute | solution.py:468
  17.5 0.0 collective-permute-start.5
  17.5 0.6 %collective-permute-start.6 = (bf16[272,128]{1,0:T(8,128)(2,1)S(1)}, bf16[272,128]{1,0:T(8,128)(2,1)S(1)}, u32[]{:S(2)}, u32[]{:S(2)}) collective-permute-start(bf16[272,128]{1,0:T(8,128)(2,1)S(1)} %get-tuple-element.26), channel_id=1, source_target_pairs={{0,16},{1,17},{2,18},{3,19},{4,20},{5,21},{6,22},{7,23},{8,24},{9,... | collective-permute-start | bytes 208904 | tf_op jit(solution)/shard_map/ppermute | solution.py:468
  18.1 2.6 %all-to-all-done = bf16[32,16,128]{2,1,0:T(8,128)(2,1)S(1)} async-done(((bf16[32,16,128]{2,1,0:T(8,128)(2,1)}), bf16[32,16,128]{2,1,0:T(8,128)(2,1)S(1)}, u32[]{:S(2)}, u32[]{:S(2)}) %all-to-all-start) | async-done | bytes 131104 | tf_op jit(solution)/shard_map/all_to_all | solution.py:542
  20.7 8.1 %condense.1 = (bf16[9,384,384]{2,1,0:T(8,128)(2,1)}, bf16[64,128]{1,0:T(8,128)(2,1)S(1)}, f32[128,128]{1,0:T(8,128)S(1)}) custom-call(bf16[512,128]{1,0:T(8,128)(2,1)S(1)} %bitcast.5, bf16[80,512]{1,0:T(8,128)(2,1)S(1)} %get-tuple-element.19.named_hbm, bf16[9,512,512]{2,1,0:T(8,128)(2,1)} %inverse_hbm.1, bf16[9,512,384]{2,1,0:T(8,128)(2,1)} %coupling_hbm.1), custom_call_target="tpu_custom_call" | custom-call | flops 3170893824 | bytes 10911744 | tf_op jit(solution)/shard_map/condense/pallas_call | solution.py:565
  28.8 0.7 %collective-permute-start.3 = (bf16[64,128]{1,0:T(8,128)(2,1)S(1)}, bf16[64,128]{1,0:T(8,128)(2,1)S(1)}, u32[]{:S(2)}, u32[]{:S(2)}) collective-permute-start(bf16[64,128]{1,0:T(8,128)(2,1)S(1)} %get-tuple-element.22), channel_id=1, source_target_pairs={{0,3},{1,2},{2,1},{3,0},{4,7},{5,6},{6,5},{7,4},{8,11},{9,10},{10,... | collective-permute-start | bytes 49160 | tf_op jit(solution)/shard_map/ppermute | solution.py:452
  29.5 1.6 %collective-permute-start.2 = (bf16[64,128]{1,0:T(8,128)(2,1)S(1)}, bf16[64,128]{1,0:T(8,128)(2,1)S(1)}, u32[]{:S(2)}, u32[]{:S(2)}) collective-permute-start(bf16[64,128]{1,0:T(8,128)(2,1)S(1)} %get-tuple-element.22), channel_id=1, source_target_pairs={{0,2},{1,3},{2,0},{3,1},{4,6},{5,7},{6,4},{7,5},{8,10},{9,11},{10,... | collective-permute-start | bytes 49160 | tf_op jit(solution)/shard_map/ppermute | solution.py:452
  31.1 0.0 collective-permute-done.4.refs_1_
  31.1 0.0 collective-permute-start.1
  31.1 0.0 collective-permute-done.5.refs_2_
  31.1 0.0 collective-permute-done.6.refs_3_
  31.1 1.9 %coarse.1 = f32[16,4096]{1,0:T(8,128)} custom-call(bf16[272,128]{1,0:T(8,128)(2,1)S(1)} %get-tuple-element.23.refs_0_, bf16[272,128]{1,0:T(8,128)(2,1)S(1)} %collective-permute-done.4.refs_1_, bf16[272,128]{1,0:T(8,128)(2,1)S(1)} %collective-permute-done.5.refs_2_, bf16[272,128]{1,0:T(8,128)(2,1)S(1)} %collective-permute-done.6.refs_3_), custom_call_target="tpu_custom_call" | custom-call | bytes 8388608 | tf_op jit(solution)/shard_map/coarse/pallas_call | solution.py:601
  33.0 0.0 collective-permute-done.3.refs_2_
  33.1 0.2 collective-permute-done.2.refs_1_
  33.3 0.0 collective-permute-done.1.refs_0_
  33.3 0.8 %residual.1 = f32[128,128]{1,0:T(8,128)} custom-call(f32[128,128]{1,0:T(8,128)S(1)} %get-tuple-element.21.left_ref, bf16[64,128]{1,0:T(8,128)(2,1)S(1)} %collective-permute-done.1.refs_0_, bf16[64,128]{1,0:T(8,128)(2,1)S(1)} %collective-permute-done.2.refs_1_, bf16[64,128]{1,0:T(8,128)(2,1)S(1)} %collective-permute-done.3.refs_2_), custom_call_target="tpu_custom_call" | custom-call | tf_op jit(solution)/shard_map/residual/pallas_call | solution.py:617
Async XLA Ops:
  4.5 7.9 %collective-permute-start = (bf16[1088,128]{1,0:T(8,128)(2,1)}, bf16[1088,128]{1,0:T(8,128)(2,1)S(1)}, u32[]{:S(2)}, u32[]{:S(2)}) collective-permute-start(bf16[1088,128]{1,0:T(8,128)(2,1)} %get-tuple-element.18), channel_id=1, source_target_pairs={{0,4},{1,9},{2,6},{3,11},{4,0},{5,13},{6,2},{7,15},{8,12},{9,1},{1... | collective-permute-start | bytes 835592 | tf_op jit(solution)/shard_map/ppermute | solution.py:468
  7.5 13.2 %all-to-all-start = ((bf16[32,16,128]{2,1,0:T(8,128)(2,1)}), bf16[32,16,128]{2,1,0:T(8,128)(2,1)S(1)}, u32[]{:S(2)}, u32[]{:S(2)}) async-start(bf16[32,16,128]{2,1,0:T(8,128)(2,1)} %bitcast.6), calls=%async_computation | async-start | bytes 262144 | tf_op jit(solution)/shard_map/all_to_all | solution.py:542
  12.4 1.0 %copy-start = (bf16[1408,128]{1,0:T(8,128)(2,1)S(1)}, bf16[1408,128]{1,0:T(8,128)(2,1)}, u32[]{:S(2)}) copy-start(bf16[1408,128]{1,0:T(8,128)(2,1)} %get-tuple-element.17.kept_ref) | copy-start | bytes 1081348
  13.5 17.6 %collective-permute-start.4 = (bf16[272,128]{1,0:T(8,128)(2,1)S(1)}, bf16[272,128]{1,0:T(8,128)(2,1)S(1)}, u32[]{:S(2)}, u32[]{:S(2)}) collective-permute-start(bf16[272,128]{1,0:T(8,128)(2,1)S(1)} %get-tuple-element.24), channel_id=1, source_target_pairs={{0,24},{1,21},{2,26},{3,23},{4,28},{5,17},{6,30},{7,19},{8,16},{9,... | collective-permute-start | bytes 208904 | tf_op jit(solution)/shard_map/ppermute | solution.py:468
  17.5 13.7 %collective-permute-start.5 = (bf16[272,128]{1,0:T(8,128)(2,1)S(1)}, bf16[272,128]{1,0:T(8,128)(2,1)S(1)}, u32[]{:S(2)}, u32[]{:S(2)}) collective-permute-start(bf16[272,128]{1,0:T(8,128)(2,1)S(1)} %get-tuple-element.25), channel_id=1, source_target_pairs={{0,8},{1,5},{2,10},{3,7},{4,12},{5,1},{6,14},{7,3},{8,0},{9,13},{1... | collective-permute-start | bytes 208904 | tf_op jit(solution)/shard_map/ppermute | solution.py:468
  17.5 13.7 %collective-permute-start.6 = (bf16[272,128]{1,0:T(8,128)(2,1)S(1)}, bf16[272,128]{1,0:T(8,128)(2,1)S(1)}, u32[]{:S(2)}, u32[]{:S(2)}) collective-permute-start(bf16[272,128]{1,0:T(8,128)(2,1)S(1)} %get-tuple-element.26), channel_id=1, source_target_pairs={{0,16},{1,17},{2,18},{3,19},{4,20},{5,21},{6,22},{7,23},{8,24},{9,... | collective-permute-start | bytes 208904 | tf_op jit(solution)/shard_map/ppermute | solution.py:468
  28.8 4.2 %collective-permute-start.3 = (bf16[64,128]{1,0:T(8,128)(2,1)S(1)}, bf16[64,128]{1,0:T(8,128)(2,1)S(1)}, u32[]{:S(2)}, u32[]{:S(2)}) collective-permute-start(bf16[64,128]{1,0:T(8,128)(2,1)S(1)} %get-tuple-element.22), channel_id=1, source_target_pairs={{0,3},{1,2},{2,1},{3,0},{4,7},{5,6},{6,5},{7,4},{8,11},{9,10},{10,... | collective-permute-start | bytes 49160 | tf_op jit(solution)/shard_map/ppermute | solution.py:452
  29.5 3.7 %collective-permute-start.2 = (bf16[64,128]{1,0:T(8,128)(2,1)S(1)}, bf16[64,128]{1,0:T(8,128)(2,1)S(1)}, u32[]{:S(2)}, u32[]{:S(2)}) collective-permute-start(bf16[64,128]{1,0:T(8,128)(2,1)S(1)} %get-tuple-element.22), channel_id=1, source_target_pairs={{0,2},{1,3},{2,0},{3,1},{4,6},{5,7},{6,4},{7,5},{8,10},{9,11},{10,... | collective-permute-start | bytes 49160 | tf_op jit(solution)/shard_map/ppermute | solution.py:452
  31.1 2.2 %collective-permute-start.1 = (bf16[64,128]{1,0:T(8,128)(2,1)S(1)}, bf16[64,128]{1,0:T(8,128)(2,1)S(1)}, u32[]{:S(2)}, u32[]{:S(2)}) collective-permute-start(bf16[64,128]{1,0:T(8,128)(2,1)S(1)} %get-tuple-element.22), channel_id=1, source_target_pairs={{0,1},{1,0},{2,3},{3,2},{4,5},{5,4},{6,7},{7,6},{8,9},{9,8},{10,11... | collective-permute-start | bytes 49160 | tf_op jit(solution)/shard_map/ppermute | solution.py:452

commit v18 on v16

--- a/solution.py
+++ b/solution.py
@@ -125,17 +125,23 @@
         return sum(bit << (bits - 1 - k) for k, bit in enumerate(place))
 
     tiles = tiles_ref.shape[0]
-    copies = [
+    copies = []
+    for k in range(2):
+        here = pl.ds(k * tiles // 2, tiles // 2)
+        copies.append(
+            pltpu.make_async_copy(tiles_hbm.at[here], tiles_ref.at[here], sems.at[4 + k])
+        )
+        copies[-1].start()
+    names = pltpu.make_async_copy(conn_hbm, conn_ref, sems.at[6])
+    names.start()
+    copies += [
         pltpu.make_async_copy(owner_hbm, owner_ref, sems.at[0]),
         pltpu.make_async_copy(coarse_hbm, coarse_ref, sems.at[1]),
         pltpu.make_async_copy(new_owner_hbm, new_owner_ref, sems.at[2]),
         pltpu.make_async_copy(trace_hbm, trace_ref, sems.at[3]),
-        pltpu.make_async_copy(tiles_hbm, tiles_ref, sems.at[4]),
+        pltpu.make_async_copy(rhs_hbm, rhs_ref, sems.at[7]),
     ]
-    names = pltpu.make_async_copy(conn_hbm, conn_ref, sems.at[5])
-    names.start()
-    copies.append(pltpu.make_async_copy(rhs_hbm, rhs_ref, sems.at[6]))
-    for copy in copies:
+    for copy in copies[2:]:
         copy.start()
     for ref in (*accs, *diags):
         ref[...] = jnp.zeros_like(ref)
@@ -280,9 +286,9 @@
         return pltpu.make_async_copy(schur_ref.at[e], schur_hbm.at[e], schur_sems.at[e])
 
     coupling_copy(0).start()
+    inverse_copy(0).start()
     for copy in small:
         copy.start()
-    inverse_copy(0).start()
     coupling_copy(1).start()
     inverse_copy(1).start()
     coupling_copy(2).start()
@@ -511,7 +517,7 @@
             pltpu.SMEM((FACES_PER_ELEM, elements), I32),
             pltpu.VMEM((elements, modes), BF16),
             pltpu.VMEM((PER_FACE, modes), F32),
-            pltpu.SemaphoreType.DMA((7,)),
+            pltpu.SemaphoreType.DMA((8,)),
         ]
         + [pltpu.VMEM(named_shape, BF16)] * paired,
         compiler_params=params(BIG),

time: 34.4 us -> 34.3 us (level)
  transfers between devices with their start and end apart: 8 -> 8, of which waited for: 2 -> 2; matrix products, arithmetic and copies ran while one was open for 0% -> 0% of each run, Pallas kernels for 30% -> 29%
where the time goes in v18:
time: 34.3 us; the launch traced here: 34 us
  starting transfers between devices  14.9 us (43%)
  Pallas kernels  14.6 us (43%)
  waiting for transfers between devices  2.85 us (8%)
  local copies, waits for them, and re-layouts  0.98 us (3%)
  between operations  0.69 us (2%)
    pallas_call x1, Pallas kernels, shards(): pl.pallas_call(functools.partial(main_kernel, elem_count, face_count), ou...  8.09 us
    ppermute x4, starting transfers between devices, trade(): return lax.ppermute(block, ('face', 'elem'), pairs)  7.67 us
    all_to_all x1, starting transfers between devices, shards(): lax.all_to_all(placed.reshape(devices, capacity, FACE_COEFFS), ('face', '...  4.89 us
    pallas_call x1, Pallas kernels, shards(): pl.pallas_call(functools.partial(gram_kernel, elem_count, face_count, cap...  3.79 us
    all_to_all x1, waiting for transfers between devices, shards(): lax.all_to_all(placed.reshape(devices, capacity, FACE_COEFFS), ('face', '...  2.56 us
    ppermute x3, starting transfers between devices, around(): lax.ppermute(block, axis, [(i, i ^ k) for i in range(count)])  2.31 us
    pallas_call x1, Pallas kernels, shards(): pl.pallas_call(coarse_kernel, out_shape=jax.ShapeDtypeStruct((NC, MROW *...  1.87 us
    unnamed x2, local copies, waits for them, and re-layouts  0.98 us
  transfers between devices with their start and end apart: 8, of which 2 were waited for; matrix products, arithmetic and copies ran while one was open for 0% of the time, Pallas kernels for 29%

profile of v18, /device:TPU:0, one launch (start us, length us, event | category | flops | bytes accessed | tf_op | source)
XLA Modules:
  0.0 34.0 jit_solution(9434034013573218667)
XLA Ops:
  0.6 3.8 %gram.1 = (bf16[512,128]{1,0:T(8,128)(2,1)}, bf16[1408,128]{1,0:T(8,128)(2,1)}, bf16[1088,128]{1,0:T(8,128)(2,1)}) custom-call(s32[96]{0:T(128)} %bitcast.8, s32[96]{0:T(128)} %coarse_hbm.1, bf16[96,6144]{1,0:T(8,128)(2,1)} %tiles_hbm.1, s32[1,64]{1,0:T(1,128)} %bitcast.9, bf16[64,128]{1,0:T(8,128)(2,1)} %trace_hbm.1, s32[3,9]{1,0:T(4,128)} %bitcast.7, ...), custom_call_target="tpu_custom_call" | custom-call | flops 201326592 | bytes 12582912 | tf_op jit(solution)/shard_map/gram/pallas_call | solution.py:501
  4.4 3.0 %collective-permute-start = (bf16[1088,128]{1,0:T(8,128)(2,1)}, bf16[1088,128]{1,0:T(8,128)(2,1)S(1)}, u32[]{:S(2)}, u32[]{:S(2)}) collective-permute-start(bf16[1088,128]{1,0:T(8,128)(2,1)} %get-tuple-element.18), channel_id=1, source_target_pairs={{0,4},{1,9},{2,6},{3,11},{4,0},{5,13},{6,2},{7,15},{8,12},{9,1},{1... | collective-permute-start | bytes 835592 | tf_op jit(solution)/shard_map/ppermute | solution.py:463
  7.5 4.9 %all-to-all-start = ((bf16[32,16,128]{2,1,0:T(8,128)(2,1)}), bf16[32,16,128]{2,1,0:T(8,128)(2,1)S(1)}, u32[]{:S(2)}, u32[]{:S(2)}) async-start(bf16[32,16,128]{2,1,0:T(8,128)(2,1)} %bitcast.6), calls=%async_computation | async-start | bytes 262144 | tf_op jit(solution)/shard_map/all_to_all | solution.py:537
  12.4 0.0 collective-permute-done.came_ref
  12.4 0.0 copy-start
  12.4 1.0 %copy-done = bf16[1408,128]{1,0:T(8,128)(2,1)S(1)} copy-done((bf16[1408,128]{1,0:T(8,128)(2,1)S(1)}, bf16[1408,128]{1,0:T(8,128)(2,1)}, u32[]{:S(2)}) %copy-start) | copy-done | bytes 360472
  13.4 0.1 join.1
  13.4 4.0 %collective-permute-start.4 = (bf16[272,128]{1,0:T(8,128)(2,1)S(1)}, bf16[272,128]{1,0:T(8,128)(2,1)S(1)}, u32[]{:S(2)}, u32[]{:S(2)}) collective-permute-start(bf16[272,128]{1,0:T(8,128)(2,1)S(1)} %get-tuple-element.24), channel_id=1, source_target_pairs={{0,24},{1,21},{2,26},{3,23},{4,28},{5,17},{6,30},{7,19},{8,16},{9,... | collective-permute-start | bytes 208904 | tf_op jit(solution)/shard_map/ppermute | solution.py:463
  17.4 0.0 collective-permute-start.5
  17.4 0.6 %collective-permute-start.6 = (bf16[272,128]{1,0:T(8,128)(2,1)S(1)}, bf16[272,128]{1,0:T(8,128)(2,1)S(1)}, u32[]{:S(2)}, u32[]{:S(2)}) collective-permute-start(bf16[272,128]{1,0:T(8,128)(2,1)S(1)} %get-tuple-element.26), channel_id=1, source_target_pairs={{0,16},{1,17},{2,18},{3,19},{4,20},{5,21},{6,22},{7,23},{8,24},{9,... | collective-permute-start | bytes 208904 | tf_op jit(solution)/shard_map/ppermute | solution.py:463
  18.1 2.6 %all-to-all-done = bf16[32,16,128]{2,1,0:T(8,128)(2,1)S(1)} async-done(((bf16[32,16,128]{2,1,0:T(8,128)(2,1)}), bf16[32,16,128]{2,1,0:T(8,128)(2,1)S(1)}, u32[]{:S(2)}, u32[]{:S(2)}) %all-to-all-start) | async-done | bytes 131104 | tf_op jit(solution)/shard_map/all_to_all | solution.py:537
  20.6 8.1 %condense.1 = (bf16[9,384,384]{2,1,0:T(8,128)(2,1)}, bf16[64,128]{1,0:T(8,128)(2,1)S(1)}, f32[128,128]{1,0:T(8,128)S(1)}) custom-call(bf16[512,128]{1,0:T(8,128)(2,1)S(1)} %bitcast.5, bf16[80,512]{1,0:T(8,128)(2,1)S(1)} %get-tuple-element.19.named_hbm, bf16[9,512,512]{2,1,0:T(8,128)(2,1)} %inverse_hbm.1, bf16[9,512,384]{2,1,0:T(8,128)(2,1)} %coupling_hbm.1), custom_call_target="tpu_custom_call" | custom-call | flops 3170893824 | bytes 10911744 | tf_op jit(solution)/shard_map/condense/pallas_call | solution.py:560
  28.7 0.7 %collective-permute-start.3 = (bf16[64,128]{1,0:T(8,128)(2,1)S(1)}, bf16[64,128]{1,0:T(8,128)(2,1)S(1)}, u32[]{:S(2)}, u32[]{:S(2)}) collective-permute-start(bf16[64,128]{1,0:T(8,128)(2,1)S(1)} %get-tuple-element.22), channel_id=1, source_target_pairs={{0,3},{1,2},{2,1},{3,0},{4,7},{5,6},{6,5},{7,4},{8,11},{9,10},{10,... | collective-permute-start | bytes 49160 | tf_op jit(solution)/shard_map/ppermute | solution.py:447
  29.5 1.6 %collective-permute-start.2 = (bf16[64,128]{1,0:T(8,128)(2,1)S(1)}, bf16[64,128]{1,0:T(8,128)(2,1)S(1)}, u32[]{:S(2)}, u32[]{:S(2)}) collective-permute-start(bf16[64,128]{1,0:T(8,128)(2,1)S(1)} %get-tuple-element.22), channel_id=1, source_target_pairs={{0,2},{1,3},{2,0},{3,1},{4,6},{5,7},{6,4},{7,5},{8,10},{9,11},{10,... | collective-permute-start | bytes 49160 | tf_op jit(solution)/shard_map/ppermute | solution.py:447
  31.0 0.0 collective-permute-done.4.refs_1_
  31.0 0.0 collective-permute-start.1
  31.0 0.0 collective-permute-done.5.refs_2_
  31.0 0.0 collective-permute-done.6.refs_3_
  31.1 1.9 %coarse.1 = f32[16,4096]{1,0:T(8,128)} custom-call(bf16[272,128]{1,0:T(8,128)(2,1)S(1)} %get-tuple-element.23.refs_0_, bf16[272,128]{1,0:T(8,128)(2,1)S(1)} %collective-permute-done.4.refs_1_, bf16[272,128]{1,0:T(8,128)(2,1)S(1)} %collective-permute-done.5.refs_2_, bf16[272,128]{1,0:T(8,128)(2,1)S(1)} %collective-permute-done.6.refs_3_), custom_call_target="tpu_custom_call" | custom-call | bytes 8388608 | tf_op jit(solution)/shard_map/coarse/pallas_call | solution.py:596
  32.9 0.0 collective-permute-done.3.refs_2_
  32.9 0.3 collective-permute-done.2.refs_1_
  33.2 0.0 collective-permute-done.1.refs_0_
  33.2 0.8 %residual.1 = f32[128,128]{1,0:T(8,128)} custom-call(f32[128,128]{1,0:T(8,128)S(1)} %get-tuple-element.21.left_ref, bf16[64,128]{1,0:T(8,128)(2,1)S(1)} %collective-permute-done.1.refs_0_, bf16[64,128]{1,0:T(8,128)(2,1)S(1)} %collective-permute-done.2.refs_1_, bf16[64,128]{1,0:T(8,128)(2,1)S(1)} %collective-permute-done.3.refs_2_), custom_call_target="tpu_custom_call" | custom-call | tf_op jit(solution)/shard_map/residual/pallas_call | solution.py:610
Async XLA Ops:
  4.4 7.9 %collective-permute-start = (bf16[1088,128]{1,0:T(8,128)(2,1)}, bf16[1088,128]{1,0:T(8,128)(2,1)S(1)}, u32[]{:S(2)}, u32[]{:S(2)}) collective-permute-start(bf16[1088,128]{1,0:T(8,128)(2,1)} %get-tuple-element.18), channel_id=1, source_target_pairs={{0,4},{1,9},{2,6},{3,11},{4,0},{5,13},{6,2},{7,15},{8,12},{9,1},{1... | collective-permute-start | bytes 835592 | tf_op jit(solution)/shard_map/ppermute | solution.py:463
  7.5 13.2 %all-to-all-start = ((bf16[32,16,128]{2,1,0:T(8,128)(2,1)}), bf16[32,16,128]{2,1,0:T(8,128)(2,1)S(1)}, u32[]{:S(2)}, u32[]{:S(2)}) async-start(bf16[32,16,128]{2,1,0:T(8,128)(2,1)} %bitcast.6), calls=%async_computation | async-start | bytes 262144 | tf_op jit(solution)/shard_map/all_to_all | solution.py:537
  12.4 1.0 %copy-start = (bf16[1408,128]{1,0:T(8,128)(2,1)S(1)}, bf16[1408,128]{1,0:T(8,128)(2,1)}, u32[]{:S(2)}) copy-start(bf16[1408,128]{1,0:T(8,128)(2,1)} %get-tuple-element.17.kept_ref) | copy-start | bytes 1081348
  13.4 17.6 %collective-permute-start.4 = (bf16[272,128]{1,0:T(8,128)(2,1)S(1)}, bf16[272,128]{1,0:T(8,128)(2,1)S(1)}, u32[]{:S(2)}, u32[]{:S(2)}) collective-permute-start(bf16[272,128]{1,0:T(8,128)(2,1)S(1)} %get-tuple-element.24), channel_id=1, source_target_pairs={{0,24},{1,21},{2,26},{3,23},{4,28},{5,17},{6,30},{7,19},{8,16},{9,... | collective-permute-start | bytes 208904 | tf_op jit(solution)/shard_map/ppermute | solution.py:463
  17.4 13.6 %collective-permute-start.5 = (bf16[272,128]{1,0:T(8,128)(2,1)S(1)}, bf16[272,128]{1,0:T(8,128)(2,1)S(1)}, u32[]{:S(2)}, u32[]{:S(2)}) collective-permute-start(bf16[272,128]{1,0:T(8,128)(2,1)S(1)} %get-tuple-element.25), channel_id=1, source_target_pairs={{0,8},{1,5},{2,10},{3,7},{4,12},{5,1},{6,14},{7,3},{8,0},{9,13},{1... | collective-permute-start | bytes 208904 | tf_op jit(solution)/shard_map/ppermute | solution.py:463
  17.4 13.6 %collective-permute-start.6 = (bf16[272,128]{1,0:T(8,128)(2,1)S(1)}, bf16[272,128]{1,0:T(8,128)(2,1)S(1)}, u32[]{:S(2)}, u32[]{:S(2)}) collective-permute-start(bf16[272,128]{1,0:T(8,128)(2,1)S(1)} %get-tuple-element.26), channel_id=1, source_target_pairs={{0,16},{1,17},{2,18},{3,19},{4,20},{5,21},{6,22},{7,23},{8,24},{9,... | collective-permute-start | bytes 208904 | tf_op jit(solution)/shard_map/ppermute | solution.py:463
  28.7 4.2 %collective-permute-start.3 = (bf16[64,128]{1,0:T(8,128)(2,1)S(1)}, bf16[64,128]{1,0:T(8,128)(2,1)S(1)}, u32[]{:S(2)}, u32[]{:S(2)}) collective-permute-start(bf16[64,128]{1,0:T(8,128)(2,1)S(1)} %get-tuple-element.22), channel_id=1, source_target_pairs={{0,3},{1,2},{2,1},{3,0},{4,7},{5,6},{6,5},{7,4},{8,11},{9,10},{10,... | collective-permute-start | bytes 49160 | tf_op jit(solution)/shard_map/ppermute | solution.py:447
  29.5 3.7 %collective-permute-start.2 = (bf16[64,128]{1,0:T(8,128)(2,1)S(1)}, bf16[64,128]{1,0:T(8,128)(2,1)S(1)}, u32[]{:S(2)}, u32[]{:S(2)}) collective-permute-start(bf16[64,128]{1,0:T(8,128)(2,1)S(1)} %get-tuple-element.22), channel_id=1, source_target_pairs={{0,2},{1,3},{2,0},{3,1},{4,6},{5,7},{6,4},{7,5},{8,10},{9,11},{10,... | collective-permute-start | bytes 49160 | tf_op jit(solution)/shard_map/ppermute | solution.py:447
  31.0 2.2 %collective-permute-start.1 = (bf16[64,128]{1,0:T(8,128)(2,1)S(1)}, bf16[64,128]{1,0:T(8,128)(2,1)S(1)}, u32[]{:S(2)}, u32[]{:S(2)}) collective-permute-start(bf16[64,128]{1,0:T(8,128)(2,1)S(1)} %get-tuple-element.22), channel_id=1, source_target_pairs={{0,1},{1,0},{2,3},{3,2},{4,5},{5,4},{6,7},{7,6},{8,9},{9,8},{10,11... | collective-permute-start | bytes 49160 | tf_op jit(solution)/shard_map/ppermute | solution.py:447

commit v19 on v18

--- a/solution.py
+++ b/solution.py
@@ -507,7 +507,7 @@
             pltpu.SMEM((tile_count,), I32),
             pltpu.SMEM((tile_count,), I32),
             pltpu.VMEM(mortar_tiles.shape, BF16),
-            pltpu.VMEM((tile_count * PITCH, LANES), F32),
+            pltpu.VMEM(((tile_count + 1) * PITCH, LANES), F32),
             pltpu.VMEM(sums_shape, F32),
             pltpu.VMEM(sums_shape, F32),
             pltpu.VMEM((blocks, LANES), F32),
@@ -600,7 +600,7 @@
         out_specs=VMEM,
         scratch_shapes=[
             pltpu.VMEM((OWNER_ROWS, LANES), F32),
-            pltpu.VMEM((NC * MROW, LANES), F32),
+            pltpu.VMEM(((NC + 1) * MROW, LANES), F32),
         ],
         compiler_params=params(SMALL),
         cost_estimate=cost(0, 8 << 20),

time: 34.3 us -> 34.3 us (level)
  no operation moved by 1% of the time
where the time goes in v19:
time: 34.3 us; the launch traced here: 34 us
  starting transfers between devices  14.9 us (43%)
  Pallas kernels  14.6 us (43%)
  waiting for transfers between devices  2.85 us (8%)
  local copies, waits for them, and re-layouts  0.98 us (3%)
  between operations  0.69 us (2%)
    pallas_call x1, Pallas kernels, shards(): pl.pallas_call(functools.partial(main_kernel, elem_count, face_count), ou...  8.09 us
    ppermute x4, starting transfers between devices, trade(): return lax.ppermute(block, ('face', 'elem'), pairs)  7.66 us
    all_to_all x1, starting transfers between devices, shards(): lax.all_to_all(placed.reshape(devices, capacity, FACE_COEFFS), ('face', '...  4.89 us
    pallas_call x1, Pallas kernels, shards(): pl.pallas_call(functools.partial(gram_kernel, elem_count, face_count, cap...  3.81 us
    all_to_all x1, waiting for transfers between devices, shards(): lax.all_to_all(placed.reshape(devices, capacity, FACE_COEFFS), ('face', '...  2.57 us
    ppermute x3, starting transfers between devices, around(): lax.ppermute(block, axis, [(i, i ^ k) for i in range(count)])  2.31 us
    pallas_call x1, Pallas kernels, shards(): pl.pallas_call(coarse_kernel, out_shape=jax.ShapeDtypeStruct((NC, MROW *...  1.87 us
    unnamed x2, local copies, waits for them, and re-layouts  0.98 us
  transfers between devices with their start and end apart: 8, of which 2 were waited for; matrix products, arithmetic and copies ran while one was open for 0% of the time, Pallas kernels for 29%

profile of v19, /device:TPU:0, one launch (start us, length us, event | category | flops | bytes accessed | tf_op | source)
XLA Modules:
  0.0 34.0 jit_solution(4375107911164847476)
XLA Ops:
  0.6 3.8 %gram.1 = (bf16[512,128]{1,0:T(8,128)(2,1)}, bf16[1408,128]{1,0:T(8,128)(2,1)}, bf16[1088,128]{1,0:T(8,128)(2,1)}) custom-call(s32[96]{0:T(128)} %bitcast.8, s32[96]{0:T(128)} %coarse_hbm.1, bf16[96,6144]{1,0:T(8,128)(2,1)} %tiles_hbm.1, s32[1,64]{1,0:T(1,128)} %bitcast.9, bf16[64,128]{1,0:T(8,128)(2,1)} %trace_hbm.1, s32[3,9]{1,0:T(4,128)} %bitcast.7, ...), custom_call_target="tpu_custom_call" | custom-call | flops 201326592 | bytes 12582912 | tf_op jit(solution)/shard_map/gram/pallas_call | solution.py:501
  4.4 3.0 %collective-permute-start = (bf16[1088,128]{1,0:T(8,128)(2,1)}, bf16[1088,128]{1,0:T(8,128)(2,1)S(1)}, u32[]{:S(2)}, u32[]{:S(2)}) collective-permute-start(bf16[1088,128]{1,0:T(8,128)(2,1)} %get-tuple-element.18), channel_id=1, source_target_pairs={{0,4},{1,9},{2,6},{3,11},{4,0},{5,13},{6,2},{7,15},{8,12},{9,1},{1... | collective-permute-start | bytes 835592 | tf_op jit(solution)/shard_map/ppermute | solution.py:463
  7.5 4.9 %all-to-all-start = ((bf16[32,16,128]{2,1,0:T(8,128)(2,1)}), bf16[32,16,128]{2,1,0:T(8,128)(2,1)S(1)}, u32[]{:S(2)}, u32[]{:S(2)}) async-start(bf16[32,16,128]{2,1,0:T(8,128)(2,1)} %bitcast.6), calls=%async_computation | async-start | bytes 262144 | tf_op jit(solution)/shard_map/all_to_all | solution.py:537
  12.4 0.0 collective-permute-done.came_ref
  12.4 0.0 copy-start
  12.4 1.0 %copy-done = bf16[1408,128]{1,0:T(8,128)(2,1)S(1)} copy-done((bf16[1408,128]{1,0:T(8,128)(2,1)S(1)}, bf16[1408,128]{1,0:T(8,128)(2,1)}, u32[]{:S(2)}) %copy-start) | copy-done | bytes 360472
  13.4 0.1 join.1
  13.4 4.0 %collective-permute-start.4 = (bf16[272,128]{1,0:T(8,128)(2,1)S(1)}, bf16[272,128]{1,0:T(8,128)(2,1)S(1)}, u32[]{:S(2)}, u32[]{:S(2)}) collective-permute-start(bf16[272,128]{1,0:T(8,128)(2,1)S(1)} %get-tuple-element.24), channel_id=1, source_target_pairs={{0,24},{1,21},{2,26},{3,23},{4,28},{5,17},{6,30},{7,19},{8,16},{9,... | collective-permute-start | bytes 208904 | tf_op jit(solution)/shard_map/ppermute | solution.py:463
  17.4 0.0 collective-permute-start.5
  17.4 0.6 %collective-permute-start.6 = (bf16[272,128]{1,0:T(8,128)(2,1)S(1)}, bf16[272,128]{1,0:T(8,128)(2,1)S(1)}, u32[]{:S(2)}, u32[]{:S(2)}) collective-permute-start(bf16[272,128]{1,0:T(8,128)(2,1)S(1)} %get-tuple-element.26), channel_id=1, source_target_pairs={{0,16},{1,17},{2,18},{3,19},{4,20},{5,21},{6,22},{7,23},{8,24},{9,... | collective-permute-start | bytes 208904 | tf_op jit(solution)/shard_map/ppermute | solution.py:463
  18.1 2.6 %all-to-all-done = bf16[32,16,128]{2,1,0:T(8,128)(2,1)S(1)} async-done(((bf16[32,16,128]{2,1,0:T(8,128)(2,1)}), bf16[32,16,128]{2,1,0:T(8,128)(2,1)S(1)}, u32[]{:S(2)}, u32[]{:S(2)}) %all-to-all-start) | async-done | bytes 131104 | tf_op jit(solution)/shard_map/all_to_all | solution.py:537
  20.6 8.1 %condense.1 = (bf16[9,384,384]{2,1,0:T(8,128)(2,1)}, bf16[64,128]{1,0:T(8,128)(2,1)S(1)}, f32[128,128]{1,0:T(8,128)S(1)}) custom-call(bf16[512,128]{1,0:T(8,128)(2,1)S(1)} %bitcast.5, bf16[80,512]{1,0:T(8,128)(2,1)S(1)} %get-tuple-element.19.named_hbm, bf16[9,512,512]{2,1,0:T(8,128)(2,1)} %inverse_hbm.1, bf16[9,512,384]{2,1,0:T(8,128)(2,1)} %coupling_hbm.1), custom_call_target="tpu_custom_call" | custom-call | flops 3170893824 | bytes 10911744 | tf_op jit(solution)/shard_map/condense/pallas_call | solution.py:560
  28.7 0.7 %collective-permute-start.3 = (bf16[64,128]{1,0:T(8,128)(2,1)S(1)}, bf16[64,128]{1,0:T(8,128)(2,1)S(1)}, u32[]{:S(2)}, u32[]{:S(2)}) collective-permute-start(bf16[64,128]{1,0:T(8,128)(2,1)S(1)} %get-tuple-element.22), channel_id=1, source_target_pairs={{0,3},{1,2},{2,1},{3,0},{4,7},{5,6},{6,5},{7,4},{8,11},{9,10},{10,... | collective-permute-start | bytes 49160 | tf_op jit(solution)/shard_map/ppermute | solution.py:447
  29.5 1.6 %collective-permute-start.2 = (bf16[64,128]{1,0:T(8,128)(2,1)S(1)}, bf16[64,128]{1,0:T(8,128)(2,1)S(1)}, u32[]{:S(2)}, u32[]{:S(2)}) collective-permute-start(bf16[64,128]{1,0:T(8,128)(2,1)S(1)} %get-tuple-element.22), channel_id=1, source_target_pairs={{0,2},{1,3},{2,0},{3,1},{4,6},{5,7},{6,4},{7,5},{8,10},{9,11},{10,... | collective-permute-start | bytes 49160 | tf_op jit(solution)/shard_map/ppermute | solution.py:447
  31.0 0.0 collective-permute-done.4.refs_1_
  31.1 0.0 collective-permute-start.1
  31.1 0.0 collective-permute-done.5.refs_2_
  31.1 0.0 collective-permute-done.6.refs_3_
  31.1 1.9 %coarse.1 = f32[16,4096]{1,0:T(8,128)} custom-call(bf16[272,128]{1,0:T(8,128)(2,1)S(1)} %get-tuple-element.23.refs_0_, bf16[272,128]{1,0:T(8,128)(2,1)S(1)} %collective-permute-done.4.refs_1_, bf16[272,128]{1,0:T(8,128)(2,1)S(1)} %collective-permute-done.5.refs_2_, bf16[272,128]{1,0:T(8,128)(2,1)S(1)} %collective-permute-done.6.refs_3_), custom_call_target="tpu_custom_call" | custom-call | bytes 8388608 | tf_op jit(solution)/shard_map/coarse/pallas_call | solution.py:596
  32.9 0.0 collective-permute-done.3.refs_2_
  32.9 0.3 collective-permute-done.2.refs_1_
  33.2 0.0 collective-permute-done.1.refs_0_
  33.2 0.8 %residual.1 = f32[128,128]{1,0:T(8,128)} custom-call(f32[128,128]{1,0:T(8,128)S(1)} %get-tuple-element.21.left_ref, bf16[64,128]{1,0:T(8,128)(2,1)S(1)} %collective-permute-done.1.refs_0_, bf16[64,128]{1,0:T(8,128)(2,1)S(1)} %collective-permute-done.2.refs_1_, bf16[64,128]{1,0:T(8,128)(2,1)S(1)} %collective-permute-done.3.refs_2_), custom_call_target="tpu_custom_call" | custom-call | tf_op jit(solution)/shard_map/residual/pallas_call | solution.py:610
Async XLA Ops:
  4.4 7.9 %collective-permute-start = (bf16[1088,128]{1,0:T(8,128)(2,1)}, bf16[1088,128]{1,0:T(8,128)(2,1)S(1)}, u32[]{:S(2)}, u32[]{:S(2)}) collective-permute-start(bf16[1088,128]{1,0:T(8,128)(2,1)} %get-tuple-element.18), channel_id=1, source_target_pairs={{0,4},{1,9},{2,6},{3,11},{4,0},{5,13},{6,2},{7,15},{8,12},{9,1},{1... | collective-permute-start | bytes 835592 | tf_op jit(solution)/shard_map/ppermute | solution.py:463
  7.5 13.2 %all-to-all-start = ((bf16[32,16,128]{2,1,0:T(8,128)(2,1)}), bf16[32,16,128]{2,1,0:T(8,128)(2,1)S(1)}, u32[]{:S(2)}, u32[]{:S(2)}) async-start(bf16[32,16,128]{2,1,0:T(8,128)(2,1)} %bitcast.6), calls=%async_computation | async-start | bytes 262144 | tf_op jit(solution)/shard_map/all_to_all | solution.py:537
  12.4 1.0 %copy-start = (bf16[1408,128]{1,0:T(8,128)(2,1)S(1)}, bf16[1408,128]{1,0:T(8,128)(2,1)}, u32[]{:S(2)}) copy-start(bf16[1408,128]{1,0:T(8,128)(2,1)} %get-tuple-element.17.kept_ref) | copy-start | bytes 1081348
  13.4 17.6 %collective-permute-start.4 = (bf16[272,128]{1,0:T(8,128)(2,1)S(1)}, bf16[272,128]{1,0:T(8,128)(2,1)S(1)}, u32[]{:S(2)}, u32[]{:S(2)}) collective-permute-start(bf16[272,128]{1,0:T(8,128)(2,1)S(1)} %get-tuple-element.24), channel_id=1, source_target_pairs={{0,24},{1,21},{2,26},{3,23},{4,28},{5,17},{6,30},{7,19},{8,16},{9,... | collective-permute-start | bytes 208904 | tf_op jit(solution)/shard_map/ppermute | solution.py:463
  17.4 13.6 %collective-permute-start.5 = (bf16[272,128]{1,0:T(8,128)(2,1)S(1)}, bf16[272,128]{1,0:T(8,128)(2,1)S(1)}, u32[]{:S(2)}, u32[]{:S(2)}) collective-permute-start(bf16[272,128]{1,0:T(8,128)(2,1)S(1)} %get-tuple-element.25), channel_id=1, source_target_pairs={{0,8},{1,5},{2,10},{3,7},{4,12},{5,1},{6,14},{7,3},{8,0},{9,13},{1... | collective-permute-start | bytes 208904 | tf_op jit(solution)/shard_map/ppermute | solution.py:463
  17.4 13.6 %collective-permute-start.6 = (bf16[272,128]{1,0:T(8,128)(2,1)S(1)}, bf16[272,128]{1,0:T(8,128)(2,1)S(1)}, u32[]{:S(2)}, u32[]{:S(2)}) collective-permute-start(bf16[272,128]{1,0:T(8,128)(2,1)S(1)} %get-tuple-element.26), channel_id=1, source_target_pairs={{0,16},{1,17},{2,18},{3,19},{4,20},{5,21},{6,22},{7,23},{8,24},{9,... | collective-permute-start | bytes 208904 | tf_op jit(solution)/shard_map/ppermute | solution.py:463
  28.7 4.2 %collective-permute-start.3 = (bf16[64,128]{1,0:T(8,128)(2,1)S(1)}, bf16[64,128]{1,0:T(8,128)(2,1)S(1)}, u32[]{:S(2)}, u32[]{:S(2)}) collective-permute-start(bf16[64,128]{1,0:T(8,128)(2,1)S(1)} %get-tuple-element.22), channel_id=1, source_target_pairs={{0,3},{1,2},{2,1},{3,0},{4,7},{5,6},{6,5},{7,4},{8,11},{9,10},{10,... | collective-permute-start | bytes 49160 | tf_op jit(solution)/shard_map/ppermute | solution.py:447
  29.5 3.7 %collective-permute-start.2 = (bf16[64,128]{1,0:T(8,128)(2,1)S(1)}, bf16[64,128]{1,0:T(8,128)(2,1)S(1)}, u32[]{:S(2)}, u32[]{:S(2)}) collective-permute-start(bf16[64,128]{1,0:T(8,128)(2,1)S(1)} %get-tuple-element.22), channel_id=1, source_target_pairs={{0,2},{1,3},{2,0},{3,1},{4,6},{5,7},{6,4},{7,5},{8,10},{9,11},{10,... | collective-permute-start | bytes 49160 | tf_op jit(solution)/shard_map/ppermute | solution.py:447
  31.1 2.2 %collective-permute-start.1 = (bf16[64,128]{1,0:T(8,128)(2,1)S(1)}, bf16[64,128]{1,0:T(8,128)(2,1)S(1)}, u32[]{:S(2)}, u32[]{:S(2)}) collective-permute-start(bf16[64,128]{1,0:T(8,128)(2,1)S(1)} %get-tuple-element.22), channel_id=1, source_target_pairs={{0,1},{1,0},{2,3},{3,2},{4,5},{5,4},{6,7},{7,6},{8,9},{9,8},{10,11... | collective-permute-start | bytes 49160 | tf_op jit(solution)/shard_map/ppermute | solution.py:447
